TPU v7x, 32 devices: a whole 2x2x4 slice. The times are simulated.
32 devices in a mesh: dp: 4 (over y, x), seq: 8 (over z, core).
Axes of the slice: x: 2, y: 2, z: 4, core: 2. Of those that a mesh axis runs over, the one named last changes fastest.
Arguments:
- tokens: bfloat16 [8, 1024, 768], P('dp', 'seq'), may hold values from -6 to 6
- query_weight: float32 [768, 768], P(('dp', 'seq')), may hold values from -0.21875 to 0.21875
- query_bias: float32 [768], P(('dp', 'seq')), may hold values from -3 to 3
- key_weight: float32 [768, 768], P(('dp', 'seq')), may hold values from -0.21875 to 0.21875
- value_weight: float32 [768, 768], P(('dp', 'seq')), may hold values from -0.21875 to 0.21875
- value_bias: float32 [768], P(('dp', 'seq')), may hold values from -3 to 3
- out_weight: float32 [768, 768], P(('dp', 'seq')), may hold values from -0.875 to 0.875
- out_bias: float32 [768], P(('dp', 'seq')), may hold values from -3 to 3
- first_gain: float32 [768], P(('dp', 'seq')), may hold values from 0.5 to 1.5
- attention_norm_shift: float32 [768], P(('dp', 'seq')), may hold values from -3 to 3
- expand_weight: float32 [768, 3072], P(('dp', 'seq')), may hold values from -0.21875 to 0.21875
- expand_bias: float32 [3072], P(('dp', 'seq')), may hold values from -3 to 3
- reduce_weight: float32 [3072, 768], P(('dp', 'seq')), may hold values from -0.109375 to 0.109375
- reduce_bias: float32 [768], P(('dp', 'seq')), may hold values from -3 to 3
- second_gain: float32 [768], P(('dp', 'seq')), may hold values from 0.5 to 1.5
- second_shift: float32 [768], P(('dp', 'seq')), may hold values from -3 to 3
- lengths: int32 [8, 64], P('dp'), may hold values from 0 to 896, as said below
- cotangent: bfloat16 [8, 1024, 768], P('dp', 'seq'), may hold values from -6 to 6
Outputs:
- activations: bfloat16 [8, 1024, 768], P('dp', 'seq')
- tokens_gradient: float32 [8, 1024, 768], P('dp', 'seq')
- query_weight_gradient: float32 [768, 768], P(('dp', 'seq'))
- query_bias_gradient: float32 [768], P(('dp', 'seq'))
- key_weight_gradient: float32 [768, 768], P(('dp', 'seq'))
- value_weight_gradient: float32 [768, 768], P(('dp', 'seq'))
- value_bias_gradient: float32 [768], P(('dp', 'seq'))
- out_weight_gradient: float32 [768, 768], P(('dp', 'seq'))
- output_bias_gradient: float32 [768], P(('dp', 'seq'))
- first_gain_gradient: float32 [768], P(('dp', 'seq'))
- first_shift_gradient: float32 [768], P(('dp', 'seq'))
- expand_weight_gradient: float32 [768, 3072], P(('dp', 'seq'))
- expand_bias_gradient: float32 [3072], P(('dp', 'seq'))
- reduce_weight_gradient: float32 [3072, 768], P(('dp', 'seq'))
- reduce_bias_gradient: float32 [768], P(('dp', 'seq'))
- second_gain_gradient: float32 [768], P(('dp', 'seq'))
- second_shift_gradient: float32 [768], P(('dp', 'seq'))
Inputs may be any that keep to these rules, and one draw needn't show every extreme that they name: The 64 lengths of a stream sum to 1024; unused slots are 0. In each group of 2 streams that share an index of dp, one stream has an item of exactly 896 rows that starts within the first 128 rows and ends within the last 128 rows.
All inputs are finite; a program needn't handle non-finite values.
Results may differ from a plain program's by a relative error of at most 0.018.
Values may be sent and summed in bfloat16 or wider, within the bound.
No kernel may reach another device: no remote copies, remote signals or barrier semaphores. Data moves between devices by JAX's collectives and lax.ppermute only.
A program may use at most 192 MiB of HBM per device.

v0:
```python
import functools

import jax
import jax.numpy as jnp
from jax import lax
from jax.experimental.layout import Layout, with_layout_constraint
from jax.experimental import pallas as pl
from jax.experimental.pallas import tpu as pltpu
from jax.sharding import PartitionSpec as P

D = 768
HEADS = 12
HD = 64
FF = 3072
HALF = D // 2
UNITS = FF // 2
PAIR = 2 * HD
PAIRS = HALF // PAIR
NEGATIVE = -1e30
EPSILON = 1e-12
BF = jnp.bfloat16
F32 = jnp.float32
VMEM_LIMIT = 56 * 1024 * 1024
QUICK = pl.CostEstimate(flops=0, bytes_accessed=0, transcendentals=0)


def nn(left, right):
    return lax.dot_general(left, right, (((1,), (0,)), ((), ())), preferred_element_type=F32)


def nt(left, right):
    return lax.dot_general(left, right, (((1,), (1,)), ((), ())), preferred_element_type=F32)


def tn(left, right):
    return lax.dot_general(left, right, (((0,), (0,)), ((), ())), preferred_element_type=F32)


def local_copies(place, sources, shapes, plan, name, late=()):
    def kernel(place_ref, *refs):
        ins = refs[: len(sources)]
        outs = refs[len(sources) + len(late) :]
        dp = place_ref[0]
        z = place_ref[1]
        for source, source_index, target, target_index in plan:
            outs[target][target_index(dp, z)] = ins[source][source_index(dp, z)]

    moved = 2 * sum(functools.reduce(lambda a, b: a * b, s) for s in shapes)
    return pl.pallas_call(
        kernel,
        in_specs=[pl.BlockSpec(memory_space=pltpu.SMEM)]
        + [pl.BlockSpec(memory_space=pltpu.VMEM)] * len(sources)
        + [pl.BlockSpec(memory_space=pl.ANY)] * len(late),
        out_specs=[pl.BlockSpec(memory_space=pltpu.VMEM)] * len(shapes),
        out_shape=[jax.ShapeDtypeStruct(shape, BF) for shape in shapes],
        compiler_params=pltpu.CompilerParams(vmem_limit_bytes=VMEM_LIMIT),
        cost_estimate=QUICK,
        name=name,
    )(place, *sources, *late)


def first_columns(place, weights, vectors):
    block = weights[0].shape[0]
    lanes = len(weights) * HALF + 128

    def kernel(place_ref, *refs):
        ins, (mine_ref, theirs_ref, square_ref) = refs[: len(weights) + len(vectors)], refs[-3:]
        core = place_ref[2]
        square_ref[...] = jnp.zeros_like(square_ref)
        row = 0
        for ref in ins[len(weights) :]:
            for part in range(ref.shape[0] // block):
                square_ref[row : row + 1, 0:block] = ref[part * block : (part + 1) * block].reshape(1, block)
                row += 1
        columns = square_ref[...].T[:block].astype(BF)
        for out, side in ((mine_ref, core), (theirs_ref, 1 - core)):
            for i in range(len(weights)):
                picked = ins[i][:, pl.ds(pl.multiple_of(side * HALF, 128), HALF)]
                out[:, i * HALF : (i + 1) * HALF] = picked.astype(BF)
            out[:, len(weights) * HALF :] = columns

    shape = jax.ShapeDtypeStruct((block, lanes), BF)
    return pl.pallas_call(
        kernel,
        in_specs=[pl.BlockSpec(memory_space=pltpu.SMEM)]
        + [pl.BlockSpec(memory_space=pltpu.VMEM)] * (len(weights) + len(vectors)),
        out_specs=[pl.BlockSpec(memory_space=pltpu.VMEM)] * 2,
        out_shape=[shape, shape],
        scratch_shapes=[pltpu.VMEM((128, 128), F32)],
        name="first_columns",
    )(place, *weights, *vectors)


def at_lanes(start, count):
    return pl.ds(start, count)


def core_swap(value, seq):
    return lax.ppermute(value, "seq", [(i, i ^ 1) for i in range(seq)])


def z_move(value, step, seq):
    return lax.ppermute(value, "seq", [(i, i ^ (2 * step)) for i in range(seq)])


def dp_move(value, step, dps):
    return lax.ppermute(value, "dp", [(i, i ^ step) for i in range(dps)])


def tied(value, *others):
    return lax.optimization_barrier((value, others))[0]


def z_moves(value, seq):
    return [value] + [z_move(value, j, seq) for j in range(1, seq // 2)]


def gather_dp_first(value, dps):
    return [value] + [dp_move(value, k, dps) for k in range(1, 3 if dps == 4 else dps)]


def gather_dp_rest(blocks, dps):
    if dps != 4:
        return blocks
    half = blocks[0].shape[0] // 2
    return blocks + [dp_move(blocks[2][:half], 1, dps), dp_move(blocks[1][half:], 2, dps)]


def dp_pieces(dps, zs):
    half = zs // 2
    for k in range(dps):
        for j in range(zs):
            if dps == 4 and k == 3:
                yield (3, j, k, j) if j < half else (4, j - half, k, j)
            else:
                yield k, j, k, j


def scatter_slots(dps, zs):
    if dps != 4:
        return {(k, j): (k, j) for k in range(dps) for j in range(zs)}, [zs] * dps
    half = zs // 2
    slots = {}
    for j in range(half):
        low, high = j, half + j
        slots[0, low], slots[0, high] = (0, low), (0, high)
        slots[1, low], slots[3, low] = (1, low), (1, half + j)
        slots[2, high], slots[3, high] = (2, j), (2, half + j)
        slots[1, high] = (3, j)
        slots[2, low] = (4, j)
    return slots, [zs, zs, zs, half, half]


def wide_sum(terms):
    return functools.reduce(jnp.add, [t.astype(F32) for t in terms])


def scatter_dp_first(packs, dps):
    if dps != 4:
        return [dp_move(packs[k], k, dps) for k in range(1, dps)]
    return [dp_move(packs[1], 1, dps), dp_move(packs[2], 2, dps)]


def scatter_dp_middle(packs, came, dps):
    if dps != 4:
        return []
    half = packs[3].shape[0]
    return [
        wide_sum([packs[4], came[0][half:]]).astype(BF),
        wide_sum([packs[3], came[1][half:]]).astype(BF),
    ]


def scatter_dp_rest(packs, came, onward, dps, tie=lambda came: came):
    if dps != 4:
        came = tie(came)
        return [wide_sum([packs[0][j]] + [c[j] for c in came]) for j in range(packs[0].shape[0])]
    half = packs[3].shape[0]
    again_two, again_one = tie([dp_move(onward[0], 2, dps), dp_move(onward[1], 1, dps)])
    low = [wide_sum([packs[0][j], came[0][j], again_two[j]]) for j in range(half)]
    return low + [wide_sum([packs[0][half + j], came[1][j], again_one[j]]) for j in range(half)]


def scatter_z(totals, seq, tie=lambda moved: moved):
    moved = tie([z_move(totals[j].astype(BF), j, seq) for j in range(1, seq // 2)])
    return wide_sum([totals[0]] + moved)


def stacked_heads(pair_rows):
    lanes = lax.broadcasted_iota(jnp.int32, pair_rows.shape, 1)
    zero = jnp.zeros_like(pair_rows)
    return jnp.concatenate(
        [jnp.where(lanes < HD, pair_rows, zero), jnp.where(lanes < HD, zero, pair_rows)], axis=0
    )


def unstacked_heads(stacked):
    rows = stacked.shape[0] // 2
    lanes = lax.broadcasted_iota(jnp.int32, (rows, PAIR), 1)
    return jnp.where(lanes < HD, stacked[:rows], stacked[rows:])


def masked_scores(queries, keys, query_ids, key_ids):
    rows = query_ids.shape[0]
    bias = jnp.where(query_ids == key_ids, 0.0, NEGATIVE)
    scores = nt(queries, keys)
    return jnp.concatenate([scores[:rows] + bias, scores[rows:] + bias], axis=0)


def forward_kernel(qid_ref, kid_ref, q_ref, k_ref, v_ref, out_ref, lse_ref):
    keys = k_ref[0]
    values = v_ref[0]
    rows = q_ref.shape[1] // 2
    for side in range(2):
        span = slice(side * rows, (side + 1) * rows)
        queries = stacked_heads(q_ref[0, span])
        scores = masked_scores(queries, keys, qid_ref[0, span][:, :1], kid_ref[0][:1, :])
        highest = jnp.max(scores, axis=-1, keepdims=True)
        weights = jnp.exp(scores - highest)
        total = jnp.sum(weights, axis=-1, keepdims=True)
        probs = (weights * (1.0 / total)).astype(BF)
        out_ref[0, span] = unstacked_heads(nn(probs, values)).astype(BF)
        lse_ref[0, 0, side] = jnp.broadcast_to(highest + jnp.log(total), lse_ref.shape[3:])


def backward_kernel(
    qid_ref, kid_ref, q_ref, k_ref, v_ref, lse_ref, up_ref, dq_ref, dk_ref, dv_ref
):
    keys = k_ref[0]
    values = v_ref[0]
    rows = q_ref.shape[1] // 2
    key_sum, value_sum = 0.0, 0.0
    for side in range(2):
        span = slice(side * rows, (side + 1) * rows)
        queries = stacked_heads(q_ref[0, span])
        upward = stacked_heads(up_ref[0, span])
        scores = masked_scores(queries, keys, qid_ref[0, span][:, :1], kid_ref[0][:1, :])
        probs = jnp.exp(scores - lse_ref[0, 0, side][:, :1])
        dprobs = nt(upward, values)
        correction = jnp.sum(probs * dprobs, axis=-1, keepdims=True)
        dscores = (probs * (dprobs - correction)).astype(BF)
        back = unstacked_heads(nn(dscores, keys)).astype(BF).astype(F32)
        dq_ref[0, span] = (back * 0.125).astype(BF)
        key_sum += tn(dscores, queries)
        value_sum += tn(probs.astype(BF), upward)
    dk_ref[0] = key_sum.astype(BF)
    dv_ref[0] = value_sum.astype(BF)


def attention_specs(rows, count):
    return dict(
        qid=pl.BlockSpec((1, rows, 128), lambda s, p: (s, 0, 0)),
        kid=pl.BlockSpec((1, 8, count), lambda s, p: (s, 0, 0)),
        row=pl.BlockSpec((1, rows, PAIR), lambda s, p: (s, 0, p)),
        key=pl.BlockSpec((1, count, PAIR), lambda s, p: (s, 0, p)),
        value=pl.BlockSpec((1, count, PAIR), lambda s, p: (s, 0, PAIRS + p)),
        lse=pl.BlockSpec((1, 1, 2, rows, 128), lambda s, p: (s, p, 0, 0, 0)),
    )


def attend(query_ids, key_ids, queries, key_values):
    streams, rows, _ = queries.shape
    count = key_values.shape[1]
    specs = attention_specs(rows, count)
    macs = streams * 2 * PAIRS * rows * count * HD
    return pl.pallas_call(
        forward_kernel,
        grid=(streams, PAIRS),
        in_specs=[specs["qid"], specs["kid"], specs["row"], specs["key"], specs["value"]],
        out_specs=[specs["row"], specs["lse"]],
        out_shape=[
            jax.ShapeDtypeStruct((streams, rows, HALF), BF),
            jax.ShapeDtypeStruct((streams, PAIRS, 2, rows, 128), F32),
        ],
        compiler_params=pltpu.CompilerParams(vmem_limit_bytes=VMEM_LIMIT),
        cost_estimate=QUICK,
        name="attend",
    )(query_ids, key_ids, queries, key_values, key_values)


def attend_back(query_ids, key_ids, queries, key_values, lse, upward):
    streams, rows, _ = queries.shape
    count = key_values.shape[1]
    specs = attention_specs(rows, count)
    macs = streams * 2 * PAIRS * rows * count * HD
    key_shape = jax.ShapeDtypeStruct((streams, count, HALF), BF)
    return pl.pallas_call(
        backward_kernel,
        grid=(streams, PAIRS),
        in_specs=[
            specs["qid"],
            specs["kid"],
            specs["row"],
            specs["key"],
            specs["value"],
            specs["lse"],
            specs["row"],
        ],
        out_specs=[specs["row"], specs["key"], specs["key"]],
        out_shape=[jax.ShapeDtypeStruct((streams, rows, HALF), BF), key_shape, key_shape],
        compiler_params=pltpu.CompilerParams(vmem_limit_bytes=VMEM_LIMIT),
        cost_estimate=QUICK,
        name="attend_back",
    )(query_ids, key_ids, queries, key_values, key_values, lse, upward)


TILE = 256
CHUNK = 384
QUERY_BIAS, VALUE_BIAS, OUT_BIAS, FIRST_GAIN, FIRST_SHIFT, REDUCE_BIAS, SECOND_GAIN, SECOND_SHIFT = range(8)


def norm_rows(value_rows):
    centre = jnp.mean(value_rows, axis=-1, keepdims=True)
    centred = value_rows - centre
    inverse = lax.rsqrt(jnp.mean(centred * centred, axis=-1, keepdims=True) + EPSILON)
    return (centred * inverse, inverse)


def norm_back(upward, normed, inverse):
    mean_up = jnp.mean(upward, axis=-1, keepdims=True)
    mean_cross = jnp.mean(upward * normed, axis=-1, keepdims=True)
    return inverse * (upward - mean_up - normed * mean_cross)


def add_rows(sum_ref, index, values):
    sum_ref[index] += jnp.sum(values.reshape(-1, 8, values.shape[1]), axis=0)


def vector_of(vec_ref, index):
    return vec_ref[index : index + 1, :]


def middle_kernel(
    place_ref, mine_ref, other_ref, tok_ref, vec_ref, unit_ref, out_ref, expand_ref,
    normed_ref, inverse_ref, low_ref, hidden_ref, slope_ref,
):
    core = place_ref[2]
    for_mine = out_ref[pl.ds(pl.multiple_of(core * HALF, 128), HALF), :]
    for_other = out_ref[pl.ds(pl.multiple_of((1 - core) * HALF, 128), HALF), :]
    branch = nn(mine_ref[...], for_mine) + nn(other_ref[...], for_other) + vector_of(vec_ref, OUT_BIAS)
    normed, inverse = norm_rows(tok_ref[...].astype(F32) + branch)
    normed_ref[...] = normed
    inverse_ref[...] = jnp.broadcast_to(inverse, inverse_ref.shape)
    first = normed * vector_of(vec_ref, FIRST_GAIN) + vector_of(vec_ref, FIRST_SHIFT)
    low = first.astype(BF)
    low_ref[...] = low
    for start in range(0, UNITS, CHUNK):
        span = slice(start, start + CHUNK)
        expanded = nn(low, expand_ref[:, span]) + unit_ref[:, span]
        share = 0.5 * (1.0 + lax.erf(expanded * (0.5**0.5)))
        hidden_ref[:, span] = (expanded * share).astype(BF)
        bell = jnp.exp(-0.5 * expanded * expanded) * 0.3989422804014327
        slope_ref[:, span] = (share + expanded * bell).astype(BF)


def turn_kernel(
    part_ref, came_ref, normed_ref, cot_ref, slope_ref, vec_ref, reduce_ref, expand_ref,
    act_ref, residual_ref, low_ref, back_ref, next_ref, sum_ref, unit_sum_ref,
):
    @pl.when(pl.program_id(0) == 0)
    def _():
        sum_ref[...] = jnp.zeros_like(sum_ref)
        unit_sum_ref[...] = jnp.zeros_like(unit_sum_ref)

    first = normed_ref[...] * vector_of(vec_ref, FIRST_GAIN) + vector_of(vec_ref, FIRST_SHIFT)
    reduced = part_ref[...] + came_ref[...] + vector_of(vec_ref, REDUCE_BIAS)
    normed, inverse = norm_rows(first + reduced)
    gain = vector_of(vec_ref, SECOND_GAIN)
    act_ref[...] = (normed * gain + vector_of(vec_ref, SECOND_SHIFT)).astype(BF)
    upward = cot_ref[...].astype(F32)
    residual = norm_back(upward * gain, normed, inverse)
    low = residual.astype(BF)
    residual_ref[...] = residual
    low_ref[...] = low
    add_rows(sum_ref, 0, low.astype(F32))
    add_rows(sum_ref, 1, upward * normed)
    add_rows(sum_ref, 2, upward)
    total = jnp.zeros(next_ref.shape, F32)
    for start in range(0, UNITS, CHUNK):
        span = slice(start, start + CHUNK)
        back = (nt(low, reduce_ref[span, :]) * slope_ref[:, span].astype(F32)).astype(BF)
        back_ref[:, span] = back
        unit_sum_ref[:, span] += jnp.sum(back.astype(F32).reshape(-1, 8, CHUNK), axis=0)
        total += nt(back, expand_ref[:, span])
    next_ref[...] = total


def first_back_kernel(
    place_ref, part_ref, came_ref, residual_ref, normed_ref, inverse_ref, vec_ref, out_ref,
    back_ref, low_ref, attended_ref, sum_ref,
):
    @pl.when(pl.program_id(0) == 0)
    def _():
        sum_ref[...] = jnp.zeros_like(sum_ref)

    core = place_ref[2]
    upward = part_ref[...] + came_ref[...] + residual_ref[...]
    normed = normed_ref[...]
    add_rows(sum_ref, 1, upward * normed)
    add_rows(sum_ref, 2, upward)
    back = norm_back(upward * vector_of(vec_ref, FIRST_GAIN), normed, inverse_ref[:, :1])
    low = back.astype(BF)
    back_ref[...] = back
    low_ref[...] = low
    add_rows(sum_ref, 0, low.astype(F32))
    mine = out_ref[pl.ds(pl.multiple_of(core * HALF, 128), HALF), :]
    attended_ref[...] = nt(low, mine).astype(BF)


def over_rows(kernel, place, tiled, whole, outs, sums, name, macs):
    rows = tiled[0].shape[0]
    tile = lambda lanes: pl.BlockSpec((TILE, lanes), lambda t: (t, 0))
    keep = lambda shape: pl.BlockSpec(shape, lambda t: (0,) * len(shape))
    places = [] if place is None else [place]
    return pl.pallas_call(
        kernel,
        grid=(rows // TILE,),
        in_specs=[pl.BlockSpec(memory_space=pltpu.SMEM)] * len(places)
        + [tile(v.shape[1]) for v in tiled]
        + [pl.BlockSpec(memory_space=pltpu.VMEM)] * len(whole),
        out_specs=[tile(lanes) for lanes, _ in outs] + [keep(shape) for shape in sums],
        out_shape=[jax.ShapeDtypeStruct((rows, lanes), dtype) for lanes, dtype in outs]
        + [jax.ShapeDtypeStruct(shape, F32) for shape in sums],
        compiler_params=pltpu.CompilerParams(vmem_limit_bytes=VMEM_LIMIT),
        cost_estimate=QUICK,
        name=name,
    )(*places, *tiled, *whole)


def column_sum(value_rows):
    return jnp.sum(value_rows.astype(F32), axis=0)


def item_ids(lengths, places):
    items = lengths.shape[1]
    slot = jnp.arange(items, dtype=jnp.int32)
    ends = jnp.sum(jnp.where(slot[:, None] <= slot[None, :], lengths[:, :, None], 0), axis=1)
    return jnp.sum((ends[:, None, :] <= places[None, :, None]).astype(jnp.int32), axis=2)


def body(
    tokens,
    query_weight,
    query_bias,
    key_weight,
    value_weight,
    value_bias,
    out_weight,
    out_bias,
    first_gain,
    attention_norm_shift,
    expand_weight,
    expand_bias,
    reduce_weight,
    reduce_bias,
    second_gain,
    second_shift,
    lengths,
    cotangent,
    *,
    dps,
    seq,
):
    streams, row_count, _ = tokens.shape
    zs = seq // 2
    chips = dps * zs
    block = D // (2 * chips)
    both = 2 * block
    wide = FF // (2 * chips)
    chip_rows = 2 * row_count
    rows = streams * chip_rows
    dp = lax.axis_index("dp")
    z = lax.axis_index("seq") // 2
    core = lax.axis_index("seq") % 2
    place = jnp.stack([dp, z, core]).astype(jnp.int32)
    swap = functools.partial(core_swap, seq=seq)

    def row_major(value):
        return with_layout_constraint(value, Layout(major_to_minor=tuple(range(value.ndim))))

    def in_core_order(mine, other, axis):
        return jnp.where(
            core == 0,
            jnp.concatenate([mine, other], axis=axis),
            jnp.concatenate([other, mine], axis=axis),
        )

    mine, theirs = first_columns(
        place,
        (query_weight, key_weight, value_weight),
        (
            query_bias,
            value_bias,
            out_bias,
            first_gain,
            attention_norm_shift,
            reduce_bias,
            second_gain,
            second_shift,
            expand_bias,
        ),
    )
    early = in_core_order(mine[None], swap(theirs)[None], 0)

    out_weight = out_weight.astype(BF)
    units = expand_weight.astype(BF).reshape(block, chips, 2, wide)

    def columns_for(side):
        unit = lax.dynamic_index_in_dim(units, side, 2, keepdims=False).reshape(block, UNITS)
        return jnp.concatenate([out_weight, unit], axis=1)

    late = in_core_order(columns_for(core)[None], swap(columns_for(1 - core))[None], 0)
    early = jnp.stack(tied(z_moves(early, seq), late))
    late = z_moves(tied(late, early), seq)
    early, late = lax.optimization_barrier((gather_dp_first(early, dps), late))
    early = gather_dp_rest(early, dps)
    late = jnp.stack(late)
    all_tokens = row_major(lax.all_gather(tied(tokens, late), "seq", axis=1, tiled=True))
    last = z_moves(tied(reduce_weight.astype(BF), late), seq)
    late = gather_dp_rest(gather_dp_first(late, dps), dps)
    last = gather_dp_first(jnp.stack(last), dps)
    cotangent = in_core_order(cotangent, swap(cotangent), 1)

    def gather_plan(parts):
        return [
            (
                piece,
                lambda dp, z, row=row, first=first, count=count: (
                    row,
                    Ellipsis,
                    at_lanes(first, count),
                ),
                target,
                lambda dp, z, j=j, k=k: (dp ^ k, z ^ j),
            )
            for piece, row, k, j in dp_pieces(dps, zs)
            for first, count, target in parts
        ]

    qkv_weight, small = local_copies(
        place,
        early,
        [(dps, zs, 2, block, 3 * HALF), (dps, zs, 2, block, 128)],
        gather_plan([(0, 3 * HALF, 0), (3 * HALF, 128, 1)]),
        "place_early",
    )
    qkv_weight = qkv_weight.reshape(D, 3 * HALF)
    small = small.astype(F32).reshape(D, 128)[:, :12].T
    query_bias, value_bias = small[QUERY_BIAS : QUERY_BIAS + 1], small[VALUE_BIAS : VALUE_BIAS + 1]
    expand_bias = small[8:12].reshape(4, chips, 2, block)
    expand_bias = lax.dynamic_index_in_dim(expand_bias, core, 2, keepdims=False)
    expand_bias = expand_bias.transpose(1, 0, 2).reshape(1, UNITS)

    def half_of(vector):
        return lax.dynamic_slice_in_dim(vector, core * HALF, HALF, 1)

    chip_tokens = lax.dynamic_slice_in_dim(all_tokens, z * chip_rows, chip_rows, 1).reshape(rows, D)
    flat_all = all_tokens.reshape(-1, D)
    ids = item_ids(lengths, jnp.arange(all_tokens.shape[1], dtype=jnp.int32))
    key_ids = jnp.broadcast_to(ids[:, None, :], (streams, 8, ids.shape[1]))
    query_ids = lax.dynamic_slice_in_dim(ids, z * chip_rows, chip_rows, 1)
    query_ids = jnp.broadcast_to(query_ids[..., None], (streams, chip_rows, 128))

    queries = ((nn(chip_tokens, qkv_weight[:, :HALF]) + half_of(query_bias)) * 0.125).astype(BF)
    queries = row_major(queries.reshape(streams, chip_rows, HALF))
    key_value_bias = jnp.concatenate([jnp.zeros((1, HALF), F32), half_of(value_bias)], axis=1)
    key_values = (nn(flat_all, qkv_weight[:, HALF:]) + key_value_bias).astype(BF)
    key_values = row_major(key_values.reshape(streams, -1, D))
    last = gather_dp_rest(tied(last, key_values), dps)
    attended, lse = attend(query_ids, key_ids, queries, key_values)
    other_attended = swap(attended).reshape(rows, HALF)
    attended = attended.reshape(rows, HALF)

    out_weight, expand_weight = local_copies(
        place,
        late,
        [(dps, zs, 2, block, D), (dps, zs, 2, block, UNITS)],
        gather_plan([(0, D, 0), (D, UNITS, 1)]),
        "place_late",
    )
    out_weight = out_weight.reshape(D, D)
    expand_weight = expand_weight.reshape(D, UNITS)
    (reduce_weight,) = local_copies(
        place, last, [(dps, zs, wide, D)], gather_plan([(0, D, 0)]), "place_last"
    )
    reduce_weight = reduce_weight.reshape(UNITS, D)

    def own(value):
        value = value.reshape(streams, chip_rows, -1)
        return lax.dynamic_slice_in_dim(value, core * row_count, row_count, 1)

    normed_one, inverse_one, first_low, hidden, slope = over_rows(
        middle_kernel,
        place,
        [attended, other_attended, chip_tokens],
        [small, expand_bias, out_weight, expand_weight],
        [(D, F32), (128, F32), (D, BF), (UNITS, BF), (UNITS, BF)],
        [],
        "middle",
        rows * D * (D + UNITS),
    )
    partial = nn(hidden, reduce_weight)
    activations, residual_two_back, reduced_back, expanded_back, next_partial, sums_two, unit_sums = over_rows(
        turn_kernel,
        None,
        [partial, swap(partial), normed_one, cotangent.reshape(rows, D), slope],
        [small, reduce_weight, expand_weight],
        [(D, BF), (D, F32), (D, BF), (UNITS, BF), (D, F32)],
        [(3, 8, D), (8, UNITS)],
        "turn",
        2 * rows * D * UNITS,
    )
    reduce_bias_grad, second_gain_grad, second_shift_grad = jnp.sum(sums_two, axis=1)
    expand_bias_grad = jnp.sum(unit_sums, axis=0)
    came_partial = swap(next_partial)
    reduce_weight_grad = tn(hidden, reduced_back).astype(BF)
    expand_weight_grad = tn(first_low, expanded_back).astype(BF)

    def scatter_plan(parts, lanes):
        slots, counts = scatter_slots(dps, zs)
        plan = [
            (
                source,
                lambda dp, z, j=j, k=k, index=index: index(dp ^ k, z ^ j),
                array,
                lambda dp, z, row=row, first=first, count=count: (
                    row,
                    slice(None),
                    at_lanes(first, count),
                ),
            )
            for (k, j), (array, row) in slots.items()
            for source, index, first, count in parts
        ]
        return [(count, both, lanes) for count in counts], plan

    wide_packs = local_copies(
        place,
        [
            reduce_weight_grad.reshape(dps, zs, 2, both, D),
            expand_weight_grad.reshape(dps, zs, both, UNITS),
        ],
        *scatter_plan(
            [
                (0, lambda d, zz: (d, zz, 0), 0, D),
                (0, lambda d, zz: (d, zz, 1), D, D),
                (1, lambda d, zz: (d, zz), 2 * D, UNITS),
            ],
            2 * D + UNITS,
        ),
        "pack_wide",
    )

    wide_came = scatter_dp_first(wide_packs, dps)

    residual_one_back, branch_back, attended_back, sums_one = over_rows(
        first_back_kernel,
        place,
        [next_partial, came_partial, residual_two_back, normed_one, inverse_one],
        [small, out_weight],
        [(D, F32), (D, BF), (HALF, BF)],
        [(3, 8, D)],
        "first_back",
        rows * D * HALF,
    )
    out_bias_grad, first_gain_grad, first_shift_grad = jnp.sum(sums_one, axis=1)
    attended_back = attended_back.reshape(streams, chip_rows, HALF)

    query_back, key_back, value_back = attend_back(
        query_ids, key_ids, queries, key_values, lse, attended_back
    )
    flat_query_back = query_back.reshape(rows, HALF)
    key_back = key_back.reshape(-1, HALF)
    value_back = value_back.reshape(-1, HALF)

    tokens_part = nt(key_back, qkv_weight[:, HALF : 2 * HALF]) + nt(value_back, qkv_weight[:, 2 * HALF :])
    tokens_part = tokens_part.astype(BF).reshape(streams, -1, D)
    tokens_total = lax.psum_scatter(tokens_part, "seq", scatter_dimension=1, tiled=True)
    wide_came = tied(wide_came, tokens_part)
    wide_onward = scatter_dp_middle(wide_packs, wide_came, dps)
    key_back, value_back, flat_query_back, out_side = tied(
        (key_back, value_back, flat_query_back, half_of(branch_back)), wide_onward
    )
    key_weight_grad = tn(flat_all, key_back).astype(BF)
    value_weight_grad = tn(flat_all, value_back).astype(BF)
    query_weight_grad = tn(chip_tokens, flat_query_back).astype(BF)
    out_weight_grad = in_core_order(tn(attended, out_side), tn(other_attended, out_side), 0).astype(BF)
    half_sums = jnp.stack([column_sum(flat_query_back), column_sum(value_back)])
    full_sums = in_core_order(half_sums, swap(half_sums), 1)
    small_grads = jnp.concatenate(
        [
            full_sums,
            jnp.stack(
                [
                    out_bias_grad,
                    first_gain_grad,
                    first_shift_grad,
                    reduce_bias_grad,
                    second_gain_grad,
                    second_shift_grad,
                ]
            ),
            expand_bias_grad.reshape(chips, 2, both).transpose(1, 0, 2).reshape(2, D),
        ],
        axis=0,
    ).T.astype(BF)
    small_grads = jnp.pad(small_grads, ((0, 0), (0, 128 - small_grads.shape[1])))
    four = (query_weight_grad, key_weight_grad, value_weight_grad, out_weight_grad)
    wide_totals = scatter_dp_rest(wide_packs, wide_came, wide_onward, dps)
    four = tied(four, wide_totals)
    narrow_packs = local_copies(
        place,
        [g.reshape(dps, zs, both, HALF) for g in four] + [small_grads.reshape(dps, zs, both, 128)],
        *scatter_plan(
            [(i, lambda d, zz: (d, zz), i * HALF, HALF) for i in range(4)]
            + [(4, lambda d, zz: (d, zz), 4 * HALF, 128)],
            4 * HALF + 128,
        ),
        "pack_narrow",
    )
    came = tied(scatter_dp_first(narrow_packs, dps), wide_totals)
    narrow_onward = scatter_dp_middle(narrow_packs, came, dps)
    wide_grads = scatter_z(wide_totals, seq, lambda moved: tied(moved, narrow_onward))
    narrow_totals = scatter_dp_rest(
        narrow_packs, came, narrow_onward, dps, lambda came: tied(came, wide_grads, tokens_total)
    )
    narrow_grads = scatter_z(narrow_totals, seq)
    query_part = nt(flat_query_back, qkv_weight[:, :HALF]).astype(BF)
    query_part = own(query_part).astype(F32) + own(swap(query_part)).astype(F32)
    tokens_gradient = own(residual_one_back) + query_part + tokens_total.astype(F32)

    def own_rows(grads):
        split = grads.reshape(2, block, grads.shape[1])
        mine = lax.dynamic_index_in_dim(split, core, 0, keepdims=False)
        return mine, swap(lax.dynamic_index_in_dim(split, 1 - core, 0, keepdims=False))

    mine, other = own_rows(narrow_grads[:, : 4 * HALF])
    matrices = [
        in_core_order(mine[:, i * HALF : (i + 1) * HALF], other[:, i * HALF : (i + 1) * HALF], 1)
        for i in range(4)
    ]
    small = narrow_grads[:, 4 * HALF :]
    own_small = lax.dynamic_slice_in_dim(small, core * block, block, 0).T
    expand_bias_grad = small[:, 8:10].T.reshape(wide)
    mine, other = own_rows(wide_grads[:, 2 * D :])
    expand_grads = in_core_order(
        mine.reshape(block, chips, 1, wide), other.reshape(block, chips, 1, wide), 2
    ).reshape(block, FF)
    reduce_grads = jnp.concatenate([wide_grads[:, :D], wide_grads[:, D : 2 * D]], axis=0)

    return (
        own(activations),
        tokens_gradient,
        matrices[0],
        own_small[0],
        matrices[1],
        matrices[2],
        own_small[1],
        matrices[3],
        own_small[2],
        own_small[3],
        own_small[4],
        expand_grads,
        expand_bias_grad,
        reduce_grads,
        own_small[5],
        own_small[6],
        own_small[7],
    )


def solution(mesh):
    sharded = ("dp", "seq")
    matrix = P(sharded, None)
    vector = P(sharded)
    token = P("dp", "seq", None)
    params = (
        matrix,
        vector,
        matrix,
        matrix,
        vector,
        matrix,
        vector,
        vector,
        vector,
        matrix,
        vector,
        matrix,
        vector,
        vector,
        vector,
    )
    return jax.shard_map(
        functools.partial(body, dps=mesh.shape["dp"], seq=mesh.shape["seq"]),
        mesh=mesh,
        in_specs=(token,) + params + (P("dp", None), token),
        out_specs=(token, token) + params,
        check_vma=False,
    )
```

profile of v0, /device:TPU:13, one launch (start us, length us, event | category | flops | bytes accessed | tf_op | source)
XLA Modules:
  0.0 303.0 jit_solution(3670043388059970816)
XLA Ops:
  7.9 1.8 first_columns.1
  11.6 1.3 dynamic-slice_reduce_fusion.1
  13.6 2.3 collective-permute-start.2
  16.1 1.7 collective-permute-done.1
  17.9 3.6 %collective-permute-done.2 = bf16[2,24,1280]{2,1,0:T(8,128)(2,1)S(1)} collective-permute-done((bf16[2,24,1280]{2,1,0:T(8,128)(2,1)S(1)}, bf16[2,24,1280]{2,1,0:T(8,128)(2,1)S(1)}, u32[]{:S(2)}, u32[]{:S(2)}) %collective-permute-start.2) | collective-permute-done | bytes 122912 | tf_op jit(solution)/shard_map/ppermute | solution.py:103
  21.5 5.2 %collective-permute-done.3 = bf16[2,24,1280]{2,1,0:T(8,128)(2,1)S(1)} collective-permute-done((bf16[2,24,1280]{2,1,0:T(8,128)(2,1)S(1)}, bf16[2,24,1280]{2,1,0:T(8,128)(2,1)S(1)}, u32[]{:S(2)}, u32[]{:S(2)}) %collective-permute-start.3) | collective-permute-done | bytes 122912 | tf_op jit(solution)/shard_map/ppermute | solution.py:103
  26.8 1.3 collective-permute-start.5
  28.3 2.5 collective-permute-start.8
  31.0 2.4 collective-permute-done.7
  33.4 5.3 %collective-permute-done.8 = bf16[2,24,2304]{2,1,0:T(8,128)(2,1)S(1)} collective-permute-done((bf16[2,24,2304]{2,1,0:T(8,128)(2,1)S(1)}, bf16[2,24,2304]{2,1,0:T(8,128)(2,1)S(1)}, u32[]{:S(2)}, u32[]{:S(2)}) %collective-permute-start.8) | collective-permute-done | bytes 221216 | tf_op jit(solution)/shard_map/ppermute | solution.py:103
  38.7 9.9 %collective-permute-done.9 = bf16[2,24,2304]{2,1,0:T(8,128)(2,1)S(1)} collective-permute-done((bf16[2,24,2304]{2,1,0:T(8,128)(2,1)S(1)}, bf16[2,24,2304]{2,1,0:T(8,128)(2,1)S(1)}, u32[]{:S(2)}, u32[]{:S(2)}) %collective-permute-start.9) | collective-permute-done | bytes 221216 | tf_op jit(solution)/shard_map/ppermute | solution.py:103
  49.9 3.4 %collective-permute-start.18 = (bf16[96,768]{1,0:T(8,128)(2,1)S(1)}, bf16[96,768]{1,0:T(8,128)(2,1)S(1)}, u32[]{:S(2)}, u32[]{:S(2)}) collective-permute-start(bf16[96,768]{1,0:T(8,128)(2,1)S(1)} %convert_element_type.246), channel_id=1, source_target_pairs={{0,4},{1,5},{2,6},{3,7},{4,0},{5,1},{6,2},{7,3},{8,12},{9,13},{10,... | collective-permute-start | bytes 442376 | tf_op jit(solution)/shard_map/ppermute | solution.py:103
  53.5 1.3 collective-permute-start.14
  55.0 1.7 slice.197
  57.7 1.3 collective-permute-start.10
  59.0 4.3 %collective-permute-done.18 = bf16[96,768]{1,0:T(8,128)(2,1)S(1)} collective-permute-done((bf16[96,768]{1,0:T(8,128)(2,1)S(1)}, bf16[96,768]{1,0:T(8,128)(2,1)S(1)}, u32[]{:S(2)}, u32[]{:S(2)}) %collective-permute-start.18) | collective-permute-done | bytes 147488 | tf_op jit(solution)/shard_map/ppermute | solution.py:103
  64.1 11.4 %collective-permute-done.19 = bf16[96,768]{1,0:T(8,128)(2,1)} collective-permute-done((bf16[96,768]{1,0:T(8,128)(2,1)S(1)}, bf16[96,768]{1,0:T(8,128)(2,1)}, u32[]{:S(2)}, u32[]{:S(2)}) %collective-permute-start.19) | collective-permute-done | bytes 147488 | tf_op jit(solution)/shard_map/ppermute | solution.py:103
  75.5 2.0 pad_maximum_fusion.1.refs_0_
  79.6 2.9 place_early.1
  87.3 5.8 %all-gather.2.cloned.1.call-done = bf16[2,1024,768]{2,1,0:T(8,128)(2,1)} async-done(((bf16[2,128,768]{2,1,0:T(8,128)(2,1)}), bf16[2,1024,768]{2,1,0:T(8,128)(2,1)}) %all-gather.2.cloned.1.call-update) | async-done | bytes 3145744 | tf_op jit(solution)/shard_map/all_gather | solution.py:518
  93.1 6.6 %add_convert_fusion.1 = bf16[2048,768]{1,0:T(8,128)(2,1)} fusion(bf16[2048,768]{1,0:T(8,128)(2,1)} %bitcast.119, f32[768]{0:T(1024)S(1)} %pad_reduce_fusion, bf16[768,1152]{1,0:T(8,128)(2,1)} %bitcast.140), kind=kOutput, calls=%fused_computation.1 | convolution fusion | flops 2419064832 | bytes 7474176 | tf_op jit(solution)/shard_map/dot_general | solution.py:28
  100.7 2.4 fusion.1
  104.5 10.5 %attend.1 = (bf16[2,256,384]{2,1,0:T(8,128)(2,1)}, f32[2,3,2,256,128]{4,3,2,1,0:T(8,128)}) custom-call(s32[2,256,128]{2,1,0:T(8,128)} %broadcast_in_dim.49.qid_ref, s32[2,8,1024]{2,1,0:T(8,128)} %broadcast_in_dim.50.kid_ref, bf16[2,256,384]{2,1,0:T(8,128)(2,1)} %bitcast.146, bf16[2,1024,768]{2,1,0:T(8,128)(2,1)} %bitcast.112, bf16[2,1024,768]{2,1,0:T(8,128)(2,1)} %bitcast.113), custom_call_target="tpu_custom_call" | custom-call | tf_op jit(solution)/shard_map/attend/pallas_call | solution.py:266
  115.3 1.7 slice.207
  117.4 1.7 slice.208
  122.5 4.0 %place_late.1 = (bf16[4,4,2,24,768]{4,3,2,1,0:T(8,128)(2,1)}, bf16[4,4,2,24,1536]{4,3,2,1,0:T(8,128)(2,1)}) custom-call(s32[3]{0:T(128)} %pad_add_fusion.place_ref, bf16[4,2,24,2304]{3,2,1,0:T(8,128)(2,1)} %copy-done.5, bf16[4,2,24,2304]{3,2,1,0:T(8,128)(2,1)} %copy-done.9, bf16[4,2,24,2304]{3,2,1,0:T(8,128)(2,1)} %copy-done.8, ...), custom_call_target="tpu_custom_call" | custom-call | tf_op jit(solution)/shard_map/place_late/pallas_call | solution.py:49
  127.6 3.2 %place_last.1 = bf16[4,4,96,768]{3,2,1,0:T(8,128)(2,1)} custom-call(s32[3]{0:T(128)} %pad_add_fusion.place_ref, bf16[4,96,768]{2,1,0:T(8,128)(2,1)} %pad_maximum_fusion.1.refs_0_, bf16[4,96,768]{2,1,0:T(8,128)(2,1)} %collective-permute-done.20.refs_1_, bf16[4,96,768]{2,1,0:T(8,128)(2,1)} %collective-permute-done.21.refs_2_, bf16[2,96,768]{2,1,0:T(8,128)(2,1)} %copy-done.28, ...), custom_call_target="tpu_custom_call" | custom-call | tf_op jit(solution)/shard_map/place_last/pallas_call | solution.py:49
  130.8 8.0 %middle.1 = (f32[512,768]{1,0:T(8,128)}, f32[512,128]{1,0:T(8,128)}, bf16[512,768]{1,0:T(8,128)(2,1)}, bf16[512,1536]{1,0:T(8,128)(2,1)}, bf16[512,1536]{1,0:T(8,128)(2,1)}) custom-call(s32[3]{0:T(128)} %pad_add_fusion.place_ref, bf16[512,384]{1,0:T(8,128)(2,1)} %bitcast.159, bf16[512,384]{1,0:T(8,128)(2,1)} %bitcast.23.other_ref, ...), custom_call_target="tpu_custom_call" | custom-call | tf_op jit(solution)/shard_map/middle/pallas_call | solution.py:415
  138.8 2.8 fusion.21.part_ref
  141.6 1.4 collective-permute-start.24
  143.1 3.5 %collective-permute-done.25 = bf16[2,128,768]{2,1,0:T(8,128)(2,1)S(1)} collective-permute-done((bf16[2,128,768]{2,1,0:T(8,128)(2,1)S(1)}, bf16[2,128,768]{2,1,0:T(8,128)(2,1)S(1)}, u32[]{:S(2)}, u32[]{:S(2)}) %collective-permute-start.25) | collective-permute-done | bytes 393248 | tf_op jit(solution)/shard_map/ppermute | solution.py:99
  148.9 10.7 %turn.1 = (bf16[512,768]{1,0:T(8,128)(2,1)}, f32[512,768]{1,0:T(8,128)}, bf16[512,768]{1,0:T(8,128)(2,1)}, bf16[512,1536]{1,0:T(8,128)(2,1)}, f32[512,768]{1,0:T...) custom-call(f32[512,768]{1,0:T(8,128)} %copy-done.13, f32[512,768]{1,0:T(8,128)} %copy-done.14, ...), custom_call_target="tpu_custom_call" | custom-call | tf_op jit(solution)/shard_map/turn/pallas_call | solution.py:415
  160.0 4.1 %convolution_convert_fusion.1 = bf16[1536,768]{1,0:T(8,128)(2,1)} fusion(bf16[512,1536]{1,0:T(8,128)(2,1)S(1)} %copy-done.42, bf16[512,768]{1,0:T(8,128)(2,1)} %get-tuple-element.126), kind=kOutput, calls=%fused_computation.3 | convolution fusion | flops 1209139200 | bytes 4718592 | tf_op jit(solution)/shard_map/dot_general | solution.py:36
  164.1 2.9 convolution_convert_fusion
  167.0 4.9 %pack_wide.1 = (bf16[4,48,3072]{2,1,0:T(8,128)(2,1)}, bf16[4,48,3072]{2,1,0:T(8,128)(2,1)}, bf16[4,48,3072]{2,1,0:T(8,128)(2,1)}, bf16[2,48,3072]{2,1,0:T(8,128)(2,1)}, bf16[2,48,3072]{2,1,0:T(8,128)(2,1)}) custom-call(s32[3]{0:T(128)} %pad_add_fusion.place_ref, bf16[4,4,2,48,768]{4,3,2,1,0:T(8,128)(2,1)} %bitcast.135, bf16[4,4,48,1536]{3,2,1,0:T(8,128)(2,1)} %bitcast.136), custom_call_target="tpu_custom_call" | custom-call | tf_op jit(solution)/shard_map/pack_wide/pallas_call | solution.py:49
  175.0 5.3 %first_back.1 = (f32[512,768]{1,0:T(8,128)}, bf16[512,768]{1,0:T(8,128)(2,1)}, bf16[512,384]{1,0:T(8,128)(2,1)}, f32[3,8,768]{2,1,0:T(8,128)}) custom-call(s32[3]{0:T(128)} %pad_add_fusion.place_ref, f32[512,768]{1,0:T(8,128)} %get-tuple-element.116.part_ref, f32[512,768]{1,0:T(8,128)} %collective-permute-done.26.came_ref, ...), custom_call_target="tpu_custom_call" | custom-call | tf_op jit(solution)/shard_map/first_back/pallas_call | solution.py:415
  180.3 14.8 %attend_back.1 = (bf16[2,256,384]{2,1,0:T(8,128)(2,1)}, bf16[2,1024,384]{2,1,0:T(8,128)(2,1)}, bf16[2,1024,384]{2,1,0:T(8,128)(2,1)}) custom-call(s32[2,256,128]{2,1,0:T(8,128)} %broadcast_in_dim.49.qid_ref, s32[2,8,1024]{2,1,0:T(8,128)} %broadcast_in_dim.50.kid_ref, bf16[2,256,384]{2,1,0:T(8,128)(2,1)} %bitcast.147, bf16[2,1024,768]{2,1,0:T(8,128)(2,1)} %bitcast.114, ...), custom_call_target="tpu_custom_call" | custom-call | tf_op jit(solution)/shard_map/attend_back/pallas_call | solution.py:287
  195.1 3.4 %fusion.4 = f32[2048,768]{1,0:T(8,128)S(1)} fusion(bf16[2048,384]{1,0:T(8,128)(2,1)} %bitcast.116, bf16[768,1152]{1,0:T(8,128)(2,1)S(1)} %bitcast.143), kind=kOutput, calls=%fused_computation.23 | convolution fusion | flops 1207959552 | bytes 8454144 | tf_op jit(solution)/shard_map/dot_general | solution.py:32
  198.4 3.6 %add_convert_fusion = bf16[2048,768]{1,0:T(8,128)(2,1)} fusion(f32[2048,768]{1,0:T(8,128)S(1)} %fusion.4, bf16[2048,384]{1,0:T(8,128)(2,1)S(1)} %bitcast.127, bf16[768,1152]{1,0:T(8,128)(2,1)S(1)} %bitcast.144), kind=kOutput, calls=%fused_computation | convolution fusion | flops 1211105280 | bytes 11599872 | tf_op jit(solution)/shard_map/dot_general | solution.py:32
  203.2 2.3 add_convert_fusion.2
  205.9 2.1 add_convert_fusion.3
  209.3 1.3 collective-permute-start.32
  211.0 1.4 convolution_convert_fusion.5
  212.4 2.7 convolution_convert_fusion.3
  215.1 2.7 convolution_convert_fusion.4
  217.8 1.5 fusion.23
  223.3 2.6 add_bitcast_fusion
  225.8 3.5 %pack_narrow.1 = (bf16[4,48,1664]{2,1,0:T(8,128)(2,1)}, bf16[4,48,1664]{2,1,0:T(8,128)(2,1)}, bf16[4,48,1664]{2,1,0:T(8,128)(2,1)}, bf16[2,48,1664]{2,1,0:T(8,128)(2,1)}, bf16[2,48,1664]{2,1,0:T(8,128)(2,1)}) custom-call(s32[3]{0:T(128)} %pad_add_fusion.place_ref, bf16[4,4,48,384]{3,2,1,0:T(8,128)(2,1)} %bitcast.156, bf16[4,4,48,384]{3,2,1,0:T(8,128)(2,1)} %bitcast.139, ...), custom_call_target="tpu_custom_call" | custom-call | tf_op jit(solution)/shard_map/pack_narrow/pallas_call | solution.py:49
  232.4 1.7 convolution_convert_fusion.2
  234.0 1.7 collective-permute-start.29
  235.8 2.5 collective-permute-start.37
  239.3 4.2 %collective-permute-done.33 = bf16[4,48,1664]{2,1,0:T(8,128)(2,1)S(1)} collective-permute-done((bf16[4,48,1664]{2,1,0:T(8,128)(2,1)}, bf16[4,48,1664]{2,1,0:T(8,128)(2,1)S(1)}, u32[]{:S(2)}, u32[]{:S(2)}) %collective-permute-start.33) | collective-permute-done | bytes 639008 | tf_op jit(solution)/shard_map/ppermute | solution.py:107
  243.5 2.1 collective-permute-start.39
  246.6 1.2 collective-permute-start.36
  248.7 4.1 %collective-permute-done.37 = bf16[48,3072]{1,0:T(8,128)(2,1)S(1)} collective-permute-done((bf16[48,3072]{1,0:T(8,128)(2,1)}, bf16[48,3072]{1,0:T(8,128)(2,1)S(1)}, u32[]{:S(2)}, u32[]{:S(2)}) %collective-permute-start.37) | collective-permute-done | bytes 294944 | tf_op jit(solution)/shard_map/ppermute | solution.py:103
  253.4 1.6 collective-permute-done.38
  255.0 11.5 %collective-permute-done.39 = bf16[48,3072]{1,0:T(8,128)(2,1)S(1)} collective-permute-done((bf16[48,3072]{1,0:T(8,128)(2,1)}, bf16[48,3072]{1,0:T(8,128)(2,1)S(1)}, u32[]{:S(2)}, u32[]{:S(2)}) %collective-permute-start.39) | collective-permute-done | bytes 294944 | tf_op jit(solution)/shard_map/ppermute | solution.py:103
  269.1 1.4 reshape.251
  272.5 1.4 fusion.12
  274.0 2.4 collective-permute-start.41
  276.6 2.2 convert_add_fusion
  279.9 3.9 %collective-permute-done.41 = bf16[48,1664]{1,0:T(8,128)(2,1)S(1)} collective-permute-done((bf16[48,1664]{1,0:T(8,128)(2,1)S(1)}, bf16[48,1664]{1,0:T(8,128)(2,1)S(1)}, u32[]{:S(2)}, u32[]{:S(2)}) %collective-permute-start.41) | collective-permute-done | bytes 159776 | tf_op jit(solution)/shard_map/ppermute | solution.py:103
  283.8 6.8 %collective-permute-done.42 = bf16[48,1664]{1,0:T(8,128)(2,1)S(1)} collective-permute-done((bf16[48,1664]{1,0:T(8,128)(2,1)S(1)}, bf16[48,1664]{1,0:T(8,128)(2,1)S(1)}, u32[]{:S(2)}, u32[]{:S(2)}) %collective-permute-start.42) | collective-permute-done | bytes 159776 | tf_op jit(solution)/shard_map/ppermute | solution.py:103
  291.8 1.4 collective-permute-start.43
  (233 shorter events, 51.2 us)
Async XLA Ops:
  7.2 85.9 %all-gather.2.cloned.1.call-start = ((), (), s32[]{:S(2)}) async-start(), calls=%async_computation.1 | async-start | bytes 3538944 | tf_op jit(solution)/shard_map/all_gather | solution.py:518
  9.7 3.7 %collective-permute-start = (bf16[24,1280]{1,0:T(8,128)(2,1)}, bf16[24,1280]{1,0:T(8,128)(2,1)S(1)}, u32[]{:S(2)}, u32[]{:S(2)}) collective-permute-start(bf16[24,1280]{1,0:T(8,128)(2,1)} %get-tuple-element.89), channel_id=1, source_target_pairs={{0,1},{1,0},{2,3},{3,2},{4,5},{5,4},{6,7},{7,6},{8,9},{9,8},{10,11... | collective-permute-start | bytes 184328 | tf_op jit(solution)/shard_map/ppermute | solution.py:99
  13.3 2.8 collective-permute-start.4
  13.4 4.5 %collective-permute-start.1 = (bf16[2,24,1280]{2,1,0:T(8,128)(2,1)S(1)}, bf16[2,24,1280]{2,1,0:T(8,128)(2,1)S(1)}, u32[]{:S(2)}, u32[]{:S(2)}) collective-permute-start(bf16[2,24,1280]{2,1,0:T(8,128)(2,1)S(1)} %maximum_select_fusion.4), channel_id=1, source_target_pairs={{0,2},{1,3},{2,0},{3,1},{4,6},{5,7},{6,4},{7,5},{8,10},{9,11},{10,... | collective-permute-start | bytes 368648 | tf_op jit(solution)/shard_map/ppermute | solution.py:103
  13.6 7.9 %collective-permute-start.2 = (bf16[2,24,1280]{2,1,0:T(8,128)(2,1)S(1)}, bf16[2,24,1280]{2,1,0:T(8,128)(2,1)S(1)}, u32[]{:S(2)}, u32[]{:S(2)}) collective-permute-start(bf16[2,24,1280]{2,1,0:T(8,128)(2,1)S(1)} %maximum_select_fusion.4), channel_id=1, source_target_pairs={{0,4},{1,5},{2,6},{3,7},{4,0},{5,1},{6,2},{7,3},{8,12},{9,13},{10,... | collective-permute-start | bytes 368648 | tf_op jit(solution)/shard_map/ppermute | solution.py:103
  15.9 10.8 %collective-permute-start.3 = (bf16[2,24,1280]{2,1,0:T(8,128)(2,1)S(1)}, bf16[2,24,1280]{2,1,0:T(8,128)(2,1)S(1)}, u32[]{:S(2)}, u32[]{:S(2)}) collective-permute-start(bf16[2,24,1280]{2,1,0:T(8,128)(2,1)S(1)} %maximum_select_fusion.4), channel_id=1, source_target_pairs={{0,6},{1,7},{2,4},{3,5},{4,2},{5,3},{6,0},{7,1},{8,14},{9,15},{10,... | collective-permute-start | bytes 368648 | tf_op jit(solution)/shard_map/ppermute | solution.py:103
  26.7 23.1 %copy-start.29 = (f32[96,768]{1,0:T(8,128)S(1)}, f32[96,768]{1,0:T(8,128)}, u32[]{:S(2)}) copy-start(f32[96,768]{1,0:T(8,128)} %param.30) | copy-start | bytes 884740
  26.7 26.6 %copy-start.41 = (s32[2,64]{1,0:T(2,128)S(1)}, s32[2,64]{1,0:T(2,128)}, u32[]{:S(2)}) copy-start(s32[2,64]{1,0:T(2,128)} %param.34) | copy-start | bytes 1540
  26.8 30.9 %copy-start.10 = (bf16[4,2,24,1280]{3,2,1,0:T(8,128)(2,1)}, bf16[4,2,24,1280]{3,2,1,0:T(8,128)(2,1)S(1)}, u32[]{:S(2)}) copy-start(bf16[4,2,24,1280]{3,2,1,0:T(8,128)(2,1)S(1)} %pad_maximum_fusion.2.refs_0_) | copy-start | bytes 1474564
  26.8 21.8 %collective-permute-start.5 = (bf16[4,2,24,1280]{3,2,1,0:T(8,128)(2,1)S(1)}, bf16[4,2,24,1280]{3,2,1,0:T(8,128)(2,1)S(1)}, u32[]{:S(2)}, u32[]{:S(2)}) collective-permute-start(bf16[4,2,24,1280]{3,2,1,0:T(8,128)(2,1)S(1)} %pad_maximum_fusion.2.refs_0_), channel_id=1, source_target_pairs={{0,8},{8,0},{16,24},{24,16},{1,9},{9,1},{17,25},{25,17},{2,10},{10... | collective-permute-start | bytes 1474568 | tf_op jit(solution)/shard_map/ppermute | solution.py:107
  28.1 20.5 %collective-permute-start.6 = (bf16[4,2,24,1280]{3,2,1,0:T(8,128)(2,1)S(1)}, bf16[4,2,24,1280]{3,2,1,0:T(8,128)(2,1)S(1)}, u32[]{:S(2)}, u32[]{:S(2)}) collective-permute-start(bf16[4,2,24,1280]{3,2,1,0:T(8,128)(2,1)S(1)} %pad_maximum_fusion.2.refs_0_), channel_id=1, source_target_pairs={{0,16},{8,24},{16,0},{24,8},{1,17},{9,25},{17,1},{25,9},{2,18},{10... | collective-permute-start | bytes 1474568 | tf_op jit(solution)/shard_map/ppermute | solution.py:107
  28.3 5.1 %collective-permute-start.7 = (bf16[2,24,2304]{2,1,0:T(8,128)(2,1)S(1)}, bf16[2,24,2304]{2,1,0:T(8,128)(2,1)S(1)}, u32[]{:S(2)}, u32[]{:S(2)}) collective-permute-start(bf16[2,24,2304]{2,1,0:T(8,128)(2,1)S(1)} %maximum_select_fusion.3), channel_id=1, source_target_pairs={{0,2},{1,3},{2,0},{3,1},{4,6},{5,7},{6,4},{7,5},{8,10},{9,11},{10,... | collective-permute-start | bytes 663560 | tf_op jit(solution)/shard_map/ppermute | solution.py:103
  28.3 10.4 %collective-permute-start.8 = (bf16[2,24,2304]{2,1,0:T(8,128)(2,1)S(1)}, bf16[2,24,2304]{2,1,0:T(8,128)(2,1)S(1)}, u32[]{:S(2)}, u32[]{:S(2)}) collective-permute-start(bf16[2,24,2304]{2,1,0:T(8,128)(2,1)S(1)} %maximum_select_fusion.3), channel_id=1, source_target_pairs={{0,4},{1,5},{2,6},{3,7},{4,0},{5,1},{6,2},{7,3},{8,12},{9,13},{10,... | collective-permute-start | bytes 663560 | tf_op jit(solution)/shard_map/ppermute | solution.py:103
  30.9 17.7 %collective-permute-start.9 = (bf16[2,24,2304]{2,1,0:T(8,128)(2,1)S(1)}, bf16[2,24,2304]{2,1,0:T(8,128)(2,1)S(1)}, u32[]{:S(2)}, u32[]{:S(2)}) collective-permute-start(bf16[2,24,2304]{2,1,0:T(8,128)(2,1)S(1)} %maximum_select_fusion.3), channel_id=1, source_target_pairs={{0,6},{1,7},{2,4},{3,5},{4,2},{5,3},{6,0},{7,1},{8,14},{9,15},{10,... | collective-permute-start | bytes 663560 | tf_op jit(solution)/shard_map/ppermute | solution.py:103
  49.7 32.9 %copy-start.5 = (bf16[4,2,24,2304]{3,2,1,0:T(8,128)(2,1)}, bf16[4,2,24,2304]{3,2,1,0:T(8,128)(2,1)S(1)}, u32[]{:S(2)}) copy-start(bf16[4,2,24,2304]{3,2,1,0:T(8,128)(2,1)S(1)} %pad_maximum_fusion.refs_0_) | copy-start | bytes 2654212
  49.7 222.8 %reduce-scatter.2.cloned.1.call-start = ((), (), s32[]{:S(2)}) async-start(), calls=%async_computation.2 | async-start | bytes 3538944 | tf_op jit(solution)/shard_map/reduce_scatter | solution.py:678
  49.8 7.8 %collective-permute-start.17 = (bf16[96,768]{1,0:T(8,128)(2,1)S(1)}, bf16[96,768]{1,0:T(8,128)(2,1)S(1)}, u32[]{:S(2)}, u32[]{:S(2)}) collective-permute-start(bf16[96,768]{1,0:T(8,128)(2,1)S(1)} %convert_element_type.246), channel_id=1, source_target_pairs={{0,2},{1,3},{2,0},{3,1},{4,6},{5,7},{6,4},{7,5},{8,10},{9,11},{10,... | collective-permute-start | bytes 442376 | tf_op jit(solution)/shard_map/ppermute | solution.py:103
  49.9 13.3 %collective-permute-start.18 = (bf16[96,768]{1,0:T(8,128)(2,1)S(1)}, bf16[96,768]{1,0:T(8,128)(2,1)S(1)}, u32[]{:S(2)}, u32[]{:S(2)}) collective-permute-start(bf16[96,768]{1,0:T(8,128)(2,1)S(1)} %convert_element_type.246), channel_id=1, source_target_pairs={{0,4},{1,5},{2,6},{3,7},{4,0},{5,1},{6,2},{7,3},{8,12},{9,13},{10,... | collective-permute-start | bytes 442376 | tf_op jit(solution)/shard_map/ppermute | solution.py:103
  53.4 22.1 %collective-permute-start.19 = (bf16[96,768]{1,0:T(8,128)(2,1)S(1)}, bf16[96,768]{1,0:T(8,128)(2,1)}, u32[]{:S(2)}, u32[]{:S(2)}) collective-permute-start(bf16[96,768]{1,0:T(8,128)(2,1)S(1)} %convert_element_type.246), channel_id=1, source_target_pairs={{0,6},{1,7},{2,4},{3,5},{4,2},{5,3},{6,0},{7,1},{8,14},{9,15},{10,... | collective-permute-start | bytes 442376 | tf_op jit(solution)/shard_map/ppermute | solution.py:103
  53.5 30.2 %collective-permute-start.14 = (bf16[4,2,24,2304]{3,2,1,0:T(8,128)(2,1)S(1)}, bf16[4,2,24,2304]{3,2,1,0:T(8,128)(2,1)S(1)}, u32[]{:S(2)}, u32[]{:S(2)}) collective-permute-start(bf16[4,2,24,2304]{3,2,1,0:T(8,128)(2,1)S(1)} %pad_maximum_fusion.refs_0_), channel_id=1, source_target_pairs={{0,16},{8,24},{16,0},{24,8},{1,17},{9,25},{17,1},{25,9},{2,18},{10... | collective-permute-start | bytes 2654216 | tf_op jit(solution)/shard_map/ppermute | solution.py:107
  54.8 31.0 %collective-permute-start.13 = (bf16[4,2,24,2304]{3,2,1,0:T(8,128)(2,1)S(1)}, bf16[4,2,24,2304]{3,2,1,0:T(8,128)(2,1)S(1)}, u32[]{:S(2)}, u32[]{:S(2)}) collective-permute-start(bf16[4,2,24,2304]{3,2,1,0:T(8,128)(2,1)S(1)} %pad_maximum_fusion.refs_0_), channel_id=1, source_target_pairs={{0,8},{8,0},{16,24},{24,16},{1,9},{9,1},{17,25},{25,17},{2,10},{10... | collective-permute-start | bytes 2654216 | tf_op jit(solution)/shard_map/ppermute | solution.py:107
  57.7 20.3 %collective-permute-start.10 = (bf16[2,2,24,1280]{3,2,1,0:T(8,128)(2,1)}, bf16[2,2,24,1280]{3,2,1,0:T(8,128)(2,1)S(1)}, u32[]{:S(2)}, u32[]{:S(2)}) collective-permute-start(bf16[2,2,24,1280]{3,2,1,0:T(8,128)(2,1)} %slice.197), channel_id=1, source_target_pairs={{0,8},{8,0},{16,24},{24,16},{1,9},{9,1},{17,25},{25,17},{2,10},{10... | collective-permute-start | bytes 737288 | tf_op jit(solution)/shard_map/ppermute | solution.py:107
  63.2 15.7 %collective-permute-start.11 = (bf16[2,2,24,1280]{3,2,1,0:T(8,128)(2,1)S(1)}, bf16[2,2,24,1280]{3,2,1,0:T(8,128)(2,1)S(1)}, u32[]{:S(2)}, u32[]{:S(2)}) collective-permute-start(bf16[2,2,24,1280]{3,2,1,0:T(8,128)(2,1)S(1)} %slice.198), channel_id=1, source_target_pairs={{0,16},{8,24},{16,0},{24,8},{1,17},{9,25},{17,1},{25,9},{2,18},{10... | collective-permute-start | bytes 737288 | tf_op jit(solution)/shard_map/ppermute | solution.py:107
  77.4 37.9 %collective-permute-start.20 = (bf16[4,96,768]{2,1,0:T(8,128)(2,1)}, bf16[4,96,768]{2,1,0:T(8,128)(2,1)}, u32[]{:S(2)}, u32[]{:S(2)}) collective-permute-start(bf16[4,96,768]{2,1,0:T(8,128)(2,1)} %pad_maximum_fusion.1.refs_0_), channel_id=1, source_target_pairs={{0,8},{8,0},{16,24},{24,16},{1,9},{9,1},{17,25},{25,17},{2,10},{10... | collective-permute-start | bytes 1769480 | tf_op jit(solution)/shard_map/ppermute | solution.py:107
  78.0 37.4 %collective-permute-start.21 = (bf16[4,96,768]{2,1,0:T(8,128)(2,1)}, bf16[4,96,768]{2,1,0:T(8,128)(2,1)}, u32[]{:S(2)}, u32[]{:S(2)}) collective-permute-start(bf16[4,96,768]{2,1,0:T(8,128)(2,1)} %pad_maximum_fusion.1.refs_0_), channel_id=1, source_target_pairs={{0,16},{8,24},{16,0},{24,8},{1,17},{9,25},{17,1},{25,9},{2,18},{10... | collective-permute-start | bytes 1769480 | tf_op jit(solution)/shard_map/ppermute | solution.py:107
  83.6 36.6 %copy-start.18 = (f32[12,768]{1,0:T(8,128)}, f32[12,768]{1,0:T(8,128)S(1)}, u32[]{:S(2)}) copy-start(f32[12,768]{1,0:T(8,128)S(1)} %convert_bitcast_fusion.vec_ref) | copy-start | bytes 110596
  83.7 9.4 %copy-start.8 = (bf16[4,2,24,2304]{3,2,1,0:T(8,128)(2,1)}, bf16[4,2,24,2304]{3,2,1,0:T(8,128)(2,1)S(1)}, u32[]{:S(2)}) copy-start(bf16[4,2,24,2304]{3,2,1,0:T(8,128)(2,1)S(1)} %collective-permute-done.14.refs_2_) | copy-start | bytes 2654212
  84.6 37.9 %collective-permute-start.15 = (bf16[2,2,24,2304]{3,2,1,0:T(8,128)(2,1)}, bf16[2,2,24,2304]{3,2,1,0:T(8,128)(2,1)}, u32[]{:S(2)}, u32[]{:S(2)}) collective-permute-start(bf16[2,2,24,2304]{3,2,1,0:T(8,128)(2,1)} %slice.267), channel_id=1, source_target_pairs={{0,8},{8,0},{16,24},{24,16},{1,9},{9,1},{17,25},{25,17},{2,10},{10... | collective-permute-start | bytes 1327112 | tf_op jit(solution)/shard_map/ppermute | solution.py:107
  85.8 7.3 %copy-start.9 = (bf16[4,2,24,2304]{3,2,1,0:T(8,128)(2,1)}, bf16[4,2,24,2304]{3,2,1,0:T(8,128)(2,1)S(1)}, u32[]{:S(2)}) copy-start(bf16[4,2,24,2304]{3,2,1,0:T(8,128)(2,1)S(1)} %collective-permute-done.13.refs_1_) | copy-start | bytes 2654212
  86.7 35.8 %collective-permute-start.16 = (bf16[2,2,24,2304]{3,2,1,0:T(8,128)(2,1)}, bf16[2,2,24,2304]{3,2,1,0:T(8,128)(2,1)}, u32[]{:S(2)}, u32[]{:S(2)}) collective-permute-start(bf16[2,2,24,2304]{3,2,1,0:T(8,128)(2,1)} %slice.268), channel_id=1, source_target_pairs={{0,16},{8,24},{16,0},{24,8},{1,17},{9,25},{17,1},{25,9},{2,18},{10... | collective-permute-start | bytes 1327112 | tf_op jit(solution)/shard_map/ppermute | solution.py:107
  93.1 6.6 %copy-start.1 = (bf16[2,1024,768]{2,1,0:T(8,128)(2,1)S(1)}, bf16[2,1024,768]{2,1,0:T(8,128)(2,1)}, u32[]{:S(2)}) copy-start(bf16[2,1024,768]{2,1,0:T(8,128)(2,1)} %all-gather.2.cloned.1.call-done) | copy-start | bytes 9437188
  115.1 15.7 %collective-permute-start.12 = (bf16[2,256,384]{2,1,0:T(8,128)(2,1)}, bf16[2,256,384]{2,1,0:T(8,128)(2,1)}, u32[]{:S(2)}, u32[]{:S(2)}) collective-permute-start(bf16[2,256,384]{2,1,0:T(8,128)(2,1)} %get-tuple-element.105), channel_id=1, source_target_pairs={{0,1},{1,0},{2,3},{3,2},{4,5},{5,4},{6,7},{7,6},{8,9},{9,8},{10,11... | collective-permute-start | bytes 1179656 | tf_op jit(solution)/shard_map/ppermute | solution.py:99
  117.0 9.5 %collective-permute-start.22 = (bf16[2,96,768]{2,1,0:T(8,128)(2,1)}, bf16[2,96,768]{2,1,0:T(8,128)(2,1)S(1)}, u32[]{:S(2)}, u32[]{:S(2)}) collective-permute-start(bf16[2,96,768]{2,1,0:T(8,128)(2,1)} %slice.207), channel_id=1, source_target_pairs={{0,8},{8,0},{16,24},{24,16},{1,9},{9,1},{17,25},{25,17},{2,10},{10... | collective-permute-start | bytes 884744 | tf_op jit(solution)/shard_map/ppermute | solution.py:107
  119.1 8.4 %collective-permute-start.23 = (bf16[2,96,768]{2,1,0:T(8,128)(2,1)}, bf16[2,96,768]{2,1,0:T(8,128)(2,1)}, u32[]{:S(2)}, u32[]{:S(2)}) collective-permute-start(bf16[2,96,768]{2,1,0:T(8,128)(2,1)} %slice.208), channel_id=1, source_target_pairs={{0,16},{8,24},{16,0},{24,8},{1,17},{9,25},{17,1},{25,9},{2,18},{10... | collective-permute-start | bytes 884744 | tf_op jit(solution)/shard_map/ppermute | solution.py:107
  130.8 8.0 %copy-start.2 = (bf16[4,4,96,768]{3,2,1,0:T(8,128)(2,1)S(1)}, bf16[4,4,96,768]{3,2,1,0:T(8,128)(2,1)}, u32[]{:S(2)}) copy-start(bf16[4,4,96,768]{3,2,1,0:T(8,128)(2,1)} %place_last.1) | copy-start | bytes 7077892
  141.6 6.2 %copy-start.13 = (f32[512,768]{1,0:T(8,128)}, f32[512,768]{1,0:T(8,128)S(1)}, u32[]{:S(2)}) copy-start(f32[512,768]{1,0:T(8,128)S(1)} %fusion.21.part_ref) | copy-start | bytes 4718596
  141.6 6.2 %collective-permute-start.24 = (f32[512,768]{1,0:T(8,128)S(1)}, f32[512,768]{1,0:T(8,128)S(1)}, u32[]{:S(2)}, u32[]{:S(2)}) collective-permute-start(f32[512,768]{1,0:T(8,128)S(1)} %fusion.21.part_ref), channel_id=1, source_target_pairs={{0,1},{1,0},{2,3},{3,2},{4,5},{5,4},{6,7},{7,6},{8,9},{9,8},{10,11... | collective-permute-start | bytes 4718600 | tf_op jit(solution)/shard_map/ppermute | solution.py:99
  143.0 3.6 %collective-permute-start.25 = (bf16[2,128,768]{2,1,0:T(8,128)(2,1)S(1)}, bf16[2,128,768]{2,1,0:T(8,128)(2,1)S(1)}, u32[]{:S(2)}, u32[]{:S(2)}) collective-permute-start(bf16[2,128,768]{2,1,0:T(8,128)(2,1)S(1)} %copy-done.25), channel_id=1, source_target_pairs={{0,1},{1,0},{2,3},{3,2},{4,5},{5,4},{6,7},{7,6},{8,9},{9,8},{10,11... | collective-permute-start | bytes 1179656 | tf_op jit(solution)/shard_map/ppermute | solution.py:99
  148.9 11.1 %copy-start.42 = (bf16[512,1536]{1,0:T(8,128)(2,1)S(1)}, bf16[512,1536]{1,0:T(8,128)(2,1)}, u32[]{:S(2)}) copy-start(bf16[512,1536]{1,0:T(8,128)(2,1)} %get-tuple-element.108) | copy-start | bytes 4718596
  159.6 15.4 %collective-permute-start.26 = (f32[512,768]{1,0:T(8,128)}, f32[512,768]{1,0:T(8,128)}, u32[]{:S(2)}, u32[]{:S(2)}) collective-permute-start(f32[512,768]{1,0:T(8,128)} %get-tuple-element.116.part_ref), channel_id=1, source_target_pairs={{0,1},{1,0},{2,3},{3,2},{4,5},{5,4},{6,7},{7,6},{8,9},{9,8},{10,11... | collective-permute-start | bytes 4718600 | tf_op jit(solution)/shard_map/ppermute | solution.py:99
  167.0 7.1 %copy-start.39 = (f32[8,1536]{1,0:T(8,128)S(1)}, f32[8,1536]{1,0:T(8,128)}, u32[]{:S(2)}) copy-start(f32[8,1536]{1,0:T(8,128)} %get-tuple-element.146) | copy-start | bytes 147460
  167.0 7.9 %copy-start.36 = (f32[3,8,768]{2,1,0:T(8,128)S(1)}, f32[3,8,768]{2,1,0:T(8,128)}, u32[]{:S(2)}) copy-start(f32[3,8,768]{2,1,0:T(8,128)} %get-tuple-element.145) | copy-start | bytes 221188
  171.9 30.1 %collective-permute-start.27 = (bf16[4,48,3072]{2,1,0:T(8,128)(2,1)}, bf16[4,48,3072]{2,1,0:T(8,128)(2,1)}, u32[]{:S(2)}, u32[]{:S(2)}) collective-permute-start(bf16[4,48,3072]{2,1,0:T(8,128)(2,1)} %get-tuple-element.130), channel_id=1, source_target_pairs={{0,8},{8,0},{16,24},{24,16},{1,9},{9,1},{17,25},{25,17},{2,10},{10... | collective-permute-start | bytes 3538952 | tf_op jit(solution)/shard_map/ppermute | solution.py:107
  173.0 29.1 %collective-permute-start.28 = (bf16[4,48,3072]{2,1,0:T(8,128)(2,1)}, bf16[4,48,3072]{2,1,0:T(8,128)(2,1)}, u32[]{:S(2)}, u32[]{:S(2)}) collective-permute-start(bf16[4,48,3072]{2,1,0:T(8,128)(2,1)} %get-tuple-element.131), channel_id=1, source_target_pairs={{0,16},{8,24},{16,0},{24,8},{1,17},{9,25},{17,1},{25,9},{2,18},{10... | collective-permute-start | bytes 3538952 | tf_op jit(solution)/shard_map/ppermute | solution.py:107
  180.3 14.8 %copy-start.11 = (bf16[4,4,2,24,1152]{4,3,2,1,0:T(8,128)(2,1)S(1)}, bf16[4,4,2,24,1152]{4,3,2,1,0:T(8,128)(2,1)}, u32[]{:S(2)}) copy-start(bf16[4,4,2,24,1152]{4,3,2,1,0:T(8,128)(2,1)} %get-tuple-element.103) | copy-start | bytes 5308420
  205.5 17.7 %collective-permute-start.31 = (bf16[2,48,3072]{2,1,0:T(8,128)(2,1)}, bf16[2,48,3072]{2,1,0:T(8,128)(2,1)}, u32[]{:S(2)}, u32[]{:S(2)}) collective-permute-start(bf16[2,48,3072]{2,1,0:T(8,128)(2,1)} %add_convert_fusion.2), channel_id=1, source_target_pairs={{0,8},{8,0},{16,24},{24,16},{1,9},{9,1},{17,25},{25,17},{2,10},{10... | collective-permute-start | bytes 1769480 | tf_op jit(solution)/shard_map/ppermute | solution.py:107
  208.0 14.1 %collective-permute-start.30 = (bf16[2,48,3072]{2,1,0:T(8,128)(2,1)}, bf16[2,48,3072]{2,1,0:T(8,128)(2,1)}, u32[]{:S(2)}, u32[]{:S(2)}) collective-permute-start(bf16[2,48,3072]{2,1,0:T(8,128)(2,1)} %add_convert_fusion.3), channel_id=1, source_target_pairs={{0,16},{8,24},{16,0},{24,8},{1,17},{9,25},{17,1},{25,9},{2,18},{10... | collective-permute-start | bytes 1769480 | tf_op jit(solution)/shard_map/ppermute | solution.py:107
  209.3 11.1 %collective-permute-start.32 = (bf16[2,384]{1,0:T(2,128)(2,1)}, bf16[2,384]{1,0:T(2,128)(2,1)}, u32[]{:S(2)}, u32[]{:S(2)}) collective-permute-start(bf16[2,384]{1,0:T(2,128)(2,1)} %pad_maximum_fusion.6), channel_id=1, source_target_pairs={{0,1},{1,0},{2,3},{3,2},{4,5},{5,4},{6,7},{7,6},{8,9},{9,8},{10,11... | collective-permute-start | bytes 4616 | tf_op jit(solution)/shard_map/ppermute | solution.py:99
  229.3 14.2 %collective-permute-start.33 = (bf16[4,48,1664]{2,1,0:T(8,128)(2,1)}, bf16[4,48,1664]{2,1,0:T(8,128)(2,1)S(1)}, u32[]{:S(2)}, u32[]{:S(2)}) collective-permute-start(bf16[4,48,1664]{2,1,0:T(8,128)(2,1)} %get-tuple-element.148), channel_id=1, source_target_pairs={{0,8},{8,0},{16,24},{24,16},{1,9},{9,1},{17,25},{25,17},{2,10},{10... | collective-permute-start | bytes 1916936 | tf_op jit(solution)/shard_map/ppermute | solution.py:107
  230.5 15.2 %collective-permute-start.34 = (bf16[4,48,1664]{2,1,0:T(8,128)(2,1)}, bf16[4,48,1664]{2,1,0:T(8,128)(2,1)S(1)}, u32[]{:S(2)}, u32[]{:S(2)}) collective-permute-start(bf16[4,48,1664]{2,1,0:T(8,128)(2,1)} %get-tuple-element.149), channel_id=1, source_target_pairs={{0,16},{8,24},{16,0},{24,8},{1,17},{9,25},{17,1},{25,9},{2,18},{10... | collective-permute-start | bytes 1916936 | tf_op jit(solution)/shard_map/ppermute | solution.py:107
  231.6 14.1 %copy-start.27 = (bf16[2,48,1664]{2,1,0:T(8,128)(2,1)S(1)}, bf16[2,48,1664]{2,1,0:T(8,128)(2,1)}, u32[]{:S(2)}) copy-start(bf16[2,48,1664]{2,1,0:T(8,128)(2,1)} %get-tuple-element.152) | copy-start | bytes 958468
  231.6 16.2 %copy-start.26 = (bf16[2,48,1664]{2,1,0:T(8,128)(2,1)S(1)}, bf16[2,48,1664]{2,1,0:T(8,128)(2,1)}, u32[]{:S(2)}) copy-start(bf16[2,48,1664]{2,1,0:T(8,128)(2,1)} %get-tuple-element.151) | copy-start | bytes 958468
  234.0 42.6 %collective-permute-start.29 = (bf16[512,768]{1,0:T(8,128)(2,1)S(1)}, bf16[512,768]{1,0:T(8,128)(2,1)}, u32[]{:S(2)}, u32[]{:S(2)}) collective-permute-start(bf16[512,768]{1,0:T(8,128)(2,1)S(1)} %convolution_convert_fusion.2), channel_id=1, source_target_pairs={{0,1},{1,0},{2,3},{3,2},{4,5},{5,4},{6,7},{7,6},{8,9},{9,8},{10,11... | collective-permute-start | bytes 2359304 | tf_op jit(solution)/shard_map/ppermute | solution.py:99
  235.8 17.0 %collective-permute-start.37 = (bf16[48,3072]{1,0:T(8,128)(2,1)}, bf16[48,3072]{1,0:T(8,128)(2,1)S(1)}, u32[]{:S(2)}, u32[]{:S(2)}) collective-permute-start(bf16[48,3072]{1,0:T(8,128)(2,1)} %get-tuple-element.173), channel_id=1, source_target_pairs={{0,2},{1,3},{2,0},{3,1},{4,6},{5,7},{6,4},{7,5},{8,10},{9,11},{10,... | collective-permute-start | bytes 884744 | tf_op jit(solution)/shard_map/ppermute | solution.py:103
  238.3 16.8 %collective-permute-start.38 = (bf16[48,3072]{1,0:T(8,128)(2,1)}, bf16[48,3072]{1,0:T(8,128)(2,1)S(1)}, u32[]{:S(2)}, u32[]{:S(2)}) collective-permute-start(bf16[48,3072]{1,0:T(8,128)(2,1)} %get-tuple-element.170), channel_id=1, source_target_pairs={{0,4},{1,5},{2,6},{3,7},{4,0},{5,1},{6,2},{7,3},{8,12},{9,13},{10,... | collective-permute-start | bytes 884744 | tf_op jit(solution)/shard_map/ppermute | solution.py:103
  243.5 23.0 %collective-permute-start.39 = (bf16[48,3072]{1,0:T(8,128)(2,1)}, bf16[48,3072]{1,0:T(8,128)(2,1)S(1)}, u32[]{:S(2)}, u32[]{:S(2)}) collective-permute-start(bf16[48,3072]{1,0:T(8,128)(2,1)} %get-tuple-element.169), channel_id=1, source_target_pairs={{0,6},{1,7},{2,4},{3,5},{4,2},{5,3},{6,0},{7,1},{8,14},{9,15},{10,... | collective-permute-start | bytes 884744 | tf_op jit(solution)/shard_map/ppermute | solution.py:103
  245.6 21.0 %copy-start.20 = (bf16[4,48,1664]{2,1,0:T(8,128)(2,1)}, bf16[4,48,1664]{2,1,0:T(8,128)(2,1)S(1)}, u32[]{:S(2)}) copy-start(bf16[4,48,1664]{2,1,0:T(8,128)(2,1)S(1)} %collective-permute-done.34) | copy-start | bytes 1916932
  246.6 25.9 %collective-permute-start.36 = (bf16[2,48,1664]{2,1,0:T(8,128)(2,1)}, bf16[2,48,1664]{2,1,0:T(8,128)(2,1)}, u32[]{:S(2)}, u32[]{:S(2)}) collective-permute-start(bf16[2,48,1664]{2,1,0:T(8,128)(2,1)} %add_convert_fusion.4), channel_id=1, source_target_pairs={{0,8},{8,0},{16,24},{24,16},{1,9},{9,1},{17,25},{25,17},{2,10},{10... | collective-permute-start | bytes 958472 | tf_op jit(solution)/shard_map/ppermute | solution.py:107
  252.8 19.7 %collective-permute-start.35 = (bf16[2,48,1664]{2,1,0:T(8,128)(2,1)}, bf16[2,48,1664]{2,1,0:T(8,128)(2,1)}, u32[]{:S(2)}, u32[]{:S(2)}) collective-permute-start(bf16[2,48,1664]{2,1,0:T(8,128)(2,1)} %add_convert_fusion.5), channel_id=1, source_target_pairs={{0,16},{8,24},{16,0},{24,8},{1,17},{9,25},{17,1},{25,9},{2,18},{10... | collective-permute-start | bytes 958472 | tf_op jit(solution)/shard_map/ppermute | solution.py:107
  266.8 2.4 collective-permute-start.44
  273.9 6.0 %collective-permute-start.40 = (bf16[48,1664]{1,0:T(8,128)(2,1)S(1)}, bf16[48,1664]{1,0:T(8,128)(2,1)S(1)}, u32[]{:S(2)}, u32[]{:S(2)}) collective-permute-start(bf16[48,1664]{1,0:T(8,128)(2,1)S(1)} %get-tuple-element.174), channel_id=1, source_target_pairs={{0,2},{1,3},{2,0},{3,1},{4,6},{5,7},{6,4},{7,5},{8,10},{9,11},{10,... | collective-permute-start | bytes 479240 | tf_op jit(solution)/shard_map/ppermute | solution.py:103
  274.0 9.8 %collective-permute-start.41 = (bf16[48,1664]{1,0:T(8,128)(2,1)S(1)}, bf16[48,1664]{1,0:T(8,128)(2,1)S(1)}, u32[]{:S(2)}, u32[]{:S(2)}) collective-permute-start(bf16[48,1664]{1,0:T(8,128)(2,1)S(1)} %get-tuple-element.171), channel_id=1, source_target_pairs={{0,4},{1,5},{2,6},{3,7},{4,0},{5,1},{6,2},{7,3},{8,12},{9,13},{10,... | collective-permute-start | bytes 479240 | tf_op jit(solution)/shard_map/ppermute | solution.py:103
  276.4 14.3 %collective-permute-start.42 = (bf16[48,1664]{1,0:T(8,128)(2,1)S(1)}, bf16[48,1664]{1,0:T(8,128)(2,1)S(1)}, u32[]{:S(2)}, u32[]{:S(2)}) collective-permute-start(bf16[48,1664]{1,0:T(8,128)(2,1)S(1)} %get-tuple-element.172), channel_id=1, source_target_pairs={{0,6},{1,7},{2,4},{3,5},{4,2},{5,3},{6,0},{7,1},{8,14},{9,15},{10,... | collective-permute-start | bytes 479240 | tf_op jit(solution)/shard_map/ppermute | solution.py:103
  291.8 3.0 collective-permute-start.43
  (28 other events, 94.6 us)
Sparse Core Ops, SparseCore 0:
  49.9 43.1 all-gather.1
  202.1 39.9 reduce-scatter.1
where the time goes:
time: 304 us; the launch traced here: 303 us
  waiting for transfers between devices  88 us (29%)
  Pallas kernels  69.6 us (23%)
  starting transfers between devices  41.8 us (14%)
  matrix products  36.1 us (12%)
  local copies, waits for them, and re-layouts  27.1 us (9%)
  other arithmetic  25.6 us (8%)
  between operations  14.8 us (5%)
    ppermute x15, waiting for transfers between devices, z_move(): return lax.ppermute(value, 'seq', [(i, i ^ 2 * step) for i in range(seq)])  73 us
    pallas_call x3, Pallas kernels, over_rows(): pl.pallas_call(kernel, grid=(rows // TILE,), in_specs=[pl.BlockSpec(memor...  23.9 us
    pallas_call x5, Pallas kernels, local_copies(): pl.pallas_call(kernel, in_specs=[pl.BlockSpec(memory_space=pltpu.SMEM)] +...  18.6 us
    ppermute x15, starting transfers between devices, z_move(): return lax.ppermute(value, 'seq', [(i, i ^ 2 * step) for i in range(seq)])  17.2 us
    ppermute x20, starting transfers between devices, dp_move(): return lax.ppermute(value, 'dp', [(i, i ^ step) for i in range(dps)])  16 us
    dot_general x7, matrix products, tn(): lax.dot_general(left, right, (((0,), (0,)), ((), ())), preferred_element_...  15.7 us
    pallas_call x1, Pallas kernels, attend_back(): pl.pallas_call(backward_kernel, grid=(streams, PAIRS), in_specs=[specs['q...  14.8 us
    dot_general x3, matrix products, nn(): lax.dot_general(left, right, (((1,), (0,)), ((), ())), preferred_element_...  11.8 us
  transfers between devices with their start and end apart: 47, of which 19 were waited for; matrix products, arithmetic and copies ran while one was open for 26% of the time, Pallas kernels for 16%

commit v1 on v0

--- a/solution.py
+++ b/solution.py
@@ -20,7 +20,8 @@
 EPSILON = 1e-12
 BF = jnp.bfloat16
 F32 = jnp.float32
-VMEM_LIMIT = 56 * 1024 * 1024
+VMEM_LIMIT = 28 * 1024 * 1024
+VMEM_LARGE = 56 * 1024 * 1024
 QUICK = pl.CostEstimate(flops=0, bytes_accessed=0, transcendentals=0)
 
 
@@ -115,6 +116,10 @@
     return [value] + [z_move(value, j, seq) for j in range(1, seq // 2)]
 
 
+def gather_dp_direct(value, dps):
+    return [value] + [dp_move(value, k, dps) for k in range(1, dps)]
+
+
 def gather_dp_first(value, dps):
     return [value] + [dp_move(value, k, dps) for k in range(1, 3 if dps == 4 else dps)]
 
@@ -126,11 +131,11 @@
     return blocks + [dp_move(blocks[2][:half], 1, dps), dp_move(blocks[1][half:], 2, dps)]
 
 
-def dp_pieces(dps, zs):
+def dp_pieces(dps, zs, direct):
     half = zs // 2
     for k in range(dps):
         for j in range(zs):
-            if dps == 4 and k == 3:
+            if dps == 4 and k == 3 and not direct:
                 yield (3, j, k, j) if j < half else (4, j - half, k, j)
             else:
                 yield k, j, k, j
@@ -272,7 +277,7 @@
             jax.ShapeDtypeStruct((streams, rows, HALF), BF),
             jax.ShapeDtypeStruct((streams, PAIRS, 2, rows, 128), F32),
         ],
-        compiler_params=pltpu.CompilerParams(vmem_limit_bytes=VMEM_LIMIT),
+        compiler_params=pltpu.CompilerParams(vmem_limit_bytes=VMEM_LIMIT if count <= 1024 else VMEM_LARGE),
         cost_estimate=QUICK,
         name="attend",
     )(query_ids, key_ids, queries, key_values, key_values)
@@ -298,13 +303,12 @@
         ],
         out_specs=[specs["row"], specs["key"], specs["key"]],
         out_shape=[jax.ShapeDtypeStruct((streams, rows, HALF), BF), key_shape, key_shape],
-        compiler_params=pltpu.CompilerParams(vmem_limit_bytes=VMEM_LIMIT),
+        compiler_params=pltpu.CompilerParams(vmem_limit_bytes=VMEM_LIMIT if count <= 1024 else VMEM_LARGE),
         cost_estimate=QUICK,
         name="attend_back",
     )(query_ids, key_ids, queries, key_values, key_values, lse, upward)
 
 
-TILE = 256
 CHUNK = 384
 QUERY_BIAS, VALUE_BIAS, OUT_BIAS, FIRST_GAIN, FIRST_SHIFT, REDUCE_BIAS, SECOND_GAIN, SECOND_SHIFT = range(8)
 
@@ -330,44 +334,140 @@
     return vec_ref[index : index + 1, :]
 
 
+def half_of_ref(place_ref):
+    return pl.ds(pl.multiple_of(place_ref[2] * HALF, 128), HALF)
+
+
+def other_half_of_ref(place_ref):
+    return pl.ds(pl.multiple_of((1 - place_ref[2]) * HALF, 128), HALF)
+
+
+def project_kernel(place_ref, tok_ref, vec_ref, weight_ref, pairs_ref, query_ref, rows_ref):
+    half = half_of_ref(place_ref)
+    pairs = nn(tok_ref[0], weight_ref[:, HALF:])
+    pairs_ref[0, :, :HALF] = pairs[:, :HALF].astype(BF)
+    pairs_ref[0, :, HALF:] = (pairs[:, HALF:] + vec_ref[VALUE_BIAS : VALUE_BIAS + 1, half]).astype(BF)
+    chip_rows = rows_ref.shape[1]
+    tiles = tok_ref.shape[1] // chip_rows
+
+    @pl.when(pl.program_id(1) == place_ref[1] // tiles)
+    def _():
+        first = pl.multiple_of(place_ref[1] % tiles * chip_rows, chip_rows)
+        tokens = tok_ref[0, pl.ds(first, chip_rows), :]
+        queries = nn(tokens, weight_ref[:, :HALF]) + vec_ref[QUERY_BIAS : QUERY_BIAS + 1, half]
+        query_ref[0] = (queries * 0.125).astype(BF)
+        rows_ref[0] = tokens
+
+
+def project(place, tokens, vectors, weight, chip_rows):
+    streams, count, _ = tokens.shape
+    shape = lambda rows, lanes: jax.ShapeDtypeStruct((streams, rows, lanes), BF)
+    tile = 4 * chip_rows
+    return pl.pallas_call(
+        project_kernel,
+        grid=(streams, count // tile),
+        in_specs=[
+            pl.BlockSpec(memory_space=pltpu.SMEM),
+            pl.BlockSpec((1, tile, D), lambda s, t: (s, t, 0)),
+            pl.BlockSpec(memory_space=pltpu.VMEM),
+            pl.BlockSpec(memory_space=pltpu.VMEM),
+        ],
+        out_specs=[
+            pl.BlockSpec((1, tile, D), lambda s, t: (s, t, 0)),
+            pl.BlockSpec((1, chip_rows, HALF), lambda s, t: (s, 0, 0)),
+            pl.BlockSpec((1, chip_rows, D), lambda s, t: (s, 0, 0)),
+        ],
+        out_shape=[shape(count, D), shape(chip_rows, HALF), shape(chip_rows, D)],
+        compiler_params=pltpu.CompilerParams(vmem_limit_bytes=VMEM_LIMIT),
+        cost_estimate=QUICK,
+        name="project",
+    )(place, tokens, vectors, weight)
+
+
+def unproject_kernel(place_ref, query_ref, key_ref, value_ref, weight_ref, out_ref):
+    back = jnp.concatenate([key_ref[0], value_ref[0]], axis=1)
+    out_ref[0] = nt(back, weight_ref[:, HALF:]).astype(BF)
+    chip_rows = query_ref.shape[1]
+    tiles = out_ref.shape[1] // chip_rows
+
+    @pl.when(pl.program_id(1) == place_ref[1] // tiles)
+    def _():
+        span = pl.ds(pl.multiple_of(place_ref[1] % tiles * chip_rows, chip_rows), chip_rows)
+        own = jnp.concatenate([query_ref[0], key_ref[0, span, :], value_ref[0, span, :]], axis=1)
+        out_ref[0, span, :] = nt(own, weight_ref[...]).astype(BF)
+
+
+def unproject(place, query_back, key_back, value_back, weight):
+    streams, count, _ = key_back.shape
+    chip_rows = query_back.shape[1]
+    tile = 4 * chip_rows
+    block = lambda lanes: pl.BlockSpec((1, tile, lanes), lambda s, t: (s, t, 0))
+    return pl.pallas_call(
+        unproject_kernel,
+        grid=(streams, count // tile),
+        in_specs=[
+            pl.BlockSpec(memory_space=pltpu.SMEM),
+            pl.BlockSpec((1, chip_rows, HALF), lambda s, t: (s, 0, 0)),
+            block(HALF),
+            block(HALF),
+            pl.BlockSpec(memory_space=pltpu.VMEM),
+        ],
+        out_specs=block(D),
+        out_shape=jax.ShapeDtypeStruct((streams, count, D), BF),
+        compiler_params=pltpu.CompilerParams(vmem_limit_bytes=VMEM_LIMIT),
+        cost_estimate=QUICK,
+        name="unproject",
+    )(place, query_back, key_back, value_back, weight)
+
+
 def middle_kernel(
-    place_ref, mine_ref, other_ref, tok_ref, vec_ref, unit_ref, out_ref, expand_ref,
-    normed_ref, inverse_ref, low_ref, hidden_ref, slope_ref,
+    place_ref, mine_ref, other_ref, tok_ref, vec_ref, unit_ref, out_ref, expand_ref, reduce_ref,
+    normed_ref, inverse_ref, low_ref, hidden_ref, slope_ref, part_ref, send_ref,
 ):
-    core = place_ref[2]
-    for_mine = out_ref[pl.ds(pl.multiple_of(core * HALF, 128), HALF), :]
-    for_other = out_ref[pl.ds(pl.multiple_of((1 - core) * HALF, 128), HALF), :]
-    branch = nn(mine_ref[...], for_mine) + nn(other_ref[...], for_other) + vector_of(vec_ref, OUT_BIAS)
+    branch = nn(mine_ref[...], out_ref[half_of_ref(place_ref), :])
+    branch += nn(other_ref[...], out_ref[other_half_of_ref(place_ref), :])
+    branch += vector_of(vec_ref, OUT_BIAS)
     normed, inverse = norm_rows(tok_ref[...].astype(F32) + branch)
     normed_ref[...] = normed
     inverse_ref[...] = jnp.broadcast_to(inverse, inverse_ref.shape)
     first = normed * vector_of(vec_ref, FIRST_GAIN) + vector_of(vec_ref, FIRST_SHIFT)
     low = first.astype(BF)
     low_ref[...] = low
+    total = jnp.zeros(part_ref.shape, F32)
     for start in range(0, UNITS, CHUNK):
         span = slice(start, start + CHUNK)
         expanded = nn(low, expand_ref[:, span]) + unit_ref[:, span]
         share = 0.5 * (1.0 + lax.erf(expanded * (0.5**0.5)))
-        hidden_ref[:, span] = (expanded * share).astype(BF)
+        hidden = (expanded * share).astype(BF)
+        hidden_ref[:, span] = hidden
         bell = jnp.exp(-0.5 * expanded * expanded) * 0.3989422804014327
         slope_ref[:, span] = (share + expanded * bell).astype(BF)
+        total += nn(hidden, reduce_ref[span, :])
+    part_ref[...] = total
+    send_ref[...] = total.astype(BF)
 
 
 def turn_kernel(
-    part_ref, came_ref, normed_ref, cot_ref, slope_ref, vec_ref, reduce_ref, expand_ref,
-    act_ref, residual_ref, low_ref, back_ref, next_ref, sum_ref, unit_sum_ref,
+    place_ref, part_ref, came_ref, normed_ref, mine_ref, other_ref, slope_ref, vec_ref, reduce_ref, expand_ref,
+    act_ref, residual_ref, low_ref, back_ref, next_ref, send_ref, sum_ref, unit_sum_ref,
 ):
     @pl.when(pl.program_id(0) == 0)
     def _():
         sum_ref[...] = jnp.zeros_like(sum_ref)
         unit_sum_ref[...] = jnp.zeros_like(unit_sum_ref)
 
+    core = place_ref[2]
     first = normed_ref[...] * vector_of(vec_ref, FIRST_GAIN) + vector_of(vec_ref, FIRST_SHIFT)
-    reduced = part_ref[...] + came_ref[...] + vector_of(vec_ref, REDUCE_BIAS)
+    reduced = part_ref[...] + came_ref[...].astype(F32) + vector_of(vec_ref, REDUCE_BIAS)
     normed, inverse = norm_rows(first + reduced)
     gain = vector_of(vec_ref, SECOND_GAIN)
-    act_ref[...] = (normed * gain + vector_of(vec_ref, SECOND_SHIFT)).astype(BF)
-    upward = cot_ref[...].astype(F32)
+    half = normed.shape[0] // 2
+    mine = jnp.where(core == 0, normed[:half], normed[half:])
+    act_ref[...] = (mine * gain + vector_of(vec_ref, SECOND_SHIFT)).astype(BF)
+    mine, other = mine_ref[...].astype(F32), other_ref[...].astype(F32)
+    upward = jnp.concatenate(
+        [jnp.where(core == 0, mine, other), jnp.where(core == 0, other, mine)], axis=0
+    )
     residual = norm_back(upward * gain, normed, inverse)
     low = residual.astype(BF)
     residual_ref[...] = residual
@@ -383,6 +483,7 @@
         unit_sum_ref[:, span] += jnp.sum(back.astype(F32).reshape(-1, 8, CHUNK), axis=0)
         total += nt(back, expand_ref[:, span])
     next_ref[...] = total
+    send_ref[...] = total.astype(BF)
 
 
 def first_back_kernel(
@@ -393,38 +494,128 @@
     def _():
         sum_ref[...] = jnp.zeros_like(sum_ref)
 
-    core = place_ref[2]
-    upward = part_ref[...] + came_ref[...] + residual_ref[...]
+    upward = part_ref[...] + came_ref[...].astype(F32) + residual_ref[...]
     normed = normed_ref[...]
     add_rows(sum_ref, 1, upward * normed)
     add_rows(sum_ref, 2, upward)
     back = norm_back(upward * vector_of(vec_ref, FIRST_GAIN), normed, inverse_ref[:, :1])
     low = back.astype(BF)
-    back_ref[...] = back
+    half = back.shape[0] // 2
+    back_ref[...] = jnp.where(place_ref[2] == 0, back[:half], back[half:])
     low_ref[...] = low
     add_rows(sum_ref, 0, low.astype(F32))
-    mine = out_ref[pl.ds(pl.multiple_of(core * HALF, 128), HALF), :]
-    attended_ref[...] = nt(low, mine).astype(BF)
-
-
-def over_rows(kernel, place, tiled, whole, outs, sums, name, macs):
-    rows = tiled[0].shape[0]
-    tile = lambda lanes: pl.BlockSpec((TILE, lanes), lambda t: (t, 0))
+    attended_ref[...] = nt(low, out_ref[half_of_ref(place_ref), :]).astype(BF)
+
+
+def over_rows(kernel, place, steps, tiled, whole, outs, sums, name):
+    tile = lambda shape: pl.BlockSpec((shape[0] // steps, shape[1]), lambda t: (t, 0))
     keep = lambda shape: pl.BlockSpec(shape, lambda t: (0,) * len(shape))
-    places = [] if place is None else [place]
     return pl.pallas_call(
         kernel,
-        grid=(rows // TILE,),
-        in_specs=[pl.BlockSpec(memory_space=pltpu.SMEM)] * len(places)
-        + [tile(v.shape[1]) for v in tiled]
+        grid=(steps,),
+        in_specs=[pl.BlockSpec(memory_space=pltpu.SMEM)]
+        + [tile(v.shape) for v in tiled]
         + [pl.BlockSpec(memory_space=pltpu.VMEM)] * len(whole),
-        out_specs=[tile(lanes) for lanes, _ in outs] + [keep(shape) for shape in sums],
-        out_shape=[jax.ShapeDtypeStruct((rows, lanes), dtype) for lanes, dtype in outs]
+        out_specs=[tile(out) for out in outs] + [keep(shape) for shape in sums],
+        out_shape=[jax.ShapeDtypeStruct(out[:2], out[2]) for out in outs]
         + [jax.ShapeDtypeStruct(shape, F32) for shape in sums],
         compiler_params=pltpu.CompilerParams(vmem_limit_bytes=VMEM_LIMIT),
         cost_estimate=QUICK,
         name=name,
-    )(*places, *tiled, *whole)
+    )(place, *tiled, *whole)
+
+
+def packed_call(kernel, place, sources, shapes, scratch, name):
+    return pl.pallas_call(
+        kernel,
+        in_specs=[pl.BlockSpec(memory_space=pltpu.SMEM)]
+        + [pl.BlockSpec(memory_space=pltpu.VMEM)] * len(sources),
+        out_specs=[pl.BlockSpec(memory_space=pltpu.VMEM)] * len(shapes),
+        out_shape=[jax.ShapeDtypeStruct(shape, BF) for shape in shapes],
+        scratch_shapes=scratch,
+        compiler_params=pltpu.CompilerParams(vmem_limit_bytes=VMEM_LIMIT),
+        cost_estimate=QUICK,
+        name=name,
+    )(place, *sources)
+
+
+def wide_packs_of(place, hidden, reduced_back, first_low, expanded_back, dps, zs):
+    chips = dps * zs
+    both, wide = D // chips, UNITS // chips
+    slots, counts = scatter_slots(dps, zs)
+    lanes = 2 * D + UNITS
+
+    def kernel(place_ref, hidden_ref, reduced_ref, low_ref, expanded_ref, *refs):
+        outs, (reduce_ref, expand_ref) = refs[: len(counts)], refs[len(counts) :]
+        for start in range(0, UNITS, CHUNK):
+            span = slice(start, start + CHUNK)
+            reduce_ref[span, :] = tn(hidden_ref[:, span], reduced_ref[...]).astype(BF)
+        for start in range(0, D, 256):
+            span = slice(start, start + 256)
+            expand_ref[span, :] = tn(low_ref[:, span], expanded_ref[...]).astype(BF)
+        for (k, j), (array, row) in slots.items():
+            chip = (place_ref[0] ^ k) * zs + (place_ref[1] ^ j)
+            first = pl.multiple_of(chip * wide, 16)
+            outs[array][row, :, :D] = reduce_ref[pl.ds(first, both), :]
+            outs[array][row, :, D : 2 * D] = reduce_ref[pl.ds(pl.multiple_of(first + both, 16), both), :]
+            outs[array][row, :, 2 * D :] = expand_ref[pl.ds(pl.multiple_of(chip * both, 16), both), :]
+
+    return packed_call(
+        kernel,
+        place,
+        [hidden, reduced_back, first_low, expanded_back],
+        [(count, both, lanes) for count in counts],
+        [pltpu.VMEM((UNITS, D), BF), pltpu.VMEM((D, UNITS), BF)],
+        "wide_packs",
+    )
+
+
+def narrow_packs_of(place, tokens, chip_tokens, backs, mine, other, branch_back, sums, dps, zs):
+    chips = dps * zs
+    both = D // chips
+    slots, counts = scatter_slots(dps, zs)
+    lanes = 4 * HALF + 128
+    query_back, key_back, value_back = backs
+
+    def kernel(
+        place_ref, tok_ref, chip_ref, query_ref, key_ref, value_ref, mine_ref, other_ref, branch_ref,
+        one_ref, two_ref, unit_ref, *refs,
+    ):
+        outs, (all_ref, square_ref) = refs[: len(counts)], refs[len(counts) :]
+        half = half_of_ref(place_ref)
+        for start in range(0, D, 256):
+            span = slice(start, start + 256)
+            turned = tok_ref[:, span].T
+            all_ref[span, :HALF] = tn(chip_ref[:, span], query_ref[...]).astype(BF)
+            all_ref[span, HALF : 2 * HALF] = nn(turned, key_ref[...]).astype(BF)
+            all_ref[span, 2 * HALF : 3 * HALF] = nn(turned, value_ref[...]).astype(BF)
+        branch = branch_ref[:, half]
+        all_ref[half, 3 * HALF : 4 * HALF] = tn(mine_ref[...], branch).astype(BF)
+        all_ref[other_half_of_ref(place_ref), 3 * HALF : 4 * HALF] = tn(other_ref[...], branch).astype(BF)
+        square_ref[...] = jnp.zeros_like(square_ref)
+        for row, ref in ((0, query_ref), (1, value_ref)):
+            square_ref[row : row + 1, half] = jnp.sum(ref[...].astype(F32), axis=0, keepdims=True)
+        for i in range(3):
+            square_ref[2 + i : 3 + i, :] = jnp.sum(one_ref[i], axis=0, keepdims=True)
+            square_ref[5 + i : 6 + i, :] = jnp.sum(two_ref[i], axis=0, keepdims=True)
+        unit = jnp.sum(unit_ref[...], axis=0, keepdims=True)
+        for chip in range(chips):
+            for h in range(2):
+                first = (2 * chip + h) * both
+                square_ref[8 + h : 9 + h, chip * both : (chip + 1) * both] = unit[:, first : first + both]
+        all_ref[:, 4 * HALF :] = square_ref[...].T.astype(BF)
+        for (k, j), (array, row) in slots.items():
+            chip = (place_ref[0] ^ k) * zs + (place_ref[1] ^ j)
+            outs[array][row] = all_ref[pl.ds(pl.multiple_of(chip * both, 16), both), :]
+
+    return packed_call(
+        kernel,
+        place,
+        [tokens, chip_tokens, query_back, key_back, value_back, mine, other, branch_back, *sums],
+        [(count, both, lanes) for count in counts],
+        [pltpu.VMEM((D, lanes), BF), pltpu.VMEM((128, D), F32)],
+        "narrow_packs",
+    )
 
 
 def column_sum(value_rows):
@@ -518,10 +709,11 @@
     all_tokens = row_major(lax.all_gather(tied(tokens, late), "seq", axis=1, tiled=True))
     last = z_moves(tied(reduce_weight.astype(BF), late), seq)
     late = gather_dp_rest(gather_dp_first(late, dps), dps)
-    last = gather_dp_first(jnp.stack(last), dps)
-    cotangent = in_core_order(cotangent, swap(cotangent), 1)
-
-    def gather_plan(parts):
+    last = gather_dp_direct(jnp.stack(last), dps)
+    other_cotangent = swap(cotangent).reshape(-1, D)
+    cotangent = cotangent.reshape(-1, D)
+
+    def gather_plan(parts, direct=False):
         return [
             (
                 piece,
@@ -533,7 +725,7 @@
                 target,
                 lambda dp, z, j=j, k=k: (dp ^ k, z ^ j),
             )
-            for piece, row, k, j in dp_pieces(dps, zs)
+            for piece, row, k, j in dp_pieces(dps, zs, direct)
             for first, count, target in parts
         ]
 
@@ -546,7 +738,6 @@
     )
     qkv_weight = qkv_weight.reshape(D, 3 * HALF)
     small = small.astype(F32).reshape(D, 128)[:, :12].T
-    query_bias, value_bias = small[QUERY_BIAS : QUERY_BIAS + 1], small[VALUE_BIAS : VALUE_BIAS + 1]
     expand_bias = small[8:12].reshape(4, chips, 2, block)
     expand_bias = lax.dynamic_index_in_dim(expand_bias, core, 2, keepdims=False)
     expand_bias = expand_bias.transpose(1, 0, 2).reshape(1, UNITS)
@@ -554,19 +745,14 @@
     def half_of(vector):
         return lax.dynamic_slice_in_dim(vector, core * HALF, HALF, 1)
 
-    chip_tokens = lax.dynamic_slice_in_dim(all_tokens, z * chip_rows, chip_rows, 1).reshape(rows, D)
     flat_all = all_tokens.reshape(-1, D)
     ids = item_ids(lengths, jnp.arange(all_tokens.shape[1], dtype=jnp.int32))
     key_ids = jnp.broadcast_to(ids[:, None, :], (streams, 8, ids.shape[1]))
     query_ids = lax.dynamic_slice_in_dim(ids, z * chip_rows, chip_rows, 1)
     query_ids = jnp.broadcast_to(query_ids[..., None], (streams, chip_rows, 128))
 
-    queries = ((nn(chip_tokens, qkv_weight[:, :HALF]) + half_of(query_bias)) * 0.125).astype(BF)
-    queries = row_major(queries.reshape(streams, chip_rows, HALF))
-    key_value_bias = jnp.concatenate([jnp.zeros((1, HALF), F32), half_of(value_bias)], axis=1)
-    key_values = (nn(flat_all, qkv_weight[:, HALF:]) + key_value_bias).astype(BF)
-    key_values = row_major(key_values.reshape(streams, -1, D))
-    last = gather_dp_rest(tied(last, key_values), dps)
+    key_values, queries, chip_tokens = project(place, all_tokens, small, qkv_weight, chip_rows)
+    chip_tokens = chip_tokens.reshape(rows, D)
     attended, lse = attend(query_ids, key_ids, queries, key_values)
     other_attended = swap(attended).reshape(rows, HALF)
     attended = attended.reshape(rows, HALF)
@@ -581,40 +767,47 @@
     out_weight = out_weight.reshape(D, D)
     expand_weight = expand_weight.reshape(D, UNITS)
     (reduce_weight,) = local_copies(
-        place, last, [(dps, zs, wide, D)], gather_plan([(0, D, 0)]), "place_last"
+        place, last, [(dps, zs, wide, D)], gather_plan([(0, D, 0)], direct=True), "place_last"
     )
     reduce_weight = reduce_weight.reshape(UNITS, D)
 
-    def own(value):
-        value = value.reshape(streams, chip_rows, -1)
-        return lax.dynamic_slice_in_dim(value, core * row_count, row_count, 1)
-
-    normed_one, inverse_one, first_low, hidden, slope = over_rows(
+    normed_one, inverse_one, first_low, hidden, slope, partial, sent = over_rows(
         middle_kernel,
         place,
+        streams,
         [attended, other_attended, chip_tokens],
-        [small, expand_bias, out_weight, expand_weight],
-        [(D, F32), (128, F32), (D, BF), (UNITS, BF), (UNITS, BF)],
+        [small, expand_bias, out_weight, expand_weight, reduce_weight],
+        [
+            (rows, D, F32),
+            (rows, 128, F32),
+            (rows, D, BF),
+            (rows, UNITS, BF),
+            (rows, UNITS, BF),
+            (rows, D, F32),
+            (rows, D, BF),
+        ],
         [],
         "middle",
-        rows * D * (D + UNITS),
-    )
-    partial = nn(hidden, reduce_weight)
-    activations, residual_two_back, reduced_back, expanded_back, next_partial, sums_two, unit_sums = over_rows(
+    )
+    activations, residual_two_back, reduced_back, expanded_back, partial, sent, sums_two, unit_sums = over_rows(
         turn_kernel,
-        None,
-        [partial, swap(partial), normed_one, cotangent.reshape(rows, D), slope],
+        place,
+        streams,
+        [partial, swap(sent), normed_one, cotangent, other_cotangent, slope],
         [small, reduce_weight, expand_weight],
-        [(D, BF), (D, F32), (D, BF), (UNITS, BF), (D, F32)],
+        [
+            (rows // 2, D, BF),
+            (rows, D, F32),
+            (rows, D, BF),
+            (rows, UNITS, BF),
+            (rows, D, F32),
+            (rows, D, BF),
+        ],
         [(3, 8, D), (8, UNITS)],
         "turn",
-        2 * rows * D * UNITS,
-    )
-    reduce_bias_grad, second_gain_grad, second_shift_grad = jnp.sum(sums_two, axis=1)
-    expand_bias_grad = jnp.sum(unit_sums, axis=0)
-    came_partial = swap(next_partial)
-    reduce_weight_grad = tn(hidden, reduced_back).astype(BF)
-    expand_weight_grad = tn(first_low, expanded_back).astype(BF)
+    )
+    came_partial = swap(sent)
+    fused = both % 16 == 0
 
     def scatter_plan(parts, lanes):
         slots, counts = scatter_slots(dps, zs)
@@ -634,90 +827,93 @@
         ]
         return [(count, both, lanes) for count in counts], plan
 
-    wide_packs = local_copies(
-        place,
-        [
-            reduce_weight_grad.reshape(dps, zs, 2, both, D),
-            expand_weight_grad.reshape(dps, zs, both, UNITS),
-        ],
-        *scatter_plan(
+    if fused:
+        wide_packs = wide_packs_of(place, hidden, reduced_back, first_low, expanded_back, dps, zs)
+    else:
+        wide_packs = local_copies(
+            place,
             [
-                (0, lambda d, zz: (d, zz, 0), 0, D),
-                (0, lambda d, zz: (d, zz, 1), D, D),
-                (1, lambda d, zz: (d, zz), 2 * D, UNITS),
+                tn(hidden, reduced_back).astype(BF).reshape(dps, zs, 2, both, D),
+                tn(first_low, expanded_back).astype(BF).reshape(dps, zs, both, UNITS),
             ],
-            2 * D + UNITS,
-        ),
-        "pack_wide",
-    )
-
+            *scatter_plan(
+                [
+                    (0, lambda d, zz: (d, zz, 0), 0, D),
+                    (0, lambda d, zz: (d, zz, 1), D, D),
+                    (1, lambda d, zz: (d, zz), 2 * D, UNITS),
+                ],
+                2 * D + UNITS,
+            ),
+            "pack_wide",
+        )
     wide_came = scatter_dp_first(wide_packs, dps)
 
     residual_one_back, branch_back, attended_back, sums_one = over_rows(
         first_back_kernel,
         place,
-        [next_partial, came_partial, residual_two_back, normed_one, inverse_one],
+        streams,
+        [partial, came_partial, residual_two_back, normed_one, inverse_one],
         [small, out_weight],
-        [(D, F32), (D, BF), (HALF, BF)],
+        [(rows // 2, D, F32), (rows, D, BF), (rows, HALF, BF)],
         [(3, 8, D)],
         "first_back",
-        rows * D * HALF,
-    )
-    out_bias_grad, first_gain_grad, first_shift_grad = jnp.sum(sums_one, axis=1)
+    )
     attended_back = attended_back.reshape(streams, chip_rows, HALF)
 
     query_back, key_back, value_back = attend_back(
         query_ids, key_ids, queries, key_values, lse, attended_back
     )
-    flat_query_back = query_back.reshape(rows, HALF)
-    key_back = key_back.reshape(-1, HALF)
-    value_back = value_back.reshape(-1, HALF)
-
-    tokens_part = nt(key_back, qkv_weight[:, HALF : 2 * HALF]) + nt(value_back, qkv_weight[:, 2 * HALF :])
-    tokens_part = tokens_part.astype(BF).reshape(streams, -1, D)
+    tokens_part = unproject(place, query_back, key_back, value_back, qkv_weight)
     tokens_total = lax.psum_scatter(tokens_part, "seq", scatter_dimension=1, tiled=True)
     wide_came = tied(wide_came, tokens_part)
     wide_onward = scatter_dp_middle(wide_packs, wide_came, dps)
-    key_back, value_back, flat_query_back, out_side = tied(
-        (key_back, value_back, flat_query_back, half_of(branch_back)), wide_onward
-    )
-    key_weight_grad = tn(flat_all, key_back).astype(BF)
-    value_weight_grad = tn(flat_all, value_back).astype(BF)
-    query_weight_grad = tn(chip_tokens, flat_query_back).astype(BF)
-    out_weight_grad = in_core_order(tn(attended, out_side), tn(other_attended, out_side), 0).astype(BF)
-    half_sums = jnp.stack([column_sum(flat_query_back), column_sum(value_back)])
-    full_sums = in_core_order(half_sums, swap(half_sums), 1)
-    small_grads = jnp.concatenate(
-        [
-            full_sums,
-            jnp.stack(
-                [
-                    out_bias_grad,
-                    first_gain_grad,
-                    first_shift_grad,
-                    reduce_bias_grad,
-                    second_gain_grad,
-                    second_shift_grad,
-                ]
+    backs = (query_back.reshape(rows, HALF), key_back.reshape(-1, HALF), value_back.reshape(-1, HALF))
+    backs = tied(backs, wide_onward)
+    if fused:
+        narrow_packs = narrow_packs_of(
+            place,
+            flat_all,
+            chip_tokens,
+            backs,
+            attended,
+            other_attended,
+            branch_back,
+            (sums_one, sums_two, unit_sums),
+            dps,
+            zs,
+        )
+        wide_totals = scatter_dp_rest(wide_packs, wide_came, wide_onward, dps)
+    else:
+        out_side = half_of(branch_back)
+        zeros = jnp.zeros((D,), F32)
+        small_grads = jnp.concatenate(
+            [
+                lax.dynamic_update_slice_in_dim(zeros, column_sum(backs[0]), core * HALF, 0)[None],
+                lax.dynamic_update_slice_in_dim(zeros, column_sum(backs[2]), core * HALF, 0)[None],
+                jnp.sum(sums_one, axis=1),
+                jnp.sum(sums_two, axis=1),
+                jnp.sum(unit_sums, axis=0).reshape(chips, 2, both).transpose(1, 0, 2).reshape(2, D),
+            ],
+            axis=0,
+        ).T.astype(BF)
+        small_grads = jnp.pad(small_grads, ((0, 0), (0, 128 - small_grads.shape[1])))
+        four = (
+            tn(chip_tokens, backs[0]).astype(BF),
+            tn(flat_all, backs[1]).astype(BF),
+            tn(flat_all, backs[2]).astype(BF),
+            in_core_order(tn(attended, out_side), tn(other_attended, out_side), 0).astype(BF),
+        )
+        wide_totals = scatter_dp_rest(wide_packs, wide_came, wide_onward, dps)
+        narrow_packs = local_copies(
+            place,
+            [g.reshape(dps, zs, both, HALF) for g in four] + [small_grads.reshape(dps, zs, both, 128)],
+            *scatter_plan(
+                [(i, lambda d, zz: (d, zz), i * HALF, HALF) for i in range(4)]
+                + [(4, lambda d, zz: (d, zz), 4 * HALF, 128)],
+                4 * HALF + 128,
             ),
-            expand_bias_grad.reshape(chips, 2, both).transpose(1, 0, 2).reshape(2, D),
-        ],
-        axis=0,
-    ).T.astype(BF)
-    small_grads = jnp.pad(small_grads, ((0, 0), (0, 128 - small_grads.shape[1])))
-    four = (query_weight_grad, key_weight_grad, value_weight_grad, out_weight_grad)
-    wide_totals = scatter_dp_rest(wide_packs, wide_came, wide_onward, dps)
-    four = tied(four, wide_totals)
-    narrow_packs = local_copies(
-        place,
-        [g.reshape(dps, zs, both, HALF) for g in four] + [small_grads.reshape(dps, zs, both, 128)],
-        *scatter_plan(
-            [(i, lambda d, zz: (d, zz), i * HALF, HALF) for i in range(4)]
-            + [(4, lambda d, zz: (d, zz), 4 * HALF, 128)],
-            4 * HALF + 128,
-        ),
-        "pack_narrow",
-    )
+            "pack_narrow",
+        )
     came = tied(scatter_dp_first(narrow_packs, dps), wide_totals)
     narrow_onward = scatter_dp_middle(narrow_packs, came, dps)
     wide_grads = scatter_z(wide_totals, seq, lambda moved: tied(moved, narrow_onward))
@@ -725,22 +921,21 @@
         narrow_packs, came, narrow_onward, dps, lambda came: tied(came, wide_grads, tokens_total)
     )
     narrow_grads = scatter_z(narrow_totals, seq)
-    query_part = nt(flat_query_back, qkv_weight[:, :HALF]).astype(BF)
-    query_part = own(query_part).astype(F32) + own(swap(query_part)).astype(F32)
-    tokens_gradient = own(residual_one_back) + query_part + tokens_total.astype(F32)
+    tokens_gradient = residual_one_back.reshape(tokens.shape) + tokens_total.astype(F32)
 
     def own_rows(grads):
         split = grads.reshape(2, block, grads.shape[1])
         mine = lax.dynamic_index_in_dim(split, core, 0, keepdims=False)
         return mine, swap(lax.dynamic_index_in_dim(split, 1 - core, 0, keepdims=False))
 
-    mine, other = own_rows(narrow_grads[:, : 4 * HALF])
+    mine, other = own_rows(narrow_grads)
     matrices = [
         in_core_order(mine[:, i * HALF : (i + 1) * HALF], other[:, i * HALF : (i + 1) * HALF], 1)
         for i in range(4)
     ]
     small = narrow_grads[:, 4 * HALF :]
-    own_small = lax.dynamic_slice_in_dim(small, core * block, block, 0).T
+    own_small = mine[:, 4 * HALF :].T
+    both_small = (mine[:, 4 * HALF : 4 * HALF + 2] + other[:, 4 * HALF : 4 * HALF + 2]).T
     expand_bias_grad = small[:, 8:10].T.reshape(wide)
     mine, other = own_rows(wide_grads[:, 2 * D :])
     expand_grads = in_core_order(
@@ -749,13 +944,13 @@
     reduce_grads = jnp.concatenate([wide_grads[:, :D], wide_grads[:, D : 2 * D]], axis=0)
 
     return (
-        own(activations),
+        activations.reshape(tokens.shape),
         tokens_gradient,
         matrices[0],
-        own_small[0],
+        both_small[0],
         matrices[1],
         matrices[2],
-        own_small[1],
+        both_small[1],
         matrices[3],
         own_small[2],
         own_small[3],

time: 304 us -> 284 us (0.934)
  matrix products: 36.1 us -> 0 us
  starting transfers between devices: 41.8 us -> 56.7 us
  other arithmetic: 25.6 us -> 16.4 us
  waiting for transfers between devices: 88 us -> 94.9 us
  local copies, waits for them, and re-layouts: 27.1 us -> 33.7 us
    dot_general x13 -> x0, matrix products: 36.1 us -> none  [the longest x7 15.7 us: tn(): lax.dot_general(left, right, (((0,), (0,)), ((), ())), preferred_element_...]
    pallas_call x5 -> x3, Pallas kernels: 18.6 us -> 4.42 us  [local_copies(): pl.pallas_call(kernel, in_specs=[pl.BlockSpec(memory_space=pltpu.SMEM)] +...]
    unnamed x92 -> x103, local copies, waits for them, and re-layouts: 5.7 us -> 19.1 us
    pallas_call x3 -> x7, Pallas kernels: 23.9 us -> 36.3 us  [the longest x3 15.4 us: over_rows(): pl.pallas_call(kernel, grid=(steps,), in_specs=[pl.BlockSpec(memory_space...]
    ppermute x10 -> x8, starting transfers between devices: 8.55 us -> 19.1 us  [core_swap(): return lax.ppermute(value, 'seq', [(i, i ^ 1) for i in range(seq)])]
    ppermute x20 -> x19, waiting for transfers between devices: 5.67 us -> 14.2 us  [dp_move(): return lax.ppermute(value, 'dp', [(i, i ^ step) for i in range(dps)])]
    all_gather x1, waiting for transfers between devices: 5.78 us -> 0.02 us  [body(): lax.all_gather(tied(tokens, late), 'seq', axis=1, tiled=True)]
    ppermute x15, waiting for transfers between devices: 73 us -> 77.4 us  [z_move(): return lax.ppermute(value, 'seq', [(i, i ^ 2 * step) for i in range(seq)])]
  transfers between devices with their start and end apart: 47 -> 44, of which waited for: 19 -> 16; matrix products, arithmetic and copies ran while one was open for 26% -> 10% of each run, Pallas kernels for 16% -> 18%
where the time goes in v1:
time: 284 us; the launch traced here: 283 us
  waiting for transfers between devices  94.9 us (33%)
  Pallas kernels  66.6 us (23%)
  starting transfers between devices  56.7 us (20%)
  local copies, waits for them, and re-layouts  33.7 us (12%)
  other arithmetic  16.4 us (6%)
  between operations  14.9 us (5%)
    ppermute x15, waiting for transfers between devices, z_move(): return lax.ppermute(value, 'seq', [(i, i ^ 2 * step) for i in range(seq)])  77.4 us
    ppermute x15, starting transfers between devices, z_move(): return lax.ppermute(value, 'seq', [(i, i ^ 2 * step) for i in range(seq)])  21.4 us
    unnamed x103, local copies, waits for them, and re-layouts  19.1 us
    ppermute x8, starting transfers between devices, core_swap(): return lax.ppermute(value, 'seq', [(i, i ^ 1) for i in range(seq)])  19.1 us
    ppermute x19, starting transfers between devices, dp_move(): return lax.ppermute(value, 'dp', [(i, i ^ step) for i in range(dps)])  16.1 us
    pallas_call x3, Pallas kernels, over_rows(): pl.pallas_call(kernel, grid=(steps,), in_specs=[pl.BlockSpec(memory_space...  15.4 us
    ppermute x19, waiting for transfers between devices, dp_move(): return lax.ppermute(value, 'dp', [(i, i ^ step) for i in range(dps)])  14.2 us
    pallas_call x1, Pallas kernels, attend_back(): pl.pallas_call(backward_kernel, grid=(streams, PAIRS), in_specs=[specs['q...  14.1 us
  transfers between devices with their start and end apart: 44, of which 16 were waited for; matrix products, arithmetic and copies ran while one was open for 10% of the time, Pallas kernels for 18%

profile of v1, /device:TPU:13, one launch (start us, length us, event | category | flops | bytes accessed | tf_op | source)
XLA Modules:
  0.0 283.2 jit_solution(2643517510612944795)
XLA Ops:
  7.8 1.8 first_columns.1
  12.5 1.3 dynamic-slice_reduce_fusion.1
  14.2 1.4 collective-permute-start.3
  15.6 1.1 collective-permute-start.2
  16.7 1.1 collective-permute-start.1
  17.8 6.2 %collective-permute-done.3 = bf16[2,24,1280]{2,1,0:T(8,128)(2,1)S(1)} collective-permute-done((bf16[2,24,1280]{2,1,0:T(8,128)(2,1)S(1)}, bf16[2,24,1280]{2,1,0:T(8,128)(2,1)S(1)}, u32[]{:S(2)}, u32[]{:S(2)}) %collective-permute-start.3) | collective-permute-done | bytes 122912 | tf_op jit(solution)/shard_map/ppermute | solution.py:104
  24.0 1.7 collective-permute-done.2
  26.4 1.2 collective-permute-start.5
  27.7 3.8 %collective-permute-start.8 = (bf16[2,24,2304]{2,1,0:T(8,128)(2,1)S(1)}, bf16[2,24,2304]{2,1,0:T(8,128)(2,1)S(1)}, u32[]{:S(2)}, u32[]{:S(2)}) collective-permute-start(bf16[2,24,2304]{2,1,0:T(8,128)(2,1)S(1)} %maximum_select_fusion.1), channel_id=1, source_target_pairs={{0,4},{1,5},{2,6},{3,7},{4,0},{5,1},{6,2},{7,3},{8,12},{9,13},{10,... | collective-permute-start | bytes 663560 | tf_op jit(solution)/shard_map/ppermute | solution.py:104
  31.6 1.1 collective-permute-done.9
  32.7 13.5 %collective-permute-done.8 = bf16[2,24,2304]{2,1,0:T(8,128)(2,1)S(1)} collective-permute-done((bf16[2,24,2304]{2,1,0:T(8,128)(2,1)S(1)}, bf16[2,24,2304]{2,1,0:T(8,128)(2,1)S(1)}, u32[]{:S(2)}, u32[]{:S(2)}) %collective-permute-start.8) | collective-permute-done | bytes 221216 | tf_op jit(solution)/shard_map/ppermute | solution.py:104
  47.3 1.3 collective-permute-start.14
  49.2 4.0 %collective-permute-start.18 = (bf16[96,768]{1,0:T(8,128)(2,1)S(1)}, bf16[96,768]{1,0:T(8,128)(2,1)S(1)}, u32[]{:S(2)}, u32[]{:S(2)}) collective-permute-start(bf16[96,768]{1,0:T(8,128)(2,1)S(1)} %convert_element_type.196), channel_id=1, source_target_pairs={{0,4},{1,5},{2,6},{3,7},{4,0},{5,1},{6,2},{7,3},{8,12},{9,13},{10,... | collective-permute-start | bytes 442376 | tf_op jit(solution)/shard_map/ppermute | solution.py:104
  53.3 15.7 %collective-permute-done.18 = bf16[96,768]{1,0:T(8,128)(2,1)S(1)} collective-permute-done((bf16[96,768]{1,0:T(8,128)(2,1)S(1)}, bf16[96,768]{1,0:T(8,128)(2,1)S(1)}, u32[]{:S(2)}, u32[]{:S(2)}) %collective-permute-start.18) | collective-permute-done | bytes 147488 | tf_op jit(solution)/shard_map/ppermute | solution.py:104
  69.9 1.2 collective-permute-start.22
  71.1 1.7 slice.175
  72.7 1.7 slice.174
  74.5 1.4 collective-permute-start.11
  76.1 6.4 %collective-permute-done.10.refs_3_ = bf16[2,2,24,1280]{3,2,1,0:T(8,128)(2,1)S(1)} collective-permute-done((bf16[2,2,24,1280]{3,2,1,0:T(8,128)(2,1)}, bf16[2,2,24,1280]{3,2,1,0:T(8,128)(2,1)S(1)}, u32[]{:S(2)}, u32[]{:S(2)}) %collective-permute-start.10) | collective-permute-done | bytes 245792 | tf_op jit(solution)/shard_map/ppermute | solution.py:108
  82.5 1.6 collective-permute-start.21
  84.1 1.2 collective-permute-start.20
  87.4 1.1 place_early.1
  88.5 1.2 copy-done.2
  93.6 1.9 copy-done
  95.5 1.5 copy-done.3
  97.0 4.1 %project.1 = (bf16[2,1024,768]{2,1,0:T(8,128)(2,1)S(1)}, bf16[2,256,384]{2,1,0:T(8,128)(2,1)S(1)}, bf16[2,256,768]{2,1,0:T(8,128)(2,1)S(1)}) custom-call(s32[3]{0:T(128)S(1)} %copy-done.44, bf16[2,1024,768]{2,1,0:T(8,128)(2,1)S(1)} %copy-done, f32[12,768]{1,0:T(8,128)S(1)} %convert_bitcast_fusion.vec_ref, bf16[768,1152]{1,0:T(8,128)(2,1)S(1)} %bitcast.84), custom_call_target="tpu_custom_call" | custom-call | tf_op jit(solution)/shard_map/project/pallas_call | solution.py:366
  102.1 10.0 %attend.1 = (bf16[2,256,384]{2,1,0:T(8,128)(2,1)}, f32[2,3,2,256,128]{4,3,2,1,0:T(8,128)S(1)}) custom-call(s32[2,256,128]{2,1,0:T(8,128)S(1)} %broadcast_in_dim.48.qid_ref, s32[2,8,1024]{2,1,0:T(8,128)S(1)} %broadcast_in_dim.49.kid_ref, bf16[2,256,384]{2,1,0:T(8,128)(2,1)S(1)} %get-tuple-element.103.q_ref, ...), custom_call_target="tpu_custom_call" | custom-call | tf_op jit(solution)/shard_map/attend/pallas_call | solution.py:271
  112.1 1.1 copy-done.22
  113.3 13.9 %collective-permute-start.12 = (bf16[2,256,384]{2,1,0:T(8,128)(2,1)}, bf16[2,256,384]{2,1,0:T(8,128)(2,1)}, u32[]{:S(2)}, u32[]{:S(2)}) collective-permute-start(bf16[2,256,384]{2,1,0:T(8,128)(2,1)} %get-tuple-element.105), channel_id=1, source_target_pairs={{0,1},{1,0},{2,3},{3,2},{4,5},{5,4},{6,7},{7,6},{8,9},{9,8},{10,11... | collective-permute-start | bytes 1179656 | tf_op jit(solution)/shard_map/ppermute | solution.py:100
  130.4 1.9 place_last.1
  132.8 1.4 place_late.1
  134.2 6.9 %middle.1 = (f32[512,768]{1,0:T(8,128)S(1)}, f32[512,128]{1,0:T(8,128)S(1)}, bf16[512,768]{1,0:T(8,128)(2,1)S(1)}, bf16[512,1536]{1,0:T(8,128)(2,1)S(1)}, bf16[5...) custom-call(s32[3]{0:T(128)S(1)} %copy-done.44, bf16[512,384]{1,0:T(8,128)(2,1)} %bitcast.18.mine_ref, ...), custom_call_target="tpu_custom_call" | custom-call | tf_op jit(solution)/shard_map/middle/pallas_call | solution.py:513
  141.7 2.3 collective-permute-done.24
  144.1 6.3 %turn.1 = (bf16[256,768]{1,0:T(8,128)(2,1)}, f32[512,768]{1,0:T(8,128)S(1)}, bf16[512,768]{1,0:T(8,128)(2,1)S(1)}, bf16[512,1536]{1,0:T(8,128)(2,1)S(1)}, f32[51...) custom-call(s32[3]{0:T(128)S(1)} %copy-done.44, ...), custom_call_target="tpu_custom_call" | custom-call | tf_op jit(solution)/shard_map/turn/pallas_call | solution.py:513
  150.6 4.8 %wide_packs.1 = (bf16[4,48,3072]{2,1,0:T(8,128)(2,1)S(1)}, bf16[4,48,3072]{2,1,0:T(8,128)(2,1)}, bf16[4,48,3072]{2,1,0:T(8,128)(2,1)}, bf16[2,48,3072]{2,1,0:T(8,128)(2,1)S(1)}, bf16[2,48,3072]{2,1,0:T(8,128)(2,1)S(1)}) custom-call(s32[3]{0:T(128)S(1)} %copy-done.44, bf16[512,1536]{1,0:T(8,128)(2,1)S(1)} %get-tuple-element.125.hidden_ref, ...), custom_call_target="tpu_custom_call" | custom-call | tf_op jit(solution)/shard_map/wide_packs/pallas_call | solution.py:529
  156.2 1.1 collective-permute-start.26
  157.3 1.6 collective-permute-start.27
  158.9 2.2 first_back.1
  162.0 14.1 %attend_back.1 = (bf16[2,256,384]{2,1,0:T(8,128)(2,1)S(1)}, bf16[2,1024,384]{2,1,0:T(8,128)(2,1)S(1)}, bf16[2,1024,384]{2,1,0:T(8,128)(2,1)S(1)}) custom-call(s32[2,256,128]{2,1,0:T(8,128)S(1)} %broadcast_in_dim.48.qid_ref, s32[2,8,1024]{2,1,0:T(8,128)S(1)} %broadcast_in_dim.49.kid_ref, bf16[2,256,384]{2,1,0:T(8,128)(2,1)S(1)} %copy-done.21, ...), custom_call_target="tpu_custom_call" | custom-call | tf_op jit(solution)/shard_map/attend_back/pallas_call | solution.py:292
  176.2 6.0 %unproject.1 = bf16[2,1024,768]{2,1,0:T(8,128)(2,1)} custom-call(s32[3]{0:T(128)S(1)} %copy-done.44, bf16[2,256,384]{2,1,0:T(8,128)(2,1)S(1)} %get-tuple-element.122.query_ref, bf16[2,1024,384]{2,1,0:T(8,128)(2,1)S(1)} %get-tuple-element.123.key_ref, bf16[2,1024,384]{2,1,0:T(8,128)(2,1)S(1)} %get-tuple-element.124.value_ref, bf16[768,1152]{1,0:T(8,128)(2,1)S(1)} %bitcast.85), custom_call_target="tpu_custom_call" | custom-call | tf_op jit(solution)/shard_map/unproject/pallas_call | solution.py:405
  182.3 1.2 copy-done.5
  183.5 1.1 copy-done.7
  185.5 1.5 add_convert_fusion.1
  187.8 1.4 add_convert_fusion
  189.7 1.1 copy-done.13
  190.8 1.1 copy-done.31
  192.0 5.9 %narrow_packs.1 = (bf16[4,48,1664]{2,1,0:T(8,128)(2,1)S(1)}, bf16[4,48,1664]{2,1,0:T(8,128)(2,1)S(1)}, bf16[4,48,1664]{2,1,0:T(8,128)(2,1)S(1)}, bf16[2,48,1664]...) custom-call(s32[3]{0:T(128)S(1)} %copy-done.44, bf16[2048,768]{1,0:T(8,128)(2,1)S(1)} %bitcast.81, ...), custom_call_target="tpu_custom_call" | custom-call | tf_op jit(solution)/shard_map/narrow_packs/pallas_call | solution.py:529
  197.9 1.1 collective-permute-start.28
  199.8 1.3 collective-permute-done.30
  201.1 1.5 collective-permute-done.31
  202.5 1.6 add_bitcast_fusion
  204.2 4.8 %collective-permute-start.35 = (bf16[48,3072]{1,0:T(8,128)(2,1)S(1)}, bf16[48,3072]{1,0:T(8,128)(2,1)S(1)}, u32[]{:S(2)}, u32[]{:S(2)}) collective-permute-start(bf16[48,3072]{1,0:T(8,128)(2,1)S(1)} %get-tuple-element.166), channel_id=1, source_target_pairs={{0,4},{1,5},{2,6},{3,7},{4,0},{5,1},{6,2},{7,3},{8,12},{9,13},{10,... | collective-permute-start | bytes 884744 | tf_op jit(solution)/shard_map/ppermute | solution.py:104
  209.0 1.1 collective-permute-start.34
  210.1 1.1 add_bitcast_fusion.3
  211.1 5.1 %collective-permute-done.28 = bf16[4,48,1664]{2,1,0:T(8,128)(2,1)S(1)} collective-permute-done((bf16[4,48,1664]{2,1,0:T(8,128)(2,1)S(1)}, bf16[4,48,1664]{2,1,0:T(8,128)(2,1)S(1)}, u32[]{:S(2)}, u32[]{:S(2)}) %collective-permute-start.28) | collective-permute-done | bytes 639008 | tf_op jit(solution)/shard_map/ppermute | solution.py:108
  217.0 1.2 collective-permute-start.32
  219.4 15.6 %collective-permute-done.36 = bf16[48,3072]{1,0:T(8,128)(2,1)S(1)} collective-permute-done((bf16[48,3072]{1,0:T(8,128)(2,1)S(1)}, bf16[48,3072]{1,0:T(8,128)(2,1)S(1)}, u32[]{:S(2)}, u32[]{:S(2)}) %collective-permute-start.36) | collective-permute-done | bytes 294944 | tf_op jit(solution)/shard_map/ppermute | solution.py:104
  235.1 10.5 %collective-permute-done.35 = bf16[48,3072]{1,0:T(8,128)(2,1)S(1)} collective-permute-done((bf16[48,3072]{1,0:T(8,128)(2,1)S(1)}, bf16[48,3072]{1,0:T(8,128)(2,1)S(1)}, u32[]{:S(2)}, u32[]{:S(2)}) %collective-permute-start.35) | collective-permute-done | bytes 294944 | tf_op jit(solution)/shard_map/ppermute | solution.py:104
  245.8 3.0 %collective-permute-start.41 = (f32[24,1536]{1,0:T(8,128)S(1)}, f32[24,1536]{1,0:T(8,128)S(1)}, u32[]{:S(2)}, u32[]{:S(2)}) collective-permute-start(f32[24,1536]{1,0:T(8,128)S(1)} %get-tuple-element.176), channel_id=1, source_target_pairs={{0,1},{1,0},{2,3},{3,2},{4,5},{5,4},{6,7},{7,6},{8,9},{9,8},{10,11... | collective-permute-start | bytes 442376 | tf_op jit(solution)/shard_map/ppermute | solution.py:100
  251.3 1.2 select_n.98
  253.4 1.2 fusion.3
  254.7 2.3 collective-permute-start.38
  259.3 7.9 %collective-permute-done.38 = bf16[48,1664]{1,0:T(8,128)(2,1)S(1)} collective-permute-done((bf16[48,1664]{1,0:T(8,128)(2,1)S(1)}, bf16[48,1664]{1,0:T(8,128)(2,1)S(1)}, u32[]{:S(2)}, u32[]{:S(2)}) %collective-permute-start.38) | collective-permute-done | bytes 159776 | tf_op jit(solution)/shard_map/ppermute | solution.py:104
  267.2 4.8 %collective-permute-done.39 = bf16[48,1664]{1,0:T(8,128)(2,1)S(1)} collective-permute-done((bf16[48,1664]{1,0:T(8,128)(2,1)S(1)}, bf16[48,1664]{1,0:T(8,128)(2,1)S(1)}, u32[]{:S(2)}, u32[]{:S(2)}) %collective-permute-start.39) | collective-permute-done | bytes 159776 | tf_op jit(solution)/shard_map/ppermute | solution.py:104
  (202 shorter events, 35.8 us)
Async XLA Ops:
  7.2 86.3 %all-gather.2.cloned.1.call-start = ((), (), s32[]{:S(2)}) async-start(), calls=%async_computation.1 | async-start | bytes 3538944 | tf_op jit(solution)/shard_map/all_gather | solution.py:709
  9.7 4.5 %collective-permute-start = (bf16[24,1280]{1,0:T(8,128)(2,1)}, bf16[24,1280]{1,0:T(8,128)(2,1)S(1)}, u32[]{:S(2)}, u32[]{:S(2)}) collective-permute-start(bf16[24,1280]{1,0:T(8,128)(2,1)} %get-tuple-element.87), channel_id=1, source_target_pairs={{0,1},{1,0},{2,3},{3,2},{4,5},{5,4},{6,7},{7,6},{8,9},{9,8},{10,11... | collective-permute-start | bytes 184328 | tf_op jit(solution)/shard_map/ppermute | solution.py:100
  14.1 3.7 %collective-permute-start.4 = (bf16[24,2304]{1,0:T(8,128)(2,1)S(1)}, bf16[24,2304]{1,0:T(8,128)(2,1)S(1)}, u32[]{:S(2)}, u32[]{:S(2)}) collective-permute-start(bf16[24,2304]{1,0:T(8,128)(2,1)S(1)} %get-tuple-element.186), channel_id=1, source_target_pairs={{0,1},{1,0},{2,3},{3,2},{4,5},{5,4},{6,7},{7,6},{8,9},{9,8},{10,11... | collective-permute-start | bytes 331784 | tf_op jit(solution)/shard_map/ppermute | solution.py:100
  14.2 9.7 %collective-permute-start.3 = (bf16[2,24,1280]{2,1,0:T(8,128)(2,1)S(1)}, bf16[2,24,1280]{2,1,0:T(8,128)(2,1)S(1)}, u32[]{:S(2)}, u32[]{:S(2)}) collective-permute-start(bf16[2,24,1280]{2,1,0:T(8,128)(2,1)S(1)} %maximum_select_fusion.2), channel_id=1, source_target_pairs={{0,6},{1,7},{2,4},{3,5},{4,2},{5,3},{6,0},{7,1},{8,14},{9,15},{10,... | collective-permute-start | bytes 368648 | tf_op jit(solution)/shard_map/ppermute | solution.py:104
  15.6 10.1 %collective-permute-start.2 = (bf16[2,24,1280]{2,1,0:T(8,128)(2,1)S(1)}, bf16[2,24,1280]{2,1,0:T(8,128)(2,1)S(1)}, u32[]{:S(2)}, u32[]{:S(2)}) collective-permute-start(bf16[2,24,1280]{2,1,0:T(8,128)(2,1)S(1)} %maximum_select_fusion.2), channel_id=1, source_target_pairs={{0,4},{1,5},{2,6},{3,7},{4,0},{5,1},{6,2},{7,3},{8,12},{9,13},{10,... | collective-permute-start | bytes 368648 | tf_op jit(solution)/shard_map/ppermute | solution.py:104
  16.7 9.4 %collective-permute-start.1 = (bf16[2,24,1280]{2,1,0:T(8,128)(2,1)S(1)}, bf16[2,24,1280]{2,1,0:T(8,128)(2,1)S(1)}, u32[]{:S(2)}, u32[]{:S(2)}) collective-permute-start(bf16[2,24,1280]{2,1,0:T(8,128)(2,1)S(1)} %maximum_select_fusion.2), channel_id=1, source_target_pairs={{0,2},{1,3},{2,0},{3,1},{4,6},{5,7},{6,4},{7,5},{8,10},{9,11},{10,... | collective-permute-start | bytes 368648 | tf_op jit(solution)/shard_map/ppermute | solution.py:104
  26.1 22.8 %copy-start.48 = (f32[96,768]{1,0:T(8,128)S(1)}, f32[96,768]{1,0:T(8,128)}, u32[]{:S(2)}) copy-start(f32[96,768]{1,0:T(8,128)} %param.30) | copy-start | bytes 884740
  26.1 20.0 %collective-permute-start.6 = (bf16[4,2,24,1280]{3,2,1,0:T(8,128)(2,1)S(1)}, bf16[4,2,24,1280]{3,2,1,0:T(8,128)(2,1)S(1)}, u32[]{:S(2)}, u32[]{:S(2)}) collective-permute-start(bf16[4,2,24,1280]{3,2,1,0:T(8,128)(2,1)S(1)} %pad_maximum_fusion.2.refs_0_), channel_id=1, source_target_pairs={{0,16},{8,24},{16,0},{24,8},{1,17},{9,25},{17,1},{25,9},{2,18},{10... | collective-permute-start | bytes 1474568 | tf_op jit(solution)/shard_map/ppermute | solution.py:108
  26.4 19.8 %collective-permute-start.5 = (bf16[4,2,24,1280]{3,2,1,0:T(8,128)(2,1)S(1)}, bf16[4,2,24,1280]{3,2,1,0:T(8,128)(2,1)S(1)}, u32[]{:S(2)}, u32[]{:S(2)}) collective-permute-start(bf16[4,2,24,1280]{3,2,1,0:T(8,128)(2,1)S(1)} %pad_maximum_fusion.2.refs_0_), channel_id=1, source_target_pairs={{0,8},{8,0},{16,24},{24,16},{1,9},{9,1},{17,25},{25,17},{2,10},{10... | collective-permute-start | bytes 1474568 | tf_op jit(solution)/shard_map/ppermute | solution.py:108
  27.6 5.1 %collective-permute-start.9 = (bf16[2,24,2304]{2,1,0:T(8,128)(2,1)S(1)}, bf16[2,24,2304]{2,1,0:T(8,128)(2,1)S(1)}, u32[]{:S(2)}, u32[]{:S(2)}) collective-permute-start(bf16[2,24,2304]{2,1,0:T(8,128)(2,1)S(1)} %maximum_select_fusion.1), channel_id=1, source_target_pairs={{0,6},{1,7},{2,4},{3,5},{4,2},{5,3},{6,0},{7,1},{8,14},{9,15},{10,... | collective-permute-start | bytes 663560 | tf_op jit(solution)/shard_map/ppermute | solution.py:104
  27.7 18.5 %collective-permute-start.8 = (bf16[2,24,2304]{2,1,0:T(8,128)(2,1)S(1)}, bf16[2,24,2304]{2,1,0:T(8,128)(2,1)S(1)}, u32[]{:S(2)}, u32[]{:S(2)}) collective-permute-start(bf16[2,24,2304]{2,1,0:T(8,128)(2,1)S(1)} %maximum_select_fusion.1), channel_id=1, source_target_pairs={{0,4},{1,5},{2,6},{3,7},{4,0},{5,1},{6,2},{7,3},{8,12},{9,13},{10,... | collective-permute-start | bytes 663560 | tf_op jit(solution)/shard_map/ppermute | solution.py:104
  31.5 14.7 %collective-permute-start.7 = (bf16[2,24,2304]{2,1,0:T(8,128)(2,1)S(1)}, bf16[2,24,2304]{2,1,0:T(8,128)(2,1)S(1)}, u32[]{:S(2)}, u32[]{:S(2)}) collective-permute-start(bf16[2,24,2304]{2,1,0:T(8,128)(2,1)S(1)} %maximum_select_fusion.1), channel_id=1, source_target_pairs={{0,2},{1,3},{2,0},{3,1},{4,6},{5,7},{6,4},{7,5},{8,10},{9,11},{10,... | collective-permute-start | bytes 663560 | tf_op jit(solution)/shard_map/ppermute | solution.py:104
  47.2 25.5 %copy-start.9 = (bf16[4,2,24,2304]{3,2,1,0:T(8,128)(2,1)}, bf16[4,2,24,2304]{3,2,1,0:T(8,128)(2,1)S(1)}, u32[]{:S(2)}) copy-start(bf16[4,2,24,2304]{3,2,1,0:T(8,128)(2,1)S(1)} %pad_maximum_fusion.refs_0_) | copy-start | bytes 2654212
  47.3 206.1 %reduce-scatter.2.cloned.1.call-start = ((), (), s32[]{:S(2)}) async-start(), calls=%async_computation.2 | async-start | bytes 3538944 | tf_op jit(solution)/shard_map/reduce_scatter | solution.py:867
  47.3 44.1 %collective-permute-start.14 = (bf16[4,2,24,2304]{3,2,1,0:T(8,128)(2,1)S(1)}, bf16[4,2,24,2304]{3,2,1,0:T(8,128)(2,1)S(1)}, u32[]{:S(2)}, u32[]{:S(2)}) collective-permute-start(bf16[4,2,24,2304]{3,2,1,0:T(8,128)(2,1)S(1)} %pad_maximum_fusion.refs_0_), channel_id=1, source_target_pairs={{0,16},{8,24},{16,0},{24,8},{1,17},{9,25},{17,1},{25,9},{2,18},{10... | collective-permute-start | bytes 2654216 | tf_op jit(solution)/shard_map/ppermute | solution.py:108
  48.6 44.0 %collective-permute-start.13 = (bf16[4,2,24,2304]{3,2,1,0:T(8,128)(2,1)S(1)}, bf16[4,2,24,2304]{3,2,1,0:T(8,128)(2,1)S(1)}, u32[]{:S(2)}, u32[]{:S(2)}) collective-permute-start(bf16[4,2,24,2304]{3,2,1,0:T(8,128)(2,1)S(1)} %pad_maximum_fusion.refs_0_), channel_id=1, source_target_pairs={{0,8},{8,0},{16,24},{24,16},{1,9},{9,1},{17,25},{25,17},{2,10},{10... | collective-permute-start | bytes 2654216 | tf_op jit(solution)/shard_map/ppermute | solution.py:108
  48.9 27.0 %copy-start.50 = (s32[2,64]{1,0:T(2,128)S(1)}, s32[2,64]{1,0:T(2,128)}, u32[]{:S(2)}) copy-start(s32[2,64]{1,0:T(2,128)} %param.34) | copy-start | bytes 1540
  48.9 36.3 %copy-start.44 = (s32[3]{0:T(128)S(1)}, s32[3]{0:T(128)}, u32[]{:S(2)}) copy-start(s32[3]{0:T(128)} %pad_add_fusion.place_ref) | copy-start | bytes 40
  48.9 4.4 %collective-permute-start.19 = (bf16[96,768]{1,0:T(8,128)(2,1)S(1)}, bf16[96,768]{1,0:T(8,128)(2,1)S(1)}, u32[]{:S(2)}, u32[]{:S(2)}) collective-permute-start(bf16[96,768]{1,0:T(8,128)(2,1)S(1)} %convert_element_type.196), channel_id=1, source_target_pairs={{0,6},{1,7},{2,4},{3,5},{4,2},{5,3},{6,0},{7,1},{8,14},{9,15},{10,... | collective-permute-start | bytes 442376 | tf_op jit(solution)/shard_map/ppermute | solution.py:104
  49.2 19.8 %collective-permute-start.18 = (bf16[96,768]{1,0:T(8,128)(2,1)S(1)}, bf16[96,768]{1,0:T(8,128)(2,1)S(1)}, u32[]{:S(2)}, u32[]{:S(2)}) collective-permute-start(bf16[96,768]{1,0:T(8,128)(2,1)S(1)} %convert_element_type.196), channel_id=1, source_target_pairs={{0,4},{1,5},{2,6},{3,7},{4,0},{5,1},{6,2},{7,3},{8,12},{9,13},{10,... | collective-permute-start | bytes 442376 | tf_op jit(solution)/shard_map/ppermute | solution.py:104
  53.2 15.8 %collective-permute-start.17 = (bf16[96,768]{1,0:T(8,128)(2,1)S(1)}, bf16[96,768]{1,0:T(8,128)(2,1)S(1)}, u32[]{:S(2)}, u32[]{:S(2)}) collective-permute-start(bf16[96,768]{1,0:T(8,128)(2,1)S(1)} %convert_element_type.196), channel_id=1, source_target_pairs={{0,2},{1,3},{2,0},{3,1},{4,6},{5,7},{6,4},{7,5},{8,10},{9,11},{10,... | collective-permute-start | bytes 442376 | tf_op jit(solution)/shard_map/ppermute | solution.py:104
  69.9 43.4 %collective-permute-start.22 = (bf16[4,96,768]{2,1,0:T(8,128)(2,1)}, bf16[4,96,768]{2,1,0:T(8,128)(2,1)}, u32[]{:S(2)}, u32[]{:S(2)}) collective-permute-start(bf16[4,96,768]{2,1,0:T(8,128)(2,1)} %pad_maximum_fusion.1.refs_0_), channel_id=1, source_target_pairs={{0,24},{8,16},{16,8},{24,0},{1,25},{9,17},{17,9},{25,1},{2,26},{10... | collective-permute-start | bytes 1769480 | tf_op jit(solution)/shard_map/ppermute | solution.py:108
  74.4 8.1 %collective-permute-start.10 = (bf16[2,2,24,1280]{3,2,1,0:T(8,128)(2,1)}, bf16[2,2,24,1280]{3,2,1,0:T(8,128)(2,1)S(1)}, u32[]{:S(2)}, u32[]{:S(2)}) collective-permute-start(bf16[2,2,24,1280]{3,2,1,0:T(8,128)(2,1)} %slice.174), channel_id=1, source_target_pairs={{0,8},{8,0},{16,24},{24,16},{1,9},{9,1},{17,25},{25,17},{2,10},{10... | collective-permute-start | bytes 737288 | tf_op jit(solution)/shard_map/ppermute | solution.py:108
  74.5 9.6 %collective-permute-start.11 = (bf16[2,2,24,1280]{3,2,1,0:T(8,128)(2,1)}, bf16[2,2,24,1280]{3,2,1,0:T(8,128)(2,1)}, u32[]{:S(2)}, u32[]{:S(2)}) collective-permute-start(bf16[2,2,24,1280]{3,2,1,0:T(8,128)(2,1)} %slice.175), channel_id=1, source_target_pairs={{0,16},{8,24},{16,0},{24,8},{1,17},{9,25},{17,1},{25,9},{2,18},{10... | collective-permute-start | bytes 737288 | tf_op jit(solution)/shard_map/ppermute | solution.py:108
  82.5 47.9 %collective-permute-start.21 = (bf16[4,96,768]{2,1,0:T(8,128)(2,1)}, bf16[4,96,768]{2,1,0:T(8,128)(2,1)}, u32[]{:S(2)}, u32[]{:S(2)}) collective-permute-start(bf16[4,96,768]{2,1,0:T(8,128)(2,1)} %pad_maximum_fusion.1.refs_0_), channel_id=1, source_target_pairs={{0,16},{8,24},{16,0},{24,8},{1,17},{9,25},{17,1},{25,9},{2,18},{10... | collective-permute-start | bytes 1769480 | tf_op jit(solution)/shard_map/ppermute | solution.py:108
  84.1 46.3 %collective-permute-start.20 = (bf16[4,96,768]{2,1,0:T(8,128)(2,1)}, bf16[4,96,768]{2,1,0:T(8,128)(2,1)}, u32[]{:S(2)}, u32[]{:S(2)}) collective-permute-start(bf16[4,96,768]{2,1,0:T(8,128)(2,1)} %pad_maximum_fusion.1.refs_0_), channel_id=1, source_target_pairs={{0,8},{8,0},{16,24},{24,16},{1,9},{9,1},{17,25},{25,17},{2,10},{10... | collective-permute-start | bytes 1769480 | tf_op jit(solution)/shard_map/ppermute | solution.py:108
  92.3 40.0 %collective-permute-start.15 = (bf16[2,2,24,2304]{3,2,1,0:T(8,128)(2,1)}, bf16[2,2,24,2304]{3,2,1,0:T(8,128)(2,1)}, u32[]{:S(2)}, u32[]{:S(2)}) collective-permute-start(bf16[2,2,24,2304]{3,2,1,0:T(8,128)(2,1)} %slice.233), channel_id=1, source_target_pairs={{0,8},{8,0},{16,24},{24,16},{1,9},{9,1},{17,25},{25,17},{2,10},{10... | collective-permute-start | bytes 1327112 | tf_op jit(solution)/shard_map/ppermute | solution.py:108
  93.4 38.9 %collective-permute-start.16 = (bf16[2,2,24,2304]{3,2,1,0:T(8,128)(2,1)}, bf16[2,2,24,2304]{3,2,1,0:T(8,128)(2,1)}, u32[]{:S(2)}, u32[]{:S(2)}) collective-permute-start(bf16[2,2,24,2304]{3,2,1,0:T(8,128)(2,1)} %slice.234), channel_id=1, source_target_pairs={{0,16},{8,24},{16,0},{24,8},{1,17},{9,25},{17,1},{25,9},{2,18},{10... | collective-permute-start | bytes 1327112 | tf_op jit(solution)/shard_map/ppermute | solution.py:108
  102.0 10.1 %copy-start.20 = (bf16[2,256,384]{2,1,0:T(8,128)(2,1)}, bf16[2,256,384]{2,1,0:T(8,128)(2,1)S(1)}, u32[]{:S(2)}) copy-start(bf16[2,256,384]{2,1,0:T(8,128)(2,1)S(1)} %get-tuple-element.103.q_ref) | copy-start | bytes 1179652
  113.3 20.9 %collective-permute-start.12 = (bf16[2,256,384]{2,1,0:T(8,128)(2,1)}, bf16[2,256,384]{2,1,0:T(8,128)(2,1)}, u32[]{:S(2)}, u32[]{:S(2)}) collective-permute-start(bf16[2,256,384]{2,1,0:T(8,128)(2,1)} %get-tuple-element.105), channel_id=1, source_target_pairs={{0,1},{1,0},{2,3},{3,2},{4,5},{5,4},{6,7},{7,6},{8,9},{9,8},{10,11... | collective-permute-start | bytes 1179656 | tf_op jit(solution)/shard_map/ppermute | solution.py:100
  134.2 7.0 %copy-start.38 = (bf16[2,128,768]{2,1,0:T(8,128)(2,1)S(1)}, bf16[2,128,768]{2,1,0:T(8,128)(2,1)}, u32[]{:S(2)}) copy-start(bf16[2,128,768]{2,1,0:T(8,128)(2,1)} %param.35) | copy-start | bytes 1179652
  141.1 2.9 %collective-permute-start.23 = (bf16[512,768]{1,0:T(8,128)(2,1)S(1)}, bf16[512,768]{1,0:T(8,128)(2,1)S(1)}, u32[]{:S(2)}, u32[]{:S(2)}) collective-permute-start(bf16[512,768]{1,0:T(8,128)(2,1)S(1)} %get-tuple-element.111), channel_id=1, source_target_pairs={{0,1},{1,0},{2,3},{3,2},{4,5},{5,4},{6,7},{7,6},{8,9},{9,8},{10,11... | collective-permute-start | bytes 2359304 | tf_op jit(solution)/shard_map/ppermute | solution.py:100
  141.2 2.8 collective-permute-start.24
  150.3 5.0 %copy-start.40 = (f32[3,8,768]{2,1,0:T(8,128)}, f32[3,8,768]{2,1,0:T(8,128)S(1)}, u32[]{:S(2)}) copy-start(f32[3,8,768]{2,1,0:T(8,128)S(1)} %get-tuple-element.140.two_ref) | copy-start | bytes 221188
  150.4 5.0 %copy-start.45 = (f32[8,1536]{1,0:T(8,128)}, f32[8,1536]{1,0:T(8,128)S(1)}, u32[]{:S(2)}) copy-start(f32[8,1536]{1,0:T(8,128)S(1)} %get-tuple-element.141.unit_ref) | copy-start | bytes 147460
  150.4 8.5 %collective-permute-start.25 = (bf16[512,768]{1,0:T(8,128)(2,1)S(1)}, bf16[512,768]{1,0:T(8,128)(2,1)S(1)}, u32[]{:S(2)}, u32[]{:S(2)}) collective-permute-start(bf16[512,768]{1,0:T(8,128)(2,1)S(1)} %get-tuple-element.116), channel_id=1, source_target_pairs={{0,1},{1,0},{2,3},{3,2},{4,5},{5,4},{6,7},{7,6},{8,9},{9,8},{10,11... | collective-permute-start | bytes 2359304 | tf_op jit(solution)/shard_map/ppermute | solution.py:100
  156.2 4.9 %copy-start.24 = (bf16[4,48,3072]{2,1,0:T(8,128)(2,1)}, bf16[4,48,3072]{2,1,0:T(8,128)(2,1)S(1)}, u32[]{:S(2)}) copy-start(bf16[4,48,3072]{2,1,0:T(8,128)(2,1)S(1)} %get-tuple-element.145) | copy-start | bytes 3538948
  156.2 4.9 %copy-start.36 = (bf16[2,48,3072]{2,1,0:T(8,128)(2,1)}, bf16[2,48,3072]{2,1,0:T(8,128)(2,1)S(1)}, u32[]{:S(2)}) copy-start(bf16[2,48,3072]{2,1,0:T(8,128)(2,1)S(1)} %get-tuple-element.133) | copy-start | bytes 1769476
  156.2 29.2 %collective-permute-start.26 = (bf16[4,48,3072]{2,1,0:T(8,128)(2,1)}, bf16[4,48,3072]{2,1,0:T(8,128)(2,1)}, u32[]{:S(2)}, u32[]{:S(2)}) collective-permute-start(bf16[4,48,3072]{2,1,0:T(8,128)(2,1)} %get-tuple-element.130), channel_id=1, source_target_pairs={{0,8},{8,0},{16,24},{24,16},{1,9},{9,1},{17,25},{25,17},{2,10},{10... | collective-permute-start | bytes 3538952 | tf_op jit(solution)/shard_map/ppermute | solution.py:108
  157.3 28.1 %collective-permute-start.27 = (bf16[4,48,3072]{2,1,0:T(8,128)(2,1)}, bf16[4,48,3072]{2,1,0:T(8,128)(2,1)}, u32[]{:S(2)}, u32[]{:S(2)}) collective-permute-start(bf16[4,48,3072]{2,1,0:T(8,128)(2,1)} %get-tuple-element.131), channel_id=1, source_target_pairs={{0,16},{8,24},{16,0},{24,8},{1,17},{9,25},{17,1},{25,9},{2,18},{10... | collective-permute-start | bytes 3538952 | tf_op jit(solution)/shard_map/ppermute | solution.py:108
  162.0 14.1 %copy-start.30 = (bf16[512,768]{1,0:T(8,128)(2,1)}, bf16[512,768]{1,0:T(8,128)(2,1)S(1)}, u32[]{:S(2)}) copy-start(bf16[512,768]{1,0:T(8,128)(2,1)S(1)} %get-tuple-element.138.branch_ref) | copy-start | bytes 2359300
  162.0 14.1 %copy-start.42 = (f32[3,8,768]{2,1,0:T(8,128)}, f32[3,8,768]{2,1,0:T(8,128)S(1)}, u32[]{:S(2)}) copy-start(f32[3,8,768]{2,1,0:T(8,128)S(1)} %get-tuple-element.139.one_ref) | copy-start | bytes 221188
  162.0 14.1 %copy-start.4 = (bf16[4,4,2,24,1152]{4,3,2,1,0:T(8,128)(2,1)S(1)}, bf16[4,4,2,24,1152]{4,3,2,1,0:T(8,128)(2,1)}, u32[]{:S(2)}) copy-start(bf16[4,4,2,24,1152]{4,3,2,1,0:T(8,128)(2,1)} %copy-done.2) | copy-start | bytes 5308420
  176.2 13.5 %copy-start.41 = (f32[3,8,768]{2,1,0:T(8,128)S(1)}, f32[3,8,768]{2,1,0:T(8,128)}, u32[]{:S(2)}) copy-start(f32[3,8,768]{2,1,0:T(8,128)} %copy-done.40) | copy-start | bytes 221188
  176.2 13.5 %copy-start.43 = (f32[3,8,768]{2,1,0:T(8,128)S(1)}, f32[3,8,768]{2,1,0:T(8,128)}, u32[]{:S(2)}) copy-start(f32[3,8,768]{2,1,0:T(8,128)} %copy-done.42) | copy-start | bytes 221188
  176.2 13.5 %copy-start.46 = (f32[8,1536]{1,0:T(8,128)S(1)}, f32[8,1536]{1,0:T(8,128)}, u32[]{:S(2)}) copy-start(f32[8,1536]{1,0:T(8,128)} %copy-done.45) | copy-start | bytes 147460
  187.0 14.1 %collective-permute-start.30 = (bf16[2,48,3072]{2,1,0:T(8,128)(2,1)S(1)}, bf16[2,48,3072]{2,1,0:T(8,128)(2,1)S(1)}, u32[]{:S(2)}, u32[]{:S(2)}) collective-permute-start(bf16[2,48,3072]{2,1,0:T(8,128)(2,1)S(1)} %add_convert_fusion.1), channel_id=1, source_target_pairs={{0,16},{8,24},{16,0},{24,8},{1,17},{9,25},{17,1},{25,9},{2,18},{10... | collective-permute-start | bytes 1769480 | tf_op jit(solution)/shard_map/ppermute | solution.py:108
  189.2 13.3 %collective-permute-start.31 = (bf16[2,48,3072]{2,1,0:T(8,128)(2,1)S(1)}, bf16[2,48,3072]{2,1,0:T(8,128)(2,1)S(1)}, u32[]{:S(2)}, u32[]{:S(2)}) collective-permute-start(bf16[2,48,3072]{2,1,0:T(8,128)(2,1)S(1)} %add_convert_fusion), channel_id=1, source_target_pairs={{0,8},{8,0},{16,24},{24,16},{1,9},{9,1},{17,25},{25,17},{2,10},{10... | collective-permute-start | bytes 1769480 | tf_op jit(solution)/shard_map/ppermute | solution.py:108
  192.0 10.6 %copy-start.25 = (bf16[4,48,3072]{2,1,0:T(8,128)(2,1)S(1)}, bf16[4,48,3072]{2,1,0:T(8,128)(2,1)}, u32[]{:S(2)}) copy-start(bf16[4,48,3072]{2,1,0:T(8,128)(2,1)} %copy-done.24) | copy-start | bytes 3538948
  197.9 6.2 %copy-start.34 = (bf16[4,48,1664]{2,1,0:T(8,128)(2,1)}, bf16[4,48,1664]{2,1,0:T(8,128)(2,1)S(1)}, u32[]{:S(2)}) copy-start(bf16[4,48,1664]{2,1,0:T(8,128)(2,1)S(1)} %get-tuple-element.142) | copy-start | bytes 1916932
  197.9 18.3 %collective-permute-start.28 = (bf16[4,48,1664]{2,1,0:T(8,128)(2,1)S(1)}, bf16[4,48,1664]{2,1,0:T(8,128)(2,1)S(1)}, u32[]{:S(2)}, u32[]{:S(2)}) collective-permute-start(bf16[4,48,1664]{2,1,0:T(8,128)(2,1)S(1)} %get-tuple-element.143), channel_id=1, source_target_pairs={{0,8},{8,0},{16,24},{24,16},{1,9},{9,1},{17,25},{25,17},{2,10},{10... | collective-permute-start | bytes 1916936 | tf_op jit(solution)/shard_map/ppermute | solution.py:108
  199.0 17.2 %collective-permute-start.29 = (bf16[4,48,1664]{2,1,0:T(8,128)(2,1)S(1)}, bf16[4,48,1664]{2,1,0:T(8,128)(2,1)S(1)}, u32[]{:S(2)}, u32[]{:S(2)}) collective-permute-start(bf16[4,48,1664]{2,1,0:T(8,128)(2,1)S(1)} %get-tuple-element.144), channel_id=1, source_target_pairs={{0,16},{8,24},{16,0},{24,8},{1,17},{9,25},{17,1},{25,9},{2,18},{10... | collective-permute-start | bytes 1916936 | tf_op jit(solution)/shard_map/ppermute | solution.py:108
  204.1 30.9 %collective-permute-start.36 = (bf16[48,3072]{1,0:T(8,128)(2,1)S(1)}, bf16[48,3072]{1,0:T(8,128)(2,1)S(1)}, u32[]{:S(2)}, u32[]{:S(2)}) collective-permute-start(bf16[48,3072]{1,0:T(8,128)(2,1)S(1)} %get-tuple-element.165), channel_id=1, source_target_pairs={{0,6},{1,7},{2,4},{3,5},{4,2},{5,3},{6,0},{7,1},{8,14},{9,15},{10,... | collective-permute-start | bytes 884744 | tf_op jit(solution)/shard_map/ppermute | solution.py:104
  204.2 41.4 %collective-permute-start.35 = (bf16[48,3072]{1,0:T(8,128)(2,1)S(1)}, bf16[48,3072]{1,0:T(8,128)(2,1)S(1)}, u32[]{:S(2)}, u32[]{:S(2)}) collective-permute-start(bf16[48,3072]{1,0:T(8,128)(2,1)S(1)} %get-tuple-element.166), channel_id=1, source_target_pairs={{0,4},{1,5},{2,6},{3,7},{4,0},{5,1},{6,2},{7,3},{8,12},{9,13},{10,... | collective-permute-start | bytes 884744 | tf_op jit(solution)/shard_map/ppermute | solution.py:104
  209.0 36.6 %collective-permute-start.34 = (bf16[48,3072]{1,0:T(8,128)(2,1)S(1)}, bf16[48,3072]{1,0:T(8,128)(2,1)S(1)}, u32[]{:S(2)}, u32[]{:S(2)}) collective-permute-start(bf16[48,3072]{1,0:T(8,128)(2,1)S(1)} %get-tuple-element.169), channel_id=1, source_target_pairs={{0,2},{1,3},{2,0},{3,1},{4,6},{5,7},{6,4},{7,5},{8,10},{9,11},{10,... | collective-permute-start | bytes 884744 | tf_op jit(solution)/shard_map/ppermute | solution.py:104
  217.0 35.5 %collective-permute-start.32 = (bf16[2,48,1664]{2,1,0:T(8,128)(2,1)}, bf16[2,48,1664]{2,1,0:T(8,128)(2,1)S(1)}, u32[]{:S(2)}, u32[]{:S(2)}) collective-permute-start(bf16[2,48,1664]{2,1,0:T(8,128)(2,1)} %add_convert_fusion.3), channel_id=1, source_target_pairs={{0,16},{8,24},{16,0},{24,8},{1,17},{9,25},{17,1},{25,9},{2,18},{10... | collective-permute-start | bytes 958472 | tf_op jit(solution)/shard_map/ppermute | solution.py:108
  219.0 33.5 %collective-permute-start.33 = (bf16[2,48,1664]{2,1,0:T(8,128)(2,1)}, bf16[2,48,1664]{2,1,0:T(8,128)(2,1)}, u32[]{:S(2)}, u32[]{:S(2)}) collective-permute-start(bf16[2,48,1664]{2,1,0:T(8,128)(2,1)} %add_convert_fusion.2), channel_id=1, source_target_pairs={{0,8},{8,0},{16,24},{24,16},{1,9},{9,1},{17,25},{25,17},{2,10},{10... | collective-permute-start | bytes 958472 | tf_op jit(solution)/shard_map/ppermute | solution.py:108
  245.8 4.3 %collective-permute-start.41 = (f32[24,1536]{1,0:T(8,128)S(1)}, f32[24,1536]{1,0:T(8,128)S(1)}, u32[]{:S(2)}, u32[]{:S(2)}) collective-permute-start(f32[24,1536]{1,0:T(8,128)S(1)} %get-tuple-element.176), channel_id=1, source_target_pairs={{0,1},{1,0},{2,3},{3,2},{4,5},{5,4},{6,7},{7,6},{8,9},{9,8},{10,11... | collective-permute-start | bytes 442376 | tf_op jit(solution)/shard_map/ppermute | solution.py:100
  251.3 7.0 %copy-start.33 = (f32[256,768]{1,0:T(8,128)S(1)}, f32[256,768]{1,0:T(8,128)}, u32[]{:S(2)}) copy-start(f32[256,768]{1,0:T(8,128)} %copy-done.32) | copy-start | bytes 2359300
  253.4 4.9 %copy-start.47 = (bf16[2,128,768]{2,1,0:T(8,128)(2,1)S(1)}, bf16[2,128,768]{2,1,0:T(8,128)(2,1)}, u32[]{:S(2)}) copy-start(bf16[2,128,768]{2,1,0:T(8,128)(2,1)} %reduce-scatter.2.cloned.1.call-done) | copy-start | bytes 1179652
  254.7 12.5 %collective-permute-start.38 = (bf16[48,1664]{1,0:T(8,128)(2,1)S(1)}, bf16[48,1664]{1,0:T(8,128)(2,1)S(1)}, u32[]{:S(2)}, u32[]{:S(2)}) collective-permute-start(bf16[48,1664]{1,0:T(8,128)(2,1)S(1)} %get-tuple-element.167), channel_id=1, source_target_pairs={{0,4},{1,5},{2,6},{3,7},{4,0},{5,1},{6,2},{7,3},{8,12},{9,13},{10,... | collective-permute-start | bytes 479240 | tf_op jit(solution)/shard_map/ppermute | solution.py:104
  257.0 15.0 %collective-permute-start.39 = (bf16[48,1664]{1,0:T(8,128)(2,1)S(1)}, bf16[48,1664]{1,0:T(8,128)(2,1)S(1)}, u32[]{:S(2)}, u32[]{:S(2)}) collective-permute-start(bf16[48,1664]{1,0:T(8,128)(2,1)S(1)} %get-tuple-element.168), channel_id=1, source_target_pairs={{0,6},{1,7},{2,4},{3,5},{4,2},{5,3},{6,0},{7,1},{8,14},{9,15},{10,... | collective-permute-start | bytes 479240 | tf_op jit(solution)/shard_map/ppermute | solution.py:104
  257.9 14.2 %collective-permute-start.37 = (bf16[48,1664]{1,0:T(8,128)(2,1)S(1)}, bf16[48,1664]{1,0:T(8,128)(2,1)S(1)}, u32[]{:S(2)}, u32[]{:S(2)}) collective-permute-start(bf16[48,1664]{1,0:T(8,128)(2,1)S(1)} %get-tuple-element.170), channel_id=1, source_target_pairs={{0,2},{1,3},{2,0},{3,1},{4,6},{5,7},{6,4},{7,5},{8,10},{9,11},{10,... | collective-permute-start | bytes 479240 | tf_op jit(solution)/shard_map/ppermute | solution.py:104
  272.3 2.0 collective-permute-start.40
  (31 other events, 60.2 us)
Sparse Core Ops, SparseCore 0:
  47.4 43.9 all-gather.1
  185.5 67.8 reduce-scatter.1

commit v2 on v1

--- a/solution.py
+++ b/solution.py
@@ -124,11 +124,15 @@
     return [value] + [dp_move(value, k, dps) for k in range(1, 3 if dps == 4 else dps)]
 
 
-def gather_dp_rest(blocks, dps):
+def gather_dp_halves(blocks, dps):
     if dps != 4:
-        return blocks
+        return []
     half = blocks[0].shape[0] // 2
-    return blocks + [dp_move(blocks[2][:half], 1, dps), dp_move(blocks[1][half:], 2, dps)]
+    return [blocks[2][:half], blocks[1][half:]]
+
+
+def gather_dp_rest(blocks, halves):
+    return blocks + [dp_move(half, step, 4) for step, half in enumerate(halves, 1)]
 
 
 def dp_pieces(dps, zs, direct):
@@ -381,7 +385,7 @@
         compiler_params=pltpu.CompilerParams(vmem_limit_bytes=VMEM_LIMIT),
         cost_estimate=QUICK,
         name="project",
-    )(place, tokens, vectors, weight)
+    )(place, pltpu.with_memory_space_constraint(tokens, pltpu.HBM), vectors, weight)
 
 
 def unproject_kernel(place_ref, query_ref, key_ref, value_ref, weight_ref, out_ref):
@@ -413,7 +417,7 @@
             pl.BlockSpec(memory_space=pltpu.VMEM),
         ],
         out_specs=block(D),
-        out_shape=jax.ShapeDtypeStruct((streams, count, D), BF),
+        out_shape=pltpu.HBM((streams, count, D), BF),
         compiler_params=pltpu.CompilerParams(vmem_limit_bytes=VMEM_LIMIT),
         cost_estimate=QUICK,
         name="unproject",
@@ -451,11 +455,6 @@
     place_ref, part_ref, came_ref, normed_ref, mine_ref, other_ref, slope_ref, vec_ref, reduce_ref, expand_ref,
     act_ref, residual_ref, low_ref, back_ref, next_ref, send_ref, sum_ref, unit_sum_ref,
 ):
-    @pl.when(pl.program_id(0) == 0)
-    def _():
-        sum_ref[...] = jnp.zeros_like(sum_ref)
-        unit_sum_ref[...] = jnp.zeros_like(unit_sum_ref)
-
     core = place_ref[2]
     first = normed_ref[...] * vector_of(vec_ref, FIRST_GAIN) + vector_of(vec_ref, FIRST_SHIFT)
     reduced = part_ref[...] + came_ref[...].astype(F32) + vector_of(vec_ref, REDUCE_BIAS)
@@ -490,10 +489,6 @@
     place_ref, part_ref, came_ref, residual_ref, normed_ref, inverse_ref, vec_ref, out_ref,
     back_ref, low_ref, attended_ref, sum_ref,
 ):
-    @pl.when(pl.program_id(0) == 0)
-    def _():
-        sum_ref[...] = jnp.zeros_like(sum_ref)
-
     upward = part_ref[...] + came_ref[...].astype(F32) + residual_ref[...]
     normed = normed_ref[...]
     add_rows(sum_ref, 1, upward * normed)
@@ -507,16 +502,31 @@
     attended_ref[...] = nt(low, out_ref[half_of_ref(place_ref), :]).astype(BF)
 
 
-def over_rows(kernel, place, steps, tiled, whole, outs, sums, name):
-    tile = lambda shape: pl.BlockSpec((shape[0] // steps, shape[1]), lambda t: (t, 0))
-    keep = lambda shape: pl.BlockSpec(shape, lambda t: (0,) * len(shape))
+def over_rows(body, place, steps, tiled, whole, outs, sums, name):
+    def tile_of(ref, step):
+        rows = ref.shape[0] // steps
+        return ref.at[step * rows : (step + 1) * rows]
+
+    def kernel(place_ref, *refs):
+        tiles, refs = refs[: len(tiled)], refs[len(tiled) :]
+        kept, refs = refs[: len(whole)], refs[len(whole) :]
+        results, totals = refs[: len(outs)], refs[len(outs) :]
+        for total in totals:
+            total[...] = jnp.zeros_like(total)
+        for step in range(steps):
+            body(
+                place_ref,
+                *[tile_of(ref, step) for ref in tiles],
+                *kept,
+                *[tile_of(ref, step) for ref in results],
+                *totals,
+            )
+
     return pl.pallas_call(
         kernel,
-        grid=(steps,),
         in_specs=[pl.BlockSpec(memory_space=pltpu.SMEM)]
-        + [tile(v.shape) for v in tiled]
-        + [pl.BlockSpec(memory_space=pltpu.VMEM)] * len(whole),
-        out_specs=[tile(out) for out in outs] + [keep(shape) for shape in sums],
+        + [pl.BlockSpec(memory_space=pltpu.VMEM)] * (len(tiled) + len(whole)),
+        out_specs=[pl.BlockSpec(memory_space=pltpu.VMEM)] * (len(outs) + len(sums)),
         out_shape=[jax.ShapeDtypeStruct(out[:2], out[2]) for out in outs]
         + [jax.ShapeDtypeStruct(shape, F32) for shape in sums],
         compiler_params=pltpu.CompilerParams(vmem_limit_bytes=VMEM_LIMIT),
@@ -704,12 +714,11 @@
     early = jnp.stack(tied(z_moves(early, seq), late))
     late = z_moves(tied(late, early), seq)
     early, late = lax.optimization_barrier((gather_dp_first(early, dps), late))
-    early = gather_dp_rest(early, dps)
-    late = jnp.stack(late)
     all_tokens = row_major(lax.all_gather(tied(tokens, late), "seq", axis=1, tiled=True))
+    early = gather_dp_rest(early, gather_dp_halves(early, dps))
+    late = jnp.stack(tied(late, early))
     last = z_moves(tied(reduce_weight.astype(BF), late), seq)
-    late = gather_dp_rest(gather_dp_first(late, dps), dps)
-    last = gather_dp_direct(jnp.stack(last), dps)
+    late = gather_dp_first(late, dps)
     other_cotangent = swap(cotangent).reshape(-1, D)
     cotangent = cotangent.reshape(-1, D)
 
@@ -745,6 +754,12 @@
     def half_of(vector):
         return lax.dynamic_slice_in_dim(vector, core * HALF, HALF, 1)
 
+    qkv_weight = tied(qkv_weight, expand_bias, other_cotangent)
+    late = tied(late, qkv_weight)
+    halves = gather_dp_halves(late, dps)
+    late = gather_dp_rest(late, halves)
+    last = gather_dp_direct(jnp.stack(tied(last, halves)), dps)
+
     flat_all = all_tokens.reshape(-1, D)
     ids = item_ids(lengths, jnp.arange(all_tokens.shape[1], dtype=jnp.int32))
     key_ids = jnp.broadcast_to(ids[:, None, :], (streams, 8, ids.shape[1]))
@@ -752,6 +767,7 @@
     query_ids = jnp.broadcast_to(query_ids[..., None], (streams, chip_rows, 128))
 
     key_values, queries, chip_tokens = project(place, all_tokens, small, qkv_weight, chip_rows)
+    queries = tied(queries, late)
     chip_tokens = chip_tokens.reshape(rows, D)
     attended, lse = attend(query_ids, key_ids, queries, key_values)
     other_attended = swap(attended).reshape(rows, HALF)

time: 284 us -> 269 us (0.947)
  starting transfers between devices: 56.7 us -> 45.3 us
    ppermute x15, waiting for transfers between devices: 77.4 us -> 67.1 us  [z_move(): return lax.ppermute(value, 'seq', [(i, i ^ 2 * step) for i in range(seq)])]
    ppermute x8, starting transfers between devices: 19.1 us -> 8.86 us  [core_swap(): return lax.ppermute(value, 'seq', [(i, i ^ 1) for i in range(seq)])]
    ppermute x19, waiting for transfers between devices: 14.2 us -> 18.8 us  [dp_move(): return lax.ppermute(value, 'dp', [(i, i ^ step) for i in range(dps)])]
    all_gather x1, waiting for transfers between devices: 0.02 us -> 4.4 us  [body(): lax.all_gather(tied(tokens, late), 'seq', axis=1, tiled=True)]
    unnamed x103 -> x85, local copies, waits for them, and re-layouts: 19.1 us -> 19.1 us
  transfers between devices with their start and end apart: 44 -> 44, of which waited for: 16 -> 18; matrix products, arithmetic and copies ran while one was open for 10% -> 11% of each run, Pallas kernels for 18% -> 19%
where the time goes in v2:
time: 269 us; the launch traced here: 268 us
  waiting for transfers between devices  92.2 us (34%)
  Pallas kernels  64.9 us (24%)
  starting transfers between devices  45.3 us (17%)
  local copies, waits for them, and re-layouts  31.6 us (12%)
  other arithmetic  19.2 us (7%)
  between operations  14.8 us (6%)
    ppermute x15, waiting for transfers between devices, z_move(): return lax.ppermute(value, 'seq', [(i, i ^ 2 * step) for i in range(seq)])  67.1 us
    ppermute x15, starting transfers between devices, z_move(): return lax.ppermute(value, 'seq', [(i, i ^ 2 * step) for i in range(seq)])  22.2 us
    unnamed x85, local copies, waits for them, and re-layouts  19.1 us
    ppermute x19, waiting for transfers between devices, dp_move(): return lax.ppermute(value, 'dp', [(i, i ^ step) for i in range(dps)])  18.8 us
    pallas_call x3, Pallas kernels, over_rows(): pl.pallas_call(kernel, in_specs=[pl.BlockSpec(memory_space=pltpu.SMEM)] +...  14.7 us
    ppermute x19, starting transfers between devices, dp_move(): return lax.ppermute(value, 'dp', [(i, i ^ step) for i in range(dps)])  14.1 us
    pallas_call x1, Pallas kernels, attend_back(): pl.pallas_call(backward_kernel, grid=(streams, PAIRS), in_specs=[specs['q...  13.8 us
    pallas_call x2, Pallas kernels, packed_call(): pl.pallas_call(kernel, in_specs=[pl.BlockSpec(memory_space=pltpu.SMEM)] +...  9.98 us
  transfers between devices with their start and end apart: 44, of which 18 were waited for; matrix products, arithmetic and copies ran while one was open for 11% of the time, Pallas kernels for 19%

profile of v2, /device:TPU:13, one launch (start us, length us, event | category | flops | bytes accessed | tf_op | source)
XLA Modules:
  0.0 268.0 jit_solution(11357690350839176215)
XLA Ops:
  7.8 1.8 first_columns.1
  11.3 1.0 convert_element_type.195
  12.5 1.3 dynamic-slice_reduce_fusion.1
  14.2 1.4 collective-permute-start.3
  15.6 1.1 collective-permute-start.2
  16.7 1.1 collective-permute-start.1
  17.8 6.2 %collective-permute-done.3 = bf16[2,24,1280]{2,1,0:T(8,128)(2,1)S(1)} collective-permute-done((bf16[2,24,1280]{2,1,0:T(8,128)(2,1)S(1)}, bf16[2,24,1280]{2,1,0:T(8,128)(2,1)S(1)}, u32[]{:S(2)}, u32[]{:S(2)}) %collective-permute-start.3) | collective-permute-done | bytes 122912 | tf_op jit(solution)/shard_map/ppermute | solution.py:104
  24.0 1.7 collective-permute-done.2
  26.4 1.2 collective-permute-start.5
  28.4 3.8 %collective-permute-start.8 = (bf16[2,24,2304]{2,1,0:T(8,128)(2,1)S(1)}, bf16[2,24,2304]{2,1,0:T(8,128)(2,1)S(1)}, u32[]{:S(2)}, u32[]{:S(2)}) collective-permute-start(bf16[2,24,2304]{2,1,0:T(8,128)(2,1)S(1)} %maximum_select_fusion.1), channel_id=1, source_target_pairs={{0,4},{1,5},{2,6},{3,7},{4,0},{5,1},{6,2},{7,3},{8,12},{9,13},{10,... | collective-permute-start | bytes 663560 | tf_op jit(solution)/shard_map/ppermute | solution.py:104
  32.4 1.1 collective-permute-done.9
  33.5 13.5 %collective-permute-done.8 = bf16[2,24,2304]{2,1,0:T(8,128)(2,1)S(1)} collective-permute-done((bf16[2,24,2304]{2,1,0:T(8,128)(2,1)S(1)}, bf16[2,24,2304]{2,1,0:T(8,128)(2,1)S(1)}, u32[]{:S(2)}, u32[]{:S(2)}) %collective-permute-start.8) | collective-permute-done | bytes 221216 | tf_op jit(solution)/shard_map/ppermute | solution.py:104
  47.4 1.2 collective-permute-start.11
  48.7 4.5 %collective-permute-done.10.refs_3_ = bf16[2,2,24,1280]{3,2,1,0:T(8,128)(2,1)S(1)} collective-permute-done((bf16[2,2,24,1280]{3,2,1,0:T(8,128)(2,1)S(1)}, bf16[2,2,24,1280]{3,2,1,0:T(8,128)(2,1)S(1)}, u32[]{:S(2)}, u32[]{:S(2)}) %collective-permute-start.10) | collective-permute-done | bytes 245792 | tf_op jit(solution)/shard_map/ppermute | solution.py:108
  54.7 1.3 collective-permute-start.14
  56.5 3.2 %collective-permute-start.12 = (bf16[2,128,768]{2,1,0:T(8,128)(2,1)}, bf16[2,128,768]{2,1,0:T(8,128)(2,1)}, u32[]{:S(2)}, u32[]{:S(2)}) collective-permute-start(bf16[2,128,768]{2,1,0:T(8,128)(2,1)} %param.35), channel_id=1, source_target_pairs={{0,1},{1,0},{2,3},{3,2},{4,5},{5,4},{6,7},{7,6},{8,9},{9,8},{10,11... | collective-permute-start | bytes 1179656 | tf_op jit(solution)/shard_map/ppermute | solution.py:100
  62.0 4.0 %collective-permute-start.19 = (bf16[96,768]{1,0:T(8,128)(2,1)}, bf16[96,768]{1,0:T(8,128)(2,1)}, u32[]{:S(2)}, u32[]{:S(2)}) collective-permute-start(bf16[96,768]{1,0:T(8,128)(2,1)} %convert_element_type.196), channel_id=1, source_target_pairs={{0,4},{1,5},{2,6},{3,7},{4,0},{5,1},{6,2},{7,3},{8,12},{9,13},{10,... | collective-permute-start | bytes 442376 | tf_op jit(solution)/shard_map/ppermute | solution.py:104
  66.0 1.1 copy-done.8
  67.0 1.0 copy-done.21
  68.1 1.1 copy-done.23
  72.4 1.7 copy.53
  78.6 2.2 slice.179
  83.0 6.6 %collective-permute-done.19 = bf16[96,768]{1,0:T(8,128)(2,1)} collective-permute-done((bf16[96,768]{1,0:T(8,128)(2,1)}, bf16[96,768]{1,0:T(8,128)(2,1)}, u32[]{:S(2)}, u32[]{:S(2)}) %collective-permute-start.19) | collective-permute-done | bytes 147488 | tf_op jit(solution)/shard_map/ppermute | solution.py:104
  89.6 1.2 pad_maximum_fusion.1.refs_0_
  90.8 1.3 collective-permute-start.23
  92.1 0.9 collective-permute-start.22
  93.7 4.4 %all-gather.2.cloned.1.call-done.tok_ref = bf16[2,1024,768]{2,1,0:T(8,128)(2,1)} async-done(((bf16[2,128,768]{2,1,0:T(8,128)(2,1)}), bf16[2,1024,768]{2,1,0:T(8,128)(2,1)}) %all-gather.2.cloned.1.call-update) | async-done | bytes 3145744 | tf_op jit(solution)/shard_map/all_gather | solution.py:717
  98.9 5.0 %project.1 = (bf16[2,1024,768]{2,1,0:T(8,128)(2,1)S(1)}, bf16[2,256,384]{2,1,0:T(8,128)(2,1)S(1)}, bf16[2,256,768]{2,1,0:T(8,128)(2,1)S(1)}) custom-call(s32[3]{0:T(128)S(1)} %copy-done.37, bf16[2,1024,768]{2,1,0:T(8,128)(2,1)} %all-gather.2.cloned.1.call-done.tok_ref, f32[12,768]{1,0:T(8,128)S(1)} %copy-done.16, bf16[768,1152]{1,0:T(8,128)(2,1)S(1)} %bitcast.84), custom_call_target="tpu_custom_call" | custom-call | tf_op jit(solution)/shard_map/project/pallas_call | solution.py:370
  104.1 9.5 %attend.1 = (bf16[2,256,384]{2,1,0:T(8,128)(2,1)S(1)}, f32[2,3,2,256,128]{4,3,2,1,0:T(8,128)S(1)}) custom-call(s32[2,256,128]{2,1,0:T(8,128)S(1)} %broadcast_in_dim.48.qid_ref, s32[2,8,1024]{2,1,0:T(8,128)S(1)} %broadcast_in_dim.49.kid_ref, bf16[2,256,384]{2,1,0:T(8,128)(2,1)S(1)} %get-tuple-element.125.q_ref, ...), custom_call_target="tpu_custom_call" | custom-call | tf_op jit(solution)/shard_map/attend/pallas_call | solution.py:275
  114.0 1.7 place_late.1
  115.7 4.1 %collective-permute-done.22.refs_2_ = bf16[4,96,768]{2,1,0:T(8,128)(2,1)} collective-permute-done((bf16[4,96,768]{2,1,0:T(8,128)(2,1)S(1)}, bf16[4,96,768]{2,1,0:T(8,128)(2,1)}, u32[]{:S(2)}, u32[]{:S(2)}) %collective-permute-start.22) | collective-permute-done | bytes 589856 | tf_op jit(solution)/shard_map/ppermute | solution.py:108
  119.8 1.6 place_last.1
  121.4 6.2 %middle.1 = (f32[512,768]{1,0:T(8,128)S(1)}, f32[512,128]{1,0:T(8,128)S(1)}, bf16[512,768]{1,0:T(8,128)(2,1)S(1)}, bf16[512,1536]{1,0:T(8,128)(2,1)S(1)}, bf16[5...) custom-call(s32[3]{0:T(128)S(1)} %copy-done.37, bf16[512,384]{1,0:T(8,128)(2,1)S(1)} %bitcast.92, ...), custom_call_target="tpu_custom_call" | custom-call | tf_op jit(solution)/shard_map/middle/pallas_call | solution.py:525
  128.2 1.9 collective-permute-done.24.refs_1_
  130.1 6.5 %turn.1 = (bf16[256,768]{1,0:T(8,128)(2,1)}, f32[512,768]{1,0:T(8,128)S(1)}, bf16[512,768]{1,0:T(8,128)(2,1)S(1)}, bf16[512,1536]{1,0:T(8,128)(2,1)S(1)}, f32[51...) custom-call(s32[3]{0:T(128)S(1)} %copy-done.37, ...), custom_call_target="tpu_custom_call" | custom-call | tf_op jit(solution)/shard_map/turn/pallas_call | solution.py:525
  137.1 4.8 %wide_packs.1 = (bf16[4,48,3072]{2,1,0:T(8,128)(2,1)S(1)}, bf16[4,48,3072]{2,1,0:T(8,128)(2,1)}, bf16[4,48,3072]{2,1,0:T(8,128)(2,1)}, bf16[2,48,3072]{2,1,0:T(8,128)(2,1)S(1)}, bf16[2,48,3072]{2,1,0:T(8,128)(2,1)S(1)}) custom-call(s32[3]{0:T(128)S(1)} %copy-done.37, bf16[512,1536]{1,0:T(8,128)(2,1)S(1)} %get-tuple-element.151.hidden_ref, ...), custom_call_target="tpu_custom_call" | custom-call | tf_op jit(solution)/shard_map/wide_packs/pallas_call | solution.py:539
  143.6 1.0 collective-permute-start.26
  145.1 1.9 first_back.1
  147.1 13.8 %attend_back.1 = (bf16[2,256,384]{2,1,0:T(8,128)(2,1)S(1)}, bf16[2,1024,384]{2,1,0:T(8,128)(2,1)S(1)}, bf16[2,1024,384]{2,1,0:T(8,128)(2,1)S(1)}) custom-call(s32[2,256,128]{2,1,0:T(8,128)S(1)} %broadcast_in_dim.48.qid_ref, s32[2,8,1024]{2,1,0:T(8,128)S(1)} %broadcast_in_dim.49.kid_ref, bf16[2,256,384]{2,1,0:T(8,128)(2,1)S(1)} %get-tuple-element.125.q_ref, ...), custom_call_target="tpu_custom_call" | custom-call | tf_op jit(solution)/shard_map/attend_back/pallas_call | solution.py:296
  161.0 6.0 %unproject.1 = bf16[2,1024,768]{2,1,0:T(8,128)(2,1)} custom-call(s32[3]{0:T(128)S(1)} %copy-done.37, bf16[2,256,384]{2,1,0:T(8,128)(2,1)S(1)} %get-tuple-element.148.query_ref, bf16[2,1024,384]{2,1,0:T(8,128)(2,1)S(1)} %get-tuple-element.149.key_ref, bf16[2,1024,384]{2,1,0:T(8,128)(2,1)S(1)} %get-tuple-element.150.value_ref, bf16[768,1152]{1,0:T(8,128)(2,1)S(1)} %bitcast.85), custom_call_target="tpu_custom_call" | custom-call | tf_op jit(solution)/shard_map/unproject/pallas_call | solution.py:409
  167.0 1.2 copy-done.1
  169.0 2.3 collective-permute-done.26
  172.0 1.5 add_convert_fusion.1
  174.2 1.4 add_convert_fusion
  176.2 1.1 copy-done.4
  177.3 1.1 copy-done.12
  178.4 1.0 copy-done.14
  179.4 1.1 copy-done.25
  180.6 5.2 %narrow_packs.1 = (bf16[4,48,1664]{2,1,0:T(8,128)(2,1)S(1)}, bf16[4,48,1664]{2,1,0:T(8,128)(2,1)S(1)}, bf16[4,48,1664]{2,1,0:T(8,128)(2,1)S(1)}, bf16[2,48,1664]...) custom-call(s32[3]{0:T(128)S(1)} %copy-done.37, bf16[2048,768]{1,0:T(8,128)(2,1)S(1)} %bitcast.81, ...), custom_call_target="tpu_custom_call" | custom-call | tf_op jit(solution)/shard_map/narrow_packs/pallas_call | solution.py:539
  186.7 0.9 collective-permute-start.29
  187.6 1.4 collective-permute-done.31
  189.0 1.6 add_bitcast_fusion
  191.0 4.7 %collective-permute-start.35 = (bf16[48,3072]{1,0:T(8,128)(2,1)S(1)}, bf16[48,3072]{1,0:T(8,128)(2,1)S(1)}, u32[]{:S(2)}, u32[]{:S(2)}) collective-permute-start(bf16[48,3072]{1,0:T(8,128)(2,1)S(1)} %get-tuple-element.192), channel_id=1, source_target_pairs={{0,4},{1,5},{2,6},{3,7},{4,0},{5,1},{6,2},{7,3},{8,12},{9,13},{10,... | collective-permute-start | bytes 884744 | tf_op jit(solution)/shard_map/ppermute | solution.py:104
  196.0 1.1 add_bitcast_fusion.3
  197.0 5.7 %collective-permute-done.28 = bf16[4,48,1664]{2,1,0:T(8,128)(2,1)S(1)} collective-permute-done((bf16[4,48,1664]{2,1,0:T(8,128)(2,1)S(1)}, bf16[4,48,1664]{2,1,0:T(8,128)(2,1)S(1)}, u32[]{:S(2)}, u32[]{:S(2)}) %collective-permute-start.28) | collective-permute-done | bytes 639008 | tf_op jit(solution)/shard_map/ppermute | solution.py:108
  205.7 16.1 %collective-permute-done.36 = bf16[48,3072]{1,0:T(8,128)(2,1)S(1)} collective-permute-done((bf16[48,3072]{1,0:T(8,128)(2,1)S(1)}, bf16[48,3072]{1,0:T(8,128)(2,1)S(1)}, u32[]{:S(2)}, u32[]{:S(2)}) %collective-permute-start.36) | collective-permute-done | bytes 294944 | tf_op jit(solution)/shard_map/ppermute | solution.py:104
  221.8 8.8 %collective-permute-done.35 = bf16[48,3072]{1,0:T(8,128)(2,1)S(1)} collective-permute-done((bf16[48,3072]{1,0:T(8,128)(2,1)S(1)}, bf16[48,3072]{1,0:T(8,128)(2,1)S(1)}, u32[]{:S(2)}, u32[]{:S(2)}) %collective-permute-start.35) | collective-permute-done | bytes 294944 | tf_op jit(solution)/shard_map/ppermute | solution.py:104
  230.9 3.0 %collective-permute-start.41 = (f32[24,1536]{1,0:T(8,128)S(1)}, f32[24,1536]{1,0:T(8,128)S(1)}, u32[]{:S(2)}, u32[]{:S(2)}) collective-permute-start(f32[24,1536]{1,0:T(8,128)S(1)} %get-tuple-element.202), channel_id=1, source_target_pairs={{0,1},{1,0},{2,3},{3,2},{4,5},{5,4},{6,7},{7,6},{8,9},{9,8},{10,11... | collective-permute-start | bytes 442376 | tf_op jit(solution)/shard_map/ppermute | solution.py:100
  236.3 1.2 select_n.98
  237.6 1.2 fusion.3
  238.8 3.2 %collective-permute-start.38 = (bf16[48,1664]{1,0:T(8,128)(2,1)S(1)}, bf16[48,1664]{1,0:T(8,128)(2,1)S(1)}, u32[]{:S(2)}, u32[]{:S(2)}) collective-permute-start(bf16[48,1664]{1,0:T(8,128)(2,1)S(1)} %get-tuple-element.193), channel_id=1, source_target_pairs={{0,4},{1,5},{2,6},{3,7},{4,0},{5,1},{6,2},{7,3},{8,12},{9,13},{10,... | collective-permute-start | bytes 479240 | tf_op jit(solution)/shard_map/ppermute | solution.py:104
  243.2 0.9 convert_add_fusion
  244.2 7.8 %collective-permute-done.38 = bf16[48,1664]{1,0:T(8,128)(2,1)S(1)} collective-permute-done((bf16[48,1664]{1,0:T(8,128)(2,1)S(1)}, bf16[48,1664]{1,0:T(8,128)(2,1)S(1)}, u32[]{:S(2)}, u32[]{:S(2)}) %collective-permute-start.38) | collective-permute-done | bytes 159776 | tf_op jit(solution)/shard_map/ppermute | solution.py:104
  252.0 4.9 %collective-permute-done.39 = bf16[48,1664]{1,0:T(8,128)(2,1)S(1)} collective-permute-done((bf16[48,1664]{1,0:T(8,128)(2,1)S(1)}, bf16[48,1664]{1,0:T(8,128)(2,1)S(1)}, u32[]{:S(2)}, u32[]{:S(2)}) %collective-permute-start.39) | collective-permute-done | bytes 159776 | tf_op jit(solution)/shard_map/ppermute | solution.py:104
  (184 shorter events, 39.5 us)
Async XLA Ops:
  7.2 90.9 %all-gather.2.cloned.1.call-start = ((), (), s32[]{:S(2)}) async-start(), calls=%async_computation.1 | async-start | bytes 3538944 | tf_op jit(solution)/shard_map/all_gather | solution.py:717
  9.7 4.5 %copy-start.40 = (bf16[24,1280]{1,0:T(8,128)(2,1)S(1)}, bf16[24,1280]{1,0:T(8,128)(2,1)}, u32[]{:S(2)}) copy-start(bf16[24,1280]{1,0:T(8,128)(2,1)} %get-tuple-element.99) | copy-start | bytes 184324
  9.7 4.5 %collective-permute-start = (bf16[24,1280]{1,0:T(8,128)(2,1)}, bf16[24,1280]{1,0:T(8,128)(2,1)S(1)}, u32[]{:S(2)}, u32[]{:S(2)}) collective-permute-start(bf16[24,1280]{1,0:T(8,128)(2,1)} %get-tuple-element.100), channel_id=1, source_target_pairs={{0,1},{1,0},{2,3},{3,2},{4,5},{5,4},{6,7},{7,6},{8,9},{9,8},{10,11... | collective-permute-start | bytes 184328 | tf_op jit(solution)/shard_map/ppermute | solution.py:100
  14.1 3.7 %collective-permute-start.4 = (bf16[24,2304]{1,0:T(8,128)(2,1)S(1)}, bf16[24,2304]{1,0:T(8,128)(2,1)S(1)}, u32[]{:S(2)}, u32[]{:S(2)}) collective-permute-start(bf16[24,2304]{1,0:T(8,128)(2,1)S(1)} %get-tuple-element.212), channel_id=1, source_target_pairs={{0,1},{1,0},{2,3},{3,2},{4,5},{5,4},{6,7},{7,6},{8,9},{9,8},{10,11... | collective-permute-start | bytes 331784 | tf_op jit(solution)/shard_map/ppermute | solution.py:100
  14.2 9.7 %collective-permute-start.3 = (bf16[2,24,1280]{2,1,0:T(8,128)(2,1)S(1)}, bf16[2,24,1280]{2,1,0:T(8,128)(2,1)S(1)}, u32[]{:S(2)}, u32[]{:S(2)}) collective-permute-start(bf16[2,24,1280]{2,1,0:T(8,128)(2,1)S(1)} %maximum_select_fusion.2), channel_id=1, source_target_pairs={{0,6},{1,7},{2,4},{3,5},{4,2},{5,3},{6,0},{7,1},{8,14},{9,15},{10,... | collective-permute-start | bytes 368648 | tf_op jit(solution)/shard_map/ppermute | solution.py:104
  15.6 10.1 %collective-permute-start.2 = (bf16[2,24,1280]{2,1,0:T(8,128)(2,1)S(1)}, bf16[2,24,1280]{2,1,0:T(8,128)(2,1)S(1)}, u32[]{:S(2)}, u32[]{:S(2)}) collective-permute-start(bf16[2,24,1280]{2,1,0:T(8,128)(2,1)S(1)} %maximum_select_fusion.2), channel_id=1, source_target_pairs={{0,4},{1,5},{2,6},{3,7},{4,0},{5,1},{6,2},{7,3},{8,12},{9,13},{10,... | collective-permute-start | bytes 368648 | tf_op jit(solution)/shard_map/ppermute | solution.py:104
  16.7 9.4 %collective-permute-start.1 = (bf16[2,24,1280]{2,1,0:T(8,128)(2,1)S(1)}, bf16[2,24,1280]{2,1,0:T(8,128)(2,1)S(1)}, u32[]{:S(2)}, u32[]{:S(2)}) collective-permute-start(bf16[2,24,1280]{2,1,0:T(8,128)(2,1)S(1)} %maximum_select_fusion.2), channel_id=1, source_target_pairs={{0,2},{1,3},{2,0},{3,1},{4,6},{5,7},{6,4},{7,5},{8,10},{9,11},{10,... | collective-permute-start | bytes 368648 | tf_op jit(solution)/shard_map/ppermute | solution.py:104
  26.1 20.8 %collective-permute-start.6 = (bf16[4,2,24,1280]{3,2,1,0:T(8,128)(2,1)S(1)}, bf16[4,2,24,1280]{3,2,1,0:T(8,128)(2,1)S(1)}, u32[]{:S(2)}, u32[]{:S(2)}) collective-permute-start(bf16[4,2,24,1280]{3,2,1,0:T(8,128)(2,1)S(1)} %pad_maximum_fusion.2.refs_0_), channel_id=1, source_target_pairs={{0,16},{8,24},{16,0},{24,8},{1,17},{9,25},{17,1},{25,9},{2,18},{10... | collective-permute-start | bytes 1474568 | tf_op jit(solution)/shard_map/ppermute | solution.py:108
  26.4 20.5 %collective-permute-start.5 = (bf16[4,2,24,1280]{3,2,1,0:T(8,128)(2,1)S(1)}, bf16[4,2,24,1280]{3,2,1,0:T(8,128)(2,1)S(1)}, u32[]{:S(2)}, u32[]{:S(2)}) collective-permute-start(bf16[4,2,24,1280]{3,2,1,0:T(8,128)(2,1)S(1)} %pad_maximum_fusion.2.refs_0_), channel_id=1, source_target_pairs={{0,8},{8,0},{16,24},{24,16},{1,9},{9,1},{17,25},{25,17},{2,10},{10... | collective-permute-start | bytes 1474568 | tf_op jit(solution)/shard_map/ppermute | solution.py:108
  28.4 5.1 %collective-permute-start.9 = (bf16[2,24,2304]{2,1,0:T(8,128)(2,1)S(1)}, bf16[2,24,2304]{2,1,0:T(8,128)(2,1)S(1)}, u32[]{:S(2)}, u32[]{:S(2)}) collective-permute-start(bf16[2,24,2304]{2,1,0:T(8,128)(2,1)S(1)} %maximum_select_fusion.1), channel_id=1, source_target_pairs={{0,6},{1,7},{2,4},{3,5},{4,2},{5,3},{6,0},{7,1},{8,14},{9,15},{10,... | collective-permute-start | bytes 663560 | tf_op jit(solution)/shard_map/ppermute | solution.py:104
  28.4 18.5 %collective-permute-start.8 = (bf16[2,24,2304]{2,1,0:T(8,128)(2,1)S(1)}, bf16[2,24,2304]{2,1,0:T(8,128)(2,1)S(1)}, u32[]{:S(2)}, u32[]{:S(2)}) collective-permute-start(bf16[2,24,2304]{2,1,0:T(8,128)(2,1)S(1)} %maximum_select_fusion.1), channel_id=1, source_target_pairs={{0,4},{1,5},{2,6},{3,7},{4,0},{5,1},{6,2},{7,3},{8,12},{9,13},{10,... | collective-permute-start | bytes 663560 | tf_op jit(solution)/shard_map/ppermute | solution.py:104
  32.3 14.7 %collective-permute-start.7 = (bf16[2,24,2304]{2,1,0:T(8,128)(2,1)S(1)}, bf16[2,24,2304]{2,1,0:T(8,128)(2,1)S(1)}, u32[]{:S(2)}, u32[]{:S(2)}) collective-permute-start(bf16[2,24,2304]{2,1,0:T(8,128)(2,1)S(1)} %maximum_select_fusion.1), channel_id=1, source_target_pairs={{0,2},{1,3},{2,0},{3,1},{4,6},{5,7},{6,4},{7,5},{8,10},{9,11},{10,... | collective-permute-start | bytes 663560 | tf_op jit(solution)/shard_map/ppermute | solution.py:104
  47.0 7.7 %copy-start.20 = (bf16[4,2,24,1280]{3,2,1,0:T(8,128)(2,1)}, bf16[4,2,24,1280]{3,2,1,0:T(8,128)(2,1)S(1)}, u32[]{:S(2)}) copy-start(bf16[4,2,24,1280]{3,2,1,0:T(8,128)(2,1)S(1)} %collective-permute-done.6.refs_2_) | copy-start | bytes 1474564
  47.0 7.8 %copy-start.22 = (bf16[4,2,24,1280]{3,2,1,0:T(8,128)(2,1)}, bf16[4,2,24,1280]{3,2,1,0:T(8,128)(2,1)S(1)}, u32[]{:S(2)}) copy-start(bf16[4,2,24,1280]{3,2,1,0:T(8,128)(2,1)S(1)} %collective-permute-done.5.refs_1_) | copy-start | bytes 1474564
  47.0 190.6 %reduce-scatter.2.cloned.1.call-start = ((), (), s32[]{:S(2)}) async-start(), calls=%async_computation.2 | async-start | bytes 3538944 | tf_op jit(solution)/shard_map/reduce_scatter | solution.py:883
  47.1 12.6 %copy-start.39 = (f32[96,768]{1,0:T(8,128)S(1)}, f32[96,768]{1,0:T(8,128)}, u32[]{:S(2)}) copy-start(f32[96,768]{1,0:T(8,128)} %param.30) | copy-start | bytes 884740
  47.1 18.8 %copy-start.37 = (s32[3]{0:T(128)S(1)}, s32[3]{0:T(128)}, u32[]{:S(2)}) copy-start(s32[3]{0:T(128)} %pad_add_fusion.place_ref) | copy-start | bytes 40
  47.1 6.1 %collective-permute-start.10 = (bf16[2,2,24,1280]{3,2,1,0:T(8,128)(2,1)S(1)}, bf16[2,2,24,1280]{3,2,1,0:T(8,128)(2,1)S(1)}, u32[]{:S(2)}, u32[]{:S(2)}) collective-permute-start(bf16[2,2,24,1280]{3,2,1,0:T(8,128)(2,1)S(1)} %slice.174), channel_id=1, source_target_pairs={{0,8},{8,0},{16,24},{24,16},{1,9},{9,1},{17,25},{25,17},{2,10},{10... | collective-permute-start | bytes 737288 | tf_op jit(solution)/shard_map/ppermute | solution.py:108
  47.4 6.4 %collective-permute-start.11 = (bf16[2,2,24,1280]{3,2,1,0:T(8,128)(2,1)S(1)}, bf16[2,2,24,1280]{3,2,1,0:T(8,128)(2,1)S(1)}, u32[]{:S(2)}, u32[]{:S(2)}) collective-permute-start(bf16[2,2,24,1280]{3,2,1,0:T(8,128)(2,1)S(1)} %slice.175), channel_id=1, source_target_pairs={{0,16},{8,24},{16,0},{24,8},{1,17},{9,25},{17,1},{25,9},{2,18},{10... | collective-permute-start | bytes 737288 | tf_op jit(solution)/shard_map/ppermute | solution.py:108
  54.7 23.9 %collective-permute-start.14 = (bf16[4,2,24,2304]{3,2,1,0:T(8,128)(2,1)S(1)}, bf16[4,2,24,2304]{3,2,1,0:T(8,128)(2,1)S(1)}, u32[]{:S(2)}, u32[]{:S(2)}) collective-permute-start(bf16[4,2,24,2304]{3,2,1,0:T(8,128)(2,1)S(1)} %pad_maximum_fusion.refs_0_), channel_id=1, source_target_pairs={{0,16},{8,24},{16,0},{24,8},{1,17},{9,25},{17,1},{25,9},{2,18},{10... | collective-permute-start | bytes 2654216 | tf_op jit(solution)/shard_map/ppermute | solution.py:108
  56.0 22.6 %collective-permute-start.13 = (bf16[4,2,24,2304]{3,2,1,0:T(8,128)(2,1)S(1)}, bf16[4,2,24,2304]{3,2,1,0:T(8,128)(2,1)}, u32[]{:S(2)}, u32[]{:S(2)}) collective-permute-start(bf16[4,2,24,2304]{3,2,1,0:T(8,128)(2,1)S(1)} %pad_maximum_fusion.refs_0_), channel_id=1, source_target_pairs={{0,8},{8,0},{16,24},{24,16},{1,9},{9,1},{17,25},{25,17},{2,10},{10... | collective-permute-start | bytes 2654216 | tf_op jit(solution)/shard_map/ppermute | solution.py:108
  56.5 19.7 %collective-permute-start.12 = (bf16[2,128,768]{2,1,0:T(8,128)(2,1)}, bf16[2,128,768]{2,1,0:T(8,128)(2,1)}, u32[]{:S(2)}, u32[]{:S(2)}) collective-permute-start(bf16[2,128,768]{2,1,0:T(8,128)(2,1)} %param.35), channel_id=1, source_target_pairs={{0,1},{1,0},{2,3},{3,2},{4,5},{5,4},{6,7},{7,6},{8,9},{9,8},{10,11... | collective-permute-start | bytes 1179656 | tf_op jit(solution)/shard_map/ppermute | solution.py:100
  61.0 22.0 %collective-permute-start.20 = (bf16[96,768]{1,0:T(8,128)(2,1)}, bf16[96,768]{1,0:T(8,128)(2,1)}, u32[]{:S(2)}, u32[]{:S(2)}) collective-permute-start(bf16[96,768]{1,0:T(8,128)(2,1)} %convert_element_type.196), channel_id=1, source_target_pairs={{0,6},{1,7},{2,4},{3,5},{4,2},{5,3},{6,0},{7,1},{8,14},{9,15},{10,... | collective-permute-start | bytes 442376 | tf_op jit(solution)/shard_map/ppermute | solution.py:104
  62.0 27.7 %collective-permute-start.19 = (bf16[96,768]{1,0:T(8,128)(2,1)}, bf16[96,768]{1,0:T(8,128)(2,1)}, u32[]{:S(2)}, u32[]{:S(2)}) collective-permute-start(bf16[96,768]{1,0:T(8,128)(2,1)} %convert_element_type.196), channel_id=1, source_target_pairs={{0,4},{1,5},{2,6},{3,7},{4,0},{5,1},{6,2},{7,3},{8,12},{9,13},{10,... | collective-permute-start | bytes 442376 | tf_op jit(solution)/shard_map/ppermute | solution.py:104
  76.2 13.4 %collective-permute-start.18 = (bf16[96,768]{1,0:T(8,128)(2,1)}, bf16[96,768]{1,0:T(8,128)(2,1)}, u32[]{:S(2)}, u32[]{:S(2)}) collective-permute-start(bf16[96,768]{1,0:T(8,128)(2,1)} %convert_element_type.196), channel_id=1, source_target_pairs={{0,2},{1,3},{2,0},{3,1},{4,6},{5,7},{6,4},{7,5},{8,10},{9,11},{10,... | collective-permute-start | bytes 442376 | tf_op jit(solution)/shard_map/ppermute | solution.py:104
  78.6 3.6 %copy-start.41 = (pred[64,64]{1,0:T(8,128)(4,1)S(1)}, pred[64,64]{1,0:T(8,128)(4,1)}, u32[]{:S(2)}) copy-start(pred[64,64]{1,0:T(8,128)(4,1)} %iota_compare_fusion.1) | copy-start | bytes 12292
  78.6 11.0 %copy-start.5 = (bf16[4,2,24,2304]{3,2,1,0:T(8,128)(2,1)}, bf16[4,2,24,2304]{3,2,1,0:T(8,128)(2,1)S(1)}, u32[]{:S(2)}) copy-start(bf16[4,2,24,2304]{3,2,1,0:T(8,128)(2,1)S(1)} %collective-permute-done.14.refs_2_) | copy-start | bytes 2654212
  81.6 22.3 %collective-permute-start.15 = (bf16[2,2,24,2304]{3,2,1,0:T(8,128)(2,1)}, bf16[2,2,24,2304]{3,2,1,0:T(8,128)(2,1)}, u32[]{:S(2)}, u32[]{:S(2)}) collective-permute-start(bf16[2,2,24,2304]{3,2,1,0:T(8,128)(2,1)} %slice.178), channel_id=1, source_target_pairs={{0,8},{8,0},{16,24},{24,16},{1,9},{9,1},{17,25},{25,17},{2,10},{10... | collective-permute-start | bytes 1327112 | tf_op jit(solution)/shard_map/ppermute | solution.py:108
  82.0 21.9 %collective-permute-start.16 = (bf16[2,2,24,2304]{3,2,1,0:T(8,128)(2,1)}, bf16[2,2,24,2304]{3,2,1,0:T(8,128)(2,1)}, u32[]{:S(2)}, u32[]{:S(2)}) collective-permute-start(bf16[2,2,24,2304]{3,2,1,0:T(8,128)(2,1)} %slice.179), channel_id=1, source_target_pairs={{0,16},{8,24},{16,0},{24,8},{1,17},{9,25},{17,1},{25,9},{2,18},{10... | collective-permute-start | bytes 1327112 | tf_op jit(solution)/shard_map/ppermute | solution.py:108
  90.8 24.8 %collective-permute-start.23 = (bf16[4,96,768]{2,1,0:T(8,128)(2,1)S(1)}, bf16[4,96,768]{2,1,0:T(8,128)(2,1)}, u32[]{:S(2)}, u32[]{:S(2)}) collective-permute-start(bf16[4,96,768]{2,1,0:T(8,128)(2,1)S(1)} %pad_maximum_fusion.1.refs_0_), channel_id=1, source_target_pairs={{0,24},{8,16},{16,8},{24,0},{1,25},{9,17},{17,9},{25,1},{2,26},{10... | collective-permute-start | bytes 1769480 | tf_op jit(solution)/shard_map/ppermute | solution.py:108
  92.1 27.7 %collective-permute-start.22 = (bf16[4,96,768]{2,1,0:T(8,128)(2,1)S(1)}, bf16[4,96,768]{2,1,0:T(8,128)(2,1)}, u32[]{:S(2)}, u32[]{:S(2)}) collective-permute-start(bf16[4,96,768]{2,1,0:T(8,128)(2,1)S(1)} %pad_maximum_fusion.1.refs_0_), channel_id=1, source_target_pairs={{0,16},{8,24},{16,0},{24,8},{1,17},{9,25},{17,1},{25,9},{2,18},{10... | collective-permute-start | bytes 1769480 | tf_op jit(solution)/shard_map/ppermute | solution.py:108
  93.1 26.7 %collective-permute-start.21 = (bf16[4,96,768]{2,1,0:T(8,128)(2,1)S(1)}, bf16[4,96,768]{2,1,0:T(8,128)(2,1)}, u32[]{:S(2)}, u32[]{:S(2)}) collective-permute-start(bf16[4,96,768]{2,1,0:T(8,128)(2,1)S(1)} %pad_maximum_fusion.1.refs_0_), channel_id=1, source_target_pairs={{0,8},{8,0},{16,24},{24,16},{1,9},{9,1},{17,25},{25,17},{2,10},{10... | collective-permute-start | bytes 1769480 | tf_op jit(solution)/shard_map/ppermute | solution.py:108
  103.9 17.5 %copy-start.3 = (bf16[2,256,768]{2,1,0:T(8,128)(2,1)}, bf16[2,256,768]{2,1,0:T(8,128)(2,1)S(1)}, u32[]{:S(2)}) copy-start(bf16[2,256,768]{2,1,0:T(8,128)(2,1)S(1)} %get-tuple-element.128) | copy-start | bytes 2359300
  104.1 9.9 %copy-start.6 = (bf16[4,2,24,2304]{3,2,1,0:T(8,128)(2,1)S(1)}, bf16[4,2,24,2304]{3,2,1,0:T(8,128)(2,1)}, u32[]{:S(2)}) copy-start(bf16[4,2,24,2304]{3,2,1,0:T(8,128)(2,1)} %copy-done.5) | copy-start | bytes 2654212
  113.6 7.8 %copy-start.9 = (bf16[2,256,384]{2,1,0:T(8,128)(2,1)}, bf16[2,256,384]{2,1,0:T(8,128)(2,1)S(1)}, u32[]{:S(2)}) copy-start(bf16[2,256,384]{2,1,0:T(8,128)(2,1)S(1)} %get-tuple-element.127) | copy-start | bytes 1179652
  113.6 7.8 %collective-permute-start.17 = (bf16[2,256,384]{2,1,0:T(8,128)(2,1)S(1)}, bf16[2,256,384]{2,1,0:T(8,128)(2,1)S(1)}, u32[]{:S(2)}, u32[]{:S(2)}) collective-permute-start(bf16[2,256,384]{2,1,0:T(8,128)(2,1)S(1)} %get-tuple-element.127), channel_id=1, source_target_pairs={{0,1},{1,0},{2,3},{3,2},{4,5},{5,4},{6,7},{7,6},{8,9},{9,8},{10,11... | collective-permute-start | bytes 1179656 | tf_op jit(solution)/shard_map/ppermute | solution.py:100
  115.6 5.8 %copy-start.17 = (f32[12,768]{1,0:T(8,128)S(1)}, f32[12,768]{1,0:T(8,128)}, u32[]{:S(2)}) copy-start(f32[12,768]{1,0:T(8,128)} %copy-done.15) | copy-start | bytes 110596
  121.4 6.3 %copy-start.11 = (bf16[2,256,384]{2,1,0:T(8,128)(2,1)}, bf16[2,256,384]{2,1,0:T(8,128)(2,1)S(1)}, u32[]{:S(2)}) copy-start(bf16[2,256,384]{2,1,0:T(8,128)(2,1)S(1)} %collective-permute-done.17) | copy-start | bytes 1179652
  127.7 2.5 collective-permute-start.24
  136.7 8.4 %collective-permute-start.25 = (bf16[512,768]{1,0:T(8,128)(2,1)S(1)}, bf16[512,768]{1,0:T(8,128)(2,1)S(1)}, u32[]{:S(2)}, u32[]{:S(2)}) collective-permute-start(bf16[512,768]{1,0:T(8,128)(2,1)S(1)} %get-tuple-element.142), channel_id=1, source_target_pairs={{0,1},{1,0},{2,3},{3,2},{4,5},{5,4},{6,7},{7,6},{8,9},{9,8},{10,11... | collective-permute-start | bytes 2359304 | tf_op jit(solution)/shard_map/ppermute | solution.py:100
  143.6 27.8 %collective-permute-start.26 = (bf16[4,48,3072]{2,1,0:T(8,128)(2,1)}, bf16[4,48,3072]{2,1,0:T(8,128)(2,1)}, u32[]{:S(2)}, u32[]{:S(2)}) collective-permute-start(bf16[4,48,3072]{2,1,0:T(8,128)(2,1)} %get-tuple-element.156), channel_id=1, source_target_pairs={{0,8},{8,0},{16,24},{24,16},{1,9},{9,1},{17,25},{25,17},{2,10},{10... | collective-permute-start | bytes 3538952 | tf_op jit(solution)/shard_map/ppermute | solution.py:108
  144.6 27.4 %collective-permute-start.27 = (bf16[4,48,3072]{2,1,0:T(8,128)(2,1)}, bf16[4,48,3072]{2,1,0:T(8,128)(2,1)}, u32[]{:S(2)}, u32[]{:S(2)}) collective-permute-start(bf16[4,48,3072]{2,1,0:T(8,128)(2,1)} %get-tuple-element.157), channel_id=1, source_target_pairs={{0,16},{8,24},{16,0},{24,8},{1,17},{9,25},{17,1},{25,9},{2,18},{10... | collective-permute-start | bytes 3538952 | tf_op jit(solution)/shard_map/ppermute | solution.py:108
  147.1 13.9 %copy-start.24 = (bf16[512,768]{1,0:T(8,128)(2,1)}, bf16[512,768]{1,0:T(8,128)(2,1)S(1)}, u32[]{:S(2)}) copy-start(bf16[512,768]{1,0:T(8,128)(2,1)S(1)} %get-tuple-element.164.branch_ref) | copy-start | bytes 2359300
  147.1 13.9 %copy-start.26 = (f32[256,768]{1,0:T(8,128)}, f32[256,768]{1,0:T(8,128)S(1)}, u32[]{:S(2)}) copy-start(f32[256,768]{1,0:T(8,128)S(1)} %get-tuple-element.145) | copy-start | bytes 2359300
  169.0 7.2 %copy-start.2 = (bf16[2,1024,384]{2,1,0:T(8,128)(2,1)S(1)}, bf16[2,1024,384]{2,1,0:T(8,128)(2,1)}, u32[]{:S(2)}) copy-start(bf16[2,1024,384]{2,1,0:T(8,128)(2,1)} %copy-done.1) | copy-start | bytes 4718596
  172.0 4.2 %copy-start = (bf16[2,1024,768]{2,1,0:T(8,128)(2,1)S(1)}, bf16[2,1024,768]{2,1,0:T(8,128)(2,1)}, u32[]{:S(2)}) copy-start(bf16[2,1024,768]{2,1,0:T(8,128)(2,1)} %all-gather.2.cloned.1.call-done.tok_ref) | copy-start | bytes 9437188
  173.6 14.0 %collective-permute-start.30 = (bf16[2,48,3072]{2,1,0:T(8,128)(2,1)S(1)}, bf16[2,48,3072]{2,1,0:T(8,128)(2,1)S(1)}, u32[]{:S(2)}, u32[]{:S(2)}) collective-permute-start(bf16[2,48,3072]{2,1,0:T(8,128)(2,1)S(1)} %add_convert_fusion.1), channel_id=1, source_target_pairs={{0,16},{8,24},{16,0},{24,8},{1,17},{9,25},{17,1},{25,9},{2,18},{10... | collective-permute-start | bytes 1769480 | tf_op jit(solution)/shard_map/ppermute | solution.py:108
  175.6 13.4 %collective-permute-start.31 = (bf16[2,48,3072]{2,1,0:T(8,128)(2,1)S(1)}, bf16[2,48,3072]{2,1,0:T(8,128)(2,1)S(1)}, u32[]{:S(2)}, u32[]{:S(2)}) collective-permute-start(bf16[2,48,3072]{2,1,0:T(8,128)(2,1)S(1)} %add_convert_fusion), channel_id=1, source_target_pairs={{0,8},{8,0},{16,24},{24,16},{1,9},{9,1},{17,25},{25,17},{2,10},{10... | collective-permute-start | bytes 1769480 | tf_op jit(solution)/shard_map/ppermute | solution.py:108
  180.6 8.4 %copy-start.19 = (bf16[4,48,3072]{2,1,0:T(8,128)(2,1)S(1)}, bf16[4,48,3072]{2,1,0:T(8,128)(2,1)}, u32[]{:S(2)}) copy-start(bf16[4,48,3072]{2,1,0:T(8,128)(2,1)} %copy-done.18) | copy-start | bytes 3538948
  185.8 4.9 %copy-start.28 = (bf16[4,48,1664]{2,1,0:T(8,128)(2,1)}, bf16[4,48,1664]{2,1,0:T(8,128)(2,1)S(1)}, u32[]{:S(2)}) copy-start(bf16[4,48,1664]{2,1,0:T(8,128)(2,1)S(1)} %get-tuple-element.168) | copy-start | bytes 1916932
  185.8 16.9 %collective-permute-start.28 = (bf16[4,48,1664]{2,1,0:T(8,128)(2,1)S(1)}, bf16[4,48,1664]{2,1,0:T(8,128)(2,1)S(1)}, u32[]{:S(2)}, u32[]{:S(2)}) collective-permute-start(bf16[4,48,1664]{2,1,0:T(8,128)(2,1)S(1)} %get-tuple-element.169), channel_id=1, source_target_pairs={{0,8},{8,0},{16,24},{24,16},{1,9},{9,1},{17,25},{25,17},{2,10},{10... | collective-permute-start | bytes 1916936 | tf_op jit(solution)/shard_map/ppermute | solution.py:108
  186.7 16.1 %collective-permute-start.29 = (bf16[4,48,1664]{2,1,0:T(8,128)(2,1)S(1)}, bf16[4,48,1664]{2,1,0:T(8,128)(2,1)S(1)}, u32[]{:S(2)}, u32[]{:S(2)}) collective-permute-start(bf16[4,48,1664]{2,1,0:T(8,128)(2,1)S(1)} %get-tuple-element.170), channel_id=1, source_target_pairs={{0,16},{8,24},{16,0},{24,8},{1,17},{9,25},{17,1},{25,9},{2,18},{10... | collective-permute-start | bytes 1916936 | tf_op jit(solution)/shard_map/ppermute | solution.py:108
  190.6 31.2 %collective-permute-start.36 = (bf16[48,3072]{1,0:T(8,128)(2,1)S(1)}, bf16[48,3072]{1,0:T(8,128)(2,1)S(1)}, u32[]{:S(2)}, u32[]{:S(2)}) collective-permute-start(bf16[48,3072]{1,0:T(8,128)(2,1)S(1)} %get-tuple-element.191), channel_id=1, source_target_pairs={{0,6},{1,7},{2,4},{3,5},{4,2},{5,3},{6,0},{7,1},{8,14},{9,15},{10,... | collective-permute-start | bytes 884744 | tf_op jit(solution)/shard_map/ppermute | solution.py:104
  191.0 39.6 %collective-permute-start.35 = (bf16[48,3072]{1,0:T(8,128)(2,1)S(1)}, bf16[48,3072]{1,0:T(8,128)(2,1)S(1)}, u32[]{:S(2)}, u32[]{:S(2)}) collective-permute-start(bf16[48,3072]{1,0:T(8,128)(2,1)S(1)} %get-tuple-element.192), channel_id=1, source_target_pairs={{0,4},{1,5},{2,6},{3,7},{4,0},{5,1},{6,2},{7,3},{8,12},{9,13},{10,... | collective-permute-start | bytes 884744 | tf_op jit(solution)/shard_map/ppermute | solution.py:104
  195.8 34.9 %collective-permute-start.34 = (bf16[48,3072]{1,0:T(8,128)(2,1)S(1)}, bf16[48,3072]{1,0:T(8,128)(2,1)S(1)}, u32[]{:S(2)}, u32[]{:S(2)}) collective-permute-start(bf16[48,3072]{1,0:T(8,128)(2,1)S(1)} %get-tuple-element.195), channel_id=1, source_target_pairs={{0,2},{1,3},{2,0},{3,1},{4,6},{5,7},{6,4},{7,5},{8,10},{9,11},{10,... | collective-permute-start | bytes 884744 | tf_op jit(solution)/shard_map/ppermute | solution.py:104
  203.5 34.0 %collective-permute-start.32 = (bf16[2,48,1664]{2,1,0:T(8,128)(2,1)}, bf16[2,48,1664]{2,1,0:T(8,128)(2,1)S(1)}, u32[]{:S(2)}, u32[]{:S(2)}) collective-permute-start(bf16[2,48,1664]{2,1,0:T(8,128)(2,1)} %add_convert_fusion.3), channel_id=1, source_target_pairs={{0,16},{8,24},{16,0},{24,8},{1,17},{9,25},{17,1},{25,9},{2,18},{10... | collective-permute-start | bytes 958472 | tf_op jit(solution)/shard_map/ppermute | solution.py:108
  205.2 32.3 %collective-permute-start.33 = (bf16[2,48,1664]{2,1,0:T(8,128)(2,1)}, bf16[2,48,1664]{2,1,0:T(8,128)(2,1)}, u32[]{:S(2)}, u32[]{:S(2)}) collective-permute-start(bf16[2,48,1664]{2,1,0:T(8,128)(2,1)} %add_convert_fusion.2), channel_id=1, source_target_pairs={{0,8},{8,0},{16,24},{24,16},{1,9},{9,1},{17,25},{25,17},{2,10},{10... | collective-permute-start | bytes 958472 | tf_op jit(solution)/shard_map/ppermute | solution.py:108
  230.9 4.2 %collective-permute-start.41 = (f32[24,1536]{1,0:T(8,128)S(1)}, f32[24,1536]{1,0:T(8,128)S(1)}, u32[]{:S(2)}, u32[]{:S(2)}) collective-permute-start(f32[24,1536]{1,0:T(8,128)S(1)} %get-tuple-element.202), channel_id=1, source_target_pairs={{0,1},{1,0},{2,3},{3,2},{4,5},{5,4},{6,7},{7,6},{8,9},{9,8},{10,11... | collective-permute-start | bytes 442376 | tf_op jit(solution)/shard_map/ppermute | solution.py:100
  236.3 6.9 %copy-start.27 = (f32[256,768]{1,0:T(8,128)S(1)}, f32[256,768]{1,0:T(8,128)}, u32[]{:S(2)}) copy-start(f32[256,768]{1,0:T(8,128)} %copy-done.26) | copy-start | bytes 2359300
  237.6 5.7 %copy-start.38 = (bf16[2,128,768]{2,1,0:T(8,128)(2,1)S(1)}, bf16[2,128,768]{2,1,0:T(8,128)(2,1)}, u32[]{:S(2)}) copy-start(bf16[2,128,768]{2,1,0:T(8,128)(2,1)} %reduce-scatter.2.cloned.1.call-done) | copy-start | bytes 1179652
  238.8 13.2 %collective-permute-start.38 = (bf16[48,1664]{1,0:T(8,128)(2,1)S(1)}, bf16[48,1664]{1,0:T(8,128)(2,1)S(1)}, u32[]{:S(2)}, u32[]{:S(2)}) collective-permute-start(bf16[48,1664]{1,0:T(8,128)(2,1)S(1)} %get-tuple-element.193), channel_id=1, source_target_pairs={{0,4},{1,5},{2,6},{3,7},{4,0},{5,1},{6,2},{7,3},{8,12},{9,13},{10,... | collective-permute-start | bytes 479240 | tf_op jit(solution)/shard_map/ppermute | solution.py:104
  242.0 14.9 %collective-permute-start.39 = (bf16[48,1664]{1,0:T(8,128)(2,1)S(1)}, bf16[48,1664]{1,0:T(8,128)(2,1)S(1)}, u32[]{:S(2)}, u32[]{:S(2)}) collective-permute-start(bf16[48,1664]{1,0:T(8,128)(2,1)S(1)} %get-tuple-element.194), channel_id=1, source_target_pairs={{0,6},{1,7},{2,4},{3,5},{4,2},{5,3},{6,0},{7,1},{8,14},{9,15},{10,... | collective-permute-start | bytes 479240 | tf_op jit(solution)/shard_map/ppermute | solution.py:104
  242.7 14.2 %collective-permute-start.37 = (bf16[48,1664]{1,0:T(8,128)(2,1)S(1)}, bf16[48,1664]{1,0:T(8,128)(2,1)S(1)}, u32[]{:S(2)}, u32[]{:S(2)}) collective-permute-start(bf16[48,1664]{1,0:T(8,128)(2,1)S(1)} %get-tuple-element.196), channel_id=1, source_target_pairs={{0,2},{1,3},{2,0},{3,1},{4,6},{5,7},{6,4},{7,5},{8,10},{9,11},{10,... | collective-permute-start | bytes 479240 | tf_op jit(solution)/shard_map/ppermute | solution.py:104
  257.2 2.0 collective-permute-start.40
  (22 other events, 26.7 us)
Sparse Core Ops, SparseCore 0:
  47.1 50.9 all-gather.1
  169.1 66.4 reduce-scatter.1

commit v3 on v2

--- a/solution.py
+++ b/solution.py
@@ -217,43 +217,46 @@
 
 
 def forward_kernel(qid_ref, kid_ref, q_ref, k_ref, v_ref, out_ref, lse_ref):
-    keys = k_ref[0]
-    values = v_ref[0]
     rows = q_ref.shape[1] // 2
-    for side in range(2):
-        span = slice(side * rows, (side + 1) * rows)
-        queries = stacked_heads(q_ref[0, span])
-        scores = masked_scores(queries, keys, qid_ref[0, span][:, :1], kid_ref[0][:1, :])
+
+    @pl.loop(0, 2)
+    def _(side):
+        span = pl.ds(pl.multiple_of(side * rows, rows), rows)
+        queries = stacked_heads(q_ref[0, span, :])
+        scores = masked_scores(queries, k_ref[0], qid_ref[0, span, :][:, :1], kid_ref[0][:1, :])
         highest = jnp.max(scores, axis=-1, keepdims=True)
         weights = jnp.exp(scores - highest)
         total = jnp.sum(weights, axis=-1, keepdims=True)
         probs = (weights * (1.0 / total)).astype(BF)
-        out_ref[0, span] = unstacked_heads(nn(probs, values)).astype(BF)
+        out_ref[0, span, :] = unstacked_heads(nn(probs, v_ref[0])).astype(BF)
         lse_ref[0, 0, side] = jnp.broadcast_to(highest + jnp.log(total), lse_ref.shape[3:])
 
 
 def backward_kernel(
-    qid_ref, kid_ref, q_ref, k_ref, v_ref, lse_ref, up_ref, dq_ref, dk_ref, dv_ref
+    qid_ref, kid_ref, q_ref, k_ref, v_ref, lse_ref, up_ref, dq_ref, dk_ref, dv_ref, key_ref, value_ref
 ):
-    keys = k_ref[0]
-    values = v_ref[0]
     rows = q_ref.shape[1] // 2
-    key_sum, value_sum = 0.0, 0.0
-    for side in range(2):
-        span = slice(side * rows, (side + 1) * rows)
-        queries = stacked_heads(q_ref[0, span])
-        upward = stacked_heads(up_ref[0, span])
-        scores = masked_scores(queries, keys, qid_ref[0, span][:, :1], kid_ref[0][:1, :])
+    key_ref[...] = jnp.zeros_like(key_ref)
+    value_ref[...] = jnp.zeros_like(value_ref)
+
+    @pl.loop(0, 2)
+    def _(side):
+        span = pl.ds(pl.multiple_of(side * rows, rows), rows)
+        keys = k_ref[0]
+        queries = stacked_heads(q_ref[0, span, :])
+        upward = stacked_heads(up_ref[0, span, :])
+        scores = masked_scores(queries, keys, qid_ref[0, span, :][:, :1], kid_ref[0][:1, :])
         probs = jnp.exp(scores - lse_ref[0, 0, side][:, :1])
-        dprobs = nt(upward, values)
+        dprobs = nt(upward, v_ref[0])
         correction = jnp.sum(probs * dprobs, axis=-1, keepdims=True)
         dscores = (probs * (dprobs - correction)).astype(BF)
         back = unstacked_heads(nn(dscores, keys)).astype(BF).astype(F32)
-        dq_ref[0, span] = (back * 0.125).astype(BF)
-        key_sum += tn(dscores, queries)
-        value_sum += tn(probs.astype(BF), upward)
-    dk_ref[0] = key_sum.astype(BF)
-    dv_ref[0] = value_sum.astype(BF)
+        dq_ref[0, span, :] = (back * 0.125).astype(BF)
+        key_ref[...] += tn(dscores, queries)
+        value_ref[...] += tn(probs.astype(BF), upward)
+
+    dk_ref[0] = key_ref[...].astype(BF)
+    dv_ref[0] = value_ref[...].astype(BF)
 
 
 def attention_specs(rows, count):
@@ -307,6 +310,7 @@
         ],
         out_specs=[specs["row"], specs["key"], specs["key"]],
         out_shape=[jax.ShapeDtypeStruct((streams, rows, HALF), BF), key_shape, key_shape],
+        scratch_shapes=[pltpu.VMEM((count, PAIR), F32)] * 2,
         compiler_params=pltpu.CompilerParams(vmem_limit_bytes=VMEM_LIMIT if count <= 1024 else VMEM_LARGE),
         cost_estimate=QUICK,
         name="attend_back",
@@ -346,79 +350,86 @@
     return pl.ds(pl.multiple_of((1 - place_ref[2]) * HALF, 128), HALF)
 
 
-def project_kernel(place_ref, tok_ref, vec_ref, weight_ref, pairs_ref, query_ref, rows_ref):
-    half = half_of_ref(place_ref)
-    pairs = nn(tok_ref[0], weight_ref[:, HALF:])
-    pairs_ref[0, :, :HALF] = pairs[:, :HALF].astype(BF)
-    pairs_ref[0, :, HALF:] = (pairs[:, HALF:] + vec_ref[VALUE_BIAS : VALUE_BIAS + 1, half]).astype(BF)
-    chip_rows = rows_ref.shape[1]
-    tiles = tok_ref.shape[1] // chip_rows
-
-    @pl.when(pl.program_id(1) == place_ref[1] // tiles)
-    def _():
-        first = pl.multiple_of(place_ref[1] % tiles * chip_rows, chip_rows)
-        tokens = tok_ref[0, pl.ds(first, chip_rows), :]
-        queries = nn(tokens, weight_ref[:, :HALF]) + vec_ref[QUERY_BIAS : QUERY_BIAS + 1, half]
-        query_ref[0] = (queries * 0.125).astype(BF)
-        rows_ref[0] = tokens
-
-
-def project(place, tokens, vectors, weight, chip_rows):
-    streams, count, _ = tokens.shape
+def project(place, mine, other, vectors, weight):
+    streams, rows, _ = mine[0].shape
+    zs = len(mine)
+    chip_rows = 2 * rows
+    count = zs * chip_rows
+    tile = min(count, 1024)
+
+    def kernel(place_ref, *refs):
+        mine_refs, other_refs, (vec_ref, weight_ref) = refs[:zs], refs[zs : 2 * zs], refs[2 * zs : 2 * zs + 2]
+        all_ref, pairs_ref, query_ref, rows_ref = refs[2 * zs + 2 :]
+        half = half_of_ref(place_ref)
+        for j in range(zs):
+            here = pl.ds(pl.multiple_of(j * chip_rows + place_ref[2] * rows, rows), rows)
+            there = pl.ds(pl.multiple_of(j * chip_rows + (1 - place_ref[2]) * rows, rows), rows)
+            for s in range(streams):
+                all_ref[s, here, :] = mine_refs[j][s]
+                all_ref[s, there, :] = other_refs[j][s]
+
+        @pl.loop(0, streams)
+        def _(s):
+            for start in range(0, count, tile):
+                span = slice(start, start + tile)
+                pairs = nn(all_ref[s, span, :], weight_ref[:, HALF:])
+                pairs_ref[s, span, :HALF] = pairs[:, :HALF].astype(BF)
+                values = pairs[:, HALF:] + vec_ref[VALUE_BIAS : VALUE_BIAS + 1, half]
+                pairs_ref[s, span, HALF:] = values.astype(BF)
+            tokens = all_ref[s, :chip_rows, :]
+            rows_ref[s] = tokens
+            queries = nn(tokens, weight_ref[:, :HALF]) + vec_ref[QUERY_BIAS : QUERY_BIAS + 1, half]
+            query_ref[s] = (queries * 0.125).astype(BF)
+
     shape = lambda rows, lanes: jax.ShapeDtypeStruct((streams, rows, lanes), BF)
-    tile = 4 * chip_rows
     return pl.pallas_call(
-        project_kernel,
-        grid=(streams, count // tile),
-        in_specs=[
-            pl.BlockSpec(memory_space=pltpu.SMEM),
-            pl.BlockSpec((1, tile, D), lambda s, t: (s, t, 0)),
-            pl.BlockSpec(memory_space=pltpu.VMEM),
-            pl.BlockSpec(memory_space=pltpu.VMEM),
-        ],
-        out_specs=[
-            pl.BlockSpec((1, tile, D), lambda s, t: (s, t, 0)),
-            pl.BlockSpec((1, chip_rows, HALF), lambda s, t: (s, 0, 0)),
-            pl.BlockSpec((1, chip_rows, D), lambda s, t: (s, 0, 0)),
-        ],
-        out_shape=[shape(count, D), shape(chip_rows, HALF), shape(chip_rows, D)],
-        compiler_params=pltpu.CompilerParams(vmem_limit_bytes=VMEM_LIMIT),
+        kernel,
+        in_specs=[pl.BlockSpec(memory_space=pltpu.SMEM)]
+        + [pl.BlockSpec(memory_space=pltpu.VMEM)] * (2 * zs + 2),
+        out_specs=[pl.BlockSpec(memory_space=pltpu.VMEM)] * 4,
+        out_shape=[shape(count, D), shape(count, D), shape(chip_rows, HALF), shape(chip_rows, D)],
+        compiler_params=pltpu.CompilerParams(
+            vmem_limit_bytes=VMEM_LIMIT if count <= 1024 else VMEM_LARGE
+        ),
         cost_estimate=QUICK,
         name="project",
-    )(place, pltpu.with_memory_space_constraint(tokens, pltpu.HBM), vectors, weight)
-
-
-def unproject_kernel(place_ref, query_ref, key_ref, value_ref, weight_ref, out_ref):
-    back = jnp.concatenate([key_ref[0], value_ref[0]], axis=1)
-    out_ref[0] = nt(back, weight_ref[:, HALF:]).astype(BF)
-    chip_rows = query_ref.shape[1]
-    tiles = out_ref.shape[1] // chip_rows
-
-    @pl.when(pl.program_id(1) == place_ref[1] // tiles)
-    def _():
-        span = pl.ds(pl.multiple_of(place_ref[1] % tiles * chip_rows, chip_rows), chip_rows)
-        own = jnp.concatenate([query_ref[0], key_ref[0, span, :], value_ref[0, span, :]], axis=1)
-        out_ref[0, span, :] = nt(own, weight_ref[...]).astype(BF)
+    )(place, *mine, *other, vectors, weight)
 
 
 def unproject(place, query_back, key_back, value_back, weight):
     streams, count, _ = key_back.shape
     chip_rows = query_back.shape[1]
-    tile = 4 * chip_rows
-    block = lambda lanes: pl.BlockSpec((1, tile, lanes), lambda s, t: (s, t, 0))
+    rows = chip_rows // 2
+    zs = count // chip_rows
+    tile = min(count, 1024)
+
+    def kernel(place_ref, query_ref, key_ref, value_ref, weight_ref, mine_ref, other_ref):
+        first_core = place_ref[2] == 0
+
+        @pl.loop(0, streams)
+        def _(s):
+            for start in range(0, count, tile):
+                span = slice(start, start + tile)
+                back = jnp.concatenate([key_ref[s, span, :], value_ref[s, span, :]], axis=1)
+                total = nt(back, weight_ref[:, HALF:])
+                for offset in range(0, tile, chip_rows):
+                    j = (start + offset) // chip_rows
+                    chip = total[offset : offset + chip_rows]
+                    if j == 0:
+                        chip += nt(query_ref[s], weight_ref[:, :HALF])
+                    mine_ref[j, s] = jnp.where(first_core, chip[:rows], chip[rows:]).astype(BF)
+                    other_ref[j, s] = jnp.where(first_core, chip[rows:], chip[:rows]).astype(BF)
+
+    shape = jax.ShapeDtypeStruct((zs, streams, rows, D), BF)
     return pl.pallas_call(
-        unproject_kernel,
-        grid=(streams, count // tile),
-        in_specs=[
-            pl.BlockSpec(memory_space=pltpu.SMEM),
-            pl.BlockSpec((1, chip_rows, HALF), lambda s, t: (s, 0, 0)),
-            block(HALF),
-            block(HALF),
-            pl.BlockSpec(memory_space=pltpu.VMEM),
-        ],
-        out_specs=block(D),
-        out_shape=pltpu.HBM((streams, count, D), BF),
-        compiler_params=pltpu.CompilerParams(vmem_limit_bytes=VMEM_LIMIT),
+        kernel,
+        in_specs=[pl.BlockSpec(memory_space=pltpu.SMEM)]
+        + [pl.BlockSpec(memory_space=pltpu.VMEM)] * 4,
+        out_specs=[pl.BlockSpec(memory_space=pltpu.VMEM)] * 2,
+        out_shape=[shape, shape],
+        compiler_params=pltpu.CompilerParams(
+            vmem_limit_bytes=VMEM_LIMIT if count <= 1024 else VMEM_LARGE
+        ),
         cost_estimate=QUICK,
         name="unproject",
     )(place, query_back, key_back, value_back, weight)
@@ -505,7 +516,7 @@
 def over_rows(body, place, steps, tiled, whole, outs, sums, name):
     def tile_of(ref, step):
         rows = ref.shape[0] // steps
-        return ref.at[step * rows : (step + 1) * rows]
+        return ref.at[pl.ds(pl.multiple_of(step * rows, rows), rows)]
 
     def kernel(place_ref, *refs):
         tiles, refs = refs[: len(tiled)], refs[len(tiled) :]
@@ -513,7 +524,9 @@
         results, totals = refs[: len(outs)], refs[len(outs) :]
         for total in totals:
             total[...] = jnp.zeros_like(total)
-        for step in range(steps):
+
+        @pl.loop(0, steps)
+        def _(step):
             body(
                 place_ref,
                 *[tile_of(ref, step) for ref in tiles],
@@ -711,16 +724,17 @@
         return jnp.concatenate([out_weight, unit], axis=1)
 
     late = in_core_order(columns_for(core)[None], swap(columns_for(1 - core))[None], 0)
-    early = jnp.stack(tied(z_moves(early, seq), late))
+    parts = reduce_weight.astype(BF).reshape(2, 2, block, D)
+    late = jnp.concatenate([late, parts[:, 0], parts[:, 1]], axis=2)
+    other_cotangent = swap(cotangent).reshape(-1, D)
+    cotangent = cotangent.reshape(-1, D)
+    other_tokens = swap(tokens)
+    early = jnp.stack(tied(z_moves(early, seq), late, other_tokens, other_cotangent))
     late = z_moves(tied(late, early), seq)
     early, late = lax.optimization_barrier((gather_dp_first(early, dps), late))
-    all_tokens = row_major(lax.all_gather(tied(tokens, late), "seq", axis=1, tiled=True))
     early = gather_dp_rest(early, gather_dp_halves(early, dps))
-    late = jnp.stack(tied(late, early))
-    last = z_moves(tied(reduce_weight.astype(BF), late), seq)
-    late = gather_dp_first(late, dps)
-    other_cotangent = swap(cotangent).reshape(-1, D)
-    cotangent = cotangent.reshape(-1, D)
+    moved = z_moves(tied(tokens, late), seq)
+    late = gather_dp_first(jnp.stack(tied(late, early)), dps)
 
     def gather_plan(parts, direct=False):
         return [
@@ -754,37 +768,48 @@
     def half_of(vector):
         return lax.dynamic_slice_in_dim(vector, core * HALF, HALF, 1)
 
-    qkv_weight = tied(qkv_weight, expand_bias, other_cotangent)
-    late = tied(late, qkv_weight)
-    halves = gather_dp_halves(late, dps)
+    qkv_weight = tied(qkv_weight, expand_bias)
+    halves = gather_dp_halves(tied(late, qkv_weight), dps)
     late = gather_dp_rest(late, halves)
-    last = gather_dp_direct(jnp.stack(tied(last, halves)), dps)
-
+    qkv_weight = tied(qkv_weight, halves)
+    others = [other_tokens] + [swap(m) for m in tied(moved[1:], halves)]
+
+    all_tokens, key_values, queries, chip_tokens = project(
+        place, moved, others, small, qkv_weight
+    )
     flat_all = all_tokens.reshape(-1, D)
-    ids = item_ids(lengths, jnp.arange(all_tokens.shape[1], dtype=jnp.int32))
+    spot = jnp.arange(row_count, dtype=jnp.int32)
+    steps = jnp.arange(zs, dtype=jnp.int32) ^ z
+    starts = (steps[:, None] * 2 + jnp.arange(2, dtype=jnp.int32)) * row_count
+    ids = item_ids(lengths, (starts[:, :, None] + spot).reshape(-1))
     key_ids = jnp.broadcast_to(ids[:, None, :], (streams, 8, ids.shape[1]))
-    query_ids = lax.dynamic_slice_in_dim(ids, z * chip_rows, chip_rows, 1)
-    query_ids = jnp.broadcast_to(query_ids[..., None], (streams, chip_rows, 128))
-
-    key_values, queries, chip_tokens = project(place, all_tokens, small, qkv_weight, chip_rows)
-    queries = tied(queries, late)
+    query_ids = jnp.broadcast_to(ids[:, :chip_rows, None], (streams, chip_rows, 128))
+
     chip_tokens = chip_tokens.reshape(rows, D)
     attended, lse = attend(query_ids, key_ids, queries, key_values)
     other_attended = swap(attended).reshape(rows, HALF)
     attended = attended.reshape(rows, HALF)
 
-    out_weight, expand_weight = local_copies(
+    out_weight, expand_weight, reduce_weight = local_copies(
         place,
         late,
-        [(dps, zs, 2, block, D), (dps, zs, 2, block, UNITS)],
-        gather_plan([(0, D, 0), (D, UNITS, 1)]),
+        [(dps, zs, 2, block, D), (dps, zs, 2, block, UNITS), (dps, zs, 4, block, D)],
+        gather_plan([(0, D, 0), (D, UNITS, 1)])
+        + [
+            (
+                piece,
+                lambda dp, z, row=row, c=c, h=h: (row, c, slice(None), at_lanes(D + UNITS + h * D, D)),
+                2,
+                lambda dp, z, j=j, k=k, c=c, h=h: (dp ^ k, z ^ j, 2 * c + h),
+            )
+            for piece, row, k, j in dp_pieces(dps, zs, False)
+            for c in range(2)
+            for h in range(2)
+        ],
         "place_late",
     )
     out_weight = out_weight.reshape(D, D)
     expand_weight = expand_weight.reshape(D, UNITS)
-    (reduce_weight,) = local_copies(
-        place, last, [(dps, zs, wide, D)], gather_plan([(0, D, 0)], direct=True), "place_last"
-    )
     reduce_weight = reduce_weight.reshape(UNITS, D)
 
     normed_one, inverse_one, first_low, hidden, slope, partial, sent = over_rows(
@@ -879,12 +904,20 @@
     query_back, key_back, value_back = attend_back(
         query_ids, key_ids, queries, key_values, lse, attended_back
     )
-    tokens_part = unproject(place, query_back, key_back, value_back, qkv_weight)
-    tokens_total = lax.psum_scatter(tokens_part, "seq", scatter_dimension=1, tiled=True)
-    wide_came = tied(wide_came, tokens_part)
+    mine_part, other_part = unproject(place, query_back, key_back, value_back, qkv_weight)
+    came_part = swap(other_part)
+    wide_came = tied(wide_came, other_part)
     wide_onward = scatter_dp_middle(wide_packs, wide_came, dps)
+    mine_part, came_part = tied((mine_part, came_part), wide_onward)
+    tokens_total = wide_sum([mine_part, came_part])
+    tokens_first = tokens_total[zs // 2 :].astype(BF)
+
+    def halved(total, bit, sent):
+        return total[:bit] + z_move(sent, bit, seq).astype(F32)
+
+    tokens_total = halved(tokens_total, zs // 2, tokens_first)
     backs = (query_back.reshape(rows, HALF), key_back.reshape(-1, HALF), value_back.reshape(-1, HALF))
-    backs = tied(backs, wide_onward)
+    backs = tied(backs, tokens_first)
     if fused:
         narrow_packs = narrow_packs_of(
             place,
@@ -898,7 +931,9 @@
             dps,
             zs,
         )
-        wide_totals = scatter_dp_rest(wide_packs, wide_came, wide_onward, dps)
+        wide_totals = scatter_dp_rest(
+            wide_packs, wide_came, wide_onward, dps, lambda came: tied(came, narrow_packs)
+        )
     else:
         out_side = half_of(branch_back)
         zeros = jnp.zeros((D,), F32)
@@ -932,32 +967,36 @@
         )
     came = tied(scatter_dp_first(narrow_packs, dps), wide_totals)
     narrow_onward = scatter_dp_middle(narrow_packs, came, dps)
-    wide_grads = scatter_z(wide_totals, seq, lambda moved: tied(moved, narrow_onward))
-    narrow_totals = scatter_dp_rest(
-        narrow_packs, came, narrow_onward, dps, lambda came: tied(came, wide_grads, tokens_total)
+    narrow_totals = scatter_dp_rest(narrow_packs, came, narrow_onward, dps)
+    wide_grads = scatter_z(tied(wide_totals, tokens_total), seq)
+    bit = zs // 4
+    while bit:
+        tokens_total = halved(tokens_total, bit, tokens_total[bit:].astype(BF))
+        bit //= 2
+    narrow_totals, tokens_total, wide_grads = lax.optimization_barrier(
+        (narrow_totals, tokens_total, wide_grads)
     )
     narrow_grads = scatter_z(narrow_totals, seq)
-    tokens_gradient = residual_one_back.reshape(tokens.shape) + tokens_total.astype(F32)
+    tokens_gradient = residual_one_back.reshape(tokens.shape) + tokens_total[0]
 
     def own_rows(grads):
         split = grads.reshape(2, block, grads.shape[1])
         mine = lax.dynamic_index_in_dim(split, core, 0, keepdims=False)
         return mine, swap(lax.dynamic_index_in_dim(split, 1 - core, 0, keepdims=False))
 
+    mine, other = own_rows(wide_grads[:, 2 * D :])
+    expand_grads = in_core_order(
+        mine.reshape(block, chips, 1, wide), other.reshape(block, chips, 1, wide), 2
+    ).reshape(block, FF)
+    reduce_grads = jnp.concatenate([wide_grads[:, :D], wide_grads[:, D : 2 * D]], axis=0)
     mine, other = own_rows(narrow_grads)
     matrices = [
         in_core_order(mine[:, i * HALF : (i + 1) * HALF], other[:, i * HALF : (i + 1) * HALF], 1)
         for i in range(4)
     ]
-    small = narrow_grads[:, 4 * HALF :]
     own_small = mine[:, 4 * HALF :].T
     both_small = (mine[:, 4 * HALF : 4 * HALF + 2] + other[:, 4 * HALF : 4 * HALF + 2]).T
-    expand_bias_grad = small[:, 8:10].T.reshape(wide)
-    mine, other = own_rows(wide_grads[:, 2 * D :])
-    expand_grads = in_core_order(
-        mine.reshape(block, chips, 1, wide), other.reshape(block, chips, 1, wide), 2
-    ).reshape(block, FF)
-    reduce_grads = jnp.concatenate([wide_grads[:, :D], wide_grads[:, D : 2 * D]], axis=0)
+    expand_bias_grad = narrow_grads[:, 4 * HALF :][:, 8:10].T.reshape(wide)
 
     return (
         activations.reshape(tokens.shape),

time: 269 us -> 260 us (0.967)
  waiting for transfers between devices: 92.2 us -> 122 us
  local copies, waits for them, and re-layouts: 31.6 us -> 10.5 us
  between operations: 14.8 us -> 1.3 us
  other arithmetic: 19.2 us -> 9.09 us
  starting transfers between devices: 45.3 us -> 52 us
    ppermute x19 -> x16, waiting for transfers between devices: 18.8 us -> 41.2 us  [dp_move(): return lax.ppermute(value, 'dp', [(i, i ^ step) for i in range(dps)])]
    unnamed x85 -> x25, local copies, waits for them, and re-layouts: 19.1 us -> 1.34 us
    ppermute x15 -> x17, waiting for transfers between devices: 67.1 us -> 75.1 us  [z_move(): return lax.ppermute(value, 'seq', [(i, i ^ 2 * step) for i in range(seq)])]
    all_gather x1 -> x0, waiting for transfers between devices: 4.4 us -> none  [body(): lax.all_gather(tied(tokens, late), 'seq', axis=1, tiled=True)]
    ppermute x8 -> x13, waiting for transfers between devices: 1.93 us -> 5.91 us  [core_swap(): return lax.ppermute(value, 'seq', [(i, i ^ 1) for i in range(seq)])]
    ppermute x8 -> x13, starting transfers between devices: 8.86 us -> 12.5 us  [core_swap(): return lax.ppermute(value, 'seq', [(i, i ^ 1) for i in range(seq)])]
    ppermute x15 -> x17, starting transfers between devices: 22.2 us -> 24.6 us  [z_move(): return lax.ppermute(value, 'seq', [(i, i ^ 2 * step) for i in range(seq)])]
    ppermute x19 -> x16, starting transfers between devices: 14.1 us -> 14.9 us  [dp_move(): return lax.ppermute(value, 'dp', [(i, i ^ step) for i in range(dps)])]
  transfers between devices with their start and end apart: 44 -> 46, of which waited for: 18 -> 24; matrix products, arithmetic and copies ran while one was open for 11% -> 6% of each run, Pallas kernels for 19% -> 18%
where the time goes in v3:
time: 260 us; the launch traced here: 259 us
  waiting for transfers between devices  122 us (47%)
  Pallas kernels  63.9 us (25%)
  starting transfers between devices  52 us (20%)
  local copies, waits for them, and re-layouts  10.5 us (4%)
  other arithmetic  9.09 us (3%)
    ppermute x17, waiting for transfers between devices, z_move(): return lax.ppermute(value, 'seq', [(i, i ^ 2 * step) for i in range(seq)])  75.1 us
    ppermute x16, waiting for transfers between devices, dp_move(): return lax.ppermute(value, 'dp', [(i, i ^ step) for i in range(dps)])  41.2 us
    ppermute x17, starting transfers between devices, z_move(): return lax.ppermute(value, 'seq', [(i, i ^ 2 * step) for i in range(seq)])  24.6 us
    pallas_call x1, Pallas kernels, attend_back(): pl.pallas_call(backward_kernel, grid=(streams, PAIRS), in_specs=[specs['q...  16 us
    pallas_call x3, Pallas kernels, over_rows(): pl.pallas_call(kernel, in_specs=[pl.BlockSpec(memory_space=pltpu.SMEM)] +...  15 us
    ppermute x16, starting transfers between devices, dp_move(): return lax.ppermute(value, 'dp', [(i, i ^ step) for i in range(dps)])  14.9 us
    ppermute x13, starting transfers between devices, core_swap(): return lax.ppermute(value, 'seq', [(i, i ^ 1) for i in range(seq)])  12.5 us
    pallas_call x1, Pallas kernels, attend(): pl.pallas_call(forward_kernel, grid=(streams, PAIRS), in_specs=[specs['qi...  10.5 us
  transfers between devices with their start and end apart: 46, of which 24 were waited for; matrix products, arithmetic and copies ran while one was open for 6% of the time, Pallas kernels for 18%

profile of v3, /device:TPU:13, one launch (start us, length us, event | category | flops | bytes accessed | tf_op | source)
XLA Modules:
  0.0 259.1 jit_solution(17168334463587483022)
XLA Ops:
  1.3 1.8 first_columns.1
  3.8 0.9 convert_element_type.196
  4.7 1.0 convert_element_type.197
  5.9 1.3 dynamic-slice_reduce_fusion.1
  8.3 1.4 collective-permute-start.3
  9.7 1.1 collective-permute-start.2
  10.8 1.1 collective-permute-start.1
  11.9 6.2 %collective-permute-done.3 = bf16[2,24,1280]{2,1,0:T(8,128)(2,1)S(1)} collective-permute-done((bf16[2,24,1280]{2,1,0:T(8,128)(2,1)S(1)}, bf16[2,24,1280]{2,1,0:T(8,128)(2,1)S(1)}, u32[]{:S(2)}, u32[]{:S(2)}) %collective-permute-start.3) | collective-permute-done | bytes 122912 | tf_op jit(solution)/shard_map/ppermute | solution.py:104
  18.1 1.7 collective-permute-done.2
  20.6 1.2 collective-permute-start.7
  21.8 3.8 %collective-permute-start.10 = (bf16[2,24,3840]{2,1,0:T(8,128)(2,1)S(1)}, bf16[2,24,3840]{2,1,0:T(8,128)(2,1)S(1)}, u32[]{:S(2)}, u32[]{:S(2)}) collective-permute-start(bf16[2,24,3840]{2,1,0:T(8,128)(2,1)S(1)} %pad_maximum_fusion.2), channel_id=1, source_target_pairs={{0,4},{1,5},{2,6},{3,7},{4,0},{5,1},{6,2},{7,3},{8,12},{9,13},{10,... | collective-permute-start | bytes 1105928 | tf_op jit(solution)/shard_map/ppermute | solution.py:104
  25.7 20.1 %collective-permute-done.11 = bf16[2,24,3840]{2,1,0:T(8,128)(2,1)S(1)} collective-permute-done((bf16[2,24,3840]{2,1,0:T(8,128)(2,1)S(1)}, bf16[2,24,3840]{2,1,0:T(8,128)(2,1)S(1)}, u32[]{:S(2)}, u32[]{:S(2)}) %collective-permute-start.11) | collective-permute-done | bytes 368672 | tf_op jit(solution)/shard_map/ppermute | solution.py:104
  45.8 5.6 %collective-permute-done.10 = bf16[2,24,3840]{2,1,0:T(8,128)(2,1)S(1)} collective-permute-done((bf16[2,24,3840]{2,1,0:T(8,128)(2,1)S(1)}, bf16[2,24,3840]{2,1,0:T(8,128)(2,1)S(1)}, u32[]{:S(2)}, u32[]{:S(2)}) %collective-permute-start.10) | collective-permute-done | bytes 368672 | tf_op jit(solution)/shard_map/ppermute | solution.py:104
  51.8 1.2 collective-permute-start.16
  53.0 3.6 %collective-permute-done.15.refs_3_ = bf16[2,2,24,1280]{3,2,1,0:T(8,128)(2,1)S(1)} collective-permute-done((bf16[2,2,24,1280]{3,2,1,0:T(8,128)(2,1)S(1)}, bf16[2,2,24,1280]{3,2,1,0:T(8,128)(2,1)S(1)}, u32[]{:S(2)}, u32[]{:S(2)}) %collective-permute-start.15) | collective-permute-done | bytes 245792 | tf_op jit(solution)/shard_map/ppermute | solution.py:108
  57.1 1.3 collective-permute-start.18
  58.4 1.5 collective-permute-start.17
  60.0 1.6 collective-permute-start.14
  61.5 4.0 %collective-permute-start.13 = (bf16[2,128,768]{2,1,0:T(8,128)(2,1)}, bf16[2,128,768]{2,1,0:T(8,128)(2,1)}, u32[]{:S(2)}, u32[]{:S(2)}) collective-permute-start(bf16[2,128,768]{2,1,0:T(8,128)(2,1)} %refs_0_.2), channel_id=1, source_target_pairs={{0,4},{1,5},{2,6},{3,7},{4,0},{5,1},{6,2},{7,3},{8,12},{9,13},{10,... | collective-permute-start | bytes 1179656 | tf_op jit(solution)/shard_map/ppermute | solution.py:104
  66.8 20.9 %collective-permute-done.18.refs_2_ = bf16[4,2,24,3840]{3,2,1,0:T(8,128)(2,1)} collective-permute-done((bf16[4,2,24,3840]{3,2,1,0:T(8,128)(2,1)S(1)}, bf16[4,2,24,3840]{3,2,1,0:T(8,128)(2,1)}, u32[]{:S(2)}, u32[]{:S(2)}) %collective-permute-start.18) | collective-permute-done | bytes 1474592 | tf_op jit(solution)/shard_map/ppermute | solution.py:108
  87.7 1.2 slice.204
  88.9 1.2 slice.205
  90.0 1.3 collective-permute-start.24
  91.4 1.5 collective-permute-start.23
  93.4 4.9 %collective-permute-start.19 = (bf16[2,128,768]{2,1,0:T(8,128)(2,1)}, bf16[2,128,768]{2,1,0:T(8,128)(2,1)S(1)}, u32[]{:S(2)}, u32[]{:S(2)}) collective-permute-start(bf16[2,128,768]{2,1,0:T(8,128)(2,1)} %collective-permute-done.12.refs_1_), channel_id=1, source_target_pairs={{0,1},{1,0},{2,3},{3,2},{4,5},{5,4},{6,7},{7,6},{8,9},{9,8},{10,11... | collective-permute-start | bytes 1179656 | tf_op jit(solution)/shard_map/ppermute | solution.py:100
  101.0 5.0 %project.1 = (bf16[2,1024,768]{2,1,0:T(8,128)(2,1)S(1)}, bf16[2,1024,768]{2,1,0:T(8,128)(2,1)S(1)}, bf16[2,256,384]{2,1,0:T(8,128)(2,1)S(1)}, bf16[2,256,768]{2,1,0:T(8,128)(2,1)S(1)}) custom-call(s32[3]{0:T(128)S(1)} %copy-done.8, bf16[2,128,768]{2,1,0:T(8,128)(2,1)} %refs_0_.2, bf16[2,128,768]{2,1,0:T(8,128)(2,1)} %collective-permute-done.12.refs_1_, ...), custom_call_target="tpu_custom_call" | custom-call | tf_op jit(solution)/shard_map/project/pallas_call | solution.py:385
  106.2 10.5 %attend.1 = (bf16[2,256,384]{2,1,0:T(8,128)(2,1)S(1)}, f32[2,3,2,256,128]{4,3,2,1,0:T(8,128)S(1)}) custom-call(s32[2,256,128]{2,1,0:T(8,128)S(1)} %broadcast_in_dim.51.qid_ref, s32[2,8,1024]{2,1,0:T(8,128)S(1)} %broadcast_in_dim.52.kid_ref, bf16[2,256,384]{2,1,0:T(8,128)(2,1)S(1)} %get-tuple-element.137.q_ref, ...), custom_call_target="tpu_custom_call" | custom-call | tf_op jit(solution)/shard_map/attend/pallas_call | solution.py:278
  116.7 1.2 copy-done
  118.2 2.2 place_late.1
  120.5 6.4 %middle.1 = (f32[512,768]{1,0:T(8,128)S(1)}, f32[512,128]{1,0:T(8,128)S(1)}, bf16[512,768]{1,0:T(8,128)(2,1)S(1)}, bf16[512,1536]{1,0:T(8,128)(2,1)S(1)}, bf16[5...) custom-call(s32[3]{0:T(128)S(1)} %copy-done.8, bf16[512,384]{1,0:T(8,128)(2,1)S(1)} %bitcast.96, ...), custom_call_target="tpu_custom_call" | custom-call | tf_op jit(solution)/shard_map/middle/pallas_call | solution.py:538
  127.1 2.1 collective-permute-done.25.refs_1_
  129.3 6.3 %turn.1 = (bf16[256,768]{1,0:T(8,128)(2,1)}, f32[512,768]{1,0:T(8,128)S(1)}, bf16[512,768]{1,0:T(8,128)(2,1)S(1)}, bf16[512,1536]{1,0:T(8,128)(2,1)S(1)}, f32[51...) custom-call(s32[3]{0:T(128)S(1)} %copy-done.8, ...), custom_call_target="tpu_custom_call" | custom-call | tf_op jit(solution)/shard_map/turn/pallas_call | solution.py:538
  135.6 3.5 %wide_packs.1 = (bf16[4,48,3072]{2,1,0:T(8,128)(2,1)S(1)}, bf16[4,48,3072]{2,1,0:T(8,128)(2,1)S(1)}, bf16[4,48,3072]{2,1,0:T(8,128)(2,1)S(1)}, bf16[2,48,3072]{2,1,0:T(8,128)(2,1)S(1)}, bf16[2,48,3072]{2,1,0:T(8,128)(2,1)S(1)}) custom-call(s32[3]{0:T(128)S(1)} %copy-done.8, bf16[512,1536]{1,0:T(8,128)(2,1)S(1)} %get-tuple-element.162.hidden_ref, ...), custom_call_target="tpu_custom_call" | custom-call | tf_op jit(solution)/shard_map/wide_packs/pallas_call | solution.py:552
  140.8 1.9 collective-permute-done.26.refs_1_
  142.7 2.3 first_back.1
  145.0 16.0 %attend_back.1 = (bf16[2,256,384]{2,1,0:T(8,128)(2,1)S(1)}, bf16[2,1024,384]{2,1,0:T(8,128)(2,1)S(1)}, bf16[2,1024,384]{2,1,0:T(8,128)(2,1)S(1)}) custom-call(s32[2,256,128]{2,1,0:T(8,128)S(1)} %broadcast_in_dim.51.qid_ref, s32[2,8,1024]{2,1,0:T(8,128)S(1)} %broadcast_in_dim.52.kid_ref, bf16[2,256,384]{2,1,0:T(8,128)(2,1)S(1)} %get-tuple-element.137.q_ref, ...), custom_call_target="tpu_custom_call" | custom-call | tf_op jit(solution)/shard_map/attend_back/pallas_call | solution.py:299
  161.0 3.9 %unproject.1 = (bf16[4,2,128,768]{3,2,1,0:T(8,128)(2,1)S(1)}, bf16[4,2,128,768]{3,2,1,0:T(8,128)(2,1)S(1)}) custom-call(s32[3]{0:T(128)S(1)} %copy-done.8, bf16[2,256,384]{2,1,0:T(8,128)(2,1)S(1)} %get-tuple-element.157.query_ref, bf16[2,1024,384]{2,1,0:T(8,128)(2,1)S(1)} %get-tuple-element.158.key_ref, ...), custom_call_target="tpu_custom_call" | custom-call | tf_op jit(solution)/shard_map/unproject/pallas_call | solution.py:424
  165.3 1.3 collective-permute-done.28
  166.8 0.9 collective-permute-start.32
  167.8 1.2 collective-permute-start.33
  169.5 3.2 %collective-permute-start.36 = (bf16[2,2,128,768]{3,2,1,0:T(8,128)(2,1)S(1)}, bf16[2,2,128,768]{3,2,1,0:T(8,128)(2,1)S(1)}, u32[]{:S(2)}, u32[]{:S(2)}) collective-permute-start(bf16[2,2,128,768]{3,2,1,0:T(8,128)(2,1)S(1)} %slice.342), channel_id=1, source_target_pairs={{0,4},{1,5},{2,6},{3,7},{4,0},{5,1},{6,2},{7,3},{8,12},{9,13},{10,... | collective-permute-start | bytes 2359304 | tf_op jit(solution)/shard_map/ppermute | solution.py:104
  172.6 5.3 %narrow_packs.1 = (bf16[4,48,1664]{2,1,0:T(8,128)(2,1)S(1)}, bf16[4,48,1664]{2,1,0:T(8,128)(2,1)S(1)}, bf16[4,48,1664]{2,1,0:T(8,128)(2,1)S(1)}, bf16[2,48,1664]...) custom-call(s32[3]{0:T(128)S(1)} %copy-done.8, bf16[2048,768]{1,0:T(8,128)(2,1)S(1)} %bitcast.93, bf16[512,768]{1,0:T(8,128)(2,1)S(1)} %bitcast.95, ...), custom_call_target="tpu_custom_call" | custom-call | tf_op jit(solution)/shard_map/narrow_packs/pallas_call | solution.py:552
  177.9 0.8 collective-permute-start.30
  179.4 1.0 collective-permute-done.32
  180.4 1.0 collective-permute-done.33
  182.0 13.1 %collective-permute-done.30 = bf16[4,48,1664]{2,1,0:T(8,128)(2,1)S(1)} collective-permute-done((bf16[4,48,1664]{2,1,0:T(8,128)(2,1)S(1)}, bf16[4,48,1664]{2,1,0:T(8,128)(2,1)S(1)}, u32[]{:S(2)}, u32[]{:S(2)}) %collective-permute-start.30) | collective-permute-done | bytes 639008 | tf_op jit(solution)/shard_map/ppermute | solution.py:108
  195.8 1.1 collective-permute-start.35
  196.9 9.7 %collective-permute-done.36 = bf16[2,2,128,768]{3,2,1,0:T(8,128)(2,1)S(1)} collective-permute-done((bf16[2,2,128,768]{3,2,1,0:T(8,128)(2,1)S(1)}, bf16[2,2,128,768]{3,2,1,0:T(8,128)(2,1)S(1)}, u32[]{:S(2)}, u32[]{:S(2)}) %collective-permute-start.36) | collective-permute-done | bytes 786464 | tf_op jit(solution)/shard_map/ppermute | solution.py:104
  206.9 2.1 collective-permute-start.38
  209.0 1.1 collective-permute-start.39
  210.3 2.2 collective-permute-start.37
  212.8 7.8 %collective-permute-done.38 = bf16[48,3072]{1,0:T(8,128)(2,1)S(1)} collective-permute-done((bf16[48,3072]{1,0:T(8,128)(2,1)S(1)}, bf16[48,3072]{1,0:T(8,128)(2,1)S(1)}, u32[]{:S(2)}, u32[]{:S(2)}) %collective-permute-start.38) | collective-permute-done | bytes 294944 | tf_op jit(solution)/shard_map/ppermute | solution.py:104
  220.6 2.7 %collective-permute-done.39 = bf16[48,3072]{1,0:T(8,128)(2,1)S(1)} collective-permute-done((bf16[48,3072]{1,0:T(8,128)(2,1)S(1)}, bf16[48,3072]{1,0:T(8,128)(2,1)S(1)}, u32[]{:S(2)}, u32[]{:S(2)}) %collective-permute-start.39) | collective-permute-done | bytes 294944 | tf_op jit(solution)/shard_map/ppermute | solution.py:104
  223.2 12.7 %collective-permute-done.40 = bf16[48,3072]{1,0:T(8,128)(2,1)S(1)} collective-permute-done((bf16[48,3072]{1,0:T(8,128)(2,1)S(1)}, bf16[48,3072]{1,0:T(8,128)(2,1)S(1)}, u32[]{:S(2)}, u32[]{:S(2)}) %collective-permute-start.40) | collective-permute-done | bytes 294944 | tf_op jit(solution)/shard_map/ppermute | solution.py:104
  236.0 1.0 collective-permute-done.37
  237.2 1.1 collective-permute-start.41
  238.3 1.3 collective-permute-start.42
  239.9 1.9 collective-permute-start.45
  241.9 1.0 bitcast_add_fusion
  244.5 0.8 maximum_select_fusion
  245.3 1.2 select_n.94
  246.5 6.7 %collective-permute-done.43 = bf16[48,1664]{1,0:T(8,128)(2,1)S(1)} collective-permute-done((bf16[48,1664]{1,0:T(8,128)(2,1)S(1)}, bf16[48,1664]{1,0:T(8,128)(2,1)S(1)}, u32[]{:S(2)}, u32[]{:S(2)}) %collective-permute-start.43) | collective-permute-done | bytes 159776 | tf_op jit(solution)/shard_map/ppermute | solution.py:104
  253.4 2.1 collective-permute-start.44
  256.2 0.8 slice_reduce_fusion
  (135 shorter events, 19.9 us)
Async XLA Ops:
  0.7 7.5 %copy-start.2 = (bf16[2,128,768]{2,1,0:T(8,128)(2,1)S(1)}, bf16[2,128,768]{2,1,0:T(8,128)(2,1)}, u32[]{:S(2)}) copy-start(bf16[2,128,768]{2,1,0:T(8,128)(2,1)} %param.35) | copy-start | bytes 1179652
  0.7 7.5 %copy-start.9 = (f32[96,768]{1,0:T(8,128)S(1)}, f32[96,768]{1,0:T(8,128)}, u32[]{:S(2)}) copy-start(f32[96,768]{1,0:T(8,128)} %param.30) | copy-start | bytes 884740
  3.1 5.2 %copy-start.10 = (bf16[24,1280]{1,0:T(8,128)(2,1)S(1)}, bf16[24,1280]{1,0:T(8,128)(2,1)}, u32[]{:S(2)}) copy-start(bf16[24,1280]{1,0:T(8,128)(2,1)} %get-tuple-element.109) | copy-start | bytes 184324
  3.1 5.1 %collective-permute-start = (bf16[24,1280]{1,0:T(8,128)(2,1)}, bf16[24,1280]{1,0:T(8,128)(2,1)S(1)}, u32[]{:S(2)}, u32[]{:S(2)}) collective-permute-start(bf16[24,1280]{1,0:T(8,128)(2,1)} %get-tuple-element.110), channel_id=1, source_target_pairs={{0,1},{1,0},{2,3},{3,2},{4,5},{5,4},{6,7},{7,6},{8,9},{9,8},{10,11... | collective-permute-start | bytes 184328 | tf_op jit(solution)/shard_map/ppermute | solution.py:100
  7.6 3.2 %collective-permute-start.4 = (bf16[24,2304]{1,0:T(8,128)(2,1)S(1)}, bf16[24,2304]{1,0:T(8,128)(2,1)S(1)}, u32[]{:S(2)}, u32[]{:S(2)}) collective-permute-start(bf16[24,2304]{1,0:T(8,128)(2,1)S(1)} %get-tuple-element.234), channel_id=1, source_target_pairs={{0,1},{1,0},{2,3},{3,2},{4,5},{5,4},{6,7},{7,6},{8,9},{9,8},{10,11... | collective-permute-start | bytes 331784 | tf_op jit(solution)/shard_map/ppermute | solution.py:100
  7.6 12.5 %collective-permute-start.5 = (bf16[2,128,768]{2,1,0:T(8,128)(2,1)}, bf16[2,128,768]{2,1,0:T(8,128)(2,1)S(1)}, u32[]{:S(2)}, u32[]{:S(2)}) collective-permute-start(bf16[2,128,768]{2,1,0:T(8,128)(2,1)} %refs_0_.2), channel_id=1, source_target_pairs={{0,1},{1,0},{2,3},{3,2},{4,5},{5,4},{6,7},{7,6},{8,9},{9,8},{10,11... | collective-permute-start | bytes 1179656 | tf_op jit(solution)/shard_map/ppermute | solution.py:100
  8.1 12.1 %collective-permute-start.6 = (bf16[2,128,768]{2,1,0:T(8,128)(2,1)S(1)}, bf16[2,128,768]{2,1,0:T(8,128)(2,1)S(1)}, u32[]{:S(2)}, u32[]{:S(2)}) collective-permute-start(bf16[2,128,768]{2,1,0:T(8,128)(2,1)S(1)} %copy-done.2), channel_id=1, source_target_pairs={{0,1},{1,0},{2,3},{3,2},{4,5},{5,4},{6,7},{7,6},{8,9},{9,8},{10,11... | collective-permute-start | bytes 1179656 | tf_op jit(solution)/shard_map/ppermute | solution.py:100
  8.3 9.8 %collective-permute-start.3 = (bf16[2,24,1280]{2,1,0:T(8,128)(2,1)S(1)}, bf16[2,24,1280]{2,1,0:T(8,128)(2,1)S(1)}, u32[]{:S(2)}, u32[]{:S(2)}) collective-permute-start(bf16[2,24,1280]{2,1,0:T(8,128)(2,1)S(1)} %maximum_select_fusion.2), channel_id=1, source_target_pairs={{0,6},{1,7},{2,4},{3,5},{4,2},{5,3},{6,0},{7,1},{8,14},{9,15},{10,... | collective-permute-start | bytes 368648 | tf_op jit(solution)/shard_map/ppermute | solution.py:104
  9.7 10.2 %collective-permute-start.2 = (bf16[2,24,1280]{2,1,0:T(8,128)(2,1)S(1)}, bf16[2,24,1280]{2,1,0:T(8,128)(2,1)S(1)}, u32[]{:S(2)}, u32[]{:S(2)}) collective-permute-start(bf16[2,24,1280]{2,1,0:T(8,128)(2,1)S(1)} %maximum_select_fusion.2), channel_id=1, source_target_pairs={{0,4},{1,5},{2,6},{3,7},{4,0},{5,1},{6,2},{7,3},{8,12},{9,13},{10,... | collective-permute-start | bytes 368648 | tf_op jit(solution)/shard_map/ppermute | solution.py:104
  10.8 9.4 %collective-permute-start.1 = (bf16[2,24,1280]{2,1,0:T(8,128)(2,1)S(1)}, bf16[2,24,1280]{2,1,0:T(8,128)(2,1)S(1)}, u32[]{:S(2)}, u32[]{:S(2)}) collective-permute-start(bf16[2,24,1280]{2,1,0:T(8,128)(2,1)S(1)} %maximum_select_fusion.2), channel_id=1, source_target_pairs={{0,2},{1,3},{2,0},{3,1},{4,6},{5,7},{6,4},{7,5},{8,10},{9,11},{10,... | collective-permute-start | bytes 368648 | tf_op jit(solution)/shard_map/ppermute | solution.py:104
  20.2 36.9 %copy-start.6 = (bf16[2,128,768]{2,1,0:T(8,128)(2,1)}, bf16[2,128,768]{2,1,0:T(8,128)(2,1)S(1)}, u32[]{:S(2)}) copy-start(bf16[2,128,768]{2,1,0:T(8,128)(2,1)S(1)} %collective-permute-done.5.refs_4_) | copy-start | bytes 1179652
  20.2 36.9 %copy-start.4 = (bf16[2,128,768]{2,1,0:T(8,128)(2,1)}, bf16[2,128,768]{2,1,0:T(8,128)(2,1)S(1)}, u32[]{:S(2)}) copy-start(bf16[2,128,768]{2,1,0:T(8,128)(2,1)S(1)} %collective-permute-done.6) | copy-start | bytes 1179652
  20.3 31.1 %collective-permute-start.8 = (bf16[4,2,24,1280]{3,2,1,0:T(8,128)(2,1)S(1)}, bf16[4,2,24,1280]{3,2,1,0:T(8,128)(2,1)S(1)}, u32[]{:S(2)}, u32[]{:S(2)}) collective-permute-start(bf16[4,2,24,1280]{3,2,1,0:T(8,128)(2,1)S(1)} %pad_maximum_fusion.1.refs_0_), channel_id=1, source_target_pairs={{0,16},{8,24},{16,0},{24,8},{1,17},{9,25},{17,1},{25,9},{2,18},{10... | collective-permute-start | bytes 1474568 | tf_op jit(solution)/shard_map/ppermute | solution.py:108
  20.6 30.9 %collective-permute-start.7 = (bf16[4,2,24,1280]{3,2,1,0:T(8,128)(2,1)S(1)}, bf16[4,2,24,1280]{3,2,1,0:T(8,128)(2,1)S(1)}, u32[]{:S(2)}, u32[]{:S(2)}) collective-permute-start(bf16[4,2,24,1280]{3,2,1,0:T(8,128)(2,1)S(1)} %pad_maximum_fusion.1.refs_0_), channel_id=1, source_target_pairs={{0,8},{8,0},{16,24},{24,16},{1,9},{9,1},{17,25},{25,17},{2,10},{10... | collective-permute-start | bytes 1474568 | tf_op jit(solution)/shard_map/ppermute | solution.py:108
  21.8 24.0 %collective-permute-start.11 = (bf16[2,24,3840]{2,1,0:T(8,128)(2,1)S(1)}, bf16[2,24,3840]{2,1,0:T(8,128)(2,1)S(1)}, u32[]{:S(2)}, u32[]{:S(2)}) collective-permute-start(bf16[2,24,3840]{2,1,0:T(8,128)(2,1)S(1)} %pad_maximum_fusion.2), channel_id=1, source_target_pairs={{0,6},{1,7},{2,4},{3,5},{4,2},{5,3},{6,0},{7,1},{8,14},{9,15},{10,... | collective-permute-start | bytes 1105928 | tf_op jit(solution)/shard_map/ppermute | solution.py:104
  21.8 29.6 %collective-permute-start.10 = (bf16[2,24,3840]{2,1,0:T(8,128)(2,1)S(1)}, bf16[2,24,3840]{2,1,0:T(8,128)(2,1)S(1)}, u32[]{:S(2)}, u32[]{:S(2)}) collective-permute-start(bf16[2,24,3840]{2,1,0:T(8,128)(2,1)S(1)} %pad_maximum_fusion.2), channel_id=1, source_target_pairs={{0,4},{1,5},{2,6},{3,7},{4,0},{5,1},{6,2},{7,3},{8,12},{9,13},{10,... | collective-permute-start | bytes 1105928 | tf_op jit(solution)/shard_map/ppermute | solution.py:104
  25.6 25.8 %collective-permute-start.9 = (bf16[2,24,3840]{2,1,0:T(8,128)(2,1)S(1)}, bf16[2,24,3840]{2,1,0:T(8,128)(2,1)S(1)}, u32[]{:S(2)}, u32[]{:S(2)}) collective-permute-start(bf16[2,24,3840]{2,1,0:T(8,128)(2,1)S(1)} %pad_maximum_fusion.2), channel_id=1, source_target_pairs={{0,2},{1,3},{2,0},{3,1},{4,6},{5,7},{6,4},{7,5},{8,10},{9,11},{10,... | collective-permute-start | bytes 1105928 | tf_op jit(solution)/shard_map/ppermute | solution.py:104
  51.5 14.1 %copy-start.8 = (s32[3]{0:T(128)S(1)}, s32[3]{0:T(128)}, u32[]{:S(2)}) copy-start(s32[3]{0:T(128)} %pad_add_fusion.place_ref) | copy-start | bytes 40
  51.5 5.1 %collective-permute-start.15 = (bf16[2,2,24,1280]{3,2,1,0:T(8,128)(2,1)S(1)}, bf16[2,2,24,1280]{3,2,1,0:T(8,128)(2,1)S(1)}, u32[]{:S(2)}, u32[]{:S(2)}) collective-permute-start(bf16[2,2,24,1280]{3,2,1,0:T(8,128)(2,1)S(1)} %slice.200), channel_id=1, source_target_pairs={{0,8},{8,0},{16,24},{24,16},{1,9},{9,1},{17,25},{25,17},{2,10},{10... | collective-permute-start | bytes 737288 | tf_op jit(solution)/shard_map/ppermute | solution.py:108
  51.8 5.0 %collective-permute-start.16 = (bf16[2,2,24,1280]{3,2,1,0:T(8,128)(2,1)S(1)}, bf16[2,2,24,1280]{3,2,1,0:T(8,128)(2,1)S(1)}, u32[]{:S(2)}, u32[]{:S(2)}) collective-permute-start(bf16[2,2,24,1280]{3,2,1,0:T(8,128)(2,1)S(1)} %slice.201), channel_id=1, source_target_pairs={{0,16},{8,24},{16,0},{24,8},{1,17},{9,25},{17,1},{25,9},{2,18},{10... | collective-permute-start | bytes 737288 | tf_op jit(solution)/shard_map/ppermute | solution.py:108
  57.1 30.6 %collective-permute-start.18 = (bf16[4,2,24,3840]{3,2,1,0:T(8,128)(2,1)S(1)}, bf16[4,2,24,3840]{3,2,1,0:T(8,128)(2,1)}, u32[]{:S(2)}, u32[]{:S(2)}) collective-permute-start(bf16[4,2,24,3840]{3,2,1,0:T(8,128)(2,1)S(1)} %pad_maximum_fusion.refs_0_), channel_id=1, source_target_pairs={{0,16},{8,24},{16,0},{24,8},{1,17},{9,25},{17,1},{25,9},{2,18},{10... | collective-permute-start | bytes 4423688 | tf_op jit(solution)/shard_map/ppermute | solution.py:108
  58.4 29.3 %collective-permute-start.17 = (bf16[4,2,24,3840]{3,2,1,0:T(8,128)(2,1)S(1)}, bf16[4,2,24,3840]{3,2,1,0:T(8,128)(2,1)}, u32[]{:S(2)}, u32[]{:S(2)}) collective-permute-start(bf16[4,2,24,3840]{3,2,1,0:T(8,128)(2,1)S(1)} %pad_maximum_fusion.refs_0_), channel_id=1, source_target_pairs={{0,8},{8,0},{16,24},{24,16},{1,9},{9,1},{17,25},{25,17},{2,10},{10... | collective-permute-start | bytes 4423688 | tf_op jit(solution)/shard_map/ppermute | solution.py:108
  60.0 32.9 %collective-permute-start.14 = (bf16[2,128,768]{2,1,0:T(8,128)(2,1)}, bf16[2,128,768]{2,1,0:T(8,128)(2,1)}, u32[]{:S(2)}, u32[]{:S(2)}) collective-permute-start(bf16[2,128,768]{2,1,0:T(8,128)(2,1)} %refs_0_.2), channel_id=1, source_target_pairs={{0,6},{1,7},{2,4},{3,5},{4,2},{5,3},{6,0},{7,1},{8,14},{9,15},{10,... | collective-permute-start | bytes 1179656 | tf_op jit(solution)/shard_map/ppermute | solution.py:104
  61.5 31.9 %collective-permute-start.13 = (bf16[2,128,768]{2,1,0:T(8,128)(2,1)}, bf16[2,128,768]{2,1,0:T(8,128)(2,1)}, u32[]{:S(2)}, u32[]{:S(2)}) collective-permute-start(bf16[2,128,768]{2,1,0:T(8,128)(2,1)} %refs_0_.2), channel_id=1, source_target_pairs={{0,4},{1,5},{2,6},{3,7},{4,0},{5,1},{6,2},{7,3},{8,12},{9,13},{10,... | collective-permute-start | bytes 1179656 | tf_op jit(solution)/shard_map/ppermute | solution.py:104
  65.5 27.9 %collective-permute-start.12 = (bf16[2,128,768]{2,1,0:T(8,128)(2,1)}, bf16[2,128,768]{2,1,0:T(8,128)(2,1)}, u32[]{:S(2)}, u32[]{:S(2)}) collective-permute-start(bf16[2,128,768]{2,1,0:T(8,128)(2,1)} %refs_0_.2), channel_id=1, source_target_pairs={{0,2},{1,3},{2,0},{3,1},{4,6},{5,7},{6,4},{7,5},{8,10},{9,11},{10,... | collective-permute-start | bytes 1179656 | tf_op jit(solution)/shard_map/ppermute | solution.py:104
  66.6 32.3 %copy-start.11 = (s32[2,64]{1,0:T(2,128)S(1)}, s32[2,64]{1,0:T(2,128)}, u32[]{:S(2)}) copy-start(s32[2,64]{1,0:T(2,128)} %param.34) | copy-start | bytes 1540
  66.8 34.3 %copy-start.7 = (bf16[2,128,768]{2,1,0:T(8,128)(2,1)S(1)}, bf16[2,128,768]{2,1,0:T(8,128)(2,1)}, u32[]{:S(2)}) copy-start(bf16[2,128,768]{2,1,0:T(8,128)(2,1)} %copy-done.6) | copy-start | bytes 1179652
  90.0 28.2 %collective-permute-start.24 = (bf16[2,2,24,3840]{3,2,1,0:T(8,128)(2,1)S(1)}, bf16[2,2,24,3840]{3,2,1,0:T(8,128)(2,1)S(1)}, u32[]{:S(2)}, u32[]{:S(2)}) collective-permute-start(bf16[2,2,24,3840]{3,2,1,0:T(8,128)(2,1)S(1)} %slice.205), channel_id=1, source_target_pairs={{0,16},{8,24},{16,0},{24,8},{1,17},{9,25},{17,1},{25,9},{2,18},{10... | collective-permute-start | bytes 2211848 | tf_op jit(solution)/shard_map/ppermute | solution.py:108
  91.4 26.9 %collective-permute-start.23 = (bf16[2,2,24,3840]{3,2,1,0:T(8,128)(2,1)S(1)}, bf16[2,2,24,3840]{3,2,1,0:T(8,128)(2,1)S(1)}, u32[]{:S(2)}, u32[]{:S(2)}) collective-permute-start(bf16[2,2,24,3840]{3,2,1,0:T(8,128)(2,1)S(1)} %slice.204), channel_id=1, source_target_pairs={{0,8},{8,0},{16,24},{24,16},{1,9},{9,1},{17,25},{25,17},{2,10},{10... | collective-permute-start | bytes 2211848 | tf_op jit(solution)/shard_map/ppermute | solution.py:108
  93.4 6.5 %collective-permute-start.19 = (bf16[2,128,768]{2,1,0:T(8,128)(2,1)}, bf16[2,128,768]{2,1,0:T(8,128)(2,1)S(1)}, u32[]{:S(2)}, u32[]{:S(2)}) collective-permute-start(bf16[2,128,768]{2,1,0:T(8,128)(2,1)} %collective-permute-done.12.refs_1_), channel_id=1, source_target_pairs={{0,1},{1,0},{2,3},{3,2},{4,5},{5,4},{6,7},{7,6},{8,9},{9,8},{10,11... | collective-permute-start | bytes 1179656 | tf_op jit(solution)/shard_map/ppermute | solution.py:100
  98.4 2.1 collective-permute-start.20
  98.4 2.6 %collective-permute-start.21 = (bf16[2,128,768]{2,1,0:T(8,128)(2,1)}, bf16[2,128,768]{2,1,0:T(8,128)(2,1)S(1)}, u32[]{:S(2)}, u32[]{:S(2)}) collective-permute-start(bf16[2,128,768]{2,1,0:T(8,128)(2,1)} %collective-permute-done.14.refs_3_), channel_id=1, source_target_pairs={{0,1},{1,0},{2,3},{3,2},{4,5},{5,4},{6,7},{7,6},{8,9},{9,8},{10,11... | collective-permute-start | bytes 1179656 | tf_op jit(solution)/shard_map/ppermute | solution.py:100
  116.7 1.2 copy-start
  117.9 2.6 %collective-permute-start.22 = (bf16[2,256,384]{2,1,0:T(8,128)(2,1)S(1)}, bf16[2,256,384]{2,1,0:T(8,128)(2,1)S(1)}, u32[]{:S(2)}, u32[]{:S(2)}) collective-permute-start(bf16[2,256,384]{2,1,0:T(8,128)(2,1)S(1)} %get-tuple-element.139), channel_id=1, source_target_pairs={{0,1},{1,0},{2,3},{3,2},{4,5},{5,4},{6,7},{7,6},{8,9},{9,8},{10,11... | collective-permute-start | bytes 1179656 | tf_op jit(solution)/shard_map/ppermute | solution.py:100
  120.5 8.8 %copy-start.3 = (bf16[2,128,768]{2,1,0:T(8,128)(2,1)S(1)}, bf16[2,128,768]{2,1,0:T(8,128)(2,1)}, u32[]{:S(2)}) copy-start(bf16[2,128,768]{2,1,0:T(8,128)(2,1)} %param.35) | copy-start | bytes 1179652
  120.5 8.8 %copy-start.5 = (bf16[2,128,768]{2,1,0:T(8,128)(2,1)S(1)}, bf16[2,128,768]{2,1,0:T(8,128)(2,1)}, u32[]{:S(2)}) copy-start(bf16[2,128,768]{2,1,0:T(8,128)(2,1)} %copy-done.4) | copy-start | bytes 1179652
  126.9 2.4 collective-permute-start.25
  139.1 27.5 %collective-permute-start.28 = (bf16[4,48,3072]{2,1,0:T(8,128)(2,1)S(1)}, bf16[4,48,3072]{2,1,0:T(8,128)(2,1)S(1)}, u32[]{:S(2)}, u32[]{:S(2)}) collective-permute-start(bf16[4,48,3072]{2,1,0:T(8,128)(2,1)S(1)} %get-tuple-element.167), channel_id=1, source_target_pairs={{0,8},{8,0},{16,24},{24,16},{1,9},{9,1},{17,25},{25,17},{2,10},{10... | collective-permute-start | bytes 3538952 | tf_op jit(solution)/shard_map/ppermute | solution.py:108
  139.5 27.2 %collective-permute-start.29 = (bf16[4,48,3072]{2,1,0:T(8,128)(2,1)S(1)}, bf16[4,48,3072]{2,1,0:T(8,128)(2,1)S(1)}, u32[]{:S(2)}, u32[]{:S(2)}) collective-permute-start(bf16[4,48,3072]{2,1,0:T(8,128)(2,1)S(1)} %get-tuple-element.168), channel_id=1, source_target_pairs={{0,16},{8,24},{16,0},{24,8},{1,17},{9,25},{17,1},{25,9},{2,18},{10... | collective-permute-start | bytes 3538952 | tf_op jit(solution)/shard_map/ppermute | solution.py:108
  140.1 2.5 collective-permute-start.26
  142.7 2.3 copy-start.1
  164.8 4.2 %collective-permute-start.27 = (bf16[4,2,128,768]{3,2,1,0:T(8,128)(2,1)S(1)}, bf16[4,2,128,768]{3,2,1,0:T(8,128)(2,1)S(1)}, u32[]{:S(2)}, u32[]{:S(2)}) collective-permute-start(bf16[4,2,128,768]{3,2,1,0:T(8,128)(2,1)S(1)} %get-tuple-element.161), channel_id=1, source_target_pairs={{0,1},{1,0},{2,3},{3,2},{4,5},{5,4},{6,7},{7,6},{8,9},{9,8},{10,11... | collective-permute-start | bytes 4718600 | tf_op jit(solution)/shard_map/ppermute | solution.py:100
  166.8 13.7 %collective-permute-start.32 = (bf16[2,48,3072]{2,1,0:T(8,128)(2,1)S(1)}, bf16[2,48,3072]{2,1,0:T(8,128)(2,1)S(1)}, u32[]{:S(2)}, u32[]{:S(2)}) collective-permute-start(bf16[2,48,3072]{2,1,0:T(8,128)(2,1)S(1)} %add_convert_fusion.1), channel_id=1, source_target_pairs={{0,16},{8,24},{16,0},{24,8},{1,17},{9,25},{17,1},{25,9},{2,18},{10... | collective-permute-start | bytes 1769480 | tf_op jit(solution)/shard_map/ppermute | solution.py:108
  167.8 13.6 %collective-permute-start.33 = (bf16[2,48,3072]{2,1,0:T(8,128)(2,1)S(1)}, bf16[2,48,3072]{2,1,0:T(8,128)(2,1)S(1)}, u32[]{:S(2)}, u32[]{:S(2)}) collective-permute-start(bf16[2,48,3072]{2,1,0:T(8,128)(2,1)S(1)} %add_convert_fusion), channel_id=1, source_target_pairs={{0,8},{8,0},{16,24},{24,16},{1,9},{9,1},{17,25},{25,17},{2,10},{10... | collective-permute-start | bytes 1769480 | tf_op jit(solution)/shard_map/ppermute | solution.py:108
  169.5 37.2 %collective-permute-start.36 = (bf16[2,2,128,768]{3,2,1,0:T(8,128)(2,1)S(1)}, bf16[2,2,128,768]{3,2,1,0:T(8,128)(2,1)S(1)}, u32[]{:S(2)}, u32[]{:S(2)}) collective-permute-start(bf16[2,2,128,768]{3,2,1,0:T(8,128)(2,1)S(1)} %slice.342), channel_id=1, source_target_pairs={{0,4},{1,5},{2,6},{3,7},{4,0},{5,1},{6,2},{7,3},{8,12},{9,13},{10,... | collective-permute-start | bytes 2359304 | tf_op jit(solution)/shard_map/ppermute | solution.py:104
  177.9 17.2 %collective-permute-start.30 = (bf16[4,48,1664]{2,1,0:T(8,128)(2,1)S(1)}, bf16[4,48,1664]{2,1,0:T(8,128)(2,1)S(1)}, u32[]{:S(2)}, u32[]{:S(2)}) collective-permute-start(bf16[4,48,1664]{2,1,0:T(8,128)(2,1)S(1)} %get-tuple-element.182), channel_id=1, source_target_pairs={{0,8},{8,0},{16,24},{24,16},{1,9},{9,1},{17,25},{25,17},{2,10},{10... | collective-permute-start | bytes 1916936 | tf_op jit(solution)/shard_map/ppermute | solution.py:108
  178.7 16.4 %collective-permute-start.31 = (bf16[4,48,1664]{2,1,0:T(8,128)(2,1)S(1)}, bf16[4,48,1664]{2,1,0:T(8,128)(2,1)S(1)}, u32[]{:S(2)}, u32[]{:S(2)}) collective-permute-start(bf16[4,48,1664]{2,1,0:T(8,128)(2,1)S(1)} %get-tuple-element.183), channel_id=1, source_target_pairs={{0,16},{8,24},{16,0},{24,8},{1,17},{9,25},{17,1},{25,9},{2,18},{10... | collective-permute-start | bytes 1916936 | tf_op jit(solution)/shard_map/ppermute | solution.py:108
  195.2 15.1 %collective-permute-start.34 = (bf16[2,48,1664]{2,1,0:T(8,128)(2,1)S(1)}, bf16[2,48,1664]{2,1,0:T(8,128)(2,1)S(1)}, u32[]{:S(2)}, u32[]{:S(2)}) collective-permute-start(bf16[2,48,1664]{2,1,0:T(8,128)(2,1)S(1)} %add_convert_fusion.3), channel_id=1, source_target_pairs={{0,16},{8,24},{16,0},{24,8},{1,17},{9,25},{17,1},{25,9},{2,18},{10... | collective-permute-start | bytes 958472 | tf_op jit(solution)/shard_map/ppermute | solution.py:108
  195.8 16.8 %collective-permute-start.35 = (bf16[2,48,1664]{2,1,0:T(8,128)(2,1)S(1)}, bf16[2,48,1664]{2,1,0:T(8,128)(2,1)S(1)}, u32[]{:S(2)}, u32[]{:S(2)}) collective-permute-start(bf16[2,48,1664]{2,1,0:T(8,128)(2,1)S(1)} %add_convert_fusion.2), channel_id=1, source_target_pairs={{0,8},{8,0},{16,24},{24,16},{1,9},{9,1},{17,25},{25,17},{2,10},{10... | collective-permute-start | bytes 958472 | tf_op jit(solution)/shard_map/ppermute | solution.py:108
  206.9 13.7 %collective-permute-start.38 = (bf16[48,3072]{1,0:T(8,128)(2,1)S(1)}, bf16[48,3072]{1,0:T(8,128)(2,1)S(1)}, u32[]{:S(2)}, u32[]{:S(2)}) collective-permute-start(bf16[48,3072]{1,0:T(8,128)(2,1)S(1)} %get-tuple-element.192), channel_id=1, source_target_pairs={{0,2},{1,3},{2,0},{3,1},{4,6},{5,7},{6,4},{7,5},{8,10},{9,11},{10,... | collective-permute-start | bytes 884744 | tf_op jit(solution)/shard_map/ppermute | solution.py:104
  209.0 14.2 %collective-permute-start.39 = (bf16[48,3072]{1,0:T(8,128)(2,1)S(1)}, bf16[48,3072]{1,0:T(8,128)(2,1)S(1)}, u32[]{:S(2)}, u32[]{:S(2)}) collective-permute-start(bf16[48,3072]{1,0:T(8,128)(2,1)S(1)} %get-tuple-element.193), channel_id=1, source_target_pairs={{0,4},{1,5},{2,6},{3,7},{4,0},{5,1},{6,2},{7,3},{8,12},{9,13},{10,... | collective-permute-start | bytes 884744 | tf_op jit(solution)/shard_map/ppermute | solution.py:104
  210.1 25.8 %collective-permute-start.40 = (bf16[48,3072]{1,0:T(8,128)(2,1)S(1)}, bf16[48,3072]{1,0:T(8,128)(2,1)S(1)}, u32[]{:S(2)}, u32[]{:S(2)}) collective-permute-start(bf16[48,3072]{1,0:T(8,128)(2,1)S(1)} %get-tuple-element.194), channel_id=1, source_target_pairs={{0,6},{1,7},{2,4},{3,5},{4,2},{5,3},{6,0},{7,1},{8,14},{9,15},{10,... | collective-permute-start | bytes 884744 | tf_op jit(solution)/shard_map/ppermute | solution.py:104
  210.3 26.8 %collective-permute-start.37 = (bf16[1,2,128,768]{3,2,1,0:T(8,128)(2,1)S(1)}, bf16[1,2,128,768]{3,2,1,0:T(8,128)(2,1)S(1)}, u32[]{:S(2)}, u32[]{:S(2)}) collective-permute-start(bf16[1,2,128,768]{3,2,1,0:T(8,128)(2,1)S(1)} %slice.343), channel_id=1, source_target_pairs={{0,2},{1,3},{2,0},{3,1},{4,6},{5,7},{6,4},{7,5},{8,10},{9,11},{10,... | collective-permute-start | bytes 1179656 | tf_op jit(solution)/shard_map/ppermute | solution.py:104
  237.2 9.4 %collective-permute-start.41 = (bf16[48,1664]{1,0:T(8,128)(2,1)S(1)}, bf16[48,1664]{1,0:T(8,128)(2,1)S(1)}, u32[]{:S(2)}, u32[]{:S(2)}) collective-permute-start(bf16[48,1664]{1,0:T(8,128)(2,1)S(1)} %get-tuple-element.197), channel_id=1, source_target_pairs={{0,2},{1,3},{2,0},{3,1},{4,6},{5,7},{6,4},{7,5},{8,10},{9,11},{10,... | collective-permute-start | bytes 479240 | tf_op jit(solution)/shard_map/ppermute | solution.py:104
  238.3 8.2 %collective-permute-start.42 = (bf16[48,1664]{1,0:T(8,128)(2,1)S(1)}, bf16[48,1664]{1,0:T(8,128)(2,1)S(1)}, u32[]{:S(2)}, u32[]{:S(2)}) collective-permute-start(bf16[48,1664]{1,0:T(8,128)(2,1)S(1)} %get-tuple-element.198), channel_id=1, source_target_pairs={{0,4},{1,5},{2,6},{3,7},{4,0},{5,1},{6,2},{7,3},{8,12},{9,13},{10,... | collective-permute-start | bytes 479240 | tf_op jit(solution)/shard_map/ppermute | solution.py:104
  239.6 13.6 %collective-permute-start.43 = (bf16[48,1664]{1,0:T(8,128)(2,1)S(1)}, bf16[48,1664]{1,0:T(8,128)(2,1)S(1)}, u32[]{:S(2)}, u32[]{:S(2)}) collective-permute-start(bf16[48,1664]{1,0:T(8,128)(2,1)S(1)} %get-tuple-element.199), channel_id=1, source_target_pairs={{0,6},{1,7},{2,4},{3,5},{4,2},{5,3},{6,0},{7,1},{8,14},{9,15},{10,... | collective-permute-start | bytes 479240 | tf_op jit(solution)/shard_map/ppermute | solution.py:104
  239.9 4.1 %collective-permute-start.45 = (f32[24,1536]{1,0:T(8,128)S(1)}, f32[24,1536]{1,0:T(8,128)S(1)}, u32[]{:S(2)}, u32[]{:S(2)}) collective-permute-start(f32[24,1536]{1,0:T(8,128)S(1)} %get-tuple-element.222), channel_id=1, source_target_pairs={{0,1},{1,0},{2,3},{3,2},{4,5},{5,4},{6,7},{7,6},{8,9},{9,8},{10,11... | collective-permute-start | bytes 442376 | tf_op jit(solution)/shard_map/ppermute | solution.py:100
  253.4 3.6 %collective-permute-start.44 = (f32[24,1664]{1,0:T(8,128)S(1)}, f32[24,1664]{1,0:T(8,128)S(1)}, u32[]{:S(2)}, u32[]{:S(2)}) collective-permute-start(f32[24,1664]{1,0:T(8,128)S(1)} %get-tuple-element.220), channel_id=1, source_target_pairs={{0,1},{1,0},{2,3},{3,2},{4,5},{5,4},{6,7},{7,6},{8,9},{9,8},{10,11... | collective-permute-start | bytes 479240 | tf_op jit(solution)/shard_map/ppermute | solution.py:100

commit v4 on v3

--- a/solution.py
+++ b/solution.py
@@ -233,15 +233,12 @@
 
 
 def backward_kernel(
-    qid_ref, kid_ref, q_ref, k_ref, v_ref, lse_ref, up_ref, dq_ref, dk_ref, dv_ref, key_ref, value_ref
+    qid_ref, kid_ref, q_ref, k_ref, v_ref, lse_ref, up_ref, dq_ref, dk_ref, dv_ref
 ):
     rows = q_ref.shape[1] // 2
-    key_ref[...] = jnp.zeros_like(key_ref)
-    value_ref[...] = jnp.zeros_like(value_ref)
-
-    @pl.loop(0, 2)
-    def _(side):
-        span = pl.ds(pl.multiple_of(side * rows, rows), rows)
+    key_sum, value_sum = 0.0, 0.0
+    for side in range(2):
+        span = slice(side * rows, (side + 1) * rows)
         keys = k_ref[0]
         queries = stacked_heads(q_ref[0, span, :])
         upward = stacked_heads(up_ref[0, span, :])
@@ -252,11 +249,10 @@
         dscores = (probs * (dprobs - correction)).astype(BF)
         back = unstacked_heads(nn(dscores, keys)).astype(BF).astype(F32)
         dq_ref[0, span, :] = (back * 0.125).astype(BF)
-        key_ref[...] += tn(dscores, queries)
-        value_ref[...] += tn(probs.astype(BF), upward)
-
-    dk_ref[0] = key_ref[...].astype(BF)
-    dv_ref[0] = value_ref[...].astype(BF)
+        key_sum += tn(dscores, queries)
+        value_sum += tn(probs.astype(BF), upward)
+    dk_ref[0] = key_sum.astype(BF)
+    dv_ref[0] = value_sum.astype(BF)
 
 
 def attention_specs(rows, count):
@@ -310,7 +306,6 @@
         ],
         out_specs=[specs["row"], specs["key"], specs["key"]],
         out_shape=[jax.ShapeDtypeStruct((streams, rows, HALF), BF), key_shape, key_shape],
-        scratch_shapes=[pltpu.VMEM((count, PAIR), F32)] * 2,
         compiler_params=pltpu.CompilerParams(vmem_limit_bytes=VMEM_LIMIT if count <= 1024 else VMEM_LARGE),
         cost_estimate=QUICK,
         name="attend_back",
@@ -771,8 +766,7 @@
     qkv_weight = tied(qkv_weight, expand_bias)
     halves = gather_dp_halves(tied(late, qkv_weight), dps)
     late = gather_dp_rest(late, halves)
-    qkv_weight = tied(qkv_weight, halves)
-    others = [other_tokens] + [swap(m) for m in tied(moved[1:], halves)]
+    others = [other_tokens] + [swap(m) for m in moved[1:]]
 
     all_tokens, key_values, queries, chip_tokens = project(
         place, moved, others, small, qkv_weight
@@ -786,6 +780,7 @@
     query_ids = jnp.broadcast_to(ids[:, :chip_rows, None], (streams, chip_rows, 128))
 
     chip_tokens = chip_tokens.reshape(rows, D)
+    queries = tied(queries, halves)
     attended, lse = attend(query_ids, key_ids, queries, key_values)
     other_attended = swap(attended).reshape(rows, HALF)
     attended = attended.reshape(rows, HALF)

time: 260 us -> 259 us (level)
  starting transfers between devices: 52 us -> 60.2 us
  waiting for transfers between devices: 122 us -> 116 us
    ppermute x16, waiting for transfers between devices: 41.2 us -> 22.1 us  [dp_move(): return lax.ppermute(value, 'dp', [(i, i ^ step) for i in range(dps)])]
    ppermute x17, waiting for transfers between devices: 75.1 us -> 89.7 us  [z_move(): return lax.ppermute(value, 'seq', [(i, i ^ 2 * step) for i in range(seq)])]
    ppermute x13, starting transfers between devices: 12.5 us -> 21.7 us  [core_swap(): return lax.ppermute(value, 'seq', [(i, i ^ 1) for i in range(seq)])]
  transfers between devices with their start and end apart: 46 -> 46, of which waited for: 24 -> 22; matrix products, arithmetic and copies ran while one was open for 6% -> 6% of each run, Pallas kernels for 18% -> 17%
where the time goes in v4:
time: 259 us
  waiting for transfers between devices  116 us (45%)
  Pallas kernels  62 us (24%)
  starting transfers between devices  60.2 us (23%)
  local copies, waits for them, and re-layouts  10.5 us (4%)
  other arithmetic  9.09 us (4%)
    ppermute x17, waiting for transfers between devices, z_move(): return lax.ppermute(value, 'seq', [(i, i ^ 2 * step) for i in range(seq)])  89.7 us
    ppermute x17, starting transfers between devices, z_move(): return lax.ppermute(value, 'seq', [(i, i ^ 2 * step) for i in range(seq)])  26 us
    ppermute x16, waiting for transfers between devices, dp_move(): return lax.ppermute(value, 'dp', [(i, i ^ step) for i in range(dps)])  22.1 us
    ppermute x13, starting transfers between devices, core_swap(): return lax.ppermute(value, 'seq', [(i, i ^ 1) for i in range(seq)])  21.7 us
    pallas_call x3, Pallas kernels, over_rows(): pl.pallas_call(kernel, in_specs=[pl.BlockSpec(memory_space=pltpu.SMEM)] +...  15 us
    pallas_call x1, Pallas kernels, attend_back(): pl.pallas_call(backward_kernel, grid=(streams, PAIRS), in_specs=[specs['q...  14.1 us
    ppermute x16, starting transfers between devices, dp_move(): return lax.ppermute(value, 'dp', [(i, i ^ step) for i in range(dps)])  12.5 us
    pallas_call x1, Pallas kernels, attend(): pl.pallas_call(forward_kernel, grid=(streams, PAIRS), in_specs=[specs['qi...  10.5 us
  transfers between devices with their start and end apart: 46, of which 22 were waited for; matrix products, arithmetic and copies ran while one was open for 6% of the time, Pallas kernels for 17%

profile of v4, /device:TPU:13, one launch (start us, length us, event | category | flops | bytes accessed | tf_op | source)
XLA Modules:
  0.0 258.9 jit_solution(18270344878280580704)
XLA Ops:
  1.3 1.8 first_columns.1
  3.8 0.9 convert_element_type.196
  4.7 1.0 convert_element_type.197
  5.9 1.3 dynamic-slice_reduce_fusion.1
  8.3 1.4 collective-permute-start.3
  9.7 1.1 collective-permute-start.2
  10.8 1.1 collective-permute-start.1
  11.9 6.2 %collective-permute-done.3 = bf16[2,24,1280]{2,1,0:T(8,128)(2,1)S(1)} collective-permute-done((bf16[2,24,1280]{2,1,0:T(8,128)(2,1)S(1)}, bf16[2,24,1280]{2,1,0:T(8,128)(2,1)S(1)}, u32[]{:S(2)}, u32[]{:S(2)}) %collective-permute-start.3) | collective-permute-done | bytes 122912 | tf_op jit(solution)/shard_map/ppermute | solution.py:104
  18.1 1.7 collective-permute-done.2
  20.6 1.2 collective-permute-start.7
  21.8 3.8 %collective-permute-start.10 = (bf16[2,24,3840]{2,1,0:T(8,128)(2,1)S(1)}, bf16[2,24,3840]{2,1,0:T(8,128)(2,1)S(1)}, u32[]{:S(2)}, u32[]{:S(2)}) collective-permute-start(bf16[2,24,3840]{2,1,0:T(8,128)(2,1)S(1)} %pad_maximum_fusion.2), channel_id=1, source_target_pairs={{0,4},{1,5},{2,6},{3,7},{4,0},{5,1},{6,2},{7,3},{8,12},{9,13},{10,... | collective-permute-start | bytes 1105928 | tf_op jit(solution)/shard_map/ppermute | solution.py:104
  25.7 20.1 %collective-permute-done.11 = bf16[2,24,3840]{2,1,0:T(8,128)(2,1)S(1)} collective-permute-done((bf16[2,24,3840]{2,1,0:T(8,128)(2,1)S(1)}, bf16[2,24,3840]{2,1,0:T(8,128)(2,1)S(1)}, u32[]{:S(2)}, u32[]{:S(2)}) %collective-permute-start.11) | collective-permute-done | bytes 368672 | tf_op jit(solution)/shard_map/ppermute | solution.py:104
  45.8 5.6 %collective-permute-done.10 = bf16[2,24,3840]{2,1,0:T(8,128)(2,1)S(1)} collective-permute-done((bf16[2,24,3840]{2,1,0:T(8,128)(2,1)S(1)}, bf16[2,24,3840]{2,1,0:T(8,128)(2,1)S(1)}, u32[]{:S(2)}, u32[]{:S(2)}) %collective-permute-start.10) | collective-permute-done | bytes 368672 | tf_op jit(solution)/shard_map/ppermute | solution.py:104
  51.8 1.2 collective-permute-start.19
  53.0 3.6 %collective-permute-done.18.refs_3_ = bf16[2,2,24,1280]{3,2,1,0:T(8,128)(2,1)S(1)} collective-permute-done((bf16[2,2,24,1280]{3,2,1,0:T(8,128)(2,1)S(1)}, bf16[2,2,24,1280]{3,2,1,0:T(8,128)(2,1)S(1)}, u32[]{:S(2)}, u32[]{:S(2)}) %collective-permute-start.18) | collective-permute-done | bytes 245792 | tf_op jit(solution)/shard_map/ppermute | solution.py:108
  57.1 1.3 collective-permute-start.21
  58.4 1.5 collective-permute-start.20
  60.0 1.6 collective-permute-start.14
  61.5 4.0 %collective-permute-start.13 = (bf16[2,128,768]{2,1,0:T(8,128)(2,1)}, bf16[2,128,768]{2,1,0:T(8,128)(2,1)}, u32[]{:S(2)}, u32[]{:S(2)}) collective-permute-start(bf16[2,128,768]{2,1,0:T(8,128)(2,1)} %refs_0_.2), channel_id=1, source_target_pairs={{0,4},{1,5},{2,6},{3,7},{4,0},{5,1},{6,2},{7,3},{8,12},{9,13},{10,... | collective-permute-start | bytes 1179656 | tf_op jit(solution)/shard_map/ppermute | solution.py:104
  66.8 15.5 %collective-permute-done.14.refs_3_ = bf16[2,128,768]{2,1,0:T(8,128)(2,1)} collective-permute-done((bf16[2,128,768]{2,1,0:T(8,128)(2,1)}, bf16[2,128,768]{2,1,0:T(8,128)(2,1)}, u32[]{:S(2)}, u32[]{:S(2)}) %collective-permute-start.14) | collective-permute-done | bytes 393248 | tf_op jit(solution)/shard_map/ppermute | solution.py:104
  82.2 10.7 %collective-permute-start.17 = (bf16[2,128,768]{2,1,0:T(8,128)(2,1)}, bf16[2,128,768]{2,1,0:T(8,128)(2,1)S(1)}, u32[]{:S(2)}, u32[]{:S(2)}) collective-permute-start(bf16[2,128,768]{2,1,0:T(8,128)(2,1)} %collective-permute-done.14.refs_3_), channel_id=1, source_target_pairs={{0,1},{1,0},{2,3},{3,2},{4,5},{5,4},{6,7},{7,6},{8,9},{9,8},{10,11... | collective-permute-start | bytes 1179656 | tf_op jit(solution)/shard_map/ppermute | solution.py:100
  93.4 3.0 %collective-permute-start.16 = (bf16[2,128,768]{2,1,0:T(8,128)(2,1)}, bf16[2,128,768]{2,1,0:T(8,128)(2,1)S(1)}, u32[]{:S(2)}, u32[]{:S(2)}) collective-permute-start(bf16[2,128,768]{2,1,0:T(8,128)(2,1)} %collective-permute-done.13.refs_2_), channel_id=1, source_target_pairs={{0,1},{1,0},{2,3},{3,2},{4,5},{5,4},{6,7},{7,6},{8,9},{9,8},{10,11... | collective-permute-start | bytes 1179656 | tf_op jit(solution)/shard_map/ppermute | solution.py:100
  96.5 1.2 slice.204
  97.7 1.2 slice.205
  99.5 5.0 %project.1 = (bf16[2,1024,768]{2,1,0:T(8,128)(2,1)S(1)}, bf16[2,1024,768]{2,1,0:T(8,128)(2,1)S(1)}, bf16[2,256,384]{2,1,0:T(8,128)(2,1)S(1)}, bf16[2,256,768]{2,1,0:T(8,128)(2,1)S(1)}) custom-call(s32[3]{0:T(128)S(1)} %copy-done.8, bf16[2,128,768]{2,1,0:T(8,128)(2,1)} %refs_0_.2, bf16[2,128,768]{2,1,0:T(8,128)(2,1)} %collective-permute-done.12.refs_1_, ...), custom_call_target="tpu_custom_call" | custom-call | tf_op jit(solution)/shard_map/project/pallas_call | solution.py:380
  104.6 10.5 %attend.1 = (bf16[2,256,384]{2,1,0:T(8,128)(2,1)S(1)}, f32[2,3,2,256,128]{4,3,2,1,0:T(8,128)S(1)}) custom-call(s32[2,256,128]{2,1,0:T(8,128)S(1)} %broadcast_in_dim.51.qid_ref, s32[2,8,1024]{2,1,0:T(8,128)S(1)} %broadcast_in_dim.52.kid_ref, bf16[2,256,384]{2,1,0:T(8,128)(2,1)S(1)} %get-tuple-element.131.q_ref, ...), custom_call_target="tpu_custom_call" | custom-call | tf_op jit(solution)/shard_map/attend/pallas_call | solution.py:274
  115.1 1.2 copy-done
  116.3 1.1 collective-permute-start.22
  117.4 2.2 place_late.1
  119.6 6.4 %middle.1 = (f32[512,768]{1,0:T(8,128)S(1)}, f32[512,128]{1,0:T(8,128)S(1)}, bf16[512,768]{1,0:T(8,128)(2,1)S(1)}, bf16[512,1536]{1,0:T(8,128)(2,1)S(1)}, bf16[5...) custom-call(s32[3]{0:T(128)S(1)} %copy-done.8, bf16[512,384]{1,0:T(8,128)(2,1)S(1)} %bitcast.96, ...), custom_call_target="tpu_custom_call" | custom-call | tf_op jit(solution)/shard_map/middle/pallas_call | solution.py:533
  126.8 1.9 collective-permute-done.25.refs_1_
  128.7 6.3 %turn.1 = (bf16[256,768]{1,0:T(8,128)(2,1)}, f32[512,768]{1,0:T(8,128)S(1)}, bf16[512,768]{1,0:T(8,128)(2,1)S(1)}, bf16[512,1536]{1,0:T(8,128)(2,1)S(1)}, f32[51...) custom-call(s32[3]{0:T(128)S(1)} %copy-done.8, ...), custom_call_target="tpu_custom_call" | custom-call | tf_op jit(solution)/shard_map/turn/pallas_call | solution.py:533
  135.0 3.5 %wide_packs.1 = (bf16[4,48,3072]{2,1,0:T(8,128)(2,1)S(1)}, bf16[4,48,3072]{2,1,0:T(8,128)(2,1)S(1)}, bf16[4,48,3072]{2,1,0:T(8,128)(2,1)S(1)}, bf16[2,48,3072]{2,1,0:T(8,128)(2,1)S(1)}, bf16[2,48,3072]{2,1,0:T(8,128)(2,1)S(1)}) custom-call(s32[3]{0:T(128)S(1)} %copy-done.8, bf16[512,1536]{1,0:T(8,128)(2,1)S(1)} %get-tuple-element.156.hidden_ref, ...), custom_call_target="tpu_custom_call" | custom-call | tf_op jit(solution)/shard_map/wide_packs/pallas_call | solution.py:547
  138.5 1.3 collective-permute-start.28
  139.8 1.2 collective-permute-start.29
  141.8 1.9 collective-permute-done.26.refs_1_
  143.7 2.3 first_back.1
  146.0 14.1 %attend_back.1 = (bf16[2,256,384]{2,1,0:T(8,128)(2,1)S(1)}, bf16[2,1024,384]{2,1,0:T(8,128)(2,1)S(1)}, bf16[2,1024,384]{2,1,0:T(8,128)(2,1)S(1)}) custom-call(s32[2,256,128]{2,1,0:T(8,128)S(1)} %broadcast_in_dim.51.qid_ref, s32[2,8,1024]{2,1,0:T(8,128)S(1)} %broadcast_in_dim.52.kid_ref, bf16[2,256,384]{2,1,0:T(8,128)(2,1)S(1)} %get-tuple-element.131.q_ref, ...), custom_call_target="tpu_custom_call" | custom-call | tf_op jit(solution)/shard_map/attend_back/pallas_call | solution.py:295
  160.1 3.9 %unproject.1 = (bf16[4,2,128,768]{3,2,1,0:T(8,128)(2,1)S(1)}, bf16[4,2,128,768]{3,2,1,0:T(8,128)(2,1)S(1)}) custom-call(s32[3]{0:T(128)S(1)} %copy-done.8, bf16[2,256,384]{2,1,0:T(8,128)(2,1)S(1)} %get-tuple-element.151.query_ref, bf16[2,1024,384]{2,1,0:T(8,128)(2,1)S(1)} %get-tuple-element.152.key_ref, ...), custom_call_target="tpu_custom_call" | custom-call | tf_op jit(solution)/shard_map/unproject/pallas_call | solution.py:419
  164.4 1.4 collective-permute-done.28
  165.8 1.1 collective-permute-done.29
  167.1 1.3 collective-permute-start.32
  169.3 3.2 %collective-permute-start.36 = (bf16[2,2,128,768]{3,2,1,0:T(8,128)(2,1)S(1)}, bf16[2,2,128,768]{3,2,1,0:T(8,128)(2,1)S(1)}, u32[]{:S(2)}, u32[]{:S(2)}) collective-permute-start(bf16[2,2,128,768]{3,2,1,0:T(8,128)(2,1)S(1)} %slice.342), channel_id=1, source_target_pairs={{0,4},{1,5},{2,6},{3,7},{4,0},{5,1},{6,2},{7,3},{8,12},{9,13},{10,... | collective-permute-start | bytes 2359304 | tf_op jit(solution)/shard_map/ppermute | solution.py:104
  172.5 5.3 %narrow_packs.1 = (bf16[4,48,1664]{2,1,0:T(8,128)(2,1)S(1)}, bf16[4,48,1664]{2,1,0:T(8,128)(2,1)S(1)}, bf16[4,48,1664]{2,1,0:T(8,128)(2,1)S(1)}, bf16[2,48,1664]...) custom-call(s32[3]{0:T(128)S(1)} %copy-done.8, bf16[2048,768]{1,0:T(8,128)(2,1)S(1)} %bitcast.93, bf16[512,768]{1,0:T(8,128)(2,1)S(1)} %bitcast.95, ...), custom_call_target="tpu_custom_call" | custom-call | tf_op jit(solution)/shard_map/narrow_packs/pallas_call | solution.py:547
  177.8 1.2 collective-permute-start.30
  179.2 1.4 collective-permute-done.32
  180.7 1.2 collective-permute-done.33
  182.4 13.1 %collective-permute-done.30 = bf16[4,48,1664]{2,1,0:T(8,128)(2,1)S(1)} collective-permute-done((bf16[4,48,1664]{2,1,0:T(8,128)(2,1)S(1)}, bf16[4,48,1664]{2,1,0:T(8,128)(2,1)S(1)}, u32[]{:S(2)}, u32[]{:S(2)}) %collective-permute-start.30) | collective-permute-done | bytes 639008 | tf_op jit(solution)/shard_map/ppermute | solution.py:108
  196.5 8.7 %collective-permute-done.36 = bf16[2,2,128,768]{3,2,1,0:T(8,128)(2,1)S(1)} collective-permute-done((bf16[2,2,128,768]{3,2,1,0:T(8,128)(2,1)S(1)}, bf16[2,2,128,768]{3,2,1,0:T(8,128)(2,1)S(1)}, u32[]{:S(2)}, u32[]{:S(2)}) %collective-permute-start.36) | collective-permute-done | bytes 786464 | tf_op jit(solution)/shard_map/ppermute | solution.py:104
  205.4 3.4 %collective-permute-start.38 = (bf16[48,3072]{1,0:T(8,128)(2,1)S(1)}, bf16[48,3072]{1,0:T(8,128)(2,1)S(1)}, u32[]{:S(2)}, u32[]{:S(2)}) collective-permute-start(bf16[48,3072]{1,0:T(8,128)(2,1)S(1)} %get-tuple-element.186), channel_id=1, source_target_pairs={{0,2},{1,3},{2,0},{3,1},{4,6},{5,7},{6,4},{7,5},{8,10},{9,11},{10,... | collective-permute-start | bytes 884744 | tf_op jit(solution)/shard_map/ppermute | solution.py:104
  208.9 1.3 collective-permute-start.40
  210.1 2.3 collective-permute-start.37
  212.7 6.9 %collective-permute-done.38 = bf16[48,3072]{1,0:T(8,128)(2,1)S(1)} collective-permute-done((bf16[48,3072]{1,0:T(8,128)(2,1)S(1)}, bf16[48,3072]{1,0:T(8,128)(2,1)S(1)}, u32[]{:S(2)}, u32[]{:S(2)}) %collective-permute-start.38) | collective-permute-done | bytes 294944 | tf_op jit(solution)/shard_map/ppermute | solution.py:104
  219.6 2.3 collective-permute-done.39
  221.9 13.9 %collective-permute-done.40 = bf16[48,3072]{1,0:T(8,128)(2,1)S(1)} collective-permute-done((bf16[48,3072]{1,0:T(8,128)(2,1)S(1)}, bf16[48,3072]{1,0:T(8,128)(2,1)S(1)}, u32[]{:S(2)}, u32[]{:S(2)}) %collective-permute-start.40) | collective-permute-done | bytes 294944 | tf_op jit(solution)/shard_map/ppermute | solution.py:104
  235.9 1.0 collective-permute-done.37
  237.0 1.1 collective-permute-start.41
  238.3 1.5 collective-permute-start.43
  239.8 1.9 collective-permute-start.45
  241.7 1.0 bitcast_add_fusion
  245.2 1.2 select_n.94
  246.4 7.0 %collective-permute-done.43 = bf16[48,1664]{1,0:T(8,128)(2,1)S(1)} collective-permute-done((bf16[48,1664]{1,0:T(8,128)(2,1)S(1)}, bf16[48,1664]{1,0:T(8,128)(2,1)S(1)}, u32[]{:S(2)}, u32[]{:S(2)}) %collective-permute-start.43) | collective-permute-done | bytes 159776 | tf_op jit(solution)/shard_map/ppermute | solution.py:104
  253.6 1.8 collective-permute-start.44
  256.0 0.8 slice_reduce_fusion
  (135 shorter events, 17.6 us)
Async XLA Ops:
  0.7 7.5 %copy-start.2 = (bf16[2,128,768]{2,1,0:T(8,128)(2,1)S(1)}, bf16[2,128,768]{2,1,0:T(8,128)(2,1)}, u32[]{:S(2)}) copy-start(bf16[2,128,768]{2,1,0:T(8,128)(2,1)} %param.35) | copy-start | bytes 1179652
  0.7 7.5 %copy-start.9 = (f32[96,768]{1,0:T(8,128)S(1)}, f32[96,768]{1,0:T(8,128)}, u32[]{:S(2)}) copy-start(f32[96,768]{1,0:T(8,128)} %param.30) | copy-start | bytes 884740
  3.1 5.2 %copy-start.10 = (bf16[24,1280]{1,0:T(8,128)(2,1)S(1)}, bf16[24,1280]{1,0:T(8,128)(2,1)}, u32[]{:S(2)}) copy-start(bf16[24,1280]{1,0:T(8,128)(2,1)} %get-tuple-element.106) | copy-start | bytes 184324
  3.1 5.1 %collective-permute-start = (bf16[24,1280]{1,0:T(8,128)(2,1)}, bf16[24,1280]{1,0:T(8,128)(2,1)S(1)}, u32[]{:S(2)}, u32[]{:S(2)}) collective-permute-start(bf16[24,1280]{1,0:T(8,128)(2,1)} %get-tuple-element.107), channel_id=1, source_target_pairs={{0,1},{1,0},{2,3},{3,2},{4,5},{5,4},{6,7},{7,6},{8,9},{9,8},{10,11... | collective-permute-start | bytes 184328 | tf_op jit(solution)/shard_map/ppermute | solution.py:100
  7.6 3.2 %collective-permute-start.4 = (bf16[24,2304]{1,0:T(8,128)(2,1)S(1)}, bf16[24,2304]{1,0:T(8,128)(2,1)S(1)}, u32[]{:S(2)}, u32[]{:S(2)}) collective-permute-start(bf16[24,2304]{1,0:T(8,128)(2,1)S(1)} %get-tuple-element.228), channel_id=1, source_target_pairs={{0,1},{1,0},{2,3},{3,2},{4,5},{5,4},{6,7},{7,6},{8,9},{9,8},{10,11... | collective-permute-start | bytes 331784 | tf_op jit(solution)/shard_map/ppermute | solution.py:100
  7.6 12.5 %collective-permute-start.5 = (bf16[2,128,768]{2,1,0:T(8,128)(2,1)}, bf16[2,128,768]{2,1,0:T(8,128)(2,1)S(1)}, u32[]{:S(2)}, u32[]{:S(2)}) collective-permute-start(bf16[2,128,768]{2,1,0:T(8,128)(2,1)} %refs_0_.2), channel_id=1, source_target_pairs={{0,1},{1,0},{2,3},{3,2},{4,5},{5,4},{6,7},{7,6},{8,9},{9,8},{10,11... | collective-permute-start | bytes 1179656 | tf_op jit(solution)/shard_map/ppermute | solution.py:100
  8.1 12.1 %collective-permute-start.6 = (bf16[2,128,768]{2,1,0:T(8,128)(2,1)S(1)}, bf16[2,128,768]{2,1,0:T(8,128)(2,1)S(1)}, u32[]{:S(2)}, u32[]{:S(2)}) collective-permute-start(bf16[2,128,768]{2,1,0:T(8,128)(2,1)S(1)} %copy-done.2), channel_id=1, source_target_pairs={{0,1},{1,0},{2,3},{3,2},{4,5},{5,4},{6,7},{7,6},{8,9},{9,8},{10,11... | collective-permute-start | bytes 1179656 | tf_op jit(solution)/shard_map/ppermute | solution.py:100
  8.3 9.8 %collective-permute-start.3 = (bf16[2,24,1280]{2,1,0:T(8,128)(2,1)S(1)}, bf16[2,24,1280]{2,1,0:T(8,128)(2,1)S(1)}, u32[]{:S(2)}, u32[]{:S(2)}) collective-permute-start(bf16[2,24,1280]{2,1,0:T(8,128)(2,1)S(1)} %maximum_select_fusion.2), channel_id=1, source_target_pairs={{0,6},{1,7},{2,4},{3,5},{4,2},{5,3},{6,0},{7,1},{8,14},{9,15},{10,... | collective-permute-start | bytes 368648 | tf_op jit(solution)/shard_map/ppermute | solution.py:104
  9.7 10.2 %collective-permute-start.2 = (bf16[2,24,1280]{2,1,0:T(8,128)(2,1)S(1)}, bf16[2,24,1280]{2,1,0:T(8,128)(2,1)S(1)}, u32[]{:S(2)}, u32[]{:S(2)}) collective-permute-start(bf16[2,24,1280]{2,1,0:T(8,128)(2,1)S(1)} %maximum_select_fusion.2), channel_id=1, source_target_pairs={{0,4},{1,5},{2,6},{3,7},{4,0},{5,1},{6,2},{7,3},{8,12},{9,13},{10,... | collective-permute-start | bytes 368648 | tf_op jit(solution)/shard_map/ppermute | solution.py:104
  10.8 9.4 %collective-permute-start.1 = (bf16[2,24,1280]{2,1,0:T(8,128)(2,1)S(1)}, bf16[2,24,1280]{2,1,0:T(8,128)(2,1)S(1)}, u32[]{:S(2)}, u32[]{:S(2)}) collective-permute-start(bf16[2,24,1280]{2,1,0:T(8,128)(2,1)S(1)} %maximum_select_fusion.2), channel_id=1, source_target_pairs={{0,2},{1,3},{2,0},{3,1},{4,6},{5,7},{6,4},{7,5},{8,10},{9,11},{10,... | collective-permute-start | bytes 368648 | tf_op jit(solution)/shard_map/ppermute | solution.py:104
  20.2 36.9 %copy-start.6 = (bf16[2,128,768]{2,1,0:T(8,128)(2,1)}, bf16[2,128,768]{2,1,0:T(8,128)(2,1)S(1)}, u32[]{:S(2)}) copy-start(bf16[2,128,768]{2,1,0:T(8,128)(2,1)S(1)} %collective-permute-done.5.refs_4_) | copy-start | bytes 1179652
  20.2 36.9 %copy-start.4 = (bf16[2,128,768]{2,1,0:T(8,128)(2,1)}, bf16[2,128,768]{2,1,0:T(8,128)(2,1)S(1)}, u32[]{:S(2)}) copy-start(bf16[2,128,768]{2,1,0:T(8,128)(2,1)S(1)} %collective-permute-done.6) | copy-start | bytes 1179652
  20.3 31.1 %collective-permute-start.8 = (bf16[4,2,24,1280]{3,2,1,0:T(8,128)(2,1)S(1)}, bf16[4,2,24,1280]{3,2,1,0:T(8,128)(2,1)S(1)}, u32[]{:S(2)}, u32[]{:S(2)}) collective-permute-start(bf16[4,2,24,1280]{3,2,1,0:T(8,128)(2,1)S(1)} %pad_maximum_fusion.1.refs_0_), channel_id=1, source_target_pairs={{0,16},{8,24},{16,0},{24,8},{1,17},{9,25},{17,1},{25,9},{2,18},{10... | collective-permute-start | bytes 1474568 | tf_op jit(solution)/shard_map/ppermute | solution.py:108
  20.6 30.9 %collective-permute-start.7 = (bf16[4,2,24,1280]{3,2,1,0:T(8,128)(2,1)S(1)}, bf16[4,2,24,1280]{3,2,1,0:T(8,128)(2,1)S(1)}, u32[]{:S(2)}, u32[]{:S(2)}) collective-permute-start(bf16[4,2,24,1280]{3,2,1,0:T(8,128)(2,1)S(1)} %pad_maximum_fusion.1.refs_0_), channel_id=1, source_target_pairs={{0,8},{8,0},{16,24},{24,16},{1,9},{9,1},{17,25},{25,17},{2,10},{10... | collective-permute-start | bytes 1474568 | tf_op jit(solution)/shard_map/ppermute | solution.py:108
  21.8 24.0 %collective-permute-start.11 = (bf16[2,24,3840]{2,1,0:T(8,128)(2,1)S(1)}, bf16[2,24,3840]{2,1,0:T(8,128)(2,1)S(1)}, u32[]{:S(2)}, u32[]{:S(2)}) collective-permute-start(bf16[2,24,3840]{2,1,0:T(8,128)(2,1)S(1)} %pad_maximum_fusion.2), channel_id=1, source_target_pairs={{0,6},{1,7},{2,4},{3,5},{4,2},{5,3},{6,0},{7,1},{8,14},{9,15},{10,... | collective-permute-start | bytes 1105928 | tf_op jit(solution)/shard_map/ppermute | solution.py:104
  21.8 29.6 %collective-permute-start.10 = (bf16[2,24,3840]{2,1,0:T(8,128)(2,1)S(1)}, bf16[2,24,3840]{2,1,0:T(8,128)(2,1)S(1)}, u32[]{:S(2)}, u32[]{:S(2)}) collective-permute-start(bf16[2,24,3840]{2,1,0:T(8,128)(2,1)S(1)} %pad_maximum_fusion.2), channel_id=1, source_target_pairs={{0,4},{1,5},{2,6},{3,7},{4,0},{5,1},{6,2},{7,3},{8,12},{9,13},{10,... | collective-permute-start | bytes 1105928 | tf_op jit(solution)/shard_map/ppermute | solution.py:104
  25.6 25.8 %collective-permute-start.9 = (bf16[2,24,3840]{2,1,0:T(8,128)(2,1)S(1)}, bf16[2,24,3840]{2,1,0:T(8,128)(2,1)S(1)}, u32[]{:S(2)}, u32[]{:S(2)}) collective-permute-start(bf16[2,24,3840]{2,1,0:T(8,128)(2,1)S(1)} %pad_maximum_fusion.2), channel_id=1, source_target_pairs={{0,2},{1,3},{2,0},{3,1},{4,6},{5,7},{6,4},{7,5},{8,10},{9,11},{10,... | collective-permute-start | bytes 1105928 | tf_op jit(solution)/shard_map/ppermute | solution.py:104
  51.5 14.1 %copy-start.8 = (s32[3]{0:T(128)S(1)}, s32[3]{0:T(128)}, u32[]{:S(2)}) copy-start(s32[3]{0:T(128)} %pad_add_fusion.place_ref) | copy-start | bytes 40
  51.5 5.1 %collective-permute-start.18 = (bf16[2,2,24,1280]{3,2,1,0:T(8,128)(2,1)S(1)}, bf16[2,2,24,1280]{3,2,1,0:T(8,128)(2,1)S(1)}, u32[]{:S(2)}, u32[]{:S(2)}) collective-permute-start(bf16[2,2,24,1280]{3,2,1,0:T(8,128)(2,1)S(1)} %slice.200), channel_id=1, source_target_pairs={{0,8},{8,0},{16,24},{24,16},{1,9},{9,1},{17,25},{25,17},{2,10},{10... | collective-permute-start | bytes 737288 | tf_op jit(solution)/shard_map/ppermute | solution.py:108
  51.8 5.0 %collective-permute-start.19 = (bf16[2,2,24,1280]{3,2,1,0:T(8,128)(2,1)S(1)}, bf16[2,2,24,1280]{3,2,1,0:T(8,128)(2,1)S(1)}, u32[]{:S(2)}, u32[]{:S(2)}) collective-permute-start(bf16[2,2,24,1280]{3,2,1,0:T(8,128)(2,1)S(1)} %slice.201), channel_id=1, source_target_pairs={{0,16},{8,24},{16,0},{24,8},{1,17},{9,25},{17,1},{25,9},{2,18},{10... | collective-permute-start | bytes 737288 | tf_op jit(solution)/shard_map/ppermute | solution.py:108
  57.1 39.4 %collective-permute-start.21 = (bf16[4,2,24,3840]{3,2,1,0:T(8,128)(2,1)S(1)}, bf16[4,2,24,3840]{3,2,1,0:T(8,128)(2,1)}, u32[]{:S(2)}, u32[]{:S(2)}) collective-permute-start(bf16[4,2,24,3840]{3,2,1,0:T(8,128)(2,1)S(1)} %pad_maximum_fusion.refs_0_), channel_id=1, source_target_pairs={{0,16},{8,24},{16,0},{24,8},{1,17},{9,25},{17,1},{25,9},{2,18},{10... | collective-permute-start | bytes 4423688 | tf_op jit(solution)/shard_map/ppermute | solution.py:108
  58.4 38.1 %collective-permute-start.20 = (bf16[4,2,24,3840]{3,2,1,0:T(8,128)(2,1)S(1)}, bf16[4,2,24,3840]{3,2,1,0:T(8,128)(2,1)}, u32[]{:S(2)}, u32[]{:S(2)}) collective-permute-start(bf16[4,2,24,3840]{3,2,1,0:T(8,128)(2,1)S(1)} %pad_maximum_fusion.refs_0_), channel_id=1, source_target_pairs={{0,8},{8,0},{16,24},{24,16},{1,9},{9,1},{17,25},{25,17},{2,10},{10... | collective-permute-start | bytes 4423688 | tf_op jit(solution)/shard_map/ppermute | solution.py:108
  60.0 22.3 %collective-permute-start.14 = (bf16[2,128,768]{2,1,0:T(8,128)(2,1)}, bf16[2,128,768]{2,1,0:T(8,128)(2,1)}, u32[]{:S(2)}, u32[]{:S(2)}) collective-permute-start(bf16[2,128,768]{2,1,0:T(8,128)(2,1)} %refs_0_.2), channel_id=1, source_target_pairs={{0,6},{1,7},{2,4},{3,5},{4,2},{5,3},{6,0},{7,1},{8,14},{9,15},{10,... | collective-permute-start | bytes 1179656 | tf_op jit(solution)/shard_map/ppermute | solution.py:104
  61.5 31.9 %collective-permute-start.13 = (bf16[2,128,768]{2,1,0:T(8,128)(2,1)}, bf16[2,128,768]{2,1,0:T(8,128)(2,1)}, u32[]{:S(2)}, u32[]{:S(2)}) collective-permute-start(bf16[2,128,768]{2,1,0:T(8,128)(2,1)} %refs_0_.2), channel_id=1, source_target_pairs={{0,4},{1,5},{2,6},{3,7},{4,0},{5,1},{6,2},{7,3},{8,12},{9,13},{10,... | collective-permute-start | bytes 1179656 | tf_op jit(solution)/shard_map/ppermute | solution.py:104
  65.5 30.9 %collective-permute-start.12 = (bf16[2,128,768]{2,1,0:T(8,128)(2,1)}, bf16[2,128,768]{2,1,0:T(8,128)(2,1)}, u32[]{:S(2)}, u32[]{:S(2)}) collective-permute-start(bf16[2,128,768]{2,1,0:T(8,128)(2,1)} %refs_0_.2), channel_id=1, source_target_pairs={{0,2},{1,3},{2,0},{3,1},{4,6},{5,7},{6,4},{7,5},{8,10},{9,11},{10,... | collective-permute-start | bytes 1179656 | tf_op jit(solution)/shard_map/ppermute | solution.py:104
  66.6 32.5 %copy-start.11 = (s32[2,64]{1,0:T(2,128)S(1)}, s32[2,64]{1,0:T(2,128)}, u32[]{:S(2)}) copy-start(s32[2,64]{1,0:T(2,128)} %param.34) | copy-start | bytes 1540
  66.8 32.7 %copy-start.7 = (bf16[2,128,768]{2,1,0:T(8,128)(2,1)S(1)}, bf16[2,128,768]{2,1,0:T(8,128)(2,1)}, u32[]{:S(2)}) copy-start(bf16[2,128,768]{2,1,0:T(8,128)(2,1)} %copy-done.6) | copy-start | bytes 1179652
  82.2 17.2 %collective-permute-start.17 = (bf16[2,128,768]{2,1,0:T(8,128)(2,1)}, bf16[2,128,768]{2,1,0:T(8,128)(2,1)S(1)}, u32[]{:S(2)}, u32[]{:S(2)}) collective-permute-start(bf16[2,128,768]{2,1,0:T(8,128)(2,1)} %collective-permute-done.14.refs_3_), channel_id=1, source_target_pairs={{0,1},{1,0},{2,3},{3,2},{4,5},{5,4},{6,7},{7,6},{8,9},{9,8},{10,11... | collective-permute-start | bytes 1179656 | tf_op jit(solution)/shard_map/ppermute | solution.py:100
  93.4 6.0 %collective-permute-start.16 = (bf16[2,128,768]{2,1,0:T(8,128)(2,1)}, bf16[2,128,768]{2,1,0:T(8,128)(2,1)S(1)}, u32[]{:S(2)}, u32[]{:S(2)}) collective-permute-start(bf16[2,128,768]{2,1,0:T(8,128)(2,1)} %collective-permute-done.13.refs_2_), channel_id=1, source_target_pairs={{0,1},{1,0},{2,3},{3,2},{4,5},{5,4},{6,7},{7,6},{8,9},{9,8},{10,11... | collective-permute-start | bytes 1179656 | tf_op jit(solution)/shard_map/ppermute | solution.py:100
  96.5 3.0 %collective-permute-start.15 = (bf16[2,128,768]{2,1,0:T(8,128)(2,1)}, bf16[2,128,768]{2,1,0:T(8,128)(2,1)S(1)}, u32[]{:S(2)}, u32[]{:S(2)}) collective-permute-start(bf16[2,128,768]{2,1,0:T(8,128)(2,1)} %collective-permute-done.12.refs_1_), channel_id=1, source_target_pairs={{0,1},{1,0},{2,3},{3,2},{4,5},{5,4},{6,7},{7,6},{8,9},{9,8},{10,11... | collective-permute-start | bytes 1179656 | tf_op jit(solution)/shard_map/ppermute | solution.py:100
  98.8 18.5 %collective-permute-start.24 = (bf16[2,2,24,3840]{3,2,1,0:T(8,128)(2,1)S(1)}, bf16[2,2,24,3840]{3,2,1,0:T(8,128)(2,1)S(1)}, u32[]{:S(2)}, u32[]{:S(2)}) collective-permute-start(bf16[2,2,24,3840]{3,2,1,0:T(8,128)(2,1)S(1)} %slice.205), channel_id=1, source_target_pairs={{0,16},{8,24},{16,0},{24,8},{1,17},{9,25},{17,1},{25,9},{2,18},{10... | collective-permute-start | bytes 2211848 | tf_op jit(solution)/shard_map/ppermute | solution.py:108
  99.1 18.2 %collective-permute-start.23 = (bf16[2,2,24,3840]{3,2,1,0:T(8,128)(2,1)S(1)}, bf16[2,2,24,3840]{3,2,1,0:T(8,128)(2,1)S(1)}, u32[]{:S(2)}, u32[]{:S(2)}) collective-permute-start(bf16[2,2,24,3840]{3,2,1,0:T(8,128)(2,1)S(1)} %slice.204), channel_id=1, source_target_pairs={{0,8},{8,0},{16,24},{24,16},{1,9},{9,1},{17,25},{25,17},{2,10},{10... | collective-permute-start | bytes 2211848 | tf_op jit(solution)/shard_map/ppermute | solution.py:108
  115.1 1.2 copy-start
  116.3 3.3 %collective-permute-start.22 = (bf16[2,256,384]{2,1,0:T(8,128)(2,1)S(1)}, bf16[2,256,384]{2,1,0:T(8,128)(2,1)S(1)}, u32[]{:S(2)}, u32[]{:S(2)}) collective-permute-start(bf16[2,256,384]{2,1,0:T(8,128)(2,1)S(1)} %get-tuple-element.133), channel_id=1, source_target_pairs={{0,1},{1,0},{2,3},{3,2},{4,5},{5,4},{6,7},{7,6},{8,9},{9,8},{10,11... | collective-permute-start | bytes 1179656 | tf_op jit(solution)/shard_map/ppermute | solution.py:100
  119.6 9.1 %copy-start.3 = (bf16[2,128,768]{2,1,0:T(8,128)(2,1)S(1)}, bf16[2,128,768]{2,1,0:T(8,128)(2,1)}, u32[]{:S(2)}) copy-start(bf16[2,128,768]{2,1,0:T(8,128)(2,1)} %param.35) | copy-start | bytes 1179652
  119.6 9.1 %copy-start.5 = (bf16[2,128,768]{2,1,0:T(8,128)(2,1)S(1)}, bf16[2,128,768]{2,1,0:T(8,128)(2,1)}, u32[]{:S(2)}) copy-start(bf16[2,128,768]{2,1,0:T(8,128)(2,1)} %copy-done.4) | copy-start | bytes 1179652
  126.1 2.6 %collective-permute-start.25 = (bf16[512,768]{1,0:T(8,128)(2,1)S(1)}, bf16[512,768]{1,0:T(8,128)(2,1)S(1)}, u32[]{:S(2)}, u32[]{:S(2)}) collective-permute-start(bf16[512,768]{1,0:T(8,128)(2,1)S(1)} %get-tuple-element.139), channel_id=1, source_target_pairs={{0,1},{1,0},{2,3},{3,2},{4,5},{5,4},{6,7},{7,6},{8,9},{9,8},{10,11... | collective-permute-start | bytes 2359304 | tf_op jit(solution)/shard_map/ppermute | solution.py:100
  138.5 27.2 %collective-permute-start.28 = (bf16[4,48,3072]{2,1,0:T(8,128)(2,1)S(1)}, bf16[4,48,3072]{2,1,0:T(8,128)(2,1)S(1)}, u32[]{:S(2)}, u32[]{:S(2)}) collective-permute-start(bf16[4,48,3072]{2,1,0:T(8,128)(2,1)S(1)} %get-tuple-element.161), channel_id=1, source_target_pairs={{0,8},{8,0},{16,24},{24,16},{1,9},{9,1},{17,25},{25,17},{2,10},{10... | collective-permute-start | bytes 3538952 | tf_op jit(solution)/shard_map/ppermute | solution.py:108
  139.8 27.1 %collective-permute-start.29 = (bf16[4,48,3072]{2,1,0:T(8,128)(2,1)S(1)}, bf16[4,48,3072]{2,1,0:T(8,128)(2,1)S(1)}, u32[]{:S(2)}, u32[]{:S(2)}) collective-permute-start(bf16[4,48,3072]{2,1,0:T(8,128)(2,1)S(1)} %get-tuple-element.162), channel_id=1, source_target_pairs={{0,16},{8,24},{16,0},{24,8},{1,17},{9,25},{17,1},{25,9},{2,18},{10... | collective-permute-start | bytes 3538952 | tf_op jit(solution)/shard_map/ppermute | solution.py:108
  141.0 2.6 %collective-permute-start.26 = (bf16[512,768]{1,0:T(8,128)(2,1)S(1)}, bf16[512,768]{1,0:T(8,128)(2,1)S(1)}, u32[]{:S(2)}, u32[]{:S(2)}) collective-permute-start(bf16[512,768]{1,0:T(8,128)(2,1)S(1)} %get-tuple-element.144), channel_id=1, source_target_pairs={{0,1},{1,0},{2,3},{3,2},{4,5},{5,4},{6,7},{7,6},{8,9},{9,8},{10,11... | collective-permute-start | bytes 2359304 | tf_op jit(solution)/shard_map/ppermute | solution.py:100
  143.7 2.3 copy-start.1
  163.9 5.0 %collective-permute-start.27 = (bf16[4,2,128,768]{3,2,1,0:T(8,128)(2,1)S(1)}, bf16[4,2,128,768]{3,2,1,0:T(8,128)(2,1)S(1)}, u32[]{:S(2)}, u32[]{:S(2)}) collective-permute-start(bf16[4,2,128,768]{3,2,1,0:T(8,128)(2,1)S(1)} %get-tuple-element.155), channel_id=1, source_target_pairs={{0,1},{1,0},{2,3},{3,2},{4,5},{5,4},{6,7},{7,6},{8,9},{9,8},{10,11... | collective-permute-start | bytes 4718600 | tf_op jit(solution)/shard_map/ppermute | solution.py:100
  167.1 13.6 %collective-permute-start.32 = (bf16[2,48,3072]{2,1,0:T(8,128)(2,1)S(1)}, bf16[2,48,3072]{2,1,0:T(8,128)(2,1)S(1)}, u32[]{:S(2)}, u32[]{:S(2)}) collective-permute-start(bf16[2,48,3072]{2,1,0:T(8,128)(2,1)S(1)} %add_convert_fusion.1), channel_id=1, source_target_pairs={{0,16},{8,24},{16,0},{24,8},{1,17},{9,25},{17,1},{25,9},{2,18},{10... | collective-permute-start | bytes 1769480 | tf_op jit(solution)/shard_map/ppermute | solution.py:108
  168.5 13.3 %collective-permute-start.33 = (bf16[2,48,3072]{2,1,0:T(8,128)(2,1)S(1)}, bf16[2,48,3072]{2,1,0:T(8,128)(2,1)S(1)}, u32[]{:S(2)}, u32[]{:S(2)}) collective-permute-start(bf16[2,48,3072]{2,1,0:T(8,128)(2,1)S(1)} %add_convert_fusion), channel_id=1, source_target_pairs={{0,8},{8,0},{16,24},{24,16},{1,9},{9,1},{17,25},{25,17},{2,10},{10... | collective-permute-start | bytes 1769480 | tf_op jit(solution)/shard_map/ppermute | solution.py:108
  169.3 35.8 %collective-permute-start.36 = (bf16[2,2,128,768]{3,2,1,0:T(8,128)(2,1)S(1)}, bf16[2,2,128,768]{3,2,1,0:T(8,128)(2,1)S(1)}, u32[]{:S(2)}, u32[]{:S(2)}) collective-permute-start(bf16[2,2,128,768]{3,2,1,0:T(8,128)(2,1)S(1)} %slice.342), channel_id=1, source_target_pairs={{0,4},{1,5},{2,6},{3,7},{4,0},{5,1},{6,2},{7,3},{8,12},{9,13},{10,... | collective-permute-start | bytes 2359304 | tf_op jit(solution)/shard_map/ppermute | solution.py:104
  177.8 17.7 %collective-permute-start.30 = (bf16[4,48,1664]{2,1,0:T(8,128)(2,1)S(1)}, bf16[4,48,1664]{2,1,0:T(8,128)(2,1)S(1)}, u32[]{:S(2)}, u32[]{:S(2)}) collective-permute-start(bf16[4,48,1664]{2,1,0:T(8,128)(2,1)S(1)} %get-tuple-element.176), channel_id=1, source_target_pairs={{0,8},{8,0},{16,24},{24,16},{1,9},{9,1},{17,25},{25,17},{2,10},{10... | collective-permute-start | bytes 1916936 | tf_op jit(solution)/shard_map/ppermute | solution.py:108
  179.0 16.5 %collective-permute-start.31 = (bf16[4,48,1664]{2,1,0:T(8,128)(2,1)S(1)}, bf16[4,48,1664]{2,1,0:T(8,128)(2,1)S(1)}, u32[]{:S(2)}, u32[]{:S(2)}) collective-permute-start(bf16[4,48,1664]{2,1,0:T(8,128)(2,1)S(1)} %get-tuple-element.177), channel_id=1, source_target_pairs={{0,16},{8,24},{16,0},{24,8},{1,17},{9,25},{17,1},{25,9},{2,18},{10... | collective-permute-start | bytes 1916936 | tf_op jit(solution)/shard_map/ppermute | solution.py:108
  195.6 14.5 %collective-permute-start.34 = (bf16[2,48,1664]{2,1,0:T(8,128)(2,1)S(1)}, bf16[2,48,1664]{2,1,0:T(8,128)(2,1)S(1)}, u32[]{:S(2)}, u32[]{:S(2)}) collective-permute-start(bf16[2,48,1664]{2,1,0:T(8,128)(2,1)S(1)} %add_convert_fusion.3), channel_id=1, source_target_pairs={{0,16},{8,24},{16,0},{24,8},{1,17},{9,25},{17,1},{25,9},{2,18},{10... | collective-permute-start | bytes 958472 | tf_op jit(solution)/shard_map/ppermute | solution.py:108
  196.0 16.4 %collective-permute-start.35 = (bf16[2,48,1664]{2,1,0:T(8,128)(2,1)S(1)}, bf16[2,48,1664]{2,1,0:T(8,128)(2,1)S(1)}, u32[]{:S(2)}, u32[]{:S(2)}) collective-permute-start(bf16[2,48,1664]{2,1,0:T(8,128)(2,1)S(1)} %add_convert_fusion.2), channel_id=1, source_target_pairs={{0,8},{8,0},{16,24},{24,16},{1,9},{9,1},{17,25},{25,17},{2,10},{10... | collective-permute-start | bytes 958472 | tf_op jit(solution)/shard_map/ppermute | solution.py:108
  205.4 14.2 %collective-permute-start.38 = (bf16[48,3072]{1,0:T(8,128)(2,1)S(1)}, bf16[48,3072]{1,0:T(8,128)(2,1)S(1)}, u32[]{:S(2)}, u32[]{:S(2)}) collective-permute-start(bf16[48,3072]{1,0:T(8,128)(2,1)S(1)} %get-tuple-element.186), channel_id=1, source_target_pairs={{0,2},{1,3},{2,0},{3,1},{4,6},{5,7},{6,4},{7,5},{8,10},{9,11},{10,... | collective-permute-start | bytes 884744 | tf_op jit(solution)/shard_map/ppermute | solution.py:104
  208.9 13.0 %collective-permute-start.39 = (bf16[48,3072]{1,0:T(8,128)(2,1)S(1)}, bf16[48,3072]{1,0:T(8,128)(2,1)S(1)}, u32[]{:S(2)}, u32[]{:S(2)}) collective-permute-start(bf16[48,3072]{1,0:T(8,128)(2,1)S(1)} %get-tuple-element.187), channel_id=1, source_target_pairs={{0,4},{1,5},{2,6},{3,7},{4,0},{5,1},{6,2},{7,3},{8,12},{9,13},{10,... | collective-permute-start | bytes 884744 | tf_op jit(solution)/shard_map/ppermute | solution.py:104
  208.9 26.9 %collective-permute-start.40 = (bf16[48,3072]{1,0:T(8,128)(2,1)S(1)}, bf16[48,3072]{1,0:T(8,128)(2,1)S(1)}, u32[]{:S(2)}, u32[]{:S(2)}) collective-permute-start(bf16[48,3072]{1,0:T(8,128)(2,1)S(1)} %get-tuple-element.188), channel_id=1, source_target_pairs={{0,6},{1,7},{2,4},{3,5},{4,2},{5,3},{6,0},{7,1},{8,14},{9,15},{10,... | collective-permute-start | bytes 884744 | tf_op jit(solution)/shard_map/ppermute | solution.py:104
  210.1 26.8 %collective-permute-start.37 = (bf16[1,2,128,768]{3,2,1,0:T(8,128)(2,1)S(1)}, bf16[1,2,128,768]{3,2,1,0:T(8,128)(2,1)S(1)}, u32[]{:S(2)}, u32[]{:S(2)}) collective-permute-start(bf16[1,2,128,768]{3,2,1,0:T(8,128)(2,1)S(1)} %slice.343), channel_id=1, source_target_pairs={{0,2},{1,3},{2,0},{3,1},{4,6},{5,7},{6,4},{7,5},{8,10},{9,11},{10,... | collective-permute-start | bytes 1179656 | tf_op jit(solution)/shard_map/ppermute | solution.py:104
  237.0 9.4 %collective-permute-start.41 = (bf16[48,1664]{1,0:T(8,128)(2,1)S(1)}, bf16[48,1664]{1,0:T(8,128)(2,1)S(1)}, u32[]{:S(2)}, u32[]{:S(2)}) collective-permute-start(bf16[48,1664]{1,0:T(8,128)(2,1)S(1)} %get-tuple-element.191), channel_id=1, source_target_pairs={{0,2},{1,3},{2,0},{3,1},{4,6},{5,7},{6,4},{7,5},{8,10},{9,11},{10,... | collective-permute-start | bytes 479240 | tf_op jit(solution)/shard_map/ppermute | solution.py:104
  238.2 8.3 %collective-permute-start.42 = (bf16[48,1664]{1,0:T(8,128)(2,1)S(1)}, bf16[48,1664]{1,0:T(8,128)(2,1)S(1)}, u32[]{:S(2)}, u32[]{:S(2)}) collective-permute-start(bf16[48,1664]{1,0:T(8,128)(2,1)S(1)} %get-tuple-element.192), channel_id=1, source_target_pairs={{0,4},{1,5},{2,6},{3,7},{4,0},{5,1},{6,2},{7,3},{8,12},{9,13},{10,... | collective-permute-start | bytes 479240 | tf_op jit(solution)/shard_map/ppermute | solution.py:104
  238.3 15.1 %collective-permute-start.43 = (bf16[48,1664]{1,0:T(8,128)(2,1)S(1)}, bf16[48,1664]{1,0:T(8,128)(2,1)S(1)}, u32[]{:S(2)}, u32[]{:S(2)}) collective-permute-start(bf16[48,1664]{1,0:T(8,128)(2,1)S(1)} %get-tuple-element.193), channel_id=1, source_target_pairs={{0,6},{1,7},{2,4},{3,5},{4,2},{5,3},{6,0},{7,1},{8,14},{9,15},{10,... | collective-permute-start | bytes 479240 | tf_op jit(solution)/shard_map/ppermute | solution.py:104
  239.8 4.1 %collective-permute-start.45 = (f32[24,1536]{1,0:T(8,128)S(1)}, f32[24,1536]{1,0:T(8,128)S(1)}, u32[]{:S(2)}, u32[]{:S(2)}) collective-permute-start(f32[24,1536]{1,0:T(8,128)S(1)} %get-tuple-element.216), channel_id=1, source_target_pairs={{0,1},{1,0},{2,3},{3,2},{4,5},{5,4},{6,7},{7,6},{8,9},{9,8},{10,11... | collective-permute-start | bytes 442376 | tf_op jit(solution)/shard_map/ppermute | solution.py:100
  253.6 3.2 %collective-permute-start.44 = (f32[24,1664]{1,0:T(8,128)S(1)}, f32[24,1664]{1,0:T(8,128)S(1)}, u32[]{:S(2)}, u32[]{:S(2)}) collective-permute-start(f32[24,1664]{1,0:T(8,128)S(1)} %get-tuple-element.214), channel_id=1, source_target_pairs={{0,1},{1,0},{2,3},{3,2},{4,5},{5,4},{6,7},{7,6},{8,9},{9,8},{10,11... | collective-permute-start | bytes 479240 | tf_op jit(solution)/shard_map/ppermute | solution.py:100

commit v5 on v4

--- a/solution.py
+++ b/solution.py
@@ -312,7 +312,7 @@
     )(query_ids, key_ids, queries, key_values, key_values, lse, upward)
 
 
-CHUNK = 384
+CHUNK = 768
 QUERY_BIAS, VALUE_BIAS, OUT_BIAS, FIRST_GAIN, FIRST_SHIFT, REDUCE_BIAS, SECOND_GAIN, SECOND_SHIFT = range(8)
 
 

time: 259 us -> 258 us (level)
  no operation moved by 1% of the time
where the time goes in v5:
time: 258 us
  waiting for transfers between devices  116 us (45%)
  Pallas kernels  60.7 us (24%)
  starting transfers between devices  60.2 us (23%)
  local copies, waits for them, and re-layouts  10.5 us (4%)
  other arithmetic  9.09 us (4%)
    ppermute x17, waiting for transfers between devices, z_move(): return lax.ppermute(value, 'seq', [(i, i ^ 2 * step) for i in range(seq)])  89.7 us
    ppermute x17, starting transfers between devices, z_move(): return lax.ppermute(value, 'seq', [(i, i ^ 2 * step) for i in range(seq)])  26 us
    ppermute x16, waiting for transfers between devices, dp_move(): return lax.ppermute(value, 'dp', [(i, i ^ step) for i in range(dps)])  22.1 us
    ppermute x13, starting transfers between devices, core_swap(): return lax.ppermute(value, 'seq', [(i, i ^ 1) for i in range(seq)])  21.7 us
    pallas_call x1, Pallas kernels, attend_back(): pl.pallas_call(backward_kernel, grid=(streams, PAIRS), in_specs=[specs['q...  14.1 us
    pallas_call x3, Pallas kernels, over_rows(): pl.pallas_call(kernel, in_specs=[pl.BlockSpec(memory_space=pltpu.SMEM)] +...  13.7 us
    ppermute x16, starting transfers between devices, dp_move(): return lax.ppermute(value, 'dp', [(i, i ^ step) for i in range(dps)])  12.5 us
    pallas_call x1, Pallas kernels, attend(): pl.pallas_call(forward_kernel, grid=(streams, PAIRS), in_specs=[specs['qi...  10.5 us
  transfers between devices with their start and end apart: 46, of which 22 were waited for; matrix products, arithmetic and copies ran while one was open for 6% of the time, Pallas kernels for 17%

profile of v5, /device:TPU:13, one launch (start us, length us, event | category | flops | bytes accessed | tf_op | source)
XLA Modules:
  0.0 257.6 jit_solution(5905212913873225951)
XLA Ops:
  1.3 1.8 first_columns.1
  3.8 0.9 convert_element_type.196
  4.7 1.0 convert_element_type.197
  5.9 1.3 dynamic-slice_reduce_fusion.1
  8.3 1.4 collective-permute-start.3
  9.7 1.1 collective-permute-start.2
  10.8 1.1 collective-permute-start.1
  11.9 6.2 %collective-permute-done.3 = bf16[2,24,1280]{2,1,0:T(8,128)(2,1)S(1)} collective-permute-done((bf16[2,24,1280]{2,1,0:T(8,128)(2,1)S(1)}, bf16[2,24,1280]{2,1,0:T(8,128)(2,1)S(1)}, u32[]{:S(2)}, u32[]{:S(2)}) %collective-permute-start.3) | collective-permute-done | bytes 122912 | tf_op jit(solution)/shard_map/ppermute | solution.py:104
  18.1 1.7 collective-permute-done.2
  20.6 1.2 collective-permute-start.7
  21.8 3.8 %collective-permute-start.10 = (bf16[2,24,3840]{2,1,0:T(8,128)(2,1)S(1)}, bf16[2,24,3840]{2,1,0:T(8,128)(2,1)S(1)}, u32[]{:S(2)}, u32[]{:S(2)}) collective-permute-start(bf16[2,24,3840]{2,1,0:T(8,128)(2,1)S(1)} %pad_maximum_fusion.2), channel_id=1, source_target_pairs={{0,4},{1,5},{2,6},{3,7},{4,0},{5,1},{6,2},{7,3},{8,12},{9,13},{10,... | collective-permute-start | bytes 1105928 | tf_op jit(solution)/shard_map/ppermute | solution.py:104
  25.7 20.1 %collective-permute-done.11 = bf16[2,24,3840]{2,1,0:T(8,128)(2,1)S(1)} collective-permute-done((bf16[2,24,3840]{2,1,0:T(8,128)(2,1)S(1)}, bf16[2,24,3840]{2,1,0:T(8,128)(2,1)S(1)}, u32[]{:S(2)}, u32[]{:S(2)}) %collective-permute-start.11) | collective-permute-done | bytes 368672 | tf_op jit(solution)/shard_map/ppermute | solution.py:104
  45.8 5.6 %collective-permute-done.10 = bf16[2,24,3840]{2,1,0:T(8,128)(2,1)S(1)} collective-permute-done((bf16[2,24,3840]{2,1,0:T(8,128)(2,1)S(1)}, bf16[2,24,3840]{2,1,0:T(8,128)(2,1)S(1)}, u32[]{:S(2)}, u32[]{:S(2)}) %collective-permute-start.10) | collective-permute-done | bytes 368672 | tf_op jit(solution)/shard_map/ppermute | solution.py:104
  51.8 1.2 collective-permute-start.19
  53.0 3.6 %collective-permute-done.18.refs_3_ = bf16[2,2,24,1280]{3,2,1,0:T(8,128)(2,1)S(1)} collective-permute-done((bf16[2,2,24,1280]{3,2,1,0:T(8,128)(2,1)S(1)}, bf16[2,2,24,1280]{3,2,1,0:T(8,128)(2,1)S(1)}, u32[]{:S(2)}, u32[]{:S(2)}) %collective-permute-start.18) | collective-permute-done | bytes 245792 | tf_op jit(solution)/shard_map/ppermute | solution.py:108
  57.1 1.3 collective-permute-start.21
  58.4 1.5 collective-permute-start.20
  60.0 1.6 collective-permute-start.14
  61.5 4.0 %collective-permute-start.13 = (bf16[2,128,768]{2,1,0:T(8,128)(2,1)}, bf16[2,128,768]{2,1,0:T(8,128)(2,1)}, u32[]{:S(2)}, u32[]{:S(2)}) collective-permute-start(bf16[2,128,768]{2,1,0:T(8,128)(2,1)} %refs_0_.2), channel_id=1, source_target_pairs={{0,4},{1,5},{2,6},{3,7},{4,0},{5,1},{6,2},{7,3},{8,12},{9,13},{10,... | collective-permute-start | bytes 1179656 | tf_op jit(solution)/shard_map/ppermute | solution.py:104
  66.8 15.5 %collective-permute-done.14.refs_3_ = bf16[2,128,768]{2,1,0:T(8,128)(2,1)} collective-permute-done((bf16[2,128,768]{2,1,0:T(8,128)(2,1)}, bf16[2,128,768]{2,1,0:T(8,128)(2,1)}, u32[]{:S(2)}, u32[]{:S(2)}) %collective-permute-start.14) | collective-permute-done | bytes 393248 | tf_op jit(solution)/shard_map/ppermute | solution.py:104
  82.2 10.7 %collective-permute-start.17 = (bf16[2,128,768]{2,1,0:T(8,128)(2,1)}, bf16[2,128,768]{2,1,0:T(8,128)(2,1)S(1)}, u32[]{:S(2)}, u32[]{:S(2)}) collective-permute-start(bf16[2,128,768]{2,1,0:T(8,128)(2,1)} %collective-permute-done.14.refs_3_), channel_id=1, source_target_pairs={{0,1},{1,0},{2,3},{3,2},{4,5},{5,4},{6,7},{7,6},{8,9},{9,8},{10,11... | collective-permute-start | bytes 1179656 | tf_op jit(solution)/shard_map/ppermute | solution.py:100
  93.4 3.0 %collective-permute-start.16 = (bf16[2,128,768]{2,1,0:T(8,128)(2,1)}, bf16[2,128,768]{2,1,0:T(8,128)(2,1)S(1)}, u32[]{:S(2)}, u32[]{:S(2)}) collective-permute-start(bf16[2,128,768]{2,1,0:T(8,128)(2,1)} %collective-permute-done.13.refs_2_), channel_id=1, source_target_pairs={{0,1},{1,0},{2,3},{3,2},{4,5},{5,4},{6,7},{7,6},{8,9},{9,8},{10,11... | collective-permute-start | bytes 1179656 | tf_op jit(solution)/shard_map/ppermute | solution.py:100
  96.5 1.2 slice.204
  97.7 1.2 slice.205
  99.5 5.0 %project.1 = (bf16[2,1024,768]{2,1,0:T(8,128)(2,1)S(1)}, bf16[2,1024,768]{2,1,0:T(8,128)(2,1)S(1)}, bf16[2,256,384]{2,1,0:T(8,128)(2,1)S(1)}, bf16[2,256,768]{2,1,0:T(8,128)(2,1)S(1)}) custom-call(s32[3]{0:T(128)S(1)} %copy-done.8, bf16[2,128,768]{2,1,0:T(8,128)(2,1)} %refs_0_.2, bf16[2,128,768]{2,1,0:T(8,128)(2,1)} %collective-permute-done.12.refs_1_, ...), custom_call_target="tpu_custom_call" | custom-call | tf_op jit(solution)/shard_map/project/pallas_call | solution.py:380
  104.6 10.5 %attend.1 = (bf16[2,256,384]{2,1,0:T(8,128)(2,1)S(1)}, f32[2,3,2,256,128]{4,3,2,1,0:T(8,128)S(1)}) custom-call(s32[2,256,128]{2,1,0:T(8,128)S(1)} %broadcast_in_dim.51.qid_ref, s32[2,8,1024]{2,1,0:T(8,128)S(1)} %broadcast_in_dim.52.kid_ref, bf16[2,256,384]{2,1,0:T(8,128)(2,1)S(1)} %get-tuple-element.131.q_ref, ...), custom_call_target="tpu_custom_call" | custom-call | tf_op jit(solution)/shard_map/attend/pallas_call | solution.py:274
  115.1 1.2 copy-done
  116.3 1.1 collective-permute-start.22
  117.4 2.2 place_late.1
  119.6 5.8 %middle.1 = (f32[512,768]{1,0:T(8,128)S(1)}, f32[512,128]{1,0:T(8,128)S(1)}, bf16[512,768]{1,0:T(8,128)(2,1)S(1)}, bf16[512,1536]{1,0:T(8,128)(2,1)S(1)}, bf16[5...) custom-call(s32[3]{0:T(128)S(1)} %copy-done.8, bf16[512,384]{1,0:T(8,128)(2,1)S(1)} %bitcast.96, ...), custom_call_target="tpu_custom_call" | custom-call | tf_op jit(solution)/shard_map/middle/pallas_call | solution.py:533
  126.1 1.9 collective-permute-done.25.refs_1_
  128.1 5.6 %turn.1 = (bf16[256,768]{1,0:T(8,128)(2,1)}, f32[512,768]{1,0:T(8,128)S(1)}, bf16[512,768]{1,0:T(8,128)(2,1)S(1)}, bf16[512,1536]{1,0:T(8,128)(2,1)S(1)}, f32[51...) custom-call(s32[3]{0:T(128)S(1)} %copy-done.8, ...), custom_call_target="tpu_custom_call" | custom-call | tf_op jit(solution)/shard_map/turn/pallas_call | solution.py:533
  133.7 3.5 %wide_packs.1 = (bf16[4,48,3072]{2,1,0:T(8,128)(2,1)S(1)}, bf16[4,48,3072]{2,1,0:T(8,128)(2,1)S(1)}, bf16[4,48,3072]{2,1,0:T(8,128)(2,1)S(1)}, bf16[2,48,3072]{2,1,0:T(8,128)(2,1)S(1)}, bf16[2,48,3072]{2,1,0:T(8,128)(2,1)S(1)}) custom-call(s32[3]{0:T(128)S(1)} %copy-done.8, bf16[512,1536]{1,0:T(8,128)(2,1)S(1)} %get-tuple-element.156.hidden_ref, ...), custom_call_target="tpu_custom_call" | custom-call | tf_op jit(solution)/shard_map/wide_packs/pallas_call | solution.py:547
  137.2 1.3 collective-permute-start.28
  138.5 1.2 collective-permute-start.29
  140.4 1.9 collective-permute-done.26.refs_1_
  142.4 2.3 first_back.1
  144.6 14.1 %attend_back.1 = (bf16[2,256,384]{2,1,0:T(8,128)(2,1)S(1)}, bf16[2,1024,384]{2,1,0:T(8,128)(2,1)S(1)}, bf16[2,1024,384]{2,1,0:T(8,128)(2,1)S(1)}) custom-call(s32[2,256,128]{2,1,0:T(8,128)S(1)} %broadcast_in_dim.51.qid_ref, s32[2,8,1024]{2,1,0:T(8,128)S(1)} %broadcast_in_dim.52.kid_ref, bf16[2,256,384]{2,1,0:T(8,128)(2,1)S(1)} %get-tuple-element.131.q_ref, ...), custom_call_target="tpu_custom_call" | custom-call | tf_op jit(solution)/shard_map/attend_back/pallas_call | solution.py:295
  158.7 3.9 %unproject.1 = (bf16[4,2,128,768]{3,2,1,0:T(8,128)(2,1)S(1)}, bf16[4,2,128,768]{3,2,1,0:T(8,128)(2,1)S(1)}) custom-call(s32[3]{0:T(128)S(1)} %copy-done.8, bf16[2,256,384]{2,1,0:T(8,128)(2,1)S(1)} %get-tuple-element.151.query_ref, bf16[2,1024,384]{2,1,0:T(8,128)(2,1)S(1)} %get-tuple-element.152.key_ref, ...), custom_call_target="tpu_custom_call" | custom-call | tf_op jit(solution)/shard_map/unproject/pallas_call | solution.py:419
  163.1 1.4 collective-permute-done.28
  164.5 1.1 collective-permute-done.29
  165.8 1.3 collective-permute-start.32
  168.0 3.2 %collective-permute-start.36 = (bf16[2,2,128,768]{3,2,1,0:T(8,128)(2,1)S(1)}, bf16[2,2,128,768]{3,2,1,0:T(8,128)(2,1)S(1)}, u32[]{:S(2)}, u32[]{:S(2)}) collective-permute-start(bf16[2,2,128,768]{3,2,1,0:T(8,128)(2,1)S(1)} %slice.342), channel_id=1, source_target_pairs={{0,4},{1,5},{2,6},{3,7},{4,0},{5,1},{6,2},{7,3},{8,12},{9,13},{10,... | collective-permute-start | bytes 2359304 | tf_op jit(solution)/shard_map/ppermute | solution.py:104
  171.2 5.3 %narrow_packs.1 = (bf16[4,48,1664]{2,1,0:T(8,128)(2,1)S(1)}, bf16[4,48,1664]{2,1,0:T(8,128)(2,1)S(1)}, bf16[4,48,1664]{2,1,0:T(8,128)(2,1)S(1)}, bf16[2,48,1664]...) custom-call(s32[3]{0:T(128)S(1)} %copy-done.8, bf16[2048,768]{1,0:T(8,128)(2,1)S(1)} %bitcast.93, bf16[512,768]{1,0:T(8,128)(2,1)S(1)} %bitcast.95, ...), custom_call_target="tpu_custom_call" | custom-call | tf_op jit(solution)/shard_map/narrow_packs/pallas_call | solution.py:547
  176.5 1.2 collective-permute-start.30
  177.9 1.4 collective-permute-done.32
  179.4 1.2 collective-permute-done.33
  181.1 13.1 %collective-permute-done.30 = bf16[4,48,1664]{2,1,0:T(8,128)(2,1)S(1)} collective-permute-done((bf16[4,48,1664]{2,1,0:T(8,128)(2,1)S(1)}, bf16[4,48,1664]{2,1,0:T(8,128)(2,1)S(1)}, u32[]{:S(2)}, u32[]{:S(2)}) %collective-permute-start.30) | collective-permute-done | bytes 639008 | tf_op jit(solution)/shard_map/ppermute | solution.py:108
  195.2 8.7 %collective-permute-done.36 = bf16[2,2,128,768]{3,2,1,0:T(8,128)(2,1)S(1)} collective-permute-done((bf16[2,2,128,768]{3,2,1,0:T(8,128)(2,1)S(1)}, bf16[2,2,128,768]{3,2,1,0:T(8,128)(2,1)S(1)}, u32[]{:S(2)}, u32[]{:S(2)}) %collective-permute-start.36) | collective-permute-done | bytes 786464 | tf_op jit(solution)/shard_map/ppermute | solution.py:104
  204.1 3.4 %collective-permute-start.38 = (bf16[48,3072]{1,0:T(8,128)(2,1)S(1)}, bf16[48,3072]{1,0:T(8,128)(2,1)S(1)}, u32[]{:S(2)}, u32[]{:S(2)}) collective-permute-start(bf16[48,3072]{1,0:T(8,128)(2,1)S(1)} %get-tuple-element.186), channel_id=1, source_target_pairs={{0,2},{1,3},{2,0},{3,1},{4,6},{5,7},{6,4},{7,5},{8,10},{9,11},{10,... | collective-permute-start | bytes 884744 | tf_op jit(solution)/shard_map/ppermute | solution.py:104
  207.5 1.3 collective-permute-start.40
  208.8 2.3 collective-permute-start.37
  211.4 6.9 %collective-permute-done.38 = bf16[48,3072]{1,0:T(8,128)(2,1)S(1)} collective-permute-done((bf16[48,3072]{1,0:T(8,128)(2,1)S(1)}, bf16[48,3072]{1,0:T(8,128)(2,1)S(1)}, u32[]{:S(2)}, u32[]{:S(2)}) %collective-permute-start.38) | collective-permute-done | bytes 294944 | tf_op jit(solution)/shard_map/ppermute | solution.py:104
  218.3 2.3 collective-permute-done.39
  220.6 13.9 %collective-permute-done.40 = bf16[48,3072]{1,0:T(8,128)(2,1)S(1)} collective-permute-done((bf16[48,3072]{1,0:T(8,128)(2,1)S(1)}, bf16[48,3072]{1,0:T(8,128)(2,1)S(1)}, u32[]{:S(2)}, u32[]{:S(2)}) %collective-permute-start.40) | collective-permute-done | bytes 294944 | tf_op jit(solution)/shard_map/ppermute | solution.py:104
  234.6 1.0 collective-permute-done.37
  235.7 1.1 collective-permute-start.41
  237.0 1.5 collective-permute-start.43
  238.5 1.9 collective-permute-start.45
  240.4 1.0 bitcast_add_fusion
  243.9 1.2 select_n.94
  245.1 7.0 %collective-permute-done.43 = bf16[48,1664]{1,0:T(8,128)(2,1)S(1)} collective-permute-done((bf16[48,1664]{1,0:T(8,128)(2,1)S(1)}, bf16[48,1664]{1,0:T(8,128)(2,1)S(1)}, u32[]{:S(2)}, u32[]{:S(2)}) %collective-permute-start.43) | collective-permute-done | bytes 159776 | tf_op jit(solution)/shard_map/ppermute | solution.py:104
  252.3 1.8 collective-permute-start.44
  254.7 0.8 slice_reduce_fusion
  (135 shorter events, 17.6 us)
Async XLA Ops:
  0.7 7.5 %copy-start.2 = (bf16[2,128,768]{2,1,0:T(8,128)(2,1)S(1)}, bf16[2,128,768]{2,1,0:T(8,128)(2,1)}, u32[]{:S(2)}) copy-start(bf16[2,128,768]{2,1,0:T(8,128)(2,1)} %param.35) | copy-start | bytes 1179652
  0.7 7.5 %copy-start.9 = (f32[96,768]{1,0:T(8,128)S(1)}, f32[96,768]{1,0:T(8,128)}, u32[]{:S(2)}) copy-start(f32[96,768]{1,0:T(8,128)} %param.30) | copy-start | bytes 884740
  3.1 5.2 %copy-start.10 = (bf16[24,1280]{1,0:T(8,128)(2,1)S(1)}, bf16[24,1280]{1,0:T(8,128)(2,1)}, u32[]{:S(2)}) copy-start(bf16[24,1280]{1,0:T(8,128)(2,1)} %get-tuple-element.106) | copy-start | bytes 184324
  3.1 5.1 %collective-permute-start = (bf16[24,1280]{1,0:T(8,128)(2,1)}, bf16[24,1280]{1,0:T(8,128)(2,1)S(1)}, u32[]{:S(2)}, u32[]{:S(2)}) collective-permute-start(bf16[24,1280]{1,0:T(8,128)(2,1)} %get-tuple-element.107), channel_id=1, source_target_pairs={{0,1},{1,0},{2,3},{3,2},{4,5},{5,4},{6,7},{7,6},{8,9},{9,8},{10,11... | collective-permute-start | bytes 184328 | tf_op jit(solution)/shard_map/ppermute | solution.py:100
  7.6 3.2 %collective-permute-start.4 = (bf16[24,2304]{1,0:T(8,128)(2,1)S(1)}, bf16[24,2304]{1,0:T(8,128)(2,1)S(1)}, u32[]{:S(2)}, u32[]{:S(2)}) collective-permute-start(bf16[24,2304]{1,0:T(8,128)(2,1)S(1)} %get-tuple-element.228), channel_id=1, source_target_pairs={{0,1},{1,0},{2,3},{3,2},{4,5},{5,4},{6,7},{7,6},{8,9},{9,8},{10,11... | collective-permute-start | bytes 331784 | tf_op jit(solution)/shard_map/ppermute | solution.py:100
  7.6 12.5 %collective-permute-start.5 = (bf16[2,128,768]{2,1,0:T(8,128)(2,1)}, bf16[2,128,768]{2,1,0:T(8,128)(2,1)S(1)}, u32[]{:S(2)}, u32[]{:S(2)}) collective-permute-start(bf16[2,128,768]{2,1,0:T(8,128)(2,1)} %refs_0_.2), channel_id=1, source_target_pairs={{0,1},{1,0},{2,3},{3,2},{4,5},{5,4},{6,7},{7,6},{8,9},{9,8},{10,11... | collective-permute-start | bytes 1179656 | tf_op jit(solution)/shard_map/ppermute | solution.py:100
  8.1 12.1 %collective-permute-start.6 = (bf16[2,128,768]{2,1,0:T(8,128)(2,1)S(1)}, bf16[2,128,768]{2,1,0:T(8,128)(2,1)S(1)}, u32[]{:S(2)}, u32[]{:S(2)}) collective-permute-start(bf16[2,128,768]{2,1,0:T(8,128)(2,1)S(1)} %copy-done.2), channel_id=1, source_target_pairs={{0,1},{1,0},{2,3},{3,2},{4,5},{5,4},{6,7},{7,6},{8,9},{9,8},{10,11... | collective-permute-start | bytes 1179656 | tf_op jit(solution)/shard_map/ppermute | solution.py:100
  8.3 9.8 %collective-permute-start.3 = (bf16[2,24,1280]{2,1,0:T(8,128)(2,1)S(1)}, bf16[2,24,1280]{2,1,0:T(8,128)(2,1)S(1)}, u32[]{:S(2)}, u32[]{:S(2)}) collective-permute-start(bf16[2,24,1280]{2,1,0:T(8,128)(2,1)S(1)} %maximum_select_fusion.2), channel_id=1, source_target_pairs={{0,6},{1,7},{2,4},{3,5},{4,2},{5,3},{6,0},{7,1},{8,14},{9,15},{10,... | collective-permute-start | bytes 368648 | tf_op jit(solution)/shard_map/ppermute | solution.py:104
  9.7 10.2 %collective-permute-start.2 = (bf16[2,24,1280]{2,1,0:T(8,128)(2,1)S(1)}, bf16[2,24,1280]{2,1,0:T(8,128)(2,1)S(1)}, u32[]{:S(2)}, u32[]{:S(2)}) collective-permute-start(bf16[2,24,1280]{2,1,0:T(8,128)(2,1)S(1)} %maximum_select_fusion.2), channel_id=1, source_target_pairs={{0,4},{1,5},{2,6},{3,7},{4,0},{5,1},{6,2},{7,3},{8,12},{9,13},{10,... | collective-permute-start | bytes 368648 | tf_op jit(solution)/shard_map/ppermute | solution.py:104
  10.8 9.4 %collective-permute-start.1 = (bf16[2,24,1280]{2,1,0:T(8,128)(2,1)S(1)}, bf16[2,24,1280]{2,1,0:T(8,128)(2,1)S(1)}, u32[]{:S(2)}, u32[]{:S(2)}) collective-permute-start(bf16[2,24,1280]{2,1,0:T(8,128)(2,1)S(1)} %maximum_select_fusion.2), channel_id=1, source_target_pairs={{0,2},{1,3},{2,0},{3,1},{4,6},{5,7},{6,4},{7,5},{8,10},{9,11},{10,... | collective-permute-start | bytes 368648 | tf_op jit(solution)/shard_map/ppermute | solution.py:104
  20.2 36.9 %copy-start.6 = (bf16[2,128,768]{2,1,0:T(8,128)(2,1)}, bf16[2,128,768]{2,1,0:T(8,128)(2,1)S(1)}, u32[]{:S(2)}) copy-start(bf16[2,128,768]{2,1,0:T(8,128)(2,1)S(1)} %collective-permute-done.5.refs_4_) | copy-start | bytes 1179652
  20.2 36.9 %copy-start.4 = (bf16[2,128,768]{2,1,0:T(8,128)(2,1)}, bf16[2,128,768]{2,1,0:T(8,128)(2,1)S(1)}, u32[]{:S(2)}) copy-start(bf16[2,128,768]{2,1,0:T(8,128)(2,1)S(1)} %collective-permute-done.6) | copy-start | bytes 1179652
  20.3 31.1 %collective-permute-start.8 = (bf16[4,2,24,1280]{3,2,1,0:T(8,128)(2,1)S(1)}, bf16[4,2,24,1280]{3,2,1,0:T(8,128)(2,1)S(1)}, u32[]{:S(2)}, u32[]{:S(2)}) collective-permute-start(bf16[4,2,24,1280]{3,2,1,0:T(8,128)(2,1)S(1)} %pad_maximum_fusion.1.refs_0_), channel_id=1, source_target_pairs={{0,16},{8,24},{16,0},{24,8},{1,17},{9,25},{17,1},{25,9},{2,18},{10... | collective-permute-start | bytes 1474568 | tf_op jit(solution)/shard_map/ppermute | solution.py:108
  20.6 30.9 %collective-permute-start.7 = (bf16[4,2,24,1280]{3,2,1,0:T(8,128)(2,1)S(1)}, bf16[4,2,24,1280]{3,2,1,0:T(8,128)(2,1)S(1)}, u32[]{:S(2)}, u32[]{:S(2)}) collective-permute-start(bf16[4,2,24,1280]{3,2,1,0:T(8,128)(2,1)S(1)} %pad_maximum_fusion.1.refs_0_), channel_id=1, source_target_pairs={{0,8},{8,0},{16,24},{24,16},{1,9},{9,1},{17,25},{25,17},{2,10},{10... | collective-permute-start | bytes 1474568 | tf_op jit(solution)/shard_map/ppermute | solution.py:108
  21.8 24.0 %collective-permute-start.11 = (bf16[2,24,3840]{2,1,0:T(8,128)(2,1)S(1)}, bf16[2,24,3840]{2,1,0:T(8,128)(2,1)S(1)}, u32[]{:S(2)}, u32[]{:S(2)}) collective-permute-start(bf16[2,24,3840]{2,1,0:T(8,128)(2,1)S(1)} %pad_maximum_fusion.2), channel_id=1, source_target_pairs={{0,6},{1,7},{2,4},{3,5},{4,2},{5,3},{6,0},{7,1},{8,14},{9,15},{10,... | collective-permute-start | bytes 1105928 | tf_op jit(solution)/shard_map/ppermute | solution.py:104
  21.8 29.6 %collective-permute-start.10 = (bf16[2,24,3840]{2,1,0:T(8,128)(2,1)S(1)}, bf16[2,24,3840]{2,1,0:T(8,128)(2,1)S(1)}, u32[]{:S(2)}, u32[]{:S(2)}) collective-permute-start(bf16[2,24,3840]{2,1,0:T(8,128)(2,1)S(1)} %pad_maximum_fusion.2), channel_id=1, source_target_pairs={{0,4},{1,5},{2,6},{3,7},{4,0},{5,1},{6,2},{7,3},{8,12},{9,13},{10,... | collective-permute-start | bytes 1105928 | tf_op jit(solution)/shard_map/ppermute | solution.py:104
  25.6 25.8 %collective-permute-start.9 = (bf16[2,24,3840]{2,1,0:T(8,128)(2,1)S(1)}, bf16[2,24,3840]{2,1,0:T(8,128)(2,1)S(1)}, u32[]{:S(2)}, u32[]{:S(2)}) collective-permute-start(bf16[2,24,3840]{2,1,0:T(8,128)(2,1)S(1)} %pad_maximum_fusion.2), channel_id=1, source_target_pairs={{0,2},{1,3},{2,0},{3,1},{4,6},{5,7},{6,4},{7,5},{8,10},{9,11},{10,... | collective-permute-start | bytes 1105928 | tf_op jit(solution)/shard_map/ppermute | solution.py:104
  51.5 14.1 %copy-start.8 = (s32[3]{0:T(128)S(1)}, s32[3]{0:T(128)}, u32[]{:S(2)}) copy-start(s32[3]{0:T(128)} %pad_add_fusion.place_ref) | copy-start | bytes 40
  51.5 5.1 %collective-permute-start.18 = (bf16[2,2,24,1280]{3,2,1,0:T(8,128)(2,1)S(1)}, bf16[2,2,24,1280]{3,2,1,0:T(8,128)(2,1)S(1)}, u32[]{:S(2)}, u32[]{:S(2)}) collective-permute-start(bf16[2,2,24,1280]{3,2,1,0:T(8,128)(2,1)S(1)} %slice.200), channel_id=1, source_target_pairs={{0,8},{8,0},{16,24},{24,16},{1,9},{9,1},{17,25},{25,17},{2,10},{10... | collective-permute-start | bytes 737288 | tf_op jit(solution)/shard_map/ppermute | solution.py:108
  51.8 5.0 %collective-permute-start.19 = (bf16[2,2,24,1280]{3,2,1,0:T(8,128)(2,1)S(1)}, bf16[2,2,24,1280]{3,2,1,0:T(8,128)(2,1)S(1)}, u32[]{:S(2)}, u32[]{:S(2)}) collective-permute-start(bf16[2,2,24,1280]{3,2,1,0:T(8,128)(2,1)S(1)} %slice.201), channel_id=1, source_target_pairs={{0,16},{8,24},{16,0},{24,8},{1,17},{9,25},{17,1},{25,9},{2,18},{10... | collective-permute-start | bytes 737288 | tf_op jit(solution)/shard_map/ppermute | solution.py:108
  57.1 39.4 %collective-permute-start.21 = (bf16[4,2,24,3840]{3,2,1,0:T(8,128)(2,1)S(1)}, bf16[4,2,24,3840]{3,2,1,0:T(8,128)(2,1)}, u32[]{:S(2)}, u32[]{:S(2)}) collective-permute-start(bf16[4,2,24,3840]{3,2,1,0:T(8,128)(2,1)S(1)} %pad_maximum_fusion.refs_0_), channel_id=1, source_target_pairs={{0,16},{8,24},{16,0},{24,8},{1,17},{9,25},{17,1},{25,9},{2,18},{10... | collective-permute-start | bytes 4423688 | tf_op jit(solution)/shard_map/ppermute | solution.py:108
  58.4 38.1 %collective-permute-start.20 = (bf16[4,2,24,3840]{3,2,1,0:T(8,128)(2,1)S(1)}, bf16[4,2,24,3840]{3,2,1,0:T(8,128)(2,1)}, u32[]{:S(2)}, u32[]{:S(2)}) collective-permute-start(bf16[4,2,24,3840]{3,2,1,0:T(8,128)(2,1)S(1)} %pad_maximum_fusion.refs_0_), channel_id=1, source_target_pairs={{0,8},{8,0},{16,24},{24,16},{1,9},{9,1},{17,25},{25,17},{2,10},{10... | collective-permute-start | bytes 4423688 | tf_op jit(solution)/shard_map/ppermute | solution.py:108
  60.0 22.3 %collective-permute-start.14 = (bf16[2,128,768]{2,1,0:T(8,128)(2,1)}, bf16[2,128,768]{2,1,0:T(8,128)(2,1)}, u32[]{:S(2)}, u32[]{:S(2)}) collective-permute-start(bf16[2,128,768]{2,1,0:T(8,128)(2,1)} %refs_0_.2), channel_id=1, source_target_pairs={{0,6},{1,7},{2,4},{3,5},{4,2},{5,3},{6,0},{7,1},{8,14},{9,15},{10,... | collective-permute-start | bytes 1179656 | tf_op jit(solution)/shard_map/ppermute | solution.py:104
  61.5 31.9 %collective-permute-start.13 = (bf16[2,128,768]{2,1,0:T(8,128)(2,1)}, bf16[2,128,768]{2,1,0:T(8,128)(2,1)}, u32[]{:S(2)}, u32[]{:S(2)}) collective-permute-start(bf16[2,128,768]{2,1,0:T(8,128)(2,1)} %refs_0_.2), channel_id=1, source_target_pairs={{0,4},{1,5},{2,6},{3,7},{4,0},{5,1},{6,2},{7,3},{8,12},{9,13},{10,... | collective-permute-start | bytes 1179656 | tf_op jit(solution)/shard_map/ppermute | solution.py:104
  65.5 30.9 %collective-permute-start.12 = (bf16[2,128,768]{2,1,0:T(8,128)(2,1)}, bf16[2,128,768]{2,1,0:T(8,128)(2,1)}, u32[]{:S(2)}, u32[]{:S(2)}) collective-permute-start(bf16[2,128,768]{2,1,0:T(8,128)(2,1)} %refs_0_.2), channel_id=1, source_target_pairs={{0,2},{1,3},{2,0},{3,1},{4,6},{5,7},{6,4},{7,5},{8,10},{9,11},{10,... | collective-permute-start | bytes 1179656 | tf_op jit(solution)/shard_map/ppermute | solution.py:104
  66.6 32.5 %copy-start.11 = (s32[2,64]{1,0:T(2,128)S(1)}, s32[2,64]{1,0:T(2,128)}, u32[]{:S(2)}) copy-start(s32[2,64]{1,0:T(2,128)} %param.34) | copy-start | bytes 1540
  66.8 32.7 %copy-start.7 = (bf16[2,128,768]{2,1,0:T(8,128)(2,1)S(1)}, bf16[2,128,768]{2,1,0:T(8,128)(2,1)}, u32[]{:S(2)}) copy-start(bf16[2,128,768]{2,1,0:T(8,128)(2,1)} %copy-done.6) | copy-start | bytes 1179652
  82.2 17.2 %collective-permute-start.17 = (bf16[2,128,768]{2,1,0:T(8,128)(2,1)}, bf16[2,128,768]{2,1,0:T(8,128)(2,1)S(1)}, u32[]{:S(2)}, u32[]{:S(2)}) collective-permute-start(bf16[2,128,768]{2,1,0:T(8,128)(2,1)} %collective-permute-done.14.refs_3_), channel_id=1, source_target_pairs={{0,1},{1,0},{2,3},{3,2},{4,5},{5,4},{6,7},{7,6},{8,9},{9,8},{10,11... | collective-permute-start | bytes 1179656 | tf_op jit(solution)/shard_map/ppermute | solution.py:100
  93.4 6.0 %collective-permute-start.16 = (bf16[2,128,768]{2,1,0:T(8,128)(2,1)}, bf16[2,128,768]{2,1,0:T(8,128)(2,1)S(1)}, u32[]{:S(2)}, u32[]{:S(2)}) collective-permute-start(bf16[2,128,768]{2,1,0:T(8,128)(2,1)} %collective-permute-done.13.refs_2_), channel_id=1, source_target_pairs={{0,1},{1,0},{2,3},{3,2},{4,5},{5,4},{6,7},{7,6},{8,9},{9,8},{10,11... | collective-permute-start | bytes 1179656 | tf_op jit(solution)/shard_map/ppermute | solution.py:100
  96.5 3.0 %collective-permute-start.15 = (bf16[2,128,768]{2,1,0:T(8,128)(2,1)}, bf16[2,128,768]{2,1,0:T(8,128)(2,1)S(1)}, u32[]{:S(2)}, u32[]{:S(2)}) collective-permute-start(bf16[2,128,768]{2,1,0:T(8,128)(2,1)} %collective-permute-done.12.refs_1_), channel_id=1, source_target_pairs={{0,1},{1,0},{2,3},{3,2},{4,5},{5,4},{6,7},{7,6},{8,9},{9,8},{10,11... | collective-permute-start | bytes 1179656 | tf_op jit(solution)/shard_map/ppermute | solution.py:100
  98.8 18.5 %collective-permute-start.24 = (bf16[2,2,24,3840]{3,2,1,0:T(8,128)(2,1)S(1)}, bf16[2,2,24,3840]{3,2,1,0:T(8,128)(2,1)S(1)}, u32[]{:S(2)}, u32[]{:S(2)}) collective-permute-start(bf16[2,2,24,3840]{3,2,1,0:T(8,128)(2,1)S(1)} %slice.205), channel_id=1, source_target_pairs={{0,16},{8,24},{16,0},{24,8},{1,17},{9,25},{17,1},{25,9},{2,18},{10... | collective-permute-start | bytes 2211848 | tf_op jit(solution)/shard_map/ppermute | solution.py:108
  99.1 18.2 %collective-permute-start.23 = (bf16[2,2,24,3840]{3,2,1,0:T(8,128)(2,1)S(1)}, bf16[2,2,24,3840]{3,2,1,0:T(8,128)(2,1)S(1)}, u32[]{:S(2)}, u32[]{:S(2)}) collective-permute-start(bf16[2,2,24,3840]{3,2,1,0:T(8,128)(2,1)S(1)} %slice.204), channel_id=1, source_target_pairs={{0,8},{8,0},{16,24},{24,16},{1,9},{9,1},{17,25},{25,17},{2,10},{10... | collective-permute-start | bytes 2211848 | tf_op jit(solution)/shard_map/ppermute | solution.py:108
  115.1 1.2 copy-start
  116.3 3.3 %collective-permute-start.22 = (bf16[2,256,384]{2,1,0:T(8,128)(2,1)S(1)}, bf16[2,256,384]{2,1,0:T(8,128)(2,1)S(1)}, u32[]{:S(2)}, u32[]{:S(2)}) collective-permute-start(bf16[2,256,384]{2,1,0:T(8,128)(2,1)S(1)} %get-tuple-element.133), channel_id=1, source_target_pairs={{0,1},{1,0},{2,3},{3,2},{4,5},{5,4},{6,7},{7,6},{8,9},{9,8},{10,11... | collective-permute-start | bytes 1179656 | tf_op jit(solution)/shard_map/ppermute | solution.py:100
  119.6 8.4 %copy-start.3 = (bf16[2,128,768]{2,1,0:T(8,128)(2,1)S(1)}, bf16[2,128,768]{2,1,0:T(8,128)(2,1)}, u32[]{:S(2)}) copy-start(bf16[2,128,768]{2,1,0:T(8,128)(2,1)} %param.35) | copy-start | bytes 1179652
  119.6 8.4 %copy-start.5 = (bf16[2,128,768]{2,1,0:T(8,128)(2,1)S(1)}, bf16[2,128,768]{2,1,0:T(8,128)(2,1)}, u32[]{:S(2)}) copy-start(bf16[2,128,768]{2,1,0:T(8,128)(2,1)} %copy-done.4) | copy-start | bytes 1179652
  125.4 2.6 %collective-permute-start.25 = (bf16[512,768]{1,0:T(8,128)(2,1)S(1)}, bf16[512,768]{1,0:T(8,128)(2,1)S(1)}, u32[]{:S(2)}, u32[]{:S(2)}) collective-permute-start(bf16[512,768]{1,0:T(8,128)(2,1)S(1)} %get-tuple-element.139), channel_id=1, source_target_pairs={{0,1},{1,0},{2,3},{3,2},{4,5},{5,4},{6,7},{7,6},{8,9},{9,8},{10,11... | collective-permute-start | bytes 2359304 | tf_op jit(solution)/shard_map/ppermute | solution.py:100
  137.2 27.2 %collective-permute-start.28 = (bf16[4,48,3072]{2,1,0:T(8,128)(2,1)S(1)}, bf16[4,48,3072]{2,1,0:T(8,128)(2,1)S(1)}, u32[]{:S(2)}, u32[]{:S(2)}) collective-permute-start(bf16[4,48,3072]{2,1,0:T(8,128)(2,1)S(1)} %get-tuple-element.161), channel_id=1, source_target_pairs={{0,8},{8,0},{16,24},{24,16},{1,9},{9,1},{17,25},{25,17},{2,10},{10... | collective-permute-start | bytes 3538952 | tf_op jit(solution)/shard_map/ppermute | solution.py:108
  138.5 27.1 %collective-permute-start.29 = (bf16[4,48,3072]{2,1,0:T(8,128)(2,1)S(1)}, bf16[4,48,3072]{2,1,0:T(8,128)(2,1)S(1)}, u32[]{:S(2)}, u32[]{:S(2)}) collective-permute-start(bf16[4,48,3072]{2,1,0:T(8,128)(2,1)S(1)} %get-tuple-element.162), channel_id=1, source_target_pairs={{0,16},{8,24},{16,0},{24,8},{1,17},{9,25},{17,1},{25,9},{2,18},{10... | collective-permute-start | bytes 3538952 | tf_op jit(solution)/shard_map/ppermute | solution.py:108
  139.7 2.6 %collective-permute-start.26 = (bf16[512,768]{1,0:T(8,128)(2,1)S(1)}, bf16[512,768]{1,0:T(8,128)(2,1)S(1)}, u32[]{:S(2)}, u32[]{:S(2)}) collective-permute-start(bf16[512,768]{1,0:T(8,128)(2,1)S(1)} %get-tuple-element.144), channel_id=1, source_target_pairs={{0,1},{1,0},{2,3},{3,2},{4,5},{5,4},{6,7},{7,6},{8,9},{9,8},{10,11... | collective-permute-start | bytes 2359304 | tf_op jit(solution)/shard_map/ppermute | solution.py:100
  142.3 2.3 copy-start.1
  162.6 5.0 %collective-permute-start.27 = (bf16[4,2,128,768]{3,2,1,0:T(8,128)(2,1)S(1)}, bf16[4,2,128,768]{3,2,1,0:T(8,128)(2,1)S(1)}, u32[]{:S(2)}, u32[]{:S(2)}) collective-permute-start(bf16[4,2,128,768]{3,2,1,0:T(8,128)(2,1)S(1)} %get-tuple-element.155), channel_id=1, source_target_pairs={{0,1},{1,0},{2,3},{3,2},{4,5},{5,4},{6,7},{7,6},{8,9},{9,8},{10,11... | collective-permute-start | bytes 4718600 | tf_op jit(solution)/shard_map/ppermute | solution.py:100
  165.8 13.6 %collective-permute-start.32 = (bf16[2,48,3072]{2,1,0:T(8,128)(2,1)S(1)}, bf16[2,48,3072]{2,1,0:T(8,128)(2,1)S(1)}, u32[]{:S(2)}, u32[]{:S(2)}) collective-permute-start(bf16[2,48,3072]{2,1,0:T(8,128)(2,1)S(1)} %add_convert_fusion.1), channel_id=1, source_target_pairs={{0,16},{8,24},{16,0},{24,8},{1,17},{9,25},{17,1},{25,9},{2,18},{10... | collective-permute-start | bytes 1769480 | tf_op jit(solution)/shard_map/ppermute | solution.py:108
  167.2 13.3 %collective-permute-start.33 = (bf16[2,48,3072]{2,1,0:T(8,128)(2,1)S(1)}, bf16[2,48,3072]{2,1,0:T(8,128)(2,1)S(1)}, u32[]{:S(2)}, u32[]{:S(2)}) collective-permute-start(bf16[2,48,3072]{2,1,0:T(8,128)(2,1)S(1)} %add_convert_fusion), channel_id=1, source_target_pairs={{0,8},{8,0},{16,24},{24,16},{1,9},{9,1},{17,25},{25,17},{2,10},{10... | collective-permute-start | bytes 1769480 | tf_op jit(solution)/shard_map/ppermute | solution.py:108
  168.0 35.8 %collective-permute-start.36 = (bf16[2,2,128,768]{3,2,1,0:T(8,128)(2,1)S(1)}, bf16[2,2,128,768]{3,2,1,0:T(8,128)(2,1)S(1)}, u32[]{:S(2)}, u32[]{:S(2)}) collective-permute-start(bf16[2,2,128,768]{3,2,1,0:T(8,128)(2,1)S(1)} %slice.342), channel_id=1, source_target_pairs={{0,4},{1,5},{2,6},{3,7},{4,0},{5,1},{6,2},{7,3},{8,12},{9,13},{10,... | collective-permute-start | bytes 2359304 | tf_op jit(solution)/shard_map/ppermute | solution.py:104
  176.5 17.7 %collective-permute-start.30 = (bf16[4,48,1664]{2,1,0:T(8,128)(2,1)S(1)}, bf16[4,48,1664]{2,1,0:T(8,128)(2,1)S(1)}, u32[]{:S(2)}, u32[]{:S(2)}) collective-permute-start(bf16[4,48,1664]{2,1,0:T(8,128)(2,1)S(1)} %get-tuple-element.176), channel_id=1, source_target_pairs={{0,8},{8,0},{16,24},{24,16},{1,9},{9,1},{17,25},{25,17},{2,10},{10... | collective-permute-start | bytes 1916936 | tf_op jit(solution)/shard_map/ppermute | solution.py:108
  177.7 16.5 %collective-permute-start.31 = (bf16[4,48,1664]{2,1,0:T(8,128)(2,1)S(1)}, bf16[4,48,1664]{2,1,0:T(8,128)(2,1)S(1)}, u32[]{:S(2)}, u32[]{:S(2)}) collective-permute-start(bf16[4,48,1664]{2,1,0:T(8,128)(2,1)S(1)} %get-tuple-element.177), channel_id=1, source_target_pairs={{0,16},{8,24},{16,0},{24,8},{1,17},{9,25},{17,1},{25,9},{2,18},{10... | collective-permute-start | bytes 1916936 | tf_op jit(solution)/shard_map/ppermute | solution.py:108
  194.3 14.5 %collective-permute-start.34 = (bf16[2,48,1664]{2,1,0:T(8,128)(2,1)S(1)}, bf16[2,48,1664]{2,1,0:T(8,128)(2,1)S(1)}, u32[]{:S(2)}, u32[]{:S(2)}) collective-permute-start(bf16[2,48,1664]{2,1,0:T(8,128)(2,1)S(1)} %add_convert_fusion.3), channel_id=1, source_target_pairs={{0,16},{8,24},{16,0},{24,8},{1,17},{9,25},{17,1},{25,9},{2,18},{10... | collective-permute-start | bytes 958472 | tf_op jit(solution)/shard_map/ppermute | solution.py:108
  194.7 16.4 %collective-permute-start.35 = (bf16[2,48,1664]{2,1,0:T(8,128)(2,1)S(1)}, bf16[2,48,1664]{2,1,0:T(8,128)(2,1)S(1)}, u32[]{:S(2)}, u32[]{:S(2)}) collective-permute-start(bf16[2,48,1664]{2,1,0:T(8,128)(2,1)S(1)} %add_convert_fusion.2), channel_id=1, source_target_pairs={{0,8},{8,0},{16,24},{24,16},{1,9},{9,1},{17,25},{25,17},{2,10},{10... | collective-permute-start | bytes 958472 | tf_op jit(solution)/shard_map/ppermute | solution.py:108
  204.1 14.2 %collective-permute-start.38 = (bf16[48,3072]{1,0:T(8,128)(2,1)S(1)}, bf16[48,3072]{1,0:T(8,128)(2,1)S(1)}, u32[]{:S(2)}, u32[]{:S(2)}) collective-permute-start(bf16[48,3072]{1,0:T(8,128)(2,1)S(1)} %get-tuple-element.186), channel_id=1, source_target_pairs={{0,2},{1,3},{2,0},{3,1},{4,6},{5,7},{6,4},{7,5},{8,10},{9,11},{10,... | collective-permute-start | bytes 884744 | tf_op jit(solution)/shard_map/ppermute | solution.py:104
  207.5 13.0 %collective-permute-start.39 = (bf16[48,3072]{1,0:T(8,128)(2,1)S(1)}, bf16[48,3072]{1,0:T(8,128)(2,1)S(1)}, u32[]{:S(2)}, u32[]{:S(2)}) collective-permute-start(bf16[48,3072]{1,0:T(8,128)(2,1)S(1)} %get-tuple-element.187), channel_id=1, source_target_pairs={{0,4},{1,5},{2,6},{3,7},{4,0},{5,1},{6,2},{7,3},{8,12},{9,13},{10,... | collective-permute-start | bytes 884744 | tf_op jit(solution)/shard_map/ppermute | solution.py:104
  207.5 26.9 %collective-permute-start.40 = (bf16[48,3072]{1,0:T(8,128)(2,1)S(1)}, bf16[48,3072]{1,0:T(8,128)(2,1)S(1)}, u32[]{:S(2)}, u32[]{:S(2)}) collective-permute-start(bf16[48,3072]{1,0:T(8,128)(2,1)S(1)} %get-tuple-element.188), channel_id=1, source_target_pairs={{0,6},{1,7},{2,4},{3,5},{4,2},{5,3},{6,0},{7,1},{8,14},{9,15},{10,... | collective-permute-start | bytes 884744 | tf_op jit(solution)/shard_map/ppermute | solution.py:104
  208.8 26.8 %collective-permute-start.37 = (bf16[1,2,128,768]{3,2,1,0:T(8,128)(2,1)S(1)}, bf16[1,2,128,768]{3,2,1,0:T(8,128)(2,1)S(1)}, u32[]{:S(2)}, u32[]{:S(2)}) collective-permute-start(bf16[1,2,128,768]{3,2,1,0:T(8,128)(2,1)S(1)} %slice.343), channel_id=1, source_target_pairs={{0,2},{1,3},{2,0},{3,1},{4,6},{5,7},{6,4},{7,5},{8,10},{9,11},{10,... | collective-permute-start | bytes 1179656 | tf_op jit(solution)/shard_map/ppermute | solution.py:104
  235.7 9.4 %collective-permute-start.41 = (bf16[48,1664]{1,0:T(8,128)(2,1)S(1)}, bf16[48,1664]{1,0:T(8,128)(2,1)S(1)}, u32[]{:S(2)}, u32[]{:S(2)}) collective-permute-start(bf16[48,1664]{1,0:T(8,128)(2,1)S(1)} %get-tuple-element.191), channel_id=1, source_target_pairs={{0,2},{1,3},{2,0},{3,1},{4,6},{5,7},{6,4},{7,5},{8,10},{9,11},{10,... | collective-permute-start | bytes 479240 | tf_op jit(solution)/shard_map/ppermute | solution.py:104
  236.8 8.3 %collective-permute-start.42 = (bf16[48,1664]{1,0:T(8,128)(2,1)S(1)}, bf16[48,1664]{1,0:T(8,128)(2,1)S(1)}, u32[]{:S(2)}, u32[]{:S(2)}) collective-permute-start(bf16[48,1664]{1,0:T(8,128)(2,1)S(1)} %get-tuple-element.192), channel_id=1, source_target_pairs={{0,4},{1,5},{2,6},{3,7},{4,0},{5,1},{6,2},{7,3},{8,12},{9,13},{10,... | collective-permute-start | bytes 479240 | tf_op jit(solution)/shard_map/ppermute | solution.py:104
  237.0 15.1 %collective-permute-start.43 = (bf16[48,1664]{1,0:T(8,128)(2,1)S(1)}, bf16[48,1664]{1,0:T(8,128)(2,1)S(1)}, u32[]{:S(2)}, u32[]{:S(2)}) collective-permute-start(bf16[48,1664]{1,0:T(8,128)(2,1)S(1)} %get-tuple-element.193), channel_id=1, source_target_pairs={{0,6},{1,7},{2,4},{3,5},{4,2},{5,3},{6,0},{7,1},{8,14},{9,15},{10,... | collective-permute-start | bytes 479240 | tf_op jit(solution)/shard_map/ppermute | solution.py:104
  238.5 4.1 %collective-permute-start.45 = (f32[24,1536]{1,0:T(8,128)S(1)}, f32[24,1536]{1,0:T(8,128)S(1)}, u32[]{:S(2)}, u32[]{:S(2)}) collective-permute-start(f32[24,1536]{1,0:T(8,128)S(1)} %get-tuple-element.216), channel_id=1, source_target_pairs={{0,1},{1,0},{2,3},{3,2},{4,5},{5,4},{6,7},{7,6},{8,9},{9,8},{10,11... | collective-permute-start | bytes 442376 | tf_op jit(solution)/shard_map/ppermute | solution.py:100
  252.3 3.2 %collective-permute-start.44 = (f32[24,1664]{1,0:T(8,128)S(1)}, f32[24,1664]{1,0:T(8,128)S(1)}, u32[]{:S(2)}, u32[]{:S(2)}) collective-permute-start(f32[24,1664]{1,0:T(8,128)S(1)} %get-tuple-element.214), channel_id=1, source_target_pairs={{0,1},{1,0},{2,3},{3,2},{4,5},{5,4},{6,7},{7,6},{8,9},{9,8},{10,11... | collective-permute-start | bytes 479240 | tf_op jit(solution)/shard_map/ppermute | solution.py:100

commit v6 on v5

--- a/solution.py
+++ b/solution.py
@@ -312,7 +312,7 @@
     )(query_ids, key_ids, queries, key_values, key_values, lse, upward)
 
 
-CHUNK = 768
+CHUNK = 1536
 QUERY_BIAS, VALUE_BIAS, OUT_BIAS, FIRST_GAIN, FIRST_SHIFT, REDUCE_BIAS, SECOND_GAIN, SECOND_SHIFT = range(8)
 
 

time: 258 us -> 257 us (level)
  no operation moved by 1% of the time
where the time goes in v6:
time: 257 us
  waiting for transfers between devices  116 us (45%)
  starting transfers between devices  60.2 us (23%)
  Pallas kernels  60 us (23%)
  local copies, waits for them, and re-layouts  10.5 us (4%)
  other arithmetic  9.09 us (4%)
    ppermute x17, waiting for transfers between devices, z_move(): return lax.ppermute(value, 'seq', [(i, i ^ 2 * step) for i in range(seq)])  89.7 us
    ppermute x17, starting transfers between devices, z_move(): return lax.ppermute(value, 'seq', [(i, i ^ 2 * step) for i in range(seq)])  26 us
    ppermute x16, waiting for transfers between devices, dp_move(): return lax.ppermute(value, 'dp', [(i, i ^ step) for i in range(dps)])  22.1 us
    ppermute x13, starting transfers between devices, core_swap(): return lax.ppermute(value, 'seq', [(i, i ^ 1) for i in range(seq)])  21.7 us
    pallas_call x1, Pallas kernels, attend_back(): pl.pallas_call(backward_kernel, grid=(streams, PAIRS), in_specs=[specs['q...  13.9 us
    pallas_call x3, Pallas kernels, over_rows(): pl.pallas_call(kernel, in_specs=[pl.BlockSpec(memory_space=pltpu.SMEM)] +...  13 us
    ppermute x16, starting transfers between devices, dp_move(): return lax.ppermute(value, 'dp', [(i, i ^ step) for i in range(dps)])  12.5 us
    pallas_call x1, Pallas kernels, attend(): pl.pallas_call(forward_kernel, grid=(streams, PAIRS), in_specs=[specs['qi...  10.5 us
  transfers between devices with their start and end apart: 46, of which 22 were waited for; matrix products, arithmetic and copies ran while one was open for 6% of the time, Pallas kernels for 17%

profile of v6, /device:TPU:13, one launch (start us, length us, event | category | flops | bytes accessed | tf_op | source)
XLA Modules:
  0.0 256.9 jit_solution(4543172618893810888)
XLA Ops:
  1.3 1.8 first_columns.1
  3.8 0.9 convert_element_type.196
  4.7 1.0 convert_element_type.197
  5.9 1.3 dynamic-slice_reduce_fusion.1
  8.3 1.4 collective-permute-start.3
  9.7 1.1 collective-permute-start.2
  10.8 1.1 collective-permute-start.1
  11.9 6.2 %collective-permute-done.3 = bf16[2,24,1280]{2,1,0:T(8,128)(2,1)S(1)} collective-permute-done((bf16[2,24,1280]{2,1,0:T(8,128)(2,1)S(1)}, bf16[2,24,1280]{2,1,0:T(8,128)(2,1)S(1)}, u32[]{:S(2)}, u32[]{:S(2)}) %collective-permute-start.3) | collective-permute-done | bytes 122912 | tf_op jit(solution)/shard_map/ppermute | solution.py:104
  18.1 1.7 collective-permute-done.2
  20.6 1.2 collective-permute-start.7
  21.8 3.8 %collective-permute-start.10 = (bf16[2,24,3840]{2,1,0:T(8,128)(2,1)S(1)}, bf16[2,24,3840]{2,1,0:T(8,128)(2,1)S(1)}, u32[]{:S(2)}, u32[]{:S(2)}) collective-permute-start(bf16[2,24,3840]{2,1,0:T(8,128)(2,1)S(1)} %pad_maximum_fusion.2), channel_id=1, source_target_pairs={{0,4},{1,5},{2,6},{3,7},{4,0},{5,1},{6,2},{7,3},{8,12},{9,13},{10,... | collective-permute-start | bytes 1105928 | tf_op jit(solution)/shard_map/ppermute | solution.py:104
  25.7 20.1 %collective-permute-done.11 = bf16[2,24,3840]{2,1,0:T(8,128)(2,1)S(1)} collective-permute-done((bf16[2,24,3840]{2,1,0:T(8,128)(2,1)S(1)}, bf16[2,24,3840]{2,1,0:T(8,128)(2,1)S(1)}, u32[]{:S(2)}, u32[]{:S(2)}) %collective-permute-start.11) | collective-permute-done | bytes 368672 | tf_op jit(solution)/shard_map/ppermute | solution.py:104
  45.8 5.6 %collective-permute-done.10 = bf16[2,24,3840]{2,1,0:T(8,128)(2,1)S(1)} collective-permute-done((bf16[2,24,3840]{2,1,0:T(8,128)(2,1)S(1)}, bf16[2,24,3840]{2,1,0:T(8,128)(2,1)S(1)}, u32[]{:S(2)}, u32[]{:S(2)}) %collective-permute-start.10) | collective-permute-done | bytes 368672 | tf_op jit(solution)/shard_map/ppermute | solution.py:104
  51.8 1.2 collective-permute-start.19
  53.0 3.6 %collective-permute-done.18.refs_3_ = bf16[2,2,24,1280]{3,2,1,0:T(8,128)(2,1)S(1)} collective-permute-done((bf16[2,2,24,1280]{3,2,1,0:T(8,128)(2,1)S(1)}, bf16[2,2,24,1280]{3,2,1,0:T(8,128)(2,1)S(1)}, u32[]{:S(2)}, u32[]{:S(2)}) %collective-permute-start.18) | collective-permute-done | bytes 245792 | tf_op jit(solution)/shard_map/ppermute | solution.py:108
  57.1 1.3 collective-permute-start.21
  58.4 1.5 collective-permute-start.20
  60.0 1.6 collective-permute-start.14
  61.5 4.0 %collective-permute-start.13 = (bf16[2,128,768]{2,1,0:T(8,128)(2,1)}, bf16[2,128,768]{2,1,0:T(8,128)(2,1)}, u32[]{:S(2)}, u32[]{:S(2)}) collective-permute-start(bf16[2,128,768]{2,1,0:T(8,128)(2,1)} %refs_0_.2), channel_id=1, source_target_pairs={{0,4},{1,5},{2,6},{3,7},{4,0},{5,1},{6,2},{7,3},{8,12},{9,13},{10,... | collective-permute-start | bytes 1179656 | tf_op jit(solution)/shard_map/ppermute | solution.py:104
  66.8 15.5 %collective-permute-done.14.refs_3_ = bf16[2,128,768]{2,1,0:T(8,128)(2,1)} collective-permute-done((bf16[2,128,768]{2,1,0:T(8,128)(2,1)}, bf16[2,128,768]{2,1,0:T(8,128)(2,1)}, u32[]{:S(2)}, u32[]{:S(2)}) %collective-permute-start.14) | collective-permute-done | bytes 393248 | tf_op jit(solution)/shard_map/ppermute | solution.py:104
  82.2 10.7 %collective-permute-start.17 = (bf16[2,128,768]{2,1,0:T(8,128)(2,1)}, bf16[2,128,768]{2,1,0:T(8,128)(2,1)S(1)}, u32[]{:S(2)}, u32[]{:S(2)}) collective-permute-start(bf16[2,128,768]{2,1,0:T(8,128)(2,1)} %collective-permute-done.14.refs_3_), channel_id=1, source_target_pairs={{0,1},{1,0},{2,3},{3,2},{4,5},{5,4},{6,7},{7,6},{8,9},{9,8},{10,11... | collective-permute-start | bytes 1179656 | tf_op jit(solution)/shard_map/ppermute | solution.py:100
  93.4 3.0 %collective-permute-start.16 = (bf16[2,128,768]{2,1,0:T(8,128)(2,1)}, bf16[2,128,768]{2,1,0:T(8,128)(2,1)S(1)}, u32[]{:S(2)}, u32[]{:S(2)}) collective-permute-start(bf16[2,128,768]{2,1,0:T(8,128)(2,1)} %collective-permute-done.13.refs_2_), channel_id=1, source_target_pairs={{0,1},{1,0},{2,3},{3,2},{4,5},{5,4},{6,7},{7,6},{8,9},{9,8},{10,11... | collective-permute-start | bytes 1179656 | tf_op jit(solution)/shard_map/ppermute | solution.py:100
  96.5 1.2 slice.204
  97.7 1.2 slice.205
  99.5 5.0 %project.1 = (bf16[2,1024,768]{2,1,0:T(8,128)(2,1)S(1)}, bf16[2,1024,768]{2,1,0:T(8,128)(2,1)S(1)}, bf16[2,256,384]{2,1,0:T(8,128)(2,1)S(1)}, bf16[2,256,768]{2,1,0:T(8,128)(2,1)S(1)}) custom-call(s32[3]{0:T(128)S(1)} %copy-done.8, bf16[2,128,768]{2,1,0:T(8,128)(2,1)} %refs_0_.2, bf16[2,128,768]{2,1,0:T(8,128)(2,1)} %collective-permute-done.12.refs_1_, ...), custom_call_target="tpu_custom_call" | custom-call | tf_op jit(solution)/shard_map/project/pallas_call | solution.py:380
  104.6 10.5 %attend.1 = (bf16[2,256,384]{2,1,0:T(8,128)(2,1)S(1)}, f32[2,3,2,256,128]{4,3,2,1,0:T(8,128)S(1)}) custom-call(s32[2,256,128]{2,1,0:T(8,128)S(1)} %broadcast_in_dim.51.qid_ref, s32[2,8,1024]{2,1,0:T(8,128)S(1)} %broadcast_in_dim.52.kid_ref, bf16[2,256,384]{2,1,0:T(8,128)(2,1)S(1)} %get-tuple-element.131.q_ref, ...), custom_call_target="tpu_custom_call" | custom-call | tf_op jit(solution)/shard_map/attend/pallas_call | solution.py:274
  115.1 1.2 copy-done
  116.3 1.1 collective-permute-start.22
  117.4 2.2 place_late.1
  119.6 5.5 %middle.1 = (f32[512,768]{1,0:T(8,128)S(1)}, f32[512,128]{1,0:T(8,128)S(1)}, bf16[512,768]{1,0:T(8,128)(2,1)S(1)}, bf16[512,1536]{1,0:T(8,128)(2,1)S(1)}, bf16[5...) custom-call(s32[3]{0:T(128)S(1)} %copy-done.8, bf16[512,384]{1,0:T(8,128)(2,1)S(1)} %bitcast.96, ...), custom_call_target="tpu_custom_call" | custom-call | tf_op jit(solution)/shard_map/middle/pallas_call | solution.py:533
  125.8 1.9 collective-permute-done.25.refs_1_
  127.7 5.2 %turn.1 = (bf16[256,768]{1,0:T(8,128)(2,1)}, f32[512,768]{1,0:T(8,128)S(1)}, bf16[512,768]{1,0:T(8,128)(2,1)S(1)}, bf16[512,1536]{1,0:T(8,128)(2,1)S(1)}, f32[51...) custom-call(s32[3]{0:T(128)S(1)} %copy-done.8, ...), custom_call_target="tpu_custom_call" | custom-call | tf_op jit(solution)/shard_map/turn/pallas_call | solution.py:533
  133.0 3.6 %wide_packs.1 = (bf16[4,48,3072]{2,1,0:T(8,128)(2,1)S(1)}, bf16[4,48,3072]{2,1,0:T(8,128)(2,1)S(1)}, bf16[4,48,3072]{2,1,0:T(8,128)(2,1)S(1)}, bf16[2,48,3072]{2,1,0:T(8,128)(2,1)S(1)}, bf16[2,48,3072]{2,1,0:T(8,128)(2,1)S(1)}) custom-call(s32[3]{0:T(128)S(1)} %copy-done.8, bf16[512,1536]{1,0:T(8,128)(2,1)S(1)} %get-tuple-element.156.hidden_ref, ...), custom_call_target="tpu_custom_call" | custom-call | tf_op jit(solution)/shard_map/wide_packs/pallas_call | solution.py:547
  136.5 1.3 collective-permute-start.28
  137.8 1.2 collective-permute-start.29
  139.7 1.9 collective-permute-done.26.refs_1_
  141.7 2.3 first_back.1
  143.9 13.9 %attend_back.1 = (bf16[2,256,384]{2,1,0:T(8,128)(2,1)S(1)}, bf16[2,1024,384]{2,1,0:T(8,128)(2,1)S(1)}, bf16[2,1024,384]{2,1,0:T(8,128)(2,1)S(1)}) custom-call(s32[2,256,128]{2,1,0:T(8,128)S(1)} %broadcast_in_dim.51.qid_ref, s32[2,8,1024]{2,1,0:T(8,128)S(1)} %broadcast_in_dim.52.kid_ref, bf16[2,256,384]{2,1,0:T(8,128)(2,1)S(1)} %get-tuple-element.131.q_ref, ...), custom_call_target="tpu_custom_call" | custom-call | tf_op jit(solution)/shard_map/attend_back/pallas_call | solution.py:295
  157.8 4.1 %unproject.1 = (bf16[4,2,128,768]{3,2,1,0:T(8,128)(2,1)S(1)}, bf16[4,2,128,768]{3,2,1,0:T(8,128)(2,1)S(1)}) custom-call(s32[3]{0:T(128)S(1)} %copy-done.8, bf16[2,256,384]{2,1,0:T(8,128)(2,1)S(1)} %get-tuple-element.151.query_ref, bf16[2,1024,384]{2,1,0:T(8,128)(2,1)S(1)} %get-tuple-element.152.key_ref, ...), custom_call_target="tpu_custom_call" | custom-call | tf_op jit(solution)/shard_map/unproject/pallas_call | solution.py:419
  162.4 1.4 collective-permute-done.28
  163.8 1.1 collective-permute-done.29
  165.1 1.3 collective-permute-start.32
  167.3 3.2 %collective-permute-start.36 = (bf16[2,2,128,768]{3,2,1,0:T(8,128)(2,1)S(1)}, bf16[2,2,128,768]{3,2,1,0:T(8,128)(2,1)S(1)}, u32[]{:S(2)}, u32[]{:S(2)}) collective-permute-start(bf16[2,2,128,768]{3,2,1,0:T(8,128)(2,1)S(1)} %slice.342), channel_id=1, source_target_pairs={{0,4},{1,5},{2,6},{3,7},{4,0},{5,1},{6,2},{7,3},{8,12},{9,13},{10,... | collective-permute-start | bytes 2359304 | tf_op jit(solution)/shard_map/ppermute | solution.py:104
  170.5 5.3 %narrow_packs.1 = (bf16[4,48,1664]{2,1,0:T(8,128)(2,1)S(1)}, bf16[4,48,1664]{2,1,0:T(8,128)(2,1)S(1)}, bf16[4,48,1664]{2,1,0:T(8,128)(2,1)S(1)}, bf16[2,48,1664]...) custom-call(s32[3]{0:T(128)S(1)} %copy-done.8, bf16[2048,768]{1,0:T(8,128)(2,1)S(1)} %bitcast.93, bf16[512,768]{1,0:T(8,128)(2,1)S(1)} %bitcast.95, ...), custom_call_target="tpu_custom_call" | custom-call | tf_op jit(solution)/shard_map/narrow_packs/pallas_call | solution.py:547
  175.8 1.2 collective-permute-start.30
  177.2 1.5 collective-permute-done.32
  178.7 1.2 collective-permute-done.33
  180.4 13.1 %collective-permute-done.30 = bf16[4,48,1664]{2,1,0:T(8,128)(2,1)S(1)} collective-permute-done((bf16[4,48,1664]{2,1,0:T(8,128)(2,1)S(1)}, bf16[4,48,1664]{2,1,0:T(8,128)(2,1)S(1)}, u32[]{:S(2)}, u32[]{:S(2)}) %collective-permute-start.30) | collective-permute-done | bytes 639008 | tf_op jit(solution)/shard_map/ppermute | solution.py:108
  194.5 8.7 %collective-permute-done.36 = bf16[2,2,128,768]{3,2,1,0:T(8,128)(2,1)S(1)} collective-permute-done((bf16[2,2,128,768]{3,2,1,0:T(8,128)(2,1)S(1)}, bf16[2,2,128,768]{3,2,1,0:T(8,128)(2,1)S(1)}, u32[]{:S(2)}, u32[]{:S(2)}) %collective-permute-start.36) | collective-permute-done | bytes 786464 | tf_op jit(solution)/shard_map/ppermute | solution.py:104
  203.4 3.4 %collective-permute-start.38 = (bf16[48,3072]{1,0:T(8,128)(2,1)S(1)}, bf16[48,3072]{1,0:T(8,128)(2,1)S(1)}, u32[]{:S(2)}, u32[]{:S(2)}) collective-permute-start(bf16[48,3072]{1,0:T(8,128)(2,1)S(1)} %get-tuple-element.186), channel_id=1, source_target_pairs={{0,2},{1,3},{2,0},{3,1},{4,6},{5,7},{6,4},{7,5},{8,10},{9,11},{10,... | collective-permute-start | bytes 884744 | tf_op jit(solution)/shard_map/ppermute | solution.py:104
  206.9 1.3 collective-permute-start.40
  208.1 2.3 collective-permute-start.37
  210.7 6.9 %collective-permute-done.38 = bf16[48,3072]{1,0:T(8,128)(2,1)S(1)} collective-permute-done((bf16[48,3072]{1,0:T(8,128)(2,1)S(1)}, bf16[48,3072]{1,0:T(8,128)(2,1)S(1)}, u32[]{:S(2)}, u32[]{:S(2)}) %collective-permute-start.38) | collective-permute-done | bytes 294944 | tf_op jit(solution)/shard_map/ppermute | solution.py:104
  217.6 2.3 collective-permute-done.39
  219.9 13.9 %collective-permute-done.40 = bf16[48,3072]{1,0:T(8,128)(2,1)S(1)} collective-permute-done((bf16[48,3072]{1,0:T(8,128)(2,1)S(1)}, bf16[48,3072]{1,0:T(8,128)(2,1)S(1)}, u32[]{:S(2)}, u32[]{:S(2)}) %collective-permute-start.40) | collective-permute-done | bytes 294944 | tf_op jit(solution)/shard_map/ppermute | solution.py:104
  233.9 1.0 collective-permute-done.37
  235.0 1.1 collective-permute-start.41
  236.3 1.5 collective-permute-start.43
  237.8 1.9 collective-permute-start.45
  239.7 1.0 bitcast_add_fusion
  243.2 1.2 select_n.94
  244.4 7.0 %collective-permute-done.43 = bf16[48,1664]{1,0:T(8,128)(2,1)S(1)} collective-permute-done((bf16[48,1664]{1,0:T(8,128)(2,1)S(1)}, bf16[48,1664]{1,0:T(8,128)(2,1)S(1)}, u32[]{:S(2)}, u32[]{:S(2)}) %collective-permute-start.43) | collective-permute-done | bytes 159776 | tf_op jit(solution)/shard_map/ppermute | solution.py:104
  251.6 1.8 collective-permute-start.44
  254.0 0.8 slice_reduce_fusion
  (135 shorter events, 17.6 us)
Async XLA Ops:
  0.7 7.5 %copy-start.2 = (bf16[2,128,768]{2,1,0:T(8,128)(2,1)S(1)}, bf16[2,128,768]{2,1,0:T(8,128)(2,1)}, u32[]{:S(2)}) copy-start(bf16[2,128,768]{2,1,0:T(8,128)(2,1)} %param.35) | copy-start | bytes 1179652
  0.7 7.5 %copy-start.9 = (f32[96,768]{1,0:T(8,128)S(1)}, f32[96,768]{1,0:T(8,128)}, u32[]{:S(2)}) copy-start(f32[96,768]{1,0:T(8,128)} %param.30) | copy-start | bytes 884740
  3.1 5.2 %copy-start.10 = (bf16[24,1280]{1,0:T(8,128)(2,1)S(1)}, bf16[24,1280]{1,0:T(8,128)(2,1)}, u32[]{:S(2)}) copy-start(bf16[24,1280]{1,0:T(8,128)(2,1)} %get-tuple-element.106) | copy-start | bytes 184324
  3.1 5.1 %collective-permute-start = (bf16[24,1280]{1,0:T(8,128)(2,1)}, bf16[24,1280]{1,0:T(8,128)(2,1)S(1)}, u32[]{:S(2)}, u32[]{:S(2)}) collective-permute-start(bf16[24,1280]{1,0:T(8,128)(2,1)} %get-tuple-element.107), channel_id=1, source_target_pairs={{0,1},{1,0},{2,3},{3,2},{4,5},{5,4},{6,7},{7,6},{8,9},{9,8},{10,11... | collective-permute-start | bytes 184328 | tf_op jit(solution)/shard_map/ppermute | solution.py:100
  7.6 3.2 %collective-permute-start.4 = (bf16[24,2304]{1,0:T(8,128)(2,1)S(1)}, bf16[24,2304]{1,0:T(8,128)(2,1)S(1)}, u32[]{:S(2)}, u32[]{:S(2)}) collective-permute-start(bf16[24,2304]{1,0:T(8,128)(2,1)S(1)} %get-tuple-element.228), channel_id=1, source_target_pairs={{0,1},{1,0},{2,3},{3,2},{4,5},{5,4},{6,7},{7,6},{8,9},{9,8},{10,11... | collective-permute-start | bytes 331784 | tf_op jit(solution)/shard_map/ppermute | solution.py:100
  7.6 12.5 %collective-permute-start.5 = (bf16[2,128,768]{2,1,0:T(8,128)(2,1)}, bf16[2,128,768]{2,1,0:T(8,128)(2,1)S(1)}, u32[]{:S(2)}, u32[]{:S(2)}) collective-permute-start(bf16[2,128,768]{2,1,0:T(8,128)(2,1)} %refs_0_.2), channel_id=1, source_target_pairs={{0,1},{1,0},{2,3},{3,2},{4,5},{5,4},{6,7},{7,6},{8,9},{9,8},{10,11... | collective-permute-start | bytes 1179656 | tf_op jit(solution)/shard_map/ppermute | solution.py:100
  8.1 12.1 %collective-permute-start.6 = (bf16[2,128,768]{2,1,0:T(8,128)(2,1)S(1)}, bf16[2,128,768]{2,1,0:T(8,128)(2,1)S(1)}, u32[]{:S(2)}, u32[]{:S(2)}) collective-permute-start(bf16[2,128,768]{2,1,0:T(8,128)(2,1)S(1)} %copy-done.2), channel_id=1, source_target_pairs={{0,1},{1,0},{2,3},{3,2},{4,5},{5,4},{6,7},{7,6},{8,9},{9,8},{10,11... | collective-permute-start | bytes 1179656 | tf_op jit(solution)/shard_map/ppermute | solution.py:100
  8.3 9.8 %collective-permute-start.3 = (bf16[2,24,1280]{2,1,0:T(8,128)(2,1)S(1)}, bf16[2,24,1280]{2,1,0:T(8,128)(2,1)S(1)}, u32[]{:S(2)}, u32[]{:S(2)}) collective-permute-start(bf16[2,24,1280]{2,1,0:T(8,128)(2,1)S(1)} %maximum_select_fusion.2), channel_id=1, source_target_pairs={{0,6},{1,7},{2,4},{3,5},{4,2},{5,3},{6,0},{7,1},{8,14},{9,15},{10,... | collective-permute-start | bytes 368648 | tf_op jit(solution)/shard_map/ppermute | solution.py:104
  9.7 10.2 %collective-permute-start.2 = (bf16[2,24,1280]{2,1,0:T(8,128)(2,1)S(1)}, bf16[2,24,1280]{2,1,0:T(8,128)(2,1)S(1)}, u32[]{:S(2)}, u32[]{:S(2)}) collective-permute-start(bf16[2,24,1280]{2,1,0:T(8,128)(2,1)S(1)} %maximum_select_fusion.2), channel_id=1, source_target_pairs={{0,4},{1,5},{2,6},{3,7},{4,0},{5,1},{6,2},{7,3},{8,12},{9,13},{10,... | collective-permute-start | bytes 368648 | tf_op jit(solution)/shard_map/ppermute | solution.py:104
  10.8 9.4 %collective-permute-start.1 = (bf16[2,24,1280]{2,1,0:T(8,128)(2,1)S(1)}, bf16[2,24,1280]{2,1,0:T(8,128)(2,1)S(1)}, u32[]{:S(2)}, u32[]{:S(2)}) collective-permute-start(bf16[2,24,1280]{2,1,0:T(8,128)(2,1)S(1)} %maximum_select_fusion.2), channel_id=1, source_target_pairs={{0,2},{1,3},{2,0},{3,1},{4,6},{5,7},{6,4},{7,5},{8,10},{9,11},{10,... | collective-permute-start | bytes 368648 | tf_op jit(solution)/shard_map/ppermute | solution.py:104
  20.2 36.9 %copy-start.6 = (bf16[2,128,768]{2,1,0:T(8,128)(2,1)}, bf16[2,128,768]{2,1,0:T(8,128)(2,1)S(1)}, u32[]{:S(2)}) copy-start(bf16[2,128,768]{2,1,0:T(8,128)(2,1)S(1)} %collective-permute-done.5.refs_4_) | copy-start | bytes 1179652
  20.2 36.9 %copy-start.4 = (bf16[2,128,768]{2,1,0:T(8,128)(2,1)}, bf16[2,128,768]{2,1,0:T(8,128)(2,1)S(1)}, u32[]{:S(2)}) copy-start(bf16[2,128,768]{2,1,0:T(8,128)(2,1)S(1)} %collective-permute-done.6) | copy-start | bytes 1179652
  20.3 31.1 %collective-permute-start.8 = (bf16[4,2,24,1280]{3,2,1,0:T(8,128)(2,1)S(1)}, bf16[4,2,24,1280]{3,2,1,0:T(8,128)(2,1)S(1)}, u32[]{:S(2)}, u32[]{:S(2)}) collective-permute-start(bf16[4,2,24,1280]{3,2,1,0:T(8,128)(2,1)S(1)} %pad_maximum_fusion.1.refs_0_), channel_id=1, source_target_pairs={{0,16},{8,24},{16,0},{24,8},{1,17},{9,25},{17,1},{25,9},{2,18},{10... | collective-permute-start | bytes 1474568 | tf_op jit(solution)/shard_map/ppermute | solution.py:108
  20.6 30.9 %collective-permute-start.7 = (bf16[4,2,24,1280]{3,2,1,0:T(8,128)(2,1)S(1)}, bf16[4,2,24,1280]{3,2,1,0:T(8,128)(2,1)S(1)}, u32[]{:S(2)}, u32[]{:S(2)}) collective-permute-start(bf16[4,2,24,1280]{3,2,1,0:T(8,128)(2,1)S(1)} %pad_maximum_fusion.1.refs_0_), channel_id=1, source_target_pairs={{0,8},{8,0},{16,24},{24,16},{1,9},{9,1},{17,25},{25,17},{2,10},{10... | collective-permute-start | bytes 1474568 | tf_op jit(solution)/shard_map/ppermute | solution.py:108
  21.8 24.0 %collective-permute-start.11 = (bf16[2,24,3840]{2,1,0:T(8,128)(2,1)S(1)}, bf16[2,24,3840]{2,1,0:T(8,128)(2,1)S(1)}, u32[]{:S(2)}, u32[]{:S(2)}) collective-permute-start(bf16[2,24,3840]{2,1,0:T(8,128)(2,1)S(1)} %pad_maximum_fusion.2), channel_id=1, source_target_pairs={{0,6},{1,7},{2,4},{3,5},{4,2},{5,3},{6,0},{7,1},{8,14},{9,15},{10,... | collective-permute-start | bytes 1105928 | tf_op jit(solution)/shard_map/ppermute | solution.py:104
  21.8 29.6 %collective-permute-start.10 = (bf16[2,24,3840]{2,1,0:T(8,128)(2,1)S(1)}, bf16[2,24,3840]{2,1,0:T(8,128)(2,1)S(1)}, u32[]{:S(2)}, u32[]{:S(2)}) collective-permute-start(bf16[2,24,3840]{2,1,0:T(8,128)(2,1)S(1)} %pad_maximum_fusion.2), channel_id=1, source_target_pairs={{0,4},{1,5},{2,6},{3,7},{4,0},{5,1},{6,2},{7,3},{8,12},{9,13},{10,... | collective-permute-start | bytes 1105928 | tf_op jit(solution)/shard_map/ppermute | solution.py:104
  25.6 25.8 %collective-permute-start.9 = (bf16[2,24,3840]{2,1,0:T(8,128)(2,1)S(1)}, bf16[2,24,3840]{2,1,0:T(8,128)(2,1)S(1)}, u32[]{:S(2)}, u32[]{:S(2)}) collective-permute-start(bf16[2,24,3840]{2,1,0:T(8,128)(2,1)S(1)} %pad_maximum_fusion.2), channel_id=1, source_target_pairs={{0,2},{1,3},{2,0},{3,1},{4,6},{5,7},{6,4},{7,5},{8,10},{9,11},{10,... | collective-permute-start | bytes 1105928 | tf_op jit(solution)/shard_map/ppermute | solution.py:104
  51.5 14.1 %copy-start.8 = (s32[3]{0:T(128)S(1)}, s32[3]{0:T(128)}, u32[]{:S(2)}) copy-start(s32[3]{0:T(128)} %pad_add_fusion.place_ref) | copy-start | bytes 40
  51.5 5.1 %collective-permute-start.18 = (bf16[2,2,24,1280]{3,2,1,0:T(8,128)(2,1)S(1)}, bf16[2,2,24,1280]{3,2,1,0:T(8,128)(2,1)S(1)}, u32[]{:S(2)}, u32[]{:S(2)}) collective-permute-start(bf16[2,2,24,1280]{3,2,1,0:T(8,128)(2,1)S(1)} %slice.200), channel_id=1, source_target_pairs={{0,8},{8,0},{16,24},{24,16},{1,9},{9,1},{17,25},{25,17},{2,10},{10... | collective-permute-start | bytes 737288 | tf_op jit(solution)/shard_map/ppermute | solution.py:108
  51.8 5.0 %collective-permute-start.19 = (bf16[2,2,24,1280]{3,2,1,0:T(8,128)(2,1)S(1)}, bf16[2,2,24,1280]{3,2,1,0:T(8,128)(2,1)S(1)}, u32[]{:S(2)}, u32[]{:S(2)}) collective-permute-start(bf16[2,2,24,1280]{3,2,1,0:T(8,128)(2,1)S(1)} %slice.201), channel_id=1, source_target_pairs={{0,16},{8,24},{16,0},{24,8},{1,17},{9,25},{17,1},{25,9},{2,18},{10... | collective-permute-start | bytes 737288 | tf_op jit(solution)/shard_map/ppermute | solution.py:108
  57.1 39.4 %collective-permute-start.21 = (bf16[4,2,24,3840]{3,2,1,0:T(8,128)(2,1)S(1)}, bf16[4,2,24,3840]{3,2,1,0:T(8,128)(2,1)}, u32[]{:S(2)}, u32[]{:S(2)}) collective-permute-start(bf16[4,2,24,3840]{3,2,1,0:T(8,128)(2,1)S(1)} %pad_maximum_fusion.refs_0_), channel_id=1, source_target_pairs={{0,16},{8,24},{16,0},{24,8},{1,17},{9,25},{17,1},{25,9},{2,18},{10... | collective-permute-start | bytes 4423688 | tf_op jit(solution)/shard_map/ppermute | solution.py:108
  58.4 38.1 %collective-permute-start.20 = (bf16[4,2,24,3840]{3,2,1,0:T(8,128)(2,1)S(1)}, bf16[4,2,24,3840]{3,2,1,0:T(8,128)(2,1)}, u32[]{:S(2)}, u32[]{:S(2)}) collective-permute-start(bf16[4,2,24,3840]{3,2,1,0:T(8,128)(2,1)S(1)} %pad_maximum_fusion.refs_0_), channel_id=1, source_target_pairs={{0,8},{8,0},{16,24},{24,16},{1,9},{9,1},{17,25},{25,17},{2,10},{10... | collective-permute-start | bytes 4423688 | tf_op jit(solution)/shard_map/ppermute | solution.py:108
  60.0 22.3 %collective-permute-start.14 = (bf16[2,128,768]{2,1,0:T(8,128)(2,1)}, bf16[2,128,768]{2,1,0:T(8,128)(2,1)}, u32[]{:S(2)}, u32[]{:S(2)}) collective-permute-start(bf16[2,128,768]{2,1,0:T(8,128)(2,1)} %refs_0_.2), channel_id=1, source_target_pairs={{0,6},{1,7},{2,4},{3,5},{4,2},{5,3},{6,0},{7,1},{8,14},{9,15},{10,... | collective-permute-start | bytes 1179656 | tf_op jit(solution)/shard_map/ppermute | solution.py:104
  61.5 31.9 %collective-permute-start.13 = (bf16[2,128,768]{2,1,0:T(8,128)(2,1)}, bf16[2,128,768]{2,1,0:T(8,128)(2,1)}, u32[]{:S(2)}, u32[]{:S(2)}) collective-permute-start(bf16[2,128,768]{2,1,0:T(8,128)(2,1)} %refs_0_.2), channel_id=1, source_target_pairs={{0,4},{1,5},{2,6},{3,7},{4,0},{5,1},{6,2},{7,3},{8,12},{9,13},{10,... | collective-permute-start | bytes 1179656 | tf_op jit(solution)/shard_map/ppermute | solution.py:104
  65.5 30.9 %collective-permute-start.12 = (bf16[2,128,768]{2,1,0:T(8,128)(2,1)}, bf16[2,128,768]{2,1,0:T(8,128)(2,1)}, u32[]{:S(2)}, u32[]{:S(2)}) collective-permute-start(bf16[2,128,768]{2,1,0:T(8,128)(2,1)} %refs_0_.2), channel_id=1, source_target_pairs={{0,2},{1,3},{2,0},{3,1},{4,6},{5,7},{6,4},{7,5},{8,10},{9,11},{10,... | collective-permute-start | bytes 1179656 | tf_op jit(solution)/shard_map/ppermute | solution.py:104
  66.6 32.5 %copy-start.11 = (s32[2,64]{1,0:T(2,128)S(1)}, s32[2,64]{1,0:T(2,128)}, u32[]{:S(2)}) copy-start(s32[2,64]{1,0:T(2,128)} %param.34) | copy-start | bytes 1540
  66.8 32.7 %copy-start.7 = (bf16[2,128,768]{2,1,0:T(8,128)(2,1)S(1)}, bf16[2,128,768]{2,1,0:T(8,128)(2,1)}, u32[]{:S(2)}) copy-start(bf16[2,128,768]{2,1,0:T(8,128)(2,1)} %copy-done.6) | copy-start | bytes 1179652
  82.2 17.2 %collective-permute-start.17 = (bf16[2,128,768]{2,1,0:T(8,128)(2,1)}, bf16[2,128,768]{2,1,0:T(8,128)(2,1)S(1)}, u32[]{:S(2)}, u32[]{:S(2)}) collective-permute-start(bf16[2,128,768]{2,1,0:T(8,128)(2,1)} %collective-permute-done.14.refs_3_), channel_id=1, source_target_pairs={{0,1},{1,0},{2,3},{3,2},{4,5},{5,4},{6,7},{7,6},{8,9},{9,8},{10,11... | collective-permute-start | bytes 1179656 | tf_op jit(solution)/shard_map/ppermute | solution.py:100
  93.4 6.0 %collective-permute-start.16 = (bf16[2,128,768]{2,1,0:T(8,128)(2,1)}, bf16[2,128,768]{2,1,0:T(8,128)(2,1)S(1)}, u32[]{:S(2)}, u32[]{:S(2)}) collective-permute-start(bf16[2,128,768]{2,1,0:T(8,128)(2,1)} %collective-permute-done.13.refs_2_), channel_id=1, source_target_pairs={{0,1},{1,0},{2,3},{3,2},{4,5},{5,4},{6,7},{7,6},{8,9},{9,8},{10,11... | collective-permute-start | bytes 1179656 | tf_op jit(solution)/shard_map/ppermute | solution.py:100
  96.5 3.0 %collective-permute-start.15 = (bf16[2,128,768]{2,1,0:T(8,128)(2,1)}, bf16[2,128,768]{2,1,0:T(8,128)(2,1)S(1)}, u32[]{:S(2)}, u32[]{:S(2)}) collective-permute-start(bf16[2,128,768]{2,1,0:T(8,128)(2,1)} %collective-permute-done.12.refs_1_), channel_id=1, source_target_pairs={{0,1},{1,0},{2,3},{3,2},{4,5},{5,4},{6,7},{7,6},{8,9},{9,8},{10,11... | collective-permute-start | bytes 1179656 | tf_op jit(solution)/shard_map/ppermute | solution.py:100
  98.8 18.5 %collective-permute-start.24 = (bf16[2,2,24,3840]{3,2,1,0:T(8,128)(2,1)S(1)}, bf16[2,2,24,3840]{3,2,1,0:T(8,128)(2,1)S(1)}, u32[]{:S(2)}, u32[]{:S(2)}) collective-permute-start(bf16[2,2,24,3840]{3,2,1,0:T(8,128)(2,1)S(1)} %slice.205), channel_id=1, source_target_pairs={{0,16},{8,24},{16,0},{24,8},{1,17},{9,25},{17,1},{25,9},{2,18},{10... | collective-permute-start | bytes 2211848 | tf_op jit(solution)/shard_map/ppermute | solution.py:108
  99.1 18.2 %collective-permute-start.23 = (bf16[2,2,24,3840]{3,2,1,0:T(8,128)(2,1)S(1)}, bf16[2,2,24,3840]{3,2,1,0:T(8,128)(2,1)S(1)}, u32[]{:S(2)}, u32[]{:S(2)}) collective-permute-start(bf16[2,2,24,3840]{3,2,1,0:T(8,128)(2,1)S(1)} %slice.204), channel_id=1, source_target_pairs={{0,8},{8,0},{16,24},{24,16},{1,9},{9,1},{17,25},{25,17},{2,10},{10... | collective-permute-start | bytes 2211848 | tf_op jit(solution)/shard_map/ppermute | solution.py:108
  115.1 1.2 copy-start
  116.3 3.3 %collective-permute-start.22 = (bf16[2,256,384]{2,1,0:T(8,128)(2,1)S(1)}, bf16[2,256,384]{2,1,0:T(8,128)(2,1)S(1)}, u32[]{:S(2)}, u32[]{:S(2)}) collective-permute-start(bf16[2,256,384]{2,1,0:T(8,128)(2,1)S(1)} %get-tuple-element.133), channel_id=1, source_target_pairs={{0,1},{1,0},{2,3},{3,2},{4,5},{5,4},{6,7},{7,6},{8,9},{9,8},{10,11... | collective-permute-start | bytes 1179656 | tf_op jit(solution)/shard_map/ppermute | solution.py:100
  119.6 8.1 %copy-start.3 = (bf16[2,128,768]{2,1,0:T(8,128)(2,1)S(1)}, bf16[2,128,768]{2,1,0:T(8,128)(2,1)}, u32[]{:S(2)}) copy-start(bf16[2,128,768]{2,1,0:T(8,128)(2,1)} %param.35) | copy-start | bytes 1179652
  119.6 8.1 %copy-start.5 = (bf16[2,128,768]{2,1,0:T(8,128)(2,1)S(1)}, bf16[2,128,768]{2,1,0:T(8,128)(2,1)}, u32[]{:S(2)}) copy-start(bf16[2,128,768]{2,1,0:T(8,128)(2,1)} %copy-done.4) | copy-start | bytes 1179652
  125.1 2.6 %collective-permute-start.25 = (bf16[512,768]{1,0:T(8,128)(2,1)S(1)}, bf16[512,768]{1,0:T(8,128)(2,1)S(1)}, u32[]{:S(2)}, u32[]{:S(2)}) collective-permute-start(bf16[512,768]{1,0:T(8,128)(2,1)S(1)} %get-tuple-element.139), channel_id=1, source_target_pairs={{0,1},{1,0},{2,3},{3,2},{4,5},{5,4},{6,7},{7,6},{8,9},{9,8},{10,11... | collective-permute-start | bytes 2359304 | tf_op jit(solution)/shard_map/ppermute | solution.py:100
  136.5 27.3 %collective-permute-start.28 = (bf16[4,48,3072]{2,1,0:T(8,128)(2,1)S(1)}, bf16[4,48,3072]{2,1,0:T(8,128)(2,1)S(1)}, u32[]{:S(2)}, u32[]{:S(2)}) collective-permute-start(bf16[4,48,3072]{2,1,0:T(8,128)(2,1)S(1)} %get-tuple-element.161), channel_id=1, source_target_pairs={{0,8},{8,0},{16,24},{24,16},{1,9},{9,1},{17,25},{25,17},{2,10},{10... | collective-permute-start | bytes 3538952 | tf_op jit(solution)/shard_map/ppermute | solution.py:108
  137.8 27.1 %collective-permute-start.29 = (bf16[4,48,3072]{2,1,0:T(8,128)(2,1)S(1)}, bf16[4,48,3072]{2,1,0:T(8,128)(2,1)S(1)}, u32[]{:S(2)}, u32[]{:S(2)}) collective-permute-start(bf16[4,48,3072]{2,1,0:T(8,128)(2,1)S(1)} %get-tuple-element.162), channel_id=1, source_target_pairs={{0,16},{8,24},{16,0},{24,8},{1,17},{9,25},{17,1},{25,9},{2,18},{10... | collective-permute-start | bytes 3538952 | tf_op jit(solution)/shard_map/ppermute | solution.py:108
  139.0 2.6 %collective-permute-start.26 = (bf16[512,768]{1,0:T(8,128)(2,1)S(1)}, bf16[512,768]{1,0:T(8,128)(2,1)S(1)}, u32[]{:S(2)}, u32[]{:S(2)}) collective-permute-start(bf16[512,768]{1,0:T(8,128)(2,1)S(1)} %get-tuple-element.144), channel_id=1, source_target_pairs={{0,1},{1,0},{2,3},{3,2},{4,5},{5,4},{6,7},{7,6},{8,9},{9,8},{10,11... | collective-permute-start | bytes 2359304 | tf_op jit(solution)/shard_map/ppermute | solution.py:100
  141.7 2.3 copy-start.1
  161.9 5.0 %collective-permute-start.27 = (bf16[4,2,128,768]{3,2,1,0:T(8,128)(2,1)S(1)}, bf16[4,2,128,768]{3,2,1,0:T(8,128)(2,1)S(1)}, u32[]{:S(2)}, u32[]{:S(2)}) collective-permute-start(bf16[4,2,128,768]{3,2,1,0:T(8,128)(2,1)S(1)} %get-tuple-element.155), channel_id=1, source_target_pairs={{0,1},{1,0},{2,3},{3,2},{4,5},{5,4},{6,7},{7,6},{8,9},{9,8},{10,11... | collective-permute-start | bytes 4718600 | tf_op jit(solution)/shard_map/ppermute | solution.py:100
  165.1 13.6 %collective-permute-start.32 = (bf16[2,48,3072]{2,1,0:T(8,128)(2,1)S(1)}, bf16[2,48,3072]{2,1,0:T(8,128)(2,1)S(1)}, u32[]{:S(2)}, u32[]{:S(2)}) collective-permute-start(bf16[2,48,3072]{2,1,0:T(8,128)(2,1)S(1)} %add_convert_fusion.1), channel_id=1, source_target_pairs={{0,16},{8,24},{16,0},{24,8},{1,17},{9,25},{17,1},{25,9},{2,18},{10... | collective-permute-start | bytes 1769480 | tf_op jit(solution)/shard_map/ppermute | solution.py:108
  166.5 13.3 %collective-permute-start.33 = (bf16[2,48,3072]{2,1,0:T(8,128)(2,1)S(1)}, bf16[2,48,3072]{2,1,0:T(8,128)(2,1)S(1)}, u32[]{:S(2)}, u32[]{:S(2)}) collective-permute-start(bf16[2,48,3072]{2,1,0:T(8,128)(2,1)S(1)} %add_convert_fusion), channel_id=1, source_target_pairs={{0,8},{8,0},{16,24},{24,16},{1,9},{9,1},{17,25},{25,17},{2,10},{10... | collective-permute-start | bytes 1769480 | tf_op jit(solution)/shard_map/ppermute | solution.py:108
  167.3 35.8 %collective-permute-start.36 = (bf16[2,2,128,768]{3,2,1,0:T(8,128)(2,1)S(1)}, bf16[2,2,128,768]{3,2,1,0:T(8,128)(2,1)S(1)}, u32[]{:S(2)}, u32[]{:S(2)}) collective-permute-start(bf16[2,2,128,768]{3,2,1,0:T(8,128)(2,1)S(1)} %slice.342), channel_id=1, source_target_pairs={{0,4},{1,5},{2,6},{3,7},{4,0},{5,1},{6,2},{7,3},{8,12},{9,13},{10,... | collective-permute-start | bytes 2359304 | tf_op jit(solution)/shard_map/ppermute | solution.py:104
  175.8 17.8 %collective-permute-start.30 = (bf16[4,48,1664]{2,1,0:T(8,128)(2,1)S(1)}, bf16[4,48,1664]{2,1,0:T(8,128)(2,1)S(1)}, u32[]{:S(2)}, u32[]{:S(2)}) collective-permute-start(bf16[4,48,1664]{2,1,0:T(8,128)(2,1)S(1)} %get-tuple-element.176), channel_id=1, source_target_pairs={{0,8},{8,0},{16,24},{24,16},{1,9},{9,1},{17,25},{25,17},{2,10},{10... | collective-permute-start | bytes 1916936 | tf_op jit(solution)/shard_map/ppermute | solution.py:108
  177.0 16.5 %collective-permute-start.31 = (bf16[4,48,1664]{2,1,0:T(8,128)(2,1)S(1)}, bf16[4,48,1664]{2,1,0:T(8,128)(2,1)S(1)}, u32[]{:S(2)}, u32[]{:S(2)}) collective-permute-start(bf16[4,48,1664]{2,1,0:T(8,128)(2,1)S(1)} %get-tuple-element.177), channel_id=1, source_target_pairs={{0,16},{8,24},{16,0},{24,8},{1,17},{9,25},{17,1},{25,9},{2,18},{10... | collective-permute-start | bytes 1916936 | tf_op jit(solution)/shard_map/ppermute | solution.py:108
  193.6 14.5 %collective-permute-start.34 = (bf16[2,48,1664]{2,1,0:T(8,128)(2,1)S(1)}, bf16[2,48,1664]{2,1,0:T(8,128)(2,1)S(1)}, u32[]{:S(2)}, u32[]{:S(2)}) collective-permute-start(bf16[2,48,1664]{2,1,0:T(8,128)(2,1)S(1)} %add_convert_fusion.3), channel_id=1, source_target_pairs={{0,16},{8,24},{16,0},{24,8},{1,17},{9,25},{17,1},{25,9},{2,18},{10... | collective-permute-start | bytes 958472 | tf_op jit(solution)/shard_map/ppermute | solution.py:108
  194.0 16.4 %collective-permute-start.35 = (bf16[2,48,1664]{2,1,0:T(8,128)(2,1)S(1)}, bf16[2,48,1664]{2,1,0:T(8,128)(2,1)S(1)}, u32[]{:S(2)}, u32[]{:S(2)}) collective-permute-start(bf16[2,48,1664]{2,1,0:T(8,128)(2,1)S(1)} %add_convert_fusion.2), channel_id=1, source_target_pairs={{0,8},{8,0},{16,24},{24,16},{1,9},{9,1},{17,25},{25,17},{2,10},{10... | collective-permute-start | bytes 958472 | tf_op jit(solution)/shard_map/ppermute | solution.py:108
  203.4 14.2 %collective-permute-start.38 = (bf16[48,3072]{1,0:T(8,128)(2,1)S(1)}, bf16[48,3072]{1,0:T(8,128)(2,1)S(1)}, u32[]{:S(2)}, u32[]{:S(2)}) collective-permute-start(bf16[48,3072]{1,0:T(8,128)(2,1)S(1)} %get-tuple-element.186), channel_id=1, source_target_pairs={{0,2},{1,3},{2,0},{3,1},{4,6},{5,7},{6,4},{7,5},{8,10},{9,11},{10,... | collective-permute-start | bytes 884744 | tf_op jit(solution)/shard_map/ppermute | solution.py:104
  206.9 13.0 %collective-permute-start.39 = (bf16[48,3072]{1,0:T(8,128)(2,1)S(1)}, bf16[48,3072]{1,0:T(8,128)(2,1)S(1)}, u32[]{:S(2)}, u32[]{:S(2)}) collective-permute-start(bf16[48,3072]{1,0:T(8,128)(2,1)S(1)} %get-tuple-element.187), channel_id=1, source_target_pairs={{0,4},{1,5},{2,6},{3,7},{4,0},{5,1},{6,2},{7,3},{8,12},{9,13},{10,... | collective-permute-start | bytes 884744 | tf_op jit(solution)/shard_map/ppermute | solution.py:104
  206.9 26.9 %collective-permute-start.40 = (bf16[48,3072]{1,0:T(8,128)(2,1)S(1)}, bf16[48,3072]{1,0:T(8,128)(2,1)S(1)}, u32[]{:S(2)}, u32[]{:S(2)}) collective-permute-start(bf16[48,3072]{1,0:T(8,128)(2,1)S(1)} %get-tuple-element.188), channel_id=1, source_target_pairs={{0,6},{1,7},{2,4},{3,5},{4,2},{5,3},{6,0},{7,1},{8,14},{9,15},{10,... | collective-permute-start | bytes 884744 | tf_op jit(solution)/shard_map/ppermute | solution.py:104
  208.1 26.8 %collective-permute-start.37 = (bf16[1,2,128,768]{3,2,1,0:T(8,128)(2,1)S(1)}, bf16[1,2,128,768]{3,2,1,0:T(8,128)(2,1)S(1)}, u32[]{:S(2)}, u32[]{:S(2)}) collective-permute-start(bf16[1,2,128,768]{3,2,1,0:T(8,128)(2,1)S(1)} %slice.343), channel_id=1, source_target_pairs={{0,2},{1,3},{2,0},{3,1},{4,6},{5,7},{6,4},{7,5},{8,10},{9,11},{10,... | collective-permute-start | bytes 1179656 | tf_op jit(solution)/shard_map/ppermute | solution.py:104
  235.0 9.4 %collective-permute-start.41 = (bf16[48,1664]{1,0:T(8,128)(2,1)S(1)}, bf16[48,1664]{1,0:T(8,128)(2,1)S(1)}, u32[]{:S(2)}, u32[]{:S(2)}) collective-permute-start(bf16[48,1664]{1,0:T(8,128)(2,1)S(1)} %get-tuple-element.191), channel_id=1, source_target_pairs={{0,2},{1,3},{2,0},{3,1},{4,6},{5,7},{6,4},{7,5},{8,10},{9,11},{10,... | collective-permute-start | bytes 479240 | tf_op jit(solution)/shard_map/ppermute | solution.py:104
  236.2 8.3 %collective-permute-start.42 = (bf16[48,1664]{1,0:T(8,128)(2,1)S(1)}, bf16[48,1664]{1,0:T(8,128)(2,1)S(1)}, u32[]{:S(2)}, u32[]{:S(2)}) collective-permute-start(bf16[48,1664]{1,0:T(8,128)(2,1)S(1)} %get-tuple-element.192), channel_id=1, source_target_pairs={{0,4},{1,5},{2,6},{3,7},{4,0},{5,1},{6,2},{7,3},{8,12},{9,13},{10,... | collective-permute-start | bytes 479240 | tf_op jit(solution)/shard_map/ppermute | solution.py:104
  236.3 15.1 %collective-permute-start.43 = (bf16[48,1664]{1,0:T(8,128)(2,1)S(1)}, bf16[48,1664]{1,0:T(8,128)(2,1)S(1)}, u32[]{:S(2)}, u32[]{:S(2)}) collective-permute-start(bf16[48,1664]{1,0:T(8,128)(2,1)S(1)} %get-tuple-element.193), channel_id=1, source_target_pairs={{0,6},{1,7},{2,4},{3,5},{4,2},{5,3},{6,0},{7,1},{8,14},{9,15},{10,... | collective-permute-start | bytes 479240 | tf_op jit(solution)/shard_map/ppermute | solution.py:104
  237.8 4.1 %collective-permute-start.45 = (f32[24,1536]{1,0:T(8,128)S(1)}, f32[24,1536]{1,0:T(8,128)S(1)}, u32[]{:S(2)}, u32[]{:S(2)}) collective-permute-start(f32[24,1536]{1,0:T(8,128)S(1)} %get-tuple-element.216), channel_id=1, source_target_pairs={{0,1},{1,0},{2,3},{3,2},{4,5},{5,4},{6,7},{7,6},{8,9},{9,8},{10,11... | collective-permute-start | bytes 442376 | tf_op jit(solution)/shard_map/ppermute | solution.py:100
  251.6 3.2 %collective-permute-start.44 = (f32[24,1664]{1,0:T(8,128)S(1)}, f32[24,1664]{1,0:T(8,128)S(1)}, u32[]{:S(2)}, u32[]{:S(2)}) collective-permute-start(f32[24,1664]{1,0:T(8,128)S(1)} %get-tuple-element.214), channel_id=1, source_target_pairs={{0,1},{1,0},{2,3},{3,2},{4,5},{5,4},{6,7},{7,6},{8,9},{9,8},{10,11... | collective-permute-start | bytes 479240 | tf_op jit(solution)/shard_map/ppermute | solution.py:100
